TPU v7x, 32 devices: a whole 2x2x4 slice. The times are simulated.
32 devices in a mesh: grp: 4 (over x, core), sub: 8 (over z, y).
Axes of the slice: x: 2, y: 2, z: 4, core: 2. Of those that a mesh axis runs over, the one named last changes fastest.
Arguments:
- states: bfloat16 [131072, 128], P(('grp', 'sub')), may hold values from -6 to 6
- cotangent: bfloat16 [131072, 128], P(('grp', 'sub')), may hold values from -6 to 6
- fine_self: bfloat16 [128, 128], replicated, may hold values from -0.5 to 0.5
- fine_other: bfloat16 [128, 128], replicated, may hold values from -0.5 to 0.5
- fine_node: bfloat16 [128, 128], replicated, may hold values from -0.375 to 0.375
- coarse_self: bfloat16 [128, 128], replicated, may hold values from -0.5 to 0.5
- coarse_other: bfloat16 [128, 128], replicated, may hold values from -0.5 to 0.5
- coarse_node: bfloat16 [128, 128], replicated, may hold values from -0.375 to 0.375
- prolong: bfloat16 [128, 128], replicated, may hold values from -0.5 to 0.5
- fine_nbr: int32 [131072, 8], P(('grp', 'sub')), may hold values from 0 to 5119, as said below
- fine_mask: int32 [131072, 8], P(('grp', 'sub')), may hold values 0 or 1
- fine_send_lo: int32 [16384], P(('grp', 'sub')), may hold values from 0 to 4095
- fine_send_hi: int32 [16384], P(('grp', 'sub')), may hold values from 0 to 4095
- coarse_nbr: int32 [8192, 8], P('sub'), may hold values from 0 to 1151, as said below
- coarse_mask: int32 [8192, 8], P('sub'), may hold values 0 or 1
- coarse_send_lo: int32 [512], P('sub'), may hold values from 0 to 1023
- coarse_send_hi: int32 [512], P('sub'), may hold values from 0 to 1023
- coarse_owner: int32 [131072], P(('grp', 'sub')), may hold values from 0 to 1023, as said below
Outputs:
- result: bfloat16 [131072, 128], P(('grp', 'sub'))
- grad_states: bfloat16 [131072, 128], P(('grp', 'sub'))
- grad_weights: float32 [7, 128, 128], replicated
Inputs may be any that keep to these rules, and one draw needn't show every extreme that they name: `coarse_owner`: on the devices of grp index 0 every mid-level cell is named by exactly 4096 // 1024 fine cells of that device; elsewhere names are drawn freely. `fine_nbr`: with B = 64, local row r of a device lies in block b = r // B; each of its slots names a row of block b of the local rows (b * B to b * B + B - 1), or row 4096 + (b % 8) * B + j, or row 4608 + (b % 8) * B + j, for some j below B. `coarse_nbr`: local row r of a partition lies in block b = r // 64; each of its slots names a row of block b of the local rows, or any of the 128 halo rows of the table.
All inputs are finite; a program needn't handle non-finite values. No bound on the sum of `fine_mask` or of `coarse_mask` on one device may be relied on, other than what follows from the above.
Results may differ from a plain program's by a relative error of at most 0.015.
Values may be sent and summed in bfloat16 or wider, within the bound.
No kernel may reach another device: no remote copies, remote signals or barrier semaphores. Data moves between devices by JAX's collectives and lax.ppermute only.
A program may use at most 128 MiB of HBM per device.

v0:
```python
import functools

import jax
import jax.numpy as jnp
from jax import lax
from jax.experimental import pallas as pl
from jax.experimental.pallas import tpu as pltpu
from jax.sharding import PartitionSpec as P

f32 = jnp.float32
bf16 = jnp.bfloat16
BLOCK = 64
PAIR = 2 * BLOCK
NEVER = -1e30
DIGIT = 64.0
VMEM = pl.BlockSpec(memory_space=pltpu.VMEM)
SMEM = pl.BlockSpec(memory_space=pltpu.SMEM)
PARAMS = pltpu.CompilerParams(vmem_limit_bytes=48 * 1024 * 1024)


def dot(a, b):
    return jnp.dot(a, b, preferred_element_type=f32)


def dot_nt(a, b):
    return lax.dot_general(a, b, (((1,), (1,)), ((), ())), preferred_element_type=f32)


def dot_tn(a, b):
    return lax.dot_general(a, b, (((0,), (0,)), ((), ())), preferred_element_type=f32)


def pick(condition):
    return jnp.where(condition, 1.0, 0.0).astype(bf16)


def pick16(values, places):
    return jnp.where(values == places, jnp.ones((), bf16), jnp.zeros((), bf16))


def call(kernel, out_shape, args, in_specs=None, scratch=()):
    many = isinstance(out_shape, (list, tuple))
    return pl.pallas_call(
        kernel,
        out_shape=out_shape,
        in_specs=in_specs or [VMEM] * len(args),
        out_specs=[VMEM] * len(out_shape) if many else VMEM,
        scratch_shapes=list(scratch),
        compiler_params=PARAMS,
    )(*args)


def shape(rows, columns, dtype):
    return jax.ShapeDtypeStruct((rows, columns), dtype)


def slot_columns(pair, nbr, mask, rows, halo_rows):
    lane = lax.broadcasted_iota(jnp.int32, nbr.shape, 1)
    block = 2 * pair + lane // BLOCK
    halo = lax.rem(block, halo_rows // BLOCK) * BLOCK
    column = jnp.where(
        nbr < rows,
        nbr - block * BLOCK,
        jnp.where(
            nbr < rows + halo_rows,
            BLOCK + nbr - rows - halo,
            2 * BLOCK + nbr - rows - halo_rows - halo,
        ),
    )
    return jnp.where(mask > 0, column, 3 * BLOCK).astype(f32)


def selector(columns_t, half):
    first = lax.broadcasted_iota(jnp.int32, (BLOCK, 128), 1).astype(bf16)
    second = (lax.broadcasted_iota(jnp.int32, (BLOCK, 128), 1) + 128).astype(bf16)
    parts = []
    for k in range(8):
        own = columns_t[half * BLOCK : (half + 1) * BLOCK, k : k + 1]
        wide = jnp.broadcast_to(own, (BLOCK, 128)).astype(bf16)
        parts.append(jnp.concatenate([pick16(wide, first), pick16(wide, second)], 1))
    return jnp.concatenate(parts, 0)


def selector_t(columns, rolled, half):
    lane = lax.broadcasted_iota(jnp.int32, (1, 128), 1)
    place = lax.broadcasted_iota(jnp.int32, (3 * BLOCK, 128), 0).astype(bf16)
    parts = []
    for j in range(4):
        left, right = (columns, rolled) if half == 0 else (rolled, columns)
        row = jnp.where(lane < BLOCK, left[2 * j : 2 * j + 1], right[2 * j + 1 : 2 * j + 2])
        wide = jnp.broadcast_to(row, (3 * BLOCK, 128)).astype(bf16)
        parts.append(pick16(wide, place))
    return jnp.concatenate(parts, 1)


def window_of(far_half, halo_ref, block, halo_rows):
    start = pl.multiple_of(lax.rem(block, halo_rows // BLOCK) * BLOCK, BLOCK)
    return jnp.concatenate(
        [
            far_half,
            halo_ref[pl.ds(start, BLOCK), :],
            halo_ref[pl.ds(halo_rows + start, BLOCK), :],
            jnp.full((BLOCK, far_half.shape[1]), NEVER, bf16),
        ],
        0,
    )


def rows_of(pair):
    return pl.ds(pl.multiple_of(pair * PAIR, PAIR), PAIR)


def gather_kernel(lo_ref, hi_ref, x_ref, up_ref, down_ref, wide, up, down):
    wide[...] = x_ref[...].astype(f32)

    def step(r, carry):
        up[pl.ds(r, 1), :] = wide[pl.ds(hi_ref[r], 1), :]
        down[pl.ds(r, 1), :] = wide[pl.ds(lo_ref[r], 1), :]
        return carry

    lax.fori_loop(0, up.shape[0], step, None, unroll=16)
    up_ref[...] = up[...].astype(bf16)
    down_ref[...] = down[...].astype(bf16)


def gather_rows(x, send_lo, send_hi):
    rows, features = x.shape
    count = send_lo.shape[0]
    out = shape(count, features, bf16)
    return call(
        gather_kernel,
        [out, out],
        [send_lo, send_hi, x],
        [SMEM, SMEM, VMEM],
        [
            pltpu.VMEM((rows, features), f32),
            pltpu.VMEM((count, features), f32),
            pltpu.VMEM((count, features), f32),
        ],
    )


def owner_sums(owner_ref, tile, values):
    place = lax.broadcasted_iota(jnp.int32, (128, 128), 0) + tile * 128
    groups = owner_ref.shape[0]
    rows = jnp.concatenate(
        [pick(owner_ref[q : q + 1, :] == place) for q in range(groups)], 1
    )
    return dot(rows, values)


def cotangent_kernel(owner_ref, g_ref, out_ref, *, coarse_rows):
    tiles = coarse_rows // 128

    def step(tile, carry):
        out_ref[rows_of(tile), :] = owner_sums(owner_ref, tile, g_ref[...]).astype(bf16)
        return carry

    lax.fori_loop(0, tiles, step, None)
    owner = owner_ref[...]
    high, low = owner // 128, lax.rem(owner, 128)
    groups = owner.shape[0]
    place = lax.broadcasted_iota(jnp.int32, (128, 128), 0)
    high_rows = jnp.concatenate(
        [pick(high[q : q + 1, :] == place[:tiles]) for q in range(groups)], 1
    )
    low_rows = jnp.concatenate(
        [pick(low[q : q + 1, :] == place) for q in range(groups)], 1
    )
    counts = dot_nt(high_rows, low_rows)
    most = jnp.floor(counts * (1 / DIGIT))
    out_ref[coarse_rows:, :] = jnp.concatenate([most, counts - DIGIT * most], 0).astype(bf16)


def fine_forward_kernel(
    h_ref,
    lower_ref,
    upper_ref,
    self_ref,
    other_ref,
    node_ref,
    nbr_ref,
    mask_ref,
    owner_ref,
    summed_ref,
    totals_ref,
    halo,
    new,
):
    rows = h_ref.shape[0]
    halo_rows = lower_ref.shape[0]
    other = other_ref[...] * 0.5
    both = jnp.concatenate([self_ref[...] * 0.5, other], 1)
    halo[:halo_rows, :] = dot(lower_ref[...], other).astype(bf16)
    halo[halo_rows:, :] = dot(upper_ref[...], other).astype(bf16)

    def step(pair, carry):
        here = rows_of(pair)
        h = h_ref[here, :]
        terms = dot(h, both)
        own, far = terms[:, :128], terms[:, 128:].astype(bf16)
        columns = slot_columns(pair, nbr_ref[:, here], mask_ref[:, here], rows, halo_rows)
        columns_t = columns.T
        sums = []
        for half in range(2):
            part = slice(half * BLOCK, (half + 1) * BLOCK)
            window = window_of(far[part], halo, 2 * pair + half, halo_rows)
            picked = dot(selector(columns_t, half), window)
            total = None
            for k in range(8):
                y = picked[k * BLOCK : (k + 1) * BLOCK] + own[part]
                value = y + y * jnp.tanh(y)
                total = value if total is None else total + value
            sums.append(total)
        summed = jnp.concatenate(sums, 0).astype(bf16)
        summed_ref[here, :] = summed
        new[here, :] = (h.astype(f32) + dot(summed, node_ref[...])).astype(bf16)
        return carry

    lax.fori_loop(0, rows // PAIR, step, None)

    def tile_step(tile, carry):
        totals_ref[rows_of(tile), :] = owner_sums(owner_ref, tile, new[...]).astype(bf16)
        return carry

    lax.fori_loop(0, totals_ref.shape[0] // 128, tile_step, None)


def count_columns(counts_ref):
    return counts_ref[...].T


def coarse_input_kernel(totals_ref, counts_ref, lo_ref, hi_ref, cin_ref, up_ref, down_ref):
    per_row = count_columns(counts_ref)
    for tile in range(totals_ref.shape[0] // 128):
        here = slice(tile * 128, (tile + 1) * 128)
        cin_ref[here, :] = (totals_ref[here, :] / per_row[:, tile : tile + 1]).astype(bf16)
    cin = cin_ref[...]
    place = lax.broadcasted_iota(jnp.int32, (cin.shape[0], lo_ref.shape[1]), 0)
    up_ref[...] = dot_tn(pick(hi_ref[...] == place), cin).astype(bf16)
    down_ref[...] = dot_tn(pick(lo_ref[...] == place), cin).astype(bf16)


def pair_backward(pair, own, far, halo, halo_rows, columns, grad_sum, halo_grad):
    columns_t = columns.T
    rolled = pltpu.roll(columns, BLOCK, 1)
    sums, downs, locals_ = [], [], []
    for half in range(2):
        part = slice(half * BLOCK, (half + 1) * BLOCK)
        block = 2 * pair + half
        window = window_of(far[part], halo, block, halo_rows)
        picked = dot(selector(columns_t, half), window)
        total, down, pieces = None, None, []
        for k in range(8):
            y = picked[k * BLOCK : (k + 1) * BLOCK] + own[part]
            t = jnp.tanh(y)
            up = 1.0 + t
            value = y * up
            grad = grad_sum[part] * (up * (1.0 + (y - y * t)))
            total = value if total is None else total + value
            down = grad if down is None else down + grad
            pieces.append(grad.astype(bf16))
        grad_window = dot(selector_t(columns, rolled, half), jnp.concatenate(pieces, 0))
        start = pl.multiple_of(lax.rem(block, halo_rows // BLOCK) * BLOCK, BLOCK)
        for side in range(2):
            place = pl.ds(side * halo_rows + start, BLOCK)
            halo_grad[place, :] += grad_window[(side + 1) * BLOCK : (side + 2) * BLOCK]
        sums.append(total)
        downs.append(down)
        locals_.append(grad_window[:BLOCK])
    return (
        jnp.concatenate(sums, 0),
        jnp.concatenate(downs, 0),
        jnp.concatenate(locals_, 0),
    )


def coarse_kernel(
    cin_ref,
    lower_ref,
    upper_ref,
    sums_ref,
    self_ref,
    other_ref,
    node_ref,
    prolong_ref,
    nbr_ref,
    mask_ref,
    part_ref,
    lower_grad_ref,
    upper_grad_ref,
    fine_ref,
    weights_ref,
    halo,
    halo_grad,
    summed,
    ups,
    downs,
):
    rows = cin_ref.shape[0]
    halo_rows = lower_ref.shape[0]
    other = other_ref[...] * 0.5
    both = jnp.concatenate([self_ref[...] * 0.5, other], 1)
    plain = jnp.concatenate([self_ref[...], other_ref[...]], 1)
    halo[:halo_rows, :] = dot(lower_ref[...], other).astype(bf16)
    halo[halo_rows:, :] = dot(upper_ref[...], other).astype(bf16)
    halo_grad[...] = jnp.zeros_like(halo_grad)

    def step(pair, carry):
        here = rows_of(pair)
        cin = cin_ref[here, :]
        grad_up = dot_nt(sums_ref[here, :], prolong_ref[...])
        up16 = grad_up.astype(bf16)
        grad_sum = dot_nt(up16, node_ref[...]) * 0.5
        terms = dot(cin, both)
        columns = slot_columns(pair, nbr_ref[:, here], mask_ref[:, here], rows, halo_rows)
        total, down, local = pair_backward(
            pair, terms[:, :128], terms[:, 128:].astype(bf16), halo, halo_rows, columns,
            grad_sum, halo_grad,
        )
        both_down = jnp.concatenate([down, local], 1).astype(bf16)
        summed[here, :] = total.astype(bf16)
        ups[here, :] = up16
        downs[here, :] = both_down
        part_ref[here, :] = grad_up + dot_nt(both_down, plain)
        return carry

    lax.fori_loop(0, rows // PAIR, step, None)
    lower_grad = halo_grad[:halo_rows, :].astype(bf16)
    upper_grad = halo_grad[halo_rows:, :].astype(bf16)
    lower_grad_ref[...] = lower_grad
    upper_grad_ref[...] = upper_grad
    cin = cin_ref[...]
    out = (cin.astype(f32) + dot(summed[...], node_ref[...])).astype(bf16)
    fine_ref[...] = dot(out, prolong_ref[...]).astype(bf16)
    pair_grad = dot_tn(cin, downs[...])
    other_grad = (
        pair_grad[:, 128:] + dot_tn(lower_ref[...], lower_grad) + dot_tn(upper_ref[...], upper_grad)
    )
    weights_ref[0:128, :] = pair_grad[:, :128]
    weights_ref[128:256, :] = other_grad
    weights_ref[256:384, :] = dot_tn(summed[...], ups[...])
    weights_ref[384:512, :] = dot_tn(out, sums_ref[...])


def owner_column(owner_ref, pair):
    row = owner_ref[pl.ds(pair, 1), :].astype(f32)
    return jnp.broadcast_to(row, (8, 128)).T[:, 0:1]


def owner_rows(owner_ref, pair, values):
    wide = jnp.broadcast_to(owner_column(owner_ref, pair), (128, 128))
    lane = lax.broadcasted_iota(jnp.int32, (128, 128), 1).astype(f32)
    tiles = values.shape[0] // 128
    rows = jnp.concatenate([pick(wide == lane + 128.0 * tile) for tile in range(tiles)], 1)
    return dot(rows, values)


def result_kernel(h_ref, summed_ref, node_ref, owner_ref, fine_ref, out_ref):
    def step(pair, carry):
        here = rows_of(pair)
        updated = h_ref[here, :].astype(f32) + dot(summed_ref[here, :], node_ref[...])
        out_ref[here, :] = (updated + owner_rows(owner_ref, pair, fine_ref[...])).astype(bf16)
        return carry

    lax.fori_loop(0, h_ref.shape[0] // PAIR, step, None)


def fine_backward_kernel(
    h_ref,
    lower_ref,
    upper_ref,
    g_ref,
    summed_ref,
    self_ref,
    other_ref,
    node_ref,
    nbr_ref,
    mask_ref,
    owner_ref,
    part_ref,
    counts_ref,
    back_ref,
    sends_ref,
    coarse_other_ref,
    out_ref,
    lower_grad_ref,
    upper_grad_ref,
    weights_ref,
    halo,
    halo_grad,
    mean,
    ups,
    downs,
):
    rows = h_ref.shape[0]
    halo_rows = lower_ref.shape[0]
    coarse_rows = part_ref.shape[0]
    other = other_ref[...] * 0.5
    both = jnp.concatenate([self_ref[...] * 0.5, other], 1)
    plain = jnp.concatenate([self_ref[...], other_ref[...]], 1)
    halo[:halo_rows, :] = dot(lower_ref[...], other).astype(bf16)
    halo[halo_rows:, :] = dot(upper_ref[...], other).astype(bf16)
    halo_grad[...] = jnp.zeros_like(halo_grad)
    place = lax.broadcasted_iota(jnp.int32, (coarse_rows, sends_ref.shape[1]), 0)
    back = dot_nt(back_ref[...], coarse_other_ref[...]).astype(bf16)
    grad_in = part_ref[...] + dot(pick(sends_ref[...] == place), back)
    per_row = count_columns(counts_ref)
    for tile in range(coarse_rows // 128):
        here = slice(tile * 128, (tile + 1) * 128)
        mean[here, :] = (grad_in[here, :] / per_row[:, tile : tile + 1]).astype(bf16)

    def step(pair, carry):
        here = rows_of(pair)
        h = h_ref[here, :]
        grad_up = g_ref[here, :].astype(f32) + owner_rows(owner_ref, pair, mean[...])
        up16 = grad_up.astype(bf16)
        grad_sum = dot_nt(up16, node_ref[...]) * 0.5
        terms = dot(h, both)
        columns = slot_columns(pair, nbr_ref[:, here], mask_ref[:, here], rows, halo_rows)
        _, down, local = pair_backward(
            pair, terms[:, :128], terms[:, 128:].astype(bf16), halo, halo_rows, columns,
            grad_sum, halo_grad,
        )
        both_down = jnp.concatenate([down, local], 1).astype(bf16)
        ups[here, :] = up16
        downs[here, :] = both_down
        out_ref[here, :] = grad_up + dot_nt(both_down, plain)
        return carry

    lax.fori_loop(0, rows // PAIR, step, None)
    lower_grad = halo_grad[:halo_rows, :].astype(bf16)
    upper_grad = halo_grad[halo_rows:, :].astype(bf16)
    lower_grad_ref[...] = lower_grad
    upper_grad_ref[...] = upper_grad
    pair_grad = dot_tn(h_ref[...], downs[...])
    weights_ref[0:128, :] = pair_grad[:, :128]
    weights_ref[128:256, :] = (
        pair_grad[:, 128:] + dot_tn(lower_ref[...], lower_grad) + dot_tn(upper_ref[...], upper_grad)
    )
    weights_ref[256:384, :] = dot_tn(summed_ref[...], ups[...])


def finish_kernel(part_ref, up_ref, down_ref, lo_ref, hi_ref, other_ref, out_ref):
    other = other_ref[...]
    back = jnp.concatenate([dot_nt(up_ref[...], other), dot_nt(down_ref[...], other)], 0)
    back = back.astype(bf16)
    sends = jnp.concatenate([lo_ref[...], hi_ref[...]], 1)
    place = lax.broadcasted_iota(jnp.int32, (PAIR, sends.shape[1]), 0)

    def step(pair, carry):
        here = rows_of(pair)
        rows = pick(sends - pair * PAIR == place)
        out_ref[here, :] = (part_ref[here, :] + dot(rows, back)).astype(bf16)
        return carry

    lax.fori_loop(0, part_ref.shape[0] // PAIR, step, None)


def shifted(block, axis, distance):
    devices = range(lax.axis_size(axis))
    route = [(i - distance, i) for i in devices if i - distance in devices]
    return lax.ppermute(block, axis, route)


def swapped(block, axis, distance):
    return lax.ppermute(block, axis, [(i, i ^ distance) for i in range(lax.axis_size(axis))])


def total_over(block, axis):
    distance = 1
    total = block
    while distance < lax.axis_size(axis):
        other = swapped(total.astype(bf16), axis, distance)
        total = total.astype(f32) + other.astype(f32)
        distance *= 2
    return total


def total_over_all(block, axes):
    devices = lax.axis_size(axes)
    share = block.shape[0] // devices
    parts = lax.all_to_all(
        block.astype(bf16).reshape(devices, share, 128), axes, 0, 0, tiled=False
    )
    mine = parts.astype(f32).sum(0).astype(bf16)
    return lax.all_to_all(
        jnp.broadcast_to(mine[None], (devices, share, 128)), axes, 0, 0, tiled=False
    ).reshape(block.shape)


def per_device(
    states,
    cotangent,
    fine_self,
    fine_other,
    fine_node,
    coarse_self,
    coarse_other,
    coarse_node,
    prolong,
    fine_nbr,
    fine_mask,
    fine_send_lo,
    fine_send_hi,
    coarse_nbr,
    coarse_mask,
    coarse_send_lo,
    coarse_send_hi,
    coarse_owner,
):
    rows, features = states.shape
    coarse_rows = coarse_nbr.shape[0]
    halo_rows = fine_send_lo.shape[0]
    coarse_halo = coarse_send_lo.shape[0]
    count_rows = coarse_rows // 128
    owner = coarse_owner.reshape(rows // 128, 128)
    fine_nbr, fine_mask = fine_nbr.T, fine_mask.T
    coarse_nbr, coarse_mask = coarse_nbr.T, coarse_mask.T
    coarse_lo, coarse_hi = coarse_send_lo[None], coarse_send_hi[None]

    going_up, going_down = gather_rows(states, fine_send_lo, fine_send_hi)
    lower = shifted(going_up, "sub", 1)
    upper = shifted(going_down, "sub", -1)

    sums_counts = call(
        functools.partial(cotangent_kernel, coarse_rows=coarse_rows),
        shape(coarse_rows + 2 * count_rows, features, bf16),
        [owner, cotangent],
    )
    sums_counts = total_over(sums_counts, "grp")
    grad_sums = sums_counts[:coarse_rows].astype(bf16)
    counts = (
        DIGIT * sums_counts[coarse_rows : coarse_rows + count_rows]
        + sums_counts[coarse_rows + count_rows :]
    )

    summed, totals = call(
        fine_forward_kernel,
        [shape(rows, features, bf16), shape(coarse_rows, features, bf16)],
        [states, lower, upper, fine_self, fine_other, fine_node, fine_nbr, fine_mask, owner],
        scratch=[
            pltpu.VMEM((2 * halo_rows, features), bf16),
            pltpu.VMEM((rows, features), bf16),
        ],
    )
    totals = total_over(totals, "grp")

    coarse_in, coarse_up, coarse_down = call(
        coarse_input_kernel,
        [
            shape(coarse_rows, features, bf16),
            shape(coarse_halo, features, bf16),
            shape(coarse_halo, features, bf16),
        ],
        [totals, counts, coarse_lo, coarse_hi],
    )
    coarse_lower = shifted(coarse_up, "sub", 1)
    coarse_upper = shifted(coarse_down, "sub", -1)

    coarse_part, lower_grad, upper_grad, fine_term, coarse_weights = call(
        coarse_kernel,
        [
            shape(coarse_rows, features, f32),
            shape(coarse_halo, features, bf16),
            shape(coarse_halo, features, bf16),
            shape(coarse_rows, features, bf16),
            shape(4 * features, features, f32),
        ],
        [
            coarse_in, coarse_lower, coarse_upper, grad_sums,
            coarse_self, coarse_other, coarse_node, prolong, coarse_nbr, coarse_mask,
        ],
        scratch=[
            pltpu.VMEM((2 * coarse_halo, features), bf16),
            pltpu.VMEM((2 * coarse_halo, features), f32),
            pltpu.VMEM((coarse_rows, features), bf16),
            pltpu.VMEM((coarse_rows, features), bf16),
            pltpu.VMEM((coarse_rows, 2 * features), bf16),
        ],
    )
    back_up = shifted(upper_grad, "sub", 1)
    back_down = shifted(lower_grad, "sub", -1)
    coarse_back = jnp.concatenate([back_up, back_down], 0)
    coarse_sends = jnp.concatenate([coarse_lo, coarse_hi], 1)

    result = call(
        result_kernel,
        shape(rows, features, bf16),
        [states, summed, fine_node, owner, fine_term],
    )

    grad_part, lower_grad, upper_grad, fine_weights = call(
        fine_backward_kernel,
        [
            shape(rows, features, f32),
            shape(halo_rows, features, bf16),
            shape(halo_rows, features, bf16),
            shape(3 * features, features, f32),
        ],
        [
            states, lower, upper, cotangent, summed, fine_self, fine_other, fine_node,
            fine_nbr, fine_mask, owner, coarse_part, counts, coarse_back, coarse_sends,
            coarse_other,
        ],
        scratch=[
            pltpu.VMEM((2 * halo_rows, features), bf16),
            pltpu.VMEM((2 * halo_rows, features), f32),
            pltpu.VMEM((coarse_rows, features), bf16),
            pltpu.VMEM((rows, features), bf16),
            pltpu.VMEM((rows, 2 * features), bf16),
        ],
    )
    back_up = shifted(upper_grad, "sub", 1)
    back_down = shifted(lower_grad, "sub", -1)

    scale = 1.0 / lax.axis_size("grp")
    weights = jnp.concatenate(
        [fine_weights, coarse_weights * scale, jnp.zeros((features, features), f32)], 0
    )
    weights = total_over_all(weights, ("grp", "sub"))
    grad_weights = weights[: 7 * features].astype(f32).reshape(7, features, features)

    grad_states = call(
        finish_kernel,
        shape(rows, features, bf16),
        [grad_part, back_up, back_down, fine_send_lo[None], fine_send_hi[None], fine_other],
    )
    return (result, grad_states, grad_weights)


def solution(mesh):
    fine = P(("grp", "sub"), None)
    fine_row = P(("grp", "sub"))
    in_specs = (
        (fine, fine)
        + (P(),) * 7
        + (fine, fine, fine_row, fine_row)
        + (P("sub", None), P("sub", None), P("sub"), P("sub"), fine_row)
    )
    return jax.shard_map(
        per_device, mesh=mesh, in_specs=in_specs, out_specs=(fine, fine, P()), check_vma=False
    )
```

profile of v0, /device:TPU:0, one launch (start us, length us, event | category | flops | bytes accessed | tf_op | source)
XLA Modules:
  0.0 179.7 jit_solution(10390800431699947931)
XLA Ops:
  0.7 1.3 copy-done.2
  2.7 3.8 %shard_map.195 = bf16[1040,128]{1,0:T(8,128)(2,1)S(1)} custom-call(s32[32,128]{1,0:T(8,128)S(1)} %bitcast.18, bf16[4096,128]{1,0:T(8,128)(2,1)S(1)} %copy-done.2), custom_call_target="tpu_custom_call" | custom-call | tf_op jit(solution)/shard_map/pallas_call | solution.py:43
  9.5 1.6 shard_map.193
  11.1 4.4 %collective-permute-start = (bf16[512,128]{1,0:T(8,128)(2,1)S(1)}, bf16[512,128]{1,0:T(8,128)(2,1)S(1)}, u32[]{:S(2)}, u32[]{:S(2)}) collective-permute-start(bf16[512,128]{1,0:T(8,128)(2,1)S(1)} %get-tuple-element.19), channel_id=1, source_target_pairs={{0,1},{1,2},{2,3},{3,4},{4,5},{5,6},{6,7},{8,9},{9,10},{10,11},{11... | collective-permute-start | bytes 393224 | tf_op jit(solution)/shard_map/ppermute | solution.py:463
  16.8 2.1 %collective-permute-done.lower_ref = bf16[512,128]{1,0:T(8,128)(2,1)S(1)} collective-permute-done((bf16[512,128]{1,0:T(8,128)(2,1)S(1)}, bf16[512,128]{1,0:T(8,128)(2,1)S(1)}, u32[]{:S(2)}, u32[]{:S(2)}) %collective-permute-start) | collective-permute-done | bytes 131104 | tf_op jit(solution)/shard_map/ppermute | solution.py:463
  18.9 4.1 %collective-permute-done.1.upper_ref = bf16[512,128]{1,0:T(8,128)(2,1)S(1)} collective-permute-done((bf16[512,128]{1,0:T(8,128)(2,1)S(1)}, bf16[512,128]{1,0:T(8,128)(2,1)S(1)}, u32[]{:S(2)}, u32[]{:S(2)}) %collective-permute-start.1) | collective-permute-done | bytes 131104 | tf_op jit(solution)/shard_map/ppermute | solution.py:463
  25.4 23.3 %shard_map.194 = (bf16[4096,128]{1,0:T(8,128)(2,1)S(1)}, bf16[1024,128]{1,0:T(8,128)(2,1)S(1)}) custom-call(bf16[4096,128]{1,0:T(8,128)(2,1)S(1)} %copy-done.1, bf16[512,128]{1,0:T(8,128)(2,1)S(1)} %collective-permute-done.lower_ref, bf16[512,128]{1,0:T(8,128)(2,1)S(1)} %collective-permute-done.1.upper_ref, bf16[128,128]{1,0:T(8,128)(2,1)S(1)} %copy-done.13, ...), custom_call_target="tpu_custom_call" | custom-call | tf_op jit(solution)/shard_map/pallas_call | solution.py:43
  48.9 1.5 collective-permute-start.5
  50.6 1.4 collective-permute-start.3
  51.9 6.3 %collective-permute-done.5 = bf16[1040,128]{1,0:T(8,128)(2,1)S(1)} collective-permute-done((bf16[1040,128]{1,0:T(8,128)(2,1)S(1)}, bf16[1040,128]{1,0:T(8,128)(2,1)S(1)}, u32[]{:S(2)}, u32[]{:S(2)}) %collective-permute-start.5) | collective-permute-done | bytes 266272 | tf_op jit(solution)/shard_map/ppermute | solution.py:467
  58.3 5.1 %collective-permute-done.3 = bf16[1024,128]{1,0:T(8,128)(2,1)S(1)} collective-permute-done((bf16[1024,128]{1,0:T(8,128)(2,1)S(1)}, bf16[1024,128]{1,0:T(8,128)(2,1)S(1)}, u32[]{:S(2)}, u32[]{:S(2)}) %collective-permute-start.3) | collective-permute-done | bytes 262176 | tf_op jit(solution)/shard_map/ppermute | solution.py:467
  64.1 4.3 %collective-permute-start.6 = (bf16[64,128]{1,0:T(8,128)(2,1)S(1)}, bf16[64,128]{1,0:T(8,128)(2,1)S(1)}, u32[]{:S(2)}, u32[]{:S(2)}) collective-permute-start(bf16[64,128]{1,0:T(8,128)(2,1)S(1)} %get-tuple-element.24), channel_id=1, source_target_pairs={{0,1},{1,2},{2,3},{3,4},{4,5},{5,6},{6,7},{8,9},{9,10},{10,11},{11... | collective-permute-start | bytes 49160 | tf_op jit(solution)/shard_map/ppermute | solution.py:463
  69.9 4.2 %collective-permute-done.7.upper_ref = bf16[64,128]{1,0:T(8,128)(2,1)S(1)} collective-permute-done((bf16[64,128]{1,0:T(8,128)(2,1)S(1)}, bf16[64,128]{1,0:T(8,128)(2,1)S(1)}, u32[]{:S(2)}, u32[]{:S(2)}) %collective-permute-start.7) | collective-permute-done | bytes 16416 | tf_op jit(solution)/shard_map/ppermute | solution.py:463
  74.1 9.4 %shard_map.197 = (f32[1024,128]{1,0:T(8,128)S(1)}, bf16[64,128]{1,0:T(8,128)(2,1)S(1)}, bf16[64,128]{1,0:T(8,128)(2,1)S(1)}, bf16[1024,128]{1,0:T(8,128)(2,1)S(1)}, f32[512,128]{1,0:T(8,128)S(1)}) custom-call(bf16[1024,128]{1,0:T(8,128)(2,1)S(1)} %get-tuple-element.23.cin_ref, bf16[64,128]{1,0:T(8,128)(2,1)S(1)} %collective-permute-done.6.lower_ref, ...), custom_call_target="tpu_custom_call" | custom-call | tf_op jit(solution)/shard_map/pallas_call | solution.py:43
  83.5 4.0 %collective-permute-start.8 = (bf16[64,128]{1,0:T(8,128)(2,1)S(1)}, bf16[64,128]{1,0:T(8,128)(2,1)S(1)}, u32[]{:S(2)}, u32[]{:S(2)}) collective-permute-start(bf16[64,128]{1,0:T(8,128)(2,1)S(1)} %get-tuple-element.28), channel_id=1, source_target_pairs={{0,1},{1,2},{2,3},{3,4},{4,5},{5,6},{6,7},{8,9},{9,10},{10,11},{11... | collective-permute-start | bytes 49160 | tf_op jit(solution)/shard_map/ppermute | solution.py:463
  87.5 1.3 collective-permute-start.9
  88.9 4.2 %collective-permute-done.9 = bf16[64,128]{1,0:T(8,128)(2,1)S(1)} collective-permute-done((bf16[64,128]{1,0:T(8,128)(2,1)S(1)}, bf16[64,128]{1,0:T(8,128)(2,1)S(1)}, u32[]{:S(2)}, u32[]{:S(2)}) %collective-permute-start.9) | collective-permute-done | bytes 16416 | tf_op jit(solution)/shard_map/ppermute | solution.py:463
  93.2 41.8 %shard_map.199 = (f32[4096,128]{1,0:T(8,128)}, bf16[512,128]{1,0:T(8,128)(2,1)S(1)}, bf16[512,128]{1,0:T(8,128)(2,1)S(1)}, f32[384,128]{1,0:T(8,128)S(1)}) custom-call(bf16[4096,128]{1,0:T(8,128)(2,1)S(1)} %copy-done.1, bf16[512,128]{1,0:T(8,128)(2,1)S(1)} %collective-permute-done.lower_ref, bf16[512,128]{1,0:T(8,128)(2,1)S(1)} %collective-permute-done.1.upper_ref, ...), custom_call_target="tpu_custom_call" | custom-call | tf_op jit(solution)/shard_map/pallas_call | solution.py:43
  135.1 14.7 %all_to_all.10 = bf16[32,32,128]{2,1,0:T(8,128)(2,1)S(1)} all-to-all(bf16[32,32,128]{2,1,0:T(8,128)(2,1)S(1)} %bitcast.30), channel_id=1, replica_groups=mesh['grp'=4,'sub'=8] {'grp','sub'}, dimensions={0} | all-to-all | bytes 524288 | tf_op jit(solution)/shard_map/all_to_all | solution.py:483
  150.7 2.6 %all-to-all-start.1 = ((bf16[32,32,128]{2,1,0:T(8,128)(2,1)}), bf16[32,32,128]{2,1,0:T(8,128)(2,1)S(1)}, u32[]{:S(2)}, u32[]{:S(2)}) async-start(bf16[32,32,128]{2,1,0:T(8,128)(2,1)} %broadcast_in_dim.26), calls=%async_computation.1 | async-start | bytes 524288 | tf_op jit(solution)/shard_map/all_to_all | solution.py:487
  153.3 3.7 %collective-permute-start.10 = (bf16[512,128]{1,0:T(8,128)(2,1)S(1)}, bf16[512,128]{1,0:T(8,128)(2,1)S(1)}, u32[]{:S(2)}, u32[]{:S(2)}) collective-permute-start(bf16[512,128]{1,0:T(8,128)(2,1)S(1)} %get-tuple-element.31), channel_id=1, source_target_pairs={{0,1},{1,2},{2,3},{3,4},{4,5},{5,6},{6,7},{8,9},{9,10},{10,11},{11... | collective-permute-start | bytes 393224 | tf_op jit(solution)/shard_map/ppermute | solution.py:463
  157.0 1.3 collective-permute-start.11
  158.3 12.3 %shard_map.198 = bf16[4096,128]{1,0:T(8,128)(2,1)} custom-call(bf16[4096,128]{1,0:T(8,128)(2,1)S(1)} %copy-done.1, bf16[4096,128]{1,0:T(8,128)(2,1)S(1)} %get-tuple-element.21.summed_ref, bf16[128,128]{1,0:T(8,128)(2,1)S(1)} %copy-done.8, s32[32,128]{1,0:T(8,128)S(1)} %bitcast.21, bf16[1024,128]{1,0:T(8,128)(2,1)S(1)} %get-tuple-element.26.fine_ref), custom_call_target="tpu_custom_call" | custom-call | tf_op jit(solution)/shard_map/pallas_call | solution.py:43
  170.6 8.3 %shard_map.200 = bf16[4096,128]{1,0:T(8,128)(2,1)} custom-call(f32[4096,128]{1,0:T(8,128)S(1)} %copy-done.4, bf16[512,128]{1,0:T(8,128)(2,1)S(1)} %collective-permute-done.10.up_ref, bf16[512,128]{1,0:T(8,128)(2,1)S(1)} %collective-permute-done.11.down_ref, s32[1,512]{1,0:T(1,128)S(1)} %bitcast.24, s32[1,512]{1,0:T(1,128)S(1)} %bitcast.25, ...), custom_call_target="tpu_custom_call" | custom-call | tf_op jit(solution)/shard_map/pallas_call | solution.py:43
  (82 shorter events, 11.8 us)
Async XLA Ops:
  0.6 22.4 %copy-start.1 = (bf16[4096,128]{1,0:T(8,128)(2,1)S(1)}, bf16[4096,128]{1,0:T(8,128)(2,1)}, u32[]{:S(2)}) copy-start(bf16[4096,128]{1,0:T(8,128)(2,1)} %h_ref.5) | copy-start | bytes 3145732
  6.5 42.3 %collective-permute-start.4 = (bf16[1040,128]{1,0:T(8,128)(2,1)S(1)}, bf16[1040,128]{1,0:T(8,128)(2,1)S(1)}, u32[]{:S(2)}, u32[]{:S(2)}) collective-permute-start(bf16[1040,128]{1,0:T(8,128)(2,1)S(1)} %shard_map.195), channel_id=1, source_target_pairs={{0,8},{8,0},{16,24},{24,16},{1,9},{9,1},{17,25},{25,17},{2,10},{10... | collective-permute-start | bytes 798728 | tf_op jit(solution)/shard_map/ppermute | solution.py:467
  11.1 7.8 %collective-permute-start = (bf16[512,128]{1,0:T(8,128)(2,1)S(1)}, bf16[512,128]{1,0:T(8,128)(2,1)S(1)}, u32[]{:S(2)}, u32[]{:S(2)}) collective-permute-start(bf16[512,128]{1,0:T(8,128)(2,1)S(1)} %get-tuple-element.19), channel_id=1, source_target_pairs={{0,1},{1,2},{2,3},{3,4},{4,5},{5,6},{6,7},{8,9},{9,10},{10,11},{11... | collective-permute-start | bytes 393224 | tf_op jit(solution)/shard_map/ppermute | solution.py:463
  15.5 7.5 %collective-permute-start.1 = (bf16[512,128]{1,0:T(8,128)(2,1)S(1)}, bf16[512,128]{1,0:T(8,128)(2,1)S(1)}, u32[]{:S(2)}, u32[]{:S(2)}) collective-permute-start(bf16[512,128]{1,0:T(8,128)(2,1)S(1)} %get-tuple-element.20), channel_id=1, source_target_pairs={{1,0},{2,1},{3,2},{4,3},{5,4},{6,5},{7,6},{9,8},{10,9},{11,10},{12... | collective-permute-start | bytes 393224 | tf_op jit(solution)/shard_map/ppermute | solution.py:463
  48.7 1.8 collective-permute-start.2
  48.9 25.2 %copy-start.15 = (bf16[128,128]{1,0:T(8,128)(2,1)S(1)}, bf16[128,128]{1,0:T(8,128)(2,1)}, u32[]{:S(2)}) copy-start(bf16[128,128]{1,0:T(8,128)(2,1)} %coarse_other_ref.1) | copy-start | bytes 98308
  48.9 25.2 %copy-start.16 = (bf16[128,128]{1,0:T(8,128)(2,1)S(1)}, bf16[128,128]{1,0:T(8,128)(2,1)}, u32[]{:S(2)}) copy-start(bf16[128,128]{1,0:T(8,128)(2,1)} %self_ref.4) | copy-start | bytes 98308
  48.9 25.2 %copy-start.17 = (bf16[128,128]{1,0:T(8,128)(2,1)S(1)}, bf16[128,128]{1,0:T(8,128)(2,1)}, u32[]{:S(2)}) copy-start(bf16[128,128]{1,0:T(8,128)(2,1)} %node_ref.5) | copy-start | bytes 98308
  48.9 25.2 %copy-start.18 = (bf16[128,128]{1,0:T(8,128)(2,1)S(1)}, bf16[128,128]{1,0:T(8,128)(2,1)}, u32[]{:S(2)}) copy-start(bf16[128,128]{1,0:T(8,128)(2,1)} %prolong_ref.1) | copy-start | bytes 98308
  48.9 25.2 %copy-start.19 = (s32[1024,8]{0,1:T(8,128)S(1)}, s32[1024,8]{0,1:T(8,128)}, u32[]{:S(2)}) copy-start(s32[1024,8]{0,1:T(8,128)} %param.31) | copy-start | bytes 98308
  48.9 25.2 %copy-start.20 = (s32[1024,8]{0,1:T(8,128)S(1)}, s32[1024,8]{0,1:T(8,128)}, u32[]{:S(2)}) copy-start(s32[1024,8]{0,1:T(8,128)} %param.32) | copy-start | bytes 98308
  48.9 9.3 %collective-permute-start.5 = (bf16[1040,128]{1,0:T(8,128)(2,1)S(1)}, bf16[1040,128]{1,0:T(8,128)(2,1)S(1)}, u32[]{:S(2)}, u32[]{:S(2)}) collective-permute-start(bf16[1040,128]{1,0:T(8,128)(2,1)S(1)} %fusion), channel_id=1, source_target_pairs={{0,16},{8,24},{16,0},{24,8},{1,17},{9,25},{17,1},{25,9},{2,18},{10... | collective-permute-start | bytes 798728 | tf_op jit(solution)/shard_map/ppermute | solution.py:467
  50.6 12.8 %collective-permute-start.3 = (bf16[1024,128]{1,0:T(8,128)(2,1)S(1)}, bf16[1024,128]{1,0:T(8,128)(2,1)S(1)}, u32[]{:S(2)}, u32[]{:S(2)}) collective-permute-start(bf16[1024,128]{1,0:T(8,128)(2,1)S(1)} %fusion.1), channel_id=1, source_target_pairs={{0,16},{8,24},{16,0},{24,8},{1,17},{9,25},{17,1},{25,9},{2,18},{10... | collective-permute-start | bytes 786440 | tf_op jit(solution)/shard_map/ppermute | solution.py:467
  58.3 34.9 %copy-start.3 = (bf16[4096,128]{1,0:T(8,128)(2,1)S(1)}, bf16[4096,128]{1,0:T(8,128)(2,1)}, u32[]{:S(2)}) copy-start(bf16[4096,128]{1,0:T(8,128)(2,1)} %g_ref.3) | copy-start | bytes 3145732
  58.3 34.8 %copy-start.8 = (bf16[128,128]{1,0:T(8,128)(2,1)S(1)}, bf16[128,128]{1,0:T(8,128)(2,1)}, u32[]{:S(2)}) copy-start(bf16[128,128]{1,0:T(8,128)(2,1)} %node_ref.7) | copy-start | bytes 98308
  58.3 34.8 %copy-start.14 = (bf16[128,128]{1,0:T(8,128)(2,1)S(1)}, bf16[128,128]{1,0:T(8,128)(2,1)}, u32[]{:S(2)}) copy-start(bf16[128,128]{1,0:T(8,128)(2,1)} %self_ref.5) | copy-start | bytes 98308
  64.1 5.8 %collective-permute-start.6 = (bf16[64,128]{1,0:T(8,128)(2,1)S(1)}, bf16[64,128]{1,0:T(8,128)(2,1)S(1)}, u32[]{:S(2)}, u32[]{:S(2)}) collective-permute-start(bf16[64,128]{1,0:T(8,128)(2,1)S(1)} %get-tuple-element.24), channel_id=1, source_target_pairs={{0,1},{1,2},{2,3},{3,4},{4,5},{5,6},{6,7},{8,9},{9,10},{10,11},{11... | collective-permute-start | bytes 49160 | tf_op jit(solution)/shard_map/ppermute | solution.py:463
  68.5 5.6 %collective-permute-start.7 = (bf16[64,128]{1,0:T(8,128)(2,1)S(1)}, bf16[64,128]{1,0:T(8,128)(2,1)S(1)}, u32[]{:S(2)}, u32[]{:S(2)}) collective-permute-start(bf16[64,128]{1,0:T(8,128)(2,1)S(1)} %get-tuple-element.25), channel_id=1, source_target_pairs={{1,0},{2,1},{3,2},{4,3},{5,4},{6,5},{7,6},{9,8},{10,9},{11,10},{12... | collective-permute-start | bytes 49160 | tf_op jit(solution)/shard_map/ppermute | solution.py:463
  83.5 5.4 %collective-permute-start.8 = (bf16[64,128]{1,0:T(8,128)(2,1)S(1)}, bf16[64,128]{1,0:T(8,128)(2,1)S(1)}, u32[]{:S(2)}, u32[]{:S(2)}) collective-permute-start(bf16[64,128]{1,0:T(8,128)(2,1)S(1)} %get-tuple-element.28), channel_id=1, source_target_pairs={{0,1},{1,2},{2,3},{3,4},{4,5},{5,6},{6,7},{8,9},{9,10},{10,11},{11... | collective-permute-start | bytes 49160 | tf_op jit(solution)/shard_map/ppermute | solution.py:463
  87.5 5.6 %collective-permute-start.9 = (bf16[64,128]{1,0:T(8,128)(2,1)S(1)}, bf16[64,128]{1,0:T(8,128)(2,1)S(1)}, u32[]{:S(2)}, u32[]{:S(2)}) collective-permute-start(bf16[64,128]{1,0:T(8,128)(2,1)S(1)} %get-tuple-element.29), channel_id=1, source_target_pairs={{1,0},{2,1},{3,2},{4,3},{5,4},{6,5},{7,6},{9,8},{10,9},{11,10},{12... | collective-permute-start | bytes 49160 | tf_op jit(solution)/shard_map/ppermute | solution.py:463
  149.9 20.7 %copy-start.10 = (bf16[128,128]{1,0:T(8,128)(2,1)S(1)}, bf16[128,128]{1,0:T(8,128)(2,1)}, u32[]{:S(2)}) copy-start(bf16[128,128]{1,0:T(8,128)(2,1)} %other_ref.7) | copy-start | bytes 98308
  150.7 28.3 %all-to-all-start.1 = ((bf16[32,32,128]{2,1,0:T(8,128)(2,1)}), bf16[32,32,128]{2,1,0:T(8,128)(2,1)S(1)}, u32[]{:S(2)}, u32[]{:S(2)}) async-start(bf16[32,32,128]{2,1,0:T(8,128)(2,1)} %broadcast_in_dim.26), calls=%async_computation.1 | async-start | bytes 524288 | tf_op jit(solution)/shard_map/all_to_all | solution.py:487
  153.3 17.3 %collective-permute-start.10 = (bf16[512,128]{1,0:T(8,128)(2,1)S(1)}, bf16[512,128]{1,0:T(8,128)(2,1)S(1)}, u32[]{:S(2)}, u32[]{:S(2)}) collective-permute-start(bf16[512,128]{1,0:T(8,128)(2,1)S(1)} %get-tuple-element.31), channel_id=1, source_target_pairs={{0,1},{1,2},{2,3},{3,4},{4,5},{5,6},{6,7},{8,9},{9,10},{10,11},{11... | collective-permute-start | bytes 393224 | tf_op jit(solution)/shard_map/ppermute | solution.py:463
  157.0 13.6 %collective-permute-start.11 = (bf16[512,128]{1,0:T(8,128)(2,1)S(1)}, bf16[512,128]{1,0:T(8,128)(2,1)S(1)}, u32[]{:S(2)}, u32[]{:S(2)}) collective-permute-start(bf16[512,128]{1,0:T(8,128)(2,1)S(1)} %get-tuple-element.32), channel_id=1, source_target_pairs={{1,0},{2,1},{3,2},{4,3},{5,4},{6,5},{7,6},{9,8},{10,9},{11,10},{12... | collective-permute-start | bytes 393224 | tf_op jit(solution)/shard_map/ppermute | solution.py:463
  (16 other events, 156.4 us)
where the time goes:
time: 181 us; the launch traced here: 180 us
  Pallas kernels  101 us (56%)
  starting transfers between devices  27.6 us (15%)
  waiting for transfers between devices  26.1 us (14%)
  blocking collectives  14.7 us (8%)
  local copies, waits for them, and re-layouts  7.78 us (4%)
    pallas_call x8, Pallas kernels, call(): pl.pallas_call(kernel, out_shape=out_shape, in_specs=in_specs or [VMEM] *...  101 us
    ppermute x8, starting transfers between devices, shifted(): return lax.ppermute(block, axis, route)  21.6 us
    ppermute x8, waiting for transfers between devices, shifted(): return lax.ppermute(block, axis, route)  14.7 us
    all_to_all x1, blocking collectives, total_over_all(): lax.all_to_all(block.astype(bf16).reshape(devices, share, 128), axes, 0,...  14.7 us
    ppermute x4, waiting for transfers between devices, swapped(): lax.ppermute(block, axis, [(i, i ^ distance) for i in range(lax.axis_size...  11.4 us
    unnamed x54, local copies, waits for them, and re-layouts  6.99 us
  transfers between devices with their start and end apart: 13, of which 7 were waited for; matrix products, arithmetic and copies ran while one was open for 0% of the time, Pallas kernels for 25%

commit v1 on v0

v1 whole, which is shorter than its diff:
```python
import functools

import jax
import jax.numpy as jnp
from jax import lax
from jax.experimental import pallas as pl
from jax.experimental.pallas import tpu as pltpu
from jax.sharding import PartitionSpec as P

f32 = jnp.float32
bf16 = jnp.bfloat16
BLOCK = 64
PAIR = 2 * BLOCK
STEP = 8
CHUNK = 512
NEVER = -1e30
DIGIT = 64.0
VMEM = pl.BlockSpec(memory_space=pltpu.VMEM)
SMEM = pl.BlockSpec(memory_space=pltpu.SMEM)
ANY = pl.BlockSpec(memory_space=pl.ANY)
PARAMS = pltpu.CompilerParams(vmem_limit_bytes=48 * 1024 * 1024)


def dot(a, b):
    return jnp.dot(a, b, preferred_element_type=f32)


def dot_nt(a, b):
    return lax.dot_general(a, b, (((1,), (1,)), ((), ())), preferred_element_type=f32)


def dot_tn(a, b):
    return lax.dot_general(a, b, (((0,), (0,)), ((), ())), preferred_element_type=f32)


def pick(condition):
    return jnp.where(condition, 1.0, 0.0).astype(bf16)


def pick16(values, places):
    return jnp.where(values == places, jnp.ones((), bf16), jnp.zeros((), bf16))


def call(kernel, out_shape, args, in_specs=None, scratch=()):
    many = isinstance(out_shape, (list, tuple))
    return pl.pallas_call(
        kernel,
        out_shape=out_shape,
        in_specs=in_specs or [VMEM] * len(args),
        out_specs=[VMEM] * len(out_shape) if many else VMEM,
        scratch_shapes=list(scratch),
        compiler_params=PARAMS,
    )(*args)


def shape(rows, columns, dtype):
    return jax.ShapeDtypeStruct((rows, columns), dtype)


def slot_columns(nbr, mask, halo_rows):
    rows = nbr.shape[1]
    block = lax.broadcasted_iota(jnp.int32, nbr.shape, 1) // BLOCK
    halo = lax.rem(block, halo_rows // BLOCK) * BLOCK
    column = jnp.where(
        nbr < rows,
        nbr - block * BLOCK,
        jnp.where(
            nbr < rows + halo_rows,
            BLOCK + nbr - rows - halo,
            2 * BLOCK + nbr - rows - halo_rows - halo,
        ),
    )
    return jnp.where(mask > 0, column, 3 * BLOCK).astype(f32)


def selector(columns_t):
    first = lax.broadcasted_iota(jnp.int32, (BLOCK, 128), 1).astype(bf16)
    second = (lax.broadcasted_iota(jnp.int32, (BLOCK, 128), 1) + 128).astype(bf16)
    parts = []
    for k in range(8):
        wide = jnp.broadcast_to(columns_t[:, k : k + 1], (BLOCK, 128)).astype(bf16)
        parts.append(jnp.concatenate([pick16(wide, first), pick16(wide, second)], 1))
    return jnp.concatenate(parts, 0)


def selector_t(columns, rolled, half):
    lane = lax.broadcasted_iota(jnp.int32, (1, 128), 1)
    place = lax.broadcasted_iota(jnp.int32, (3 * BLOCK, 128), 0).astype(bf16)
    parts = []
    for j in range(4):
        left, right = (columns, rolled) if half == 0 else (rolled, columns)
        row = jnp.where(lane < BLOCK, left[2 * j : 2 * j + 1], right[2 * j + 1 : 2 * j + 2])
        wide = jnp.broadcast_to(row, (3 * BLOCK, 128)).astype(bf16)
        parts.append(pick16(wide, place))
    return jnp.concatenate(parts, 1)


def window_of(far, halo, place):
    halo_rows = halo.shape[0] // 2
    start = place * BLOCK
    return jnp.concatenate(
        [
            far,
            halo[start : start + BLOCK, :],
            halo[halo_rows + start : halo_rows + start + BLOCK, :],
            jnp.full((BLOCK, far.shape[1]), NEVER, bf16),
        ],
        0,
    )


def chunk_of(index, count):
    return pl.ds(pl.multiple_of(index * count, count), count)


def level_terms(h_ref, lower_ref, upper_ref, self_ref, other_ref, own, far, halo):
    halo_rows = lower_ref.shape[0]
    other = other_ref[...] * 0.5
    h = h_ref[...]
    own[...] = dot(h, self_ref[...] * 0.5)
    far[...] = dot(h, other).astype(bf16)
    halo[:halo_rows, :] = dot(lower_ref[...], other).astype(bf16)
    halo[halo_rows:, :] = dot(upper_ref[...], other).astype(bf16)


def edge_loop(own, far, halo, columns, columns_t, finish):
    places = halo.shape[0] // (2 * BLOCK)
    assert STEP % places == 0

    def step(index, carry):
        own_rows = own[chunk_of(index, STEP * BLOCK), :]
        far_rows = far[chunk_of(index, STEP * BLOCK), :]
        slots = columns_t[chunk_of(index, STEP * BLOCK), :]
        tables = []
        for n in range(STEP):
            part = slice(n * BLOCK, (n + 1) * BLOCK)
            window = window_of(far_rows[part], halo, n % places)
            tables.append((own_rows[part], dot(selector(slots[part]), window)))
        finish(index, tables)
        return carry

    lax.fori_loop(0, own.shape[0] // (STEP * BLOCK), step, None)


def forward_sums(tables):
    sums = []
    for own, picked in tables:
        total = None
        for k in range(8):
            y = picked[k * BLOCK : (k + 1) * BLOCK] + own
            value = y + y * jnp.tanh(y)
            total = value if total is None else total + value
        sums.append(total)
    return jnp.concatenate(sums, 0).astype(bf16)


def backward_edges(tables, grad_sum, columns, halo_grad, summed=None):
    places = halo_grad.shape[0] // (2 * BLOCK)
    halo_rows = halo_grad.shape[0] // 2
    sums, downs, grads = [], [], []
    for n, (own, picked) in enumerate(tables):
        part = grad_sum[n * BLOCK : (n + 1) * BLOCK]
        total, down, pieces = None, None, []
        for k in range(8):
            y = picked[k * BLOCK : (k + 1) * BLOCK] + own
            t = jnp.tanh(y)
            up = 1.0 + t
            if summed is not None:
                total = y * up if total is None else total + y * up
            grad = part * (up * (1.0 + (y - y * t)))
            down = grad if down is None else down + grad
            pieces.append(grad.astype(bf16))
        sums.append(total)
        downs.append(down)
        grads.append(jnp.concatenate(pieces, 0))
    windows = []
    for n, grad in enumerate(grads):
        mine = columns[:, n // 2 * PAIR : (n // 2 + 1) * PAIR]
        windows.append(dot(selector_t(mine, pltpu.roll(mine, BLOCK, 1), n % 2), grad))
    for place in range(places):
        for side in range(2):
            start = side * halo_rows + place * BLOCK
            total = halo_grad[start : start + BLOCK, :]
            for window in windows[place::places]:
                total = total + window[(side + 1) * BLOCK : (side + 2) * BLOCK]
            halo_grad[start : start + BLOCK, :] = total
    local = jnp.concatenate([window[:BLOCK] for window in windows], 0)
    down = jnp.concatenate(downs, 0)
    if summed is None:
        return None, down, local
    return jnp.concatenate(sums, 0).astype(bf16), down, local


def gather_kernel(lo_ref, hi_ref, x_ref, up_ref, down_ref, wide, up, down):
    wide[...] = x_ref[...].astype(f32)

    def step(r, carry):
        up[pl.ds(r, 1), :] = wide[pl.ds(hi_ref[r], 1), :]
        down[pl.ds(r, 1), :] = wide[pl.ds(lo_ref[r], 1), :]
        return carry

    lax.fori_loop(0, up.shape[0], step, None, unroll=16)
    up_ref[...] = up[...].astype(bf16)
    down_ref[...] = down[...].astype(bf16)


def gather_rows(x, send_lo, send_hi):
    rows, features = x.shape
    count = send_lo.shape[0]
    out = shape(count, features, bf16)
    return call(
        gather_kernel,
        [out, out],
        [send_lo, send_hi, x],
        [SMEM, SMEM, VMEM],
        [
            pltpu.VMEM((rows, features), f32),
            pltpu.VMEM((count, features), f32),
            pltpu.VMEM((count, features), f32),
        ],
    )


def owner_sums(owner_ref, tile, values):
    place = lax.broadcasted_iota(jnp.int32, (128, 128), 0) + tile * 128
    groups = owner_ref.shape[0]
    rows = jnp.concatenate(
        [pick(owner_ref[q : q + 1, :] == place) for q in range(groups)], 1
    )
    return dot(rows, values)


def cotangent_kernel(owner_ref, g_ref, after_ref, out_ref, *, coarse_rows):
    tiles = coarse_rows // 128

    def step(tile, carry):
        out_ref[chunk_of(tile, 128), :] = owner_sums(owner_ref, tile, g_ref[...]).astype(bf16)
        return carry

    lax.fori_loop(0, tiles, step, None)
    owner = owner_ref[...]
    high, low = owner // 128, lax.rem(owner, 128)
    groups = owner.shape[0]
    place = lax.broadcasted_iota(jnp.int32, (128, 128), 0)
    high_rows = jnp.concatenate(
        [pick(high[q : q + 1, :] == place[:tiles]) for q in range(groups)], 1
    )
    low_rows = jnp.concatenate(
        [pick(low[q : q + 1, :] == place) for q in range(groups)], 1
    )
    counts = dot_nt(high_rows, low_rows)
    most = jnp.floor(counts * (1 / DIGIT))
    out_ref[coarse_rows:, :] = jnp.concatenate([most, counts - DIGIT * most], 0).astype(bf16)


def fine_forward_kernel(
    h_ref,
    lower_ref,
    upper_ref,
    self_ref,
    other_ref,
    node_ref,
    nbr_ref,
    mask_ref,
    owner_ref,
    after_ref,
    summed_ref,
    totals_ref,
    own,
    far,
    halo,
    columns_t,
    new,
):
    level_terms(h_ref, lower_ref, upper_ref, self_ref, other_ref, own, far, halo)
    columns_t[...] = slot_columns(nbr_ref[...], mask_ref[...], lower_ref.shape[0]).T

    def finish(index, tables):
        summed_ref[chunk_of(index, STEP * BLOCK), :] = forward_sums(tables)

    edge_loop(own, far, halo, None, columns_t, finish)
    new[...] = (h_ref[...].astype(f32) + dot(summed_ref[...], node_ref[...])).astype(bf16)

    def tile_step(tile, carry):
        totals_ref[chunk_of(tile, 128), :] = owner_sums(owner_ref, tile, new[...]).astype(bf16)
        return carry

    lax.fori_loop(0, totals_ref.shape[0] // 128, tile_step, None)


def count_columns(counts_ref):
    return counts_ref[...].T


def coarse_input_kernel(totals_ref, counts_ref, lo_ref, hi_ref, cin_ref, up_ref, down_ref):
    per_row = count_columns(counts_ref)
    for tile in range(totals_ref.shape[0] // 128):
        here = slice(tile * 128, (tile + 1) * 128)
        cin_ref[here, :] = (totals_ref[here, :] / per_row[:, tile : tile + 1]).astype(bf16)
    cin = cin_ref[...]
    place = lax.broadcasted_iota(jnp.int32, (cin.shape[0], lo_ref.shape[1]), 0)
    up_ref[...] = dot_tn(pick(hi_ref[...] == place), cin).astype(bf16)
    down_ref[...] = dot_tn(pick(lo_ref[...] == place), cin).astype(bf16)


def coarse_kernel(
    cin_ref,
    lower_ref,
    upper_ref,
    sums_ref,
    self_ref,
    other_ref,
    node_ref,
    prolong_ref,
    nbr_ref,
    mask_ref,
    part_ref,
    lower_grad_ref,
    upper_grad_ref,
    summed_ref,
    ups_ref,
    downs_ref,
    own,
    far,
    halo,
    columns,
    columns_t,
    grad_sum,
    halo_grad,
):
    halo_rows = lower_ref.shape[0]
    level_terms(cin_ref, lower_ref, upper_ref, self_ref, other_ref, own, far, halo)
    columns[...] = slot_columns(nbr_ref[...], mask_ref[...], halo_rows)
    columns_t[...] = columns[...].T
    halo_grad[...] = jnp.zeros_like(halo_grad)
    part_ref[...] = dot_nt(sums_ref[...], prolong_ref[...])
    ups_ref[...] = part_ref[...].astype(bf16)
    grad_sum[...] = dot_nt(ups_ref[...], node_ref[...]) * 0.5

    def finish(index, tables):
        here = chunk_of(index, STEP * BLOCK)
        total, down, local = backward_edges(
            tables, grad_sum[here, :], columns[:, here], halo_grad, summed_ref
        )
        summed_ref[here, :] = total
        downs_ref[here, :] = jnp.concatenate([down, local], 1).astype(bf16)

    edge_loop(own, far, halo, columns, columns_t, finish)
    lower_grad_ref[...] = halo_grad[:halo_rows, :].astype(bf16)
    upper_grad_ref[...] = halo_grad[halo_rows:, :].astype(bf16)


def coarse_tail_kernel(
    cin_ref,
    lower_ref,
    upper_ref,
    sums_ref,
    node_ref,
    prolong_ref,
    lower_grad_ref,
    upper_grad_ref,
    summed_ref,
    ups_ref,
    downs_ref,
    fine_ref,
    weights_ref,
):
    cin = cin_ref[...]
    out = (cin.astype(f32) + dot(summed_ref[...], node_ref[...])).astype(bf16)
    fine_ref[...] = dot(out, prolong_ref[...]).astype(bf16)
    pair_grad = dot_tn(cin, downs_ref[...])
    weights_ref[0:128, :] = pair_grad[:, :128]
    weights_ref[128:256, :] = (
        pair_grad[:, 128:]
        + dot_tn(lower_ref[...], lower_grad_ref[...])
        + dot_tn(upper_ref[...], upper_grad_ref[...])
    )
    weights_ref[256:384, :] = dot_tn(summed_ref[...], ups_ref[...])
    weights_ref[384:512, :] = dot_tn(out, sums_ref[...])


def owner_columns(owner_ref):
    owner = owner_ref[...].astype(f32)
    row = jnp.concatenate([owner[q : q + 1, :] for q in range(owner.shape[0])], 1)
    return jnp.broadcast_to(row, (8, row.shape[1])).T


def owner_rows(owners, values):
    count = owners.shape[0]
    wide = jnp.broadcast_to(owners[:, 0:1], (count, 128))
    lane = lax.broadcasted_iota(jnp.int32, (count, 128), 1).astype(f32)
    tiles = values.shape[0] // 128
    rows = jnp.concatenate([pick(wide == lane + 128.0 * tile) for tile in range(tiles)], 1)
    return dot(rows, values)


def result_kernel(h_ref, summed_ref, node_ref, owner_ref, fine_ref, out_ref, owners):
    owners[...] = owner_columns(owner_ref)

    def step(index, carry):
        here = chunk_of(index, CHUNK)
        updated = h_ref[here, :].astype(f32) + dot(summed_ref[here, :], node_ref[...])
        out_ref[here, :] = (updated + owner_rows(owners[here, :], fine_ref[...])).astype(bf16)
        return carry

    lax.fori_loop(0, h_ref.shape[0] // CHUNK, step, None)


def fine_backward_kernel(
    h_ref,
    lower_ref,
    upper_ref,
    g_ref,
    summed_ref,
    self_ref,
    other_ref,
    node_ref,
    nbr_ref,
    mask_ref,
    owner_ref,
    part_ref,
    counts_ref,
    coarse_downs_ref,
    back_ref,
    sends_ref,
    coarse_self_ref,
    coarse_other_ref,
    ups_ref,
    downs_ref,
    lower_grad_ref,
    upper_grad_ref,
    weights_ref,
    own,
    far,
    halo,
    columns,
    columns_t,
    grad_sum,
    halo_grad,
    mean,
):
    halo_rows = lower_ref.shape[0]
    coarse_rows = part_ref.shape[0]
    level_terms(h_ref, lower_ref, upper_ref, self_ref, other_ref, own, far, halo)
    columns[...] = slot_columns(nbr_ref[...], mask_ref[...], halo_rows)
    halo_grad[...] = jnp.zeros_like(halo_grad)

    place = lax.broadcasted_iota(jnp.int32, (coarse_rows, sends_ref.shape[1]), 0)
    back = dot_nt(back_ref[...], coarse_other_ref[...]).astype(bf16)
    plain = jnp.concatenate([coarse_self_ref[...], coarse_other_ref[...]], 1)
    grad_in = (
        part_ref[...]
        + dot_nt(coarse_downs_ref[...], plain)
        + dot(pick(sends_ref[...] == place), back)
    )
    per_row = count_columns(counts_ref)
    for tile in range(coarse_rows // 128):
        here = slice(tile * 128, (tile + 1) * 128)
        mean[here, :] = (grad_in[here, :] / per_row[:, tile : tile + 1]).astype(bf16)

    columns_t[...] = owner_columns(owner_ref)

    def owner_step(index, carry):
        here = chunk_of(index, CHUNK)
        grad_up = g_ref[here, :].astype(f32) + owner_rows(columns_t[here, :], mean[...])
        ups_ref[here, :] = grad_up.astype(bf16)
        return carry

    lax.fori_loop(0, h_ref.shape[0] // CHUNK, owner_step, None)
    grad_sum[...] = dot_nt(ups_ref[...], node_ref[...]) * 0.5
    columns_t[...] = columns[...].T

    def finish(index, tables):
        here = chunk_of(index, STEP * BLOCK)
        _, down, local = backward_edges(
            tables, grad_sum[here, :], columns[:, here], halo_grad
        )
        downs_ref[here, :] = jnp.concatenate([down, local], 1).astype(bf16)

    edge_loop(own, far, halo, columns, columns_t, finish)
    lower_grad = halo_grad[:halo_rows, :].astype(bf16)
    upper_grad = halo_grad[halo_rows:, :].astype(bf16)
    lower_grad_ref[...] = lower_grad
    upper_grad_ref[...] = upper_grad
    pair_grad = dot_tn(h_ref[...], downs_ref[...])
    weights_ref[0:128, :] = pair_grad[:, :128]
    weights_ref[128:256, :] = (
        pair_grad[:, 128:] + dot_tn(lower_ref[...], lower_grad) + dot_tn(upper_ref[...], upper_grad)
    )
    weights_ref[256:384, :] = dot_tn(summed_ref[...], ups_ref[...])


def finish_kernel(
    ups_ref, downs_ref, up_ref, down_ref, lo_ref, hi_ref, self_ref, other_ref, out_ref
):
    other = other_ref[...]
    plain = jnp.concatenate([self_ref[...], other], 1)
    back = jnp.concatenate([dot_nt(up_ref[...], other), dot_nt(down_ref[...], other)], 0)
    back = back.astype(bf16)
    sends = jnp.concatenate([lo_ref[...], hi_ref[...]], 1)
    place = lax.broadcasted_iota(jnp.int32, (CHUNK, sends.shape[1]), 0)

    def step(index, carry):
        here = chunk_of(index, CHUNK)
        rows = pick(sends - index * CHUNK == place)
        grad = ups_ref[here, :].astype(f32) + dot_nt(downs_ref[here, :], plain)
        out_ref[here, :] = (grad + dot(rows, back)).astype(bf16)
        return carry

    lax.fori_loop(0, ups_ref.shape[0] // CHUNK, step, None)


def shifted(block, axis, distance):
    devices = range(lax.axis_size(axis))
    route = [(i - distance, i) for i in devices if i - distance in devices]
    return lax.ppermute(block, axis, route)


def swapped(block, axis, distance):
    return lax.ppermute(block, axis, [(i, i ^ distance) for i in range(lax.axis_size(axis))])


def total_over(block, axis):
    distance = 1
    total = block
    while distance < lax.axis_size(axis):
        sent = total.astype(bf16)
        total = total.astype(f32) + swapped(sent, axis, distance).astype(f32)
        distance *= 2
    return sent, total


def total_over_all(block, axes):
    devices = lax.axis_size(axes)
    share = block.shape[0] // devices
    parts = lax.all_to_all(
        block.astype(bf16).reshape(devices, share, 128), axes, 0, 0, tiled=False
    )
    mine = parts.astype(f32).sum(0).astype(bf16)
    return lax.all_to_all(
        jnp.broadcast_to(mine[None], (devices, share, 128)), axes, 0, 0, tiled=False
    ).reshape(block.shape)


def per_device(
    states,
    cotangent,
    fine_self,
    fine_other,
    fine_node,
    coarse_self,
    coarse_other,
    coarse_node,
    prolong,
    fine_nbr,
    fine_mask,
    fine_send_lo,
    fine_send_hi,
    coarse_nbr,
    coarse_mask,
    coarse_send_lo,
    coarse_send_hi,
    coarse_owner,
):
    rows, features = states.shape
    coarse_rows = coarse_nbr.shape[0]
    halo_rows = fine_send_lo.shape[0]
    coarse_halo = coarse_send_lo.shape[0]
    count_rows = coarse_rows // 128
    owner = coarse_owner.reshape(rows // 128, 128)
    fine_nbr, fine_mask = fine_nbr.T, fine_mask.T
    coarse_nbr, coarse_mask = coarse_nbr.T, coarse_mask.T
    coarse_lo, coarse_hi = coarse_send_lo[None], coarse_send_hi[None]

    def buffer(count, columns, dtype):
        return pltpu.VMEM((count, columns), dtype)

    going_up, going_down = gather_rows(states, fine_send_lo, fine_send_hi)
    lower = shifted(going_up, "sub", 1)
    upper = shifted(going_down, "sub", -1)

    sums_counts = call(
        functools.partial(cotangent_kernel, coarse_rows=coarse_rows),
        shape(coarse_rows + 2 * count_rows, features, bf16),
        [owner, cotangent, going_up],
        [VMEM, VMEM, ANY],
    )
    chip_sums, sums_counts = total_over(sums_counts, "grp")
    grad_sums = sums_counts[:coarse_rows].astype(bf16)
    counts = (
        DIGIT * sums_counts[coarse_rows : coarse_rows + count_rows]
        + sums_counts[coarse_rows + count_rows :]
    )

    summed, totals = call(
        fine_forward_kernel,
        [shape(rows, features, bf16), shape(coarse_rows, features, bf16)],
        [
            states, lower, upper, fine_self, fine_other, fine_node, fine_nbr, fine_mask, owner,
            chip_sums,
        ],
        [VMEM] * 9 + [ANY],
        [
            buffer(rows, features, f32),
            buffer(rows, features, bf16),
            buffer(2 * halo_rows, features, bf16),
            buffer(rows, 8, f32),
            buffer(rows, features, bf16),
        ],
    )
    _, totals = total_over(totals, "grp")

    coarse_in, coarse_up, coarse_down = call(
        coarse_input_kernel,
        [
            shape(coarse_rows, features, bf16),
            shape(coarse_halo, features, bf16),
            shape(coarse_halo, features, bf16),
        ],
        [totals, counts, coarse_lo, coarse_hi],
    )
    coarse_lower = shifted(coarse_up, "sub", 1)
    coarse_upper = shifted(coarse_down, "sub", -1)

    coarse_part, lower_grad, upper_grad, coarse_sum, coarse_ups, coarse_downs = call(
        coarse_kernel,
        [
            shape(coarse_rows, features, f32),
            shape(coarse_halo, features, bf16),
            shape(coarse_halo, features, bf16),
            shape(coarse_rows, features, bf16),
            shape(coarse_rows, features, bf16),
            shape(coarse_rows, 2 * features, bf16),
        ],
        [
            coarse_in, coarse_lower, coarse_upper, grad_sums,
            coarse_self, coarse_other, coarse_node, prolong, coarse_nbr, coarse_mask,
        ],
        scratch=[
            buffer(coarse_rows, features, f32),
            buffer(coarse_rows, features, bf16),
            buffer(2 * coarse_halo, features, bf16),
            buffer(8, coarse_rows, f32),
            buffer(coarse_rows, 8, f32),
            buffer(coarse_rows, features, f32),
            buffer(2 * coarse_halo, features, f32),
        ],
    )
    back_up = shifted(upper_grad, "sub", 1)
    back_down = shifted(lower_grad, "sub", -1)
    coarse_back = jnp.concatenate([back_up, back_down], 0)
    coarse_sends = jnp.concatenate([coarse_lo, coarse_hi], 1)

    fine_term, coarse_weights = call(
        coarse_tail_kernel,
        [shape(coarse_rows, features, bf16), shape(4 * features, features, f32)],
        [
            coarse_in, coarse_lower, coarse_upper, grad_sums, coarse_node, prolong,
            lower_grad, upper_grad, coarse_sum, coarse_ups, coarse_downs,
        ],
    )
    result = call(
        result_kernel,
        shape(rows, features, bf16),
        [states, summed, fine_node, owner, fine_term],
        scratch=[buffer(rows, 8, f32)],
    )

    ups, downs, lower_grad, upper_grad, fine_weights = call(
        fine_backward_kernel,
        [
            shape(rows, features, bf16),
            shape(rows, 2 * features, bf16),
            shape(halo_rows, features, bf16),
            shape(halo_rows, features, bf16),
            shape(3 * features, features, f32),
        ],
        [
            states, lower, upper, cotangent, summed, fine_self, fine_other, fine_node,
            fine_nbr, fine_mask, owner, coarse_part, counts, coarse_downs, coarse_back,
            coarse_sends, coarse_self, coarse_other,
        ],
        scratch=[
            buffer(rows, features, f32),
            buffer(rows, features, bf16),
            buffer(2 * halo_rows, features, bf16),
            buffer(8, rows, f32),
            buffer(rows, 8, f32),
            buffer(rows, features, f32),
            buffer(2 * halo_rows, features, f32),
            buffer(coarse_rows, features, bf16),
        ],
    )
    back_up = shifted(upper_grad, "sub", 1)
    back_down = shifted(lower_grad, "sub", -1)

    scale = 1.0 / lax.axis_size("grp")
    weights = jnp.concatenate(
        [fine_weights, coarse_weights * scale, jnp.zeros((features, features), f32)], 0
    )
    weights = total_over_all(weights, ("grp", "sub"))
    grad_weights = weights[: 7 * features].astype(f32).reshape(7, features, features)

    grad_states = call(
        finish_kernel,
        shape(rows, features, bf16),
        [
            ups, downs, back_up, back_down, fine_send_lo[None], fine_send_hi[None],
            fine_self, fine_other,
        ],
    )
    return (result, grad_states, grad_weights)


def solution(mesh):
    fine = P(("grp", "sub"), None)
    fine_row = P(("grp", "sub"))
    in_specs = (
        (fine, fine)
        + (P(),) * 7
        + (fine, fine, fine_row, fine_row)
        + (P("sub", None), P("sub", None), P("sub"), P("sub"), fine_row)
    )
    return jax.shard_map(
        per_device, mesh=mesh, in_specs=in_specs, out_specs=(fine, fine, P()), check_vma=False
    )
```

time: 181 us -> 135 us (0.75)
  Pallas kernels: 101 us -> 54.7 us
    pallas_call x8 -> x9, Pallas kernels: 101 us -> 54.7 us  [call(): pl.pallas_call(kernel, out_shape=out_shape, in_specs=in_specs or [VMEM] *...]
    unnamed x54 -> x56, local copies, waits for them, and re-layouts: 6.99 us -> 5.26 us
  transfers between devices with their start and end apart: 13 -> 13, of which waited for: 7 -> 6; matrix products, arithmetic and copies ran while one was open for 0% -> 0% of each run, Pallas kernels for 25% -> 9%
where the time goes in v1:
time: 135 us; the launch traced here: 134 us
  Pallas kernels  54.7 us (41%)
  starting transfers between devices  28.6 us (21%)
  waiting for transfers between devices  25 us (19%)
  blocking collectives  14.8 us (11%)
  local copies, waits for them, and re-layouts  6.99 us (5%)
  other arithmetic  2.49 us (2%)
    pallas_call x9, Pallas kernels, call(): pl.pallas_call(kernel, out_shape=out_shape, in_specs=in_specs or [VMEM] *...  54.7 us
    ppermute x8, starting transfers between devices, shifted(): return lax.ppermute(block, axis, route)  21.7 us
    all_to_all x1, blocking collectives, total_over_all(): lax.all_to_all(block.astype(bf16).reshape(devices, share, 128), axes, 0,...  14.8 us
    ppermute x8, waiting for transfers between devices, shifted(): return lax.ppermute(block, axis, route)  13.8 us
    ppermute x4, waiting for transfers between devices, swapped(): lax.ppermute(block, axis, [(i, i ^ distance) for i in range(lax.axis_size...  11.1 us
    unnamed x56, local copies, waits for them, and re-layouts  5.26 us
    ppermute x4, starting transfers between devices, swapped(): lax.ppermute(block, axis, [(i, i ^ distance) for i in range(lax.axis_size...  3.63 us
    all_to_all x1, starting transfers between devices, total_over_all(): lax.all_to_all(jnp.broadcast_to(mine[None], (devices, share, 128)), axes,...  3.31 us
  transfers between devices with their start and end apart: 13, of which 6 were waited for; matrix products, arithmetic and copies ran while one was open for 0% of the time, Pallas kernels for 9%

profile of v1, /device:TPU:0, one launch (start us, length us, event | category | flops | bytes accessed | tf_op | source)
XLA Modules:
  0.0 133.6 jit_solution(16605267440998120072)
XLA Ops:
  3.2 1.6 %shard_map.193 = (bf16[512,128]{1,0:T(8,128)(2,1)S(1)}, bf16[512,128]{1,0:T(8,128)(2,1)S(1)}) custom-call(s32[512]{0:T(512)S(1)} %copy-done.20, s32[512]{0:T(512)S(1)} %copy-done.22, bf16[4096,128]{1,0:T(8,128)(2,1)S(1)} %copy-done), custom_call_target="tpu_custom_call" | custom-call | tf_op jit(solution)/shard_map/pallas_call | solution.py:46
  6.8 3.8 %shard_map.194 = bf16[1040,128]{1,0:T(8,128)(2,1)S(1)} custom-call(s32[32,128]{1,0:T(8,128)S(1)} %bitcast.18, bf16[4096,128]{1,0:T(8,128)(2,1)S(1)} %copy-done.2, bf16[512,128]{1,0:T(8,128)(2,1)S(1)} %get-tuple-element.23.after_ref), custom_call_target="tpu_custom_call" | custom-call | tf_op jit(solution)/shard_map/pallas_call | solution.py:46
  11.0 4.4 %collective-permute-start = (bf16[512,128]{1,0:T(8,128)(2,1)S(1)}, bf16[512,128]{1,0:T(8,128)(2,1)S(1)}, u32[]{:S(2)}, u32[]{:S(2)}) collective-permute-start(bf16[512,128]{1,0:T(8,128)(2,1)S(1)} %get-tuple-element.23.after_ref), channel_id=1, source_target_pairs={{0,1},{1,2},{2,3},{3,4},{4,5},{5,6},{6,7},{8,9},{9,10},{10,11},{11... | collective-permute-start | bytes 393224 | tf_op jit(solution)/shard_map/ppermute | solution.py:516
  16.8 2.0 %collective-permute-done.lower_ref = bf16[512,128]{1,0:T(8,128)(2,1)S(1)} collective-permute-done((bf16[512,128]{1,0:T(8,128)(2,1)S(1)}, bf16[512,128]{1,0:T(8,128)(2,1)S(1)}, u32[]{:S(2)}, u32[]{:S(2)}) %collective-permute-start) | collective-permute-done | bytes 131104 | tf_op jit(solution)/shard_map/ppermute | solution.py:516
  18.8 4.1 %collective-permute-done.1.upper_ref = bf16[512,128]{1,0:T(8,128)(2,1)S(1)} collective-permute-done((bf16[512,128]{1,0:T(8,128)(2,1)S(1)}, bf16[512,128]{1,0:T(8,128)(2,1)S(1)}, u32[]{:S(2)}, u32[]{:S(2)}) %collective-permute-start.1) | collective-permute-done | bytes 131104 | tf_op jit(solution)/shard_map/ppermute | solution.py:516
  23.0 11.0 %shard_map.195 = (bf16[4096,128]{1,0:T(8,128)(2,1)S(1)}, bf16[1024,128]{1,0:T(8,128)(2,1)S(1)}) custom-call(bf16[4096,128]{1,0:T(8,128)(2,1)S(1)} %copy-done.1, bf16[512,128]{1,0:T(8,128)(2,1)S(1)} %collective-permute-done.lower_ref, bf16[512,128]{1,0:T(8,128)(2,1)S(1)} %collective-permute-done.1.upper_ref, bf16[128,128]{1,0:T(8,128)(2,1)S(1)} %copy-done.10, ...), custom_call_target="tpu_custom_call" | custom-call | tf_op jit(solution)/shard_map/pallas_call | solution.py:46
  34.2 1.6 %collective-permute-start.5 = (bf16[1040,128]{1,0:T(8,128)(2,1)S(1)}, bf16[1040,128]{1,0:T(8,128)(2,1)S(1)}, u32[]{:S(2)}, u32[]{:S(2)}) collective-permute-start(bf16[1040,128]{1,0:T(8,128)(2,1)S(1)} %fusion.after_ref), channel_id=1, source_target_pairs={{0,16},{8,24},{16,0},{24,8},{1,17},{9,25},{17,1},{25,9},{2,18},{10... | collective-permute-start | bytes 798728 | tf_op jit(solution)/shard_map/ppermute | solution.py:520
  35.9 1.5 %collective-permute-start.4 = (bf16[1024,128]{1,0:T(8,128)(2,1)S(1)}, bf16[1024,128]{1,0:T(8,128)(2,1)S(1)}, u32[]{:S(2)}, u32[]{:S(2)}) collective-permute-start(bf16[1024,128]{1,0:T(8,128)(2,1)S(1)} %fusion.1), channel_id=1, source_target_pairs={{0,16},{8,24},{16,0},{24,8},{1,17},{9,25},{17,1},{25,9},{2,18},{10... | collective-permute-start | bytes 786440 | tf_op jit(solution)/shard_map/ppermute | solution.py:520
  37.4 6.1 %collective-permute-done.5 = bf16[1040,128]{1,0:T(8,128)(2,1)S(1)} collective-permute-done((bf16[1040,128]{1,0:T(8,128)(2,1)S(1)}, bf16[1040,128]{1,0:T(8,128)(2,1)S(1)}, u32[]{:S(2)}, u32[]{:S(2)}) %collective-permute-start.5) | collective-permute-done | bytes 266272 | tf_op jit(solution)/shard_map/ppermute | solution.py:520
  43.6 5.0 %collective-permute-done.4 = bf16[1024,128]{1,0:T(8,128)(2,1)S(1)} collective-permute-done((bf16[1024,128]{1,0:T(8,128)(2,1)S(1)}, bf16[1024,128]{1,0:T(8,128)(2,1)S(1)}, u32[]{:S(2)}, u32[]{:S(2)}) %collective-permute-start.4) | collective-permute-done | bytes 262176 | tf_op jit(solution)/shard_map/ppermute | solution.py:520
  49.4 4.3 %collective-permute-start.6 = (bf16[64,128]{1,0:T(8,128)(2,1)S(1)}, bf16[64,128]{1,0:T(8,128)(2,1)S(1)}, u32[]{:S(2)}, u32[]{:S(2)}) collective-permute-start(bf16[64,128]{1,0:T(8,128)(2,1)S(1)} %get-tuple-element.28), channel_id=1, source_target_pairs={{0,1},{1,2},{2,3},{3,4},{4,5},{5,6},{6,7},{8,9},{9,10},{10,11},{11... | collective-permute-start | bytes 49160 | tf_op jit(solution)/shard_map/ppermute | solution.py:516
  53.7 1.3 collective-permute-start.7
  55.2 4.2 %collective-permute-done.7.upper_ref = bf16[64,128]{1,0:T(8,128)(2,1)S(1)} collective-permute-done((bf16[64,128]{1,0:T(8,128)(2,1)S(1)}, bf16[64,128]{1,0:T(8,128)(2,1)S(1)}, u32[]{:S(2)}, u32[]{:S(2)}) %collective-permute-start.7) | collective-permute-done | bytes 16416 | tf_op jit(solution)/shard_map/ppermute | solution.py:516
  59.4 4.1 %shard_map.197 = (f32[1024,128]{1,0:T(8,128)S(1)}, bf16[64,128]{1,0:T(8,128)(2,1)S(1)}, bf16[64,128]{1,0:T(8,128)(2,1)S(1)}, bf16[1024,128]{1,0:T(8,128)(2,1)S(1...) custom-call(bf16[1024,128]{1,0:T(8,128)(2,1)S(1)} %get-tuple-element.27.cin_ref, ...), custom_call_target="tpu_custom_call" | custom-call | tf_op jit(solution)/shard_map/pallas_call | solution.py:46
  63.5 4.0 %collective-permute-start.8 = (bf16[64,128]{1,0:T(8,128)(2,1)S(1)}, bf16[64,128]{1,0:T(8,128)(2,1)S(1)}, u32[]{:S(2)}, u32[]{:S(2)}) collective-permute-start(bf16[64,128]{1,0:T(8,128)(2,1)S(1)} %get-tuple-element.31.upper_grad_ref), channel_id=1, source_target_pairs={{0,1},{1,2},{2,3},{3,4},{4,5},{5,6},{6,7},{8,9},{9,10},{10,11},{11... | collective-permute-start | bytes 49160 | tf_op jit(solution)/shard_map/ppermute | solution.py:516
  67.5 1.5 %collective-permute-start.9 = (bf16[64,128]{1,0:T(8,128)(2,1)S(1)}, bf16[64,128]{1,0:T(8,128)(2,1)S(1)}, u32[]{:S(2)}, u32[]{:S(2)}) collective-permute-start(bf16[64,128]{1,0:T(8,128)(2,1)S(1)} %get-tuple-element.30.lower_grad_ref), channel_id=1, source_target_pairs={{1,0},{2,1},{3,2},{4,3},{5,4},{6,5},{7,6},{9,8},{10,9},{11,10},{12... | collective-permute-start | bytes 49160 | tf_op jit(solution)/shard_map/ppermute | solution.py:516
  69.6 3.5 %collective-permute-done.9 = bf16[64,128]{1,0:T(8,128)(2,1)S(1)} collective-permute-done((bf16[64,128]{1,0:T(8,128)(2,1)S(1)}, bf16[64,128]{1,0:T(8,128)(2,1)S(1)}, u32[]{:S(2)}, u32[]{:S(2)}) %collective-permute-start.9) | collective-permute-done | bytes 16416 | tf_op jit(solution)/shard_map/ppermute | solution.py:516
  73.1 21.0 %shard_map.200 = (bf16[4096,128]{1,0:T(8,128)(2,1)S(1)}, bf16[4096,256]{1,0:T(8,128)(2,1)}, bf16[512,128]{1,0:T(8,128)(2,1)S(1)}, bf16[512,128]{1,0:T(8,128)(2,1)S(1)}, f32[384,128]{1,0:T(8,128)S(1)}) custom-call(bf16[4096,128]{1,0:T(8,128)(2,1)S(1)} %copy-done.1, bf16[512,128]{1,0:T(8,128)(2,1)S(1)} %collective-permute-done.lower_ref, ...), custom_call_target="tpu_custom_call" | custom-call | tf_op jit(solution)/shard_map/pallas_call | solution.py:46
  95.0 14.8 %all_to_all.10 = bf16[32,32,128]{2,1,0:T(8,128)(2,1)} all-to-all(bf16[32,32,128]{2,1,0:T(8,128)(2,1)S(1)} %bitcast.30), channel_id=1, replica_groups=mesh['grp'=4,'sub'=8] {'grp','sub'}, dimensions={0} | all-to-all | bytes 524288 | tf_op jit(solution)/shard_map/all_to_all | solution.py:536
  111.5 3.3 %all-to-all-start.1 = ((bf16[32,32,128]{2,1,0:T(8,128)(2,1)}), bf16[32,32,128]{2,1,0:T(8,128)(2,1)}, u32[]{:S(2)}, u32[]{:S(2)}) async-start(bf16[32,32,128]{2,1,0:T(8,128)(2,1)} %broadcast_in_dim.26), calls=%async_computation.1 | async-start | bytes 524288 | tf_op jit(solution)/shard_map/all_to_all | solution.py:540
  114.8 3.6 %collective-permute-start.10 = (bf16[512,128]{1,0:T(8,128)(2,1)}, bf16[512,128]{1,0:T(8,128)(2,1)S(1)}, u32[]{:S(2)}, u32[]{:S(2)}) collective-permute-start(bf16[512,128]{1,0:T(8,128)(2,1)} %copy-done.27), channel_id=1, source_target_pairs={{0,1},{1,2},{2,3},{3,4},{4,5},{5,6},{6,7},{8,9},{9,10},{10,11},{11... | collective-permute-start | bytes 393224 | tf_op jit(solution)/shard_map/ppermute | solution.py:516
  118.5 1.3 collective-permute-start.11
  119.8 6.6 %shard_map.199 = bf16[4096,128]{1,0:T(8,128)(2,1)} custom-call(bf16[4096,128]{1,0:T(8,128)(2,1)S(1)} %copy-done.1, bf16[4096,128]{1,0:T(8,128)(2,1)S(1)} %copy-done.5, bf16[128,128]{1,0:T(8,128)(2,1)S(1)} %copy-done.9, s32[32,128]{1,0:T(8,128)S(1)} %bitcast.21, bf16[1024,128]{1,0:T(8,128)(2,1)S(1)} %get-tuple-element.35.fine_ref), custom_call_target="tpu_custom_call" | custom-call | tf_op jit(solution)/shard_map/pallas_call | solution.py:46
  126.5 5.4 %shard_map.201 = bf16[4096,128]{1,0:T(8,128)(2,1)} custom-call(bf16[4096,128]{1,0:T(8,128)(2,1)S(1)} %get-tuple-element.37.ups_ref, bf16[4096,256]{1,0:T(8,128)(2,1)S(1)} %copy-done.6, bf16[512,128]{1,0:T(8,128)(2,1)S(1)} %collective-permute-done.10.up_ref, bf16[512,128]{1,0:T(8,128)(2,1)S(1)} %collective-permute-done.11.down_ref, s32[1,512]{1,0:T(1,128)S(1)} %bitcast.24, ...), custom_call_target="tpu_custom_call" | custom-call | tf_op jit(solution)/shard_map/pallas_call | solution.py:46
  (85 shorter events, 12.6 us)
Async XLA Ops:
  3.2 19.8 %copy-start.1 = (bf16[4096,128]{1,0:T(8,128)(2,1)S(1)}, bf16[4096,128]{1,0:T(8,128)(2,1)}, u32[]{:S(2)}) copy-start(bf16[4096,128]{1,0:T(8,128)(2,1)} %h_ref.5) | copy-start | bytes 3145732
  6.8 16.3 %copy-start.11 = (bf16[128,128]{1,0:T(8,128)(2,1)S(1)}, bf16[128,128]{1,0:T(8,128)(2,1)}, u32[]{:S(2)}) copy-start(bf16[128,128]{1,0:T(8,128)(2,1)} %other_ref.7) | copy-start | bytes 98308
  6.8 16.2 %copy-start.13 = (s32[4096]{0:T(1024)S(1)}, s32[4096]{0:T(1024)}, u32[]{:S(2)}) copy-start(s32[4096]{0:T(1024)} %param.35) | copy-start | bytes 49156
  10.6 6.2 %collective-permute-start.2 = (bf16[1040,128]{1,0:T(8,128)(2,1)S(1)}, bf16[1040,128]{1,0:T(8,128)(2,1)S(1)}, u32[]{:S(2)}, u32[]{:S(2)}) collective-permute-start(bf16[1040,128]{1,0:T(8,128)(2,1)S(1)} %shard_map.194), channel_id=1, source_target_pairs={{0,8},{8,0},{16,24},{24,16},{1,9},{9,1},{17,25},{25,17},{2,10},{10... | collective-permute-start | bytes 798728 | tf_op jit(solution)/shard_map/ppermute | solution.py:520
  11.0 7.8 %collective-permute-start = (bf16[512,128]{1,0:T(8,128)(2,1)S(1)}, bf16[512,128]{1,0:T(8,128)(2,1)S(1)}, u32[]{:S(2)}, u32[]{:S(2)}) collective-permute-start(bf16[512,128]{1,0:T(8,128)(2,1)S(1)} %get-tuple-element.23.after_ref), channel_id=1, source_target_pairs={{0,1},{1,2},{2,3},{3,4},{4,5},{5,6},{6,7},{8,9},{9,10},{10,11},{11... | collective-permute-start | bytes 393224 | tf_op jit(solution)/shard_map/ppermute | solution.py:516
  15.4 7.5 %collective-permute-start.1 = (bf16[512,128]{1,0:T(8,128)(2,1)S(1)}, bf16[512,128]{1,0:T(8,128)(2,1)S(1)}, u32[]{:S(2)}, u32[]{:S(2)}) collective-permute-start(bf16[512,128]{1,0:T(8,128)(2,1)S(1)} %get-tuple-element.24), channel_id=1, source_target_pairs={{1,0},{2,1},{3,2},{4,3},{5,4},{6,5},{7,6},{9,8},{10,9},{11,10},{12... | collective-permute-start | bytes 393224 | tf_op jit(solution)/shard_map/ppermute | solution.py:516
  34.1 25.3 %copy-start.14 = (bf16[128,128]{1,0:T(8,128)(2,1)S(1)}, bf16[128,128]{1,0:T(8,128)(2,1)}, u32[]{:S(2)}) copy-start(bf16[128,128]{1,0:T(8,128)(2,1)} %coarse_self_ref.1) | copy-start | bytes 98308
  34.1 25.3 %copy-start.15 = (bf16[128,128]{1,0:T(8,128)(2,1)S(1)}, bf16[128,128]{1,0:T(8,128)(2,1)}, u32[]{:S(2)}) copy-start(bf16[128,128]{1,0:T(8,128)(2,1)} %coarse_other_ref.1) | copy-start | bytes 98308
  34.1 25.3 %copy-start.16 = (bf16[128,128]{1,0:T(8,128)(2,1)S(1)}, bf16[128,128]{1,0:T(8,128)(2,1)}, u32[]{:S(2)}) copy-start(bf16[128,128]{1,0:T(8,128)(2,1)} %node_ref.7) | copy-start | bytes 98308
  34.1 25.3 %copy-start.17 = (bf16[128,128]{1,0:T(8,128)(2,1)S(1)}, bf16[128,128]{1,0:T(8,128)(2,1)}, u32[]{:S(2)}) copy-start(bf16[128,128]{1,0:T(8,128)(2,1)} %prolong_ref.3) | copy-start | bytes 98308
  34.1 25.3 %copy-start.18 = (s32[1024,8]{0,1:T(8,128)S(1)}, s32[1024,8]{0,1:T(8,128)}, u32[]{:S(2)}) copy-start(s32[1024,8]{0,1:T(8,128)} %param.31) | copy-start | bytes 98308
  34.1 25.3 %copy-start.19 = (s32[1024,8]{0,1:T(8,128)S(1)}, s32[1024,8]{0,1:T(8,128)}, u32[]{:S(2)}) copy-start(s32[1024,8]{0,1:T(8,128)} %param.32) | copy-start | bytes 98308
  34.1 1.6 %collective-permute-start.3 = (bf16[1024,128]{1,0:T(8,128)(2,1)S(1)}, bf16[1024,128]{1,0:T(8,128)(2,1)S(1)}, u32[]{:S(2)}, u32[]{:S(2)}) collective-permute-start(bf16[1024,128]{1,0:T(8,128)(2,1)S(1)} %get-tuple-element.26), channel_id=1, source_target_pairs={{0,8},{8,0},{16,24},{24,16},{1,9},{9,1},{17,25},{25,17},{2,10},{10... | collective-permute-start | bytes 786440 | tf_op jit(solution)/shard_map/ppermute | solution.py:520
  34.2 9.3 %collective-permute-start.5 = (bf16[1040,128]{1,0:T(8,128)(2,1)S(1)}, bf16[1040,128]{1,0:T(8,128)(2,1)S(1)}, u32[]{:S(2)}, u32[]{:S(2)}) collective-permute-start(bf16[1040,128]{1,0:T(8,128)(2,1)S(1)} %fusion.after_ref), channel_id=1, source_target_pairs={{0,16},{8,24},{16,0},{24,8},{1,17},{9,25},{17,1},{25,9},{2,18},{10... | collective-permute-start | bytes 798728 | tf_op jit(solution)/shard_map/ppermute | solution.py:520
  35.9 12.8 %collective-permute-start.4 = (bf16[1024,128]{1,0:T(8,128)(2,1)S(1)}, bf16[1024,128]{1,0:T(8,128)(2,1)S(1)}, u32[]{:S(2)}, u32[]{:S(2)}) collective-permute-start(bf16[1024,128]{1,0:T(8,128)(2,1)S(1)} %fusion.1), channel_id=1, source_target_pairs={{0,16},{8,24},{16,0},{24,8},{1,17},{9,25},{17,1},{25,9},{2,18},{10... | collective-permute-start | bytes 786440 | tf_op jit(solution)/shard_map/ppermute | solution.py:520
  48.8 24.4 %copy-start.3 = (bf16[4096,128]{1,0:T(8,128)(2,1)S(1)}, bf16[4096,128]{1,0:T(8,128)(2,1)}, u32[]{:S(2)}) copy-start(bf16[4096,128]{1,0:T(8,128)(2,1)} %g_ref.3) | copy-start | bytes 3145732
  49.4 5.8 %collective-permute-start.6 = (bf16[64,128]{1,0:T(8,128)(2,1)S(1)}, bf16[64,128]{1,0:T(8,128)(2,1)S(1)}, u32[]{:S(2)}, u32[]{:S(2)}) collective-permute-start(bf16[64,128]{1,0:T(8,128)(2,1)S(1)} %get-tuple-element.28), channel_id=1, source_target_pairs={{0,1},{1,2},{2,3},{3,4},{4,5},{5,6},{6,7},{8,9},{9,10},{10,11},{11... | collective-permute-start | bytes 49160 | tf_op jit(solution)/shard_map/ppermute | solution.py:516
  53.7 5.6 %collective-permute-start.7 = (bf16[64,128]{1,0:T(8,128)(2,1)S(1)}, bf16[64,128]{1,0:T(8,128)(2,1)S(1)}, u32[]{:S(2)}, u32[]{:S(2)}) collective-permute-start(bf16[64,128]{1,0:T(8,128)(2,1)S(1)} %get-tuple-element.29), channel_id=1, source_target_pairs={{1,0},{2,1},{3,2},{4,3},{5,4},{6,5},{7,6},{9,8},{10,9},{11,10},{12... | collective-permute-start | bytes 49160 | tf_op jit(solution)/shard_map/ppermute | solution.py:516
  63.5 6.1 %collective-permute-start.8 = (bf16[64,128]{1,0:T(8,128)(2,1)S(1)}, bf16[64,128]{1,0:T(8,128)(2,1)S(1)}, u32[]{:S(2)}, u32[]{:S(2)}) collective-permute-start(bf16[64,128]{1,0:T(8,128)(2,1)S(1)} %get-tuple-element.31.upper_grad_ref), channel_id=1, source_target_pairs={{0,1},{1,2},{2,3},{3,4},{4,5},{5,6},{6,7},{8,9},{9,10},{10,11},{11... | collective-permute-start | bytes 49160 | tf_op jit(solution)/shard_map/ppermute | solution.py:516
  67.5 5.6 %collective-permute-start.9 = (bf16[64,128]{1,0:T(8,128)(2,1)S(1)}, bf16[64,128]{1,0:T(8,128)(2,1)S(1)}, u32[]{:S(2)}, u32[]{:S(2)}) collective-permute-start(bf16[64,128]{1,0:T(8,128)(2,1)S(1)} %get-tuple-element.30.lower_grad_ref), channel_id=1, source_target_pairs={{1,0},{2,1},{3,2},{4,3},{5,4},{6,5},{7,6},{9,8},{10,9},{11,10},{12... | collective-permute-start | bytes 49160 | tf_op jit(solution)/shard_map/ppermute | solution.py:516
  94.1 25.7 %copy-start.5 = (bf16[4096,128]{1,0:T(8,128)(2,1)S(1)}, bf16[4096,128]{1,0:T(8,128)(2,1)}, u32[]{:S(2)}) copy-start(bf16[4096,128]{1,0:T(8,128)(2,1)} %copy-done.4) | copy-start | bytes 3145732
  111.5 20.3 %all-to-all-start.1 = ((bf16[32,32,128]{2,1,0:T(8,128)(2,1)}), bf16[32,32,128]{2,1,0:T(8,128)(2,1)}, u32[]{:S(2)}, u32[]{:S(2)}) async-start(bf16[32,32,128]{2,1,0:T(8,128)(2,1)} %broadcast_in_dim.26), calls=%async_computation.1 | async-start | bytes 524288 | tf_op jit(solution)/shard_map/all_to_all | solution.py:540
  114.8 11.6 %collective-permute-start.10 = (bf16[512,128]{1,0:T(8,128)(2,1)}, bf16[512,128]{1,0:T(8,128)(2,1)S(1)}, u32[]{:S(2)}, u32[]{:S(2)}) collective-permute-start(bf16[512,128]{1,0:T(8,128)(2,1)} %copy-done.27), channel_id=1, source_target_pairs={{0,1},{1,2},{2,3},{3,4},{4,5},{5,6},{6,7},{8,9},{9,10},{10,11},{11... | collective-permute-start | bytes 393224 | tf_op jit(solution)/shard_map/ppermute | solution.py:516
  118.5 8.0 %collective-permute-start.11 = (bf16[512,128]{1,0:T(8,128)(2,1)}, bf16[512,128]{1,0:T(8,128)(2,1)S(1)}, u32[]{:S(2)}, u32[]{:S(2)}) collective-permute-start(bf16[512,128]{1,0:T(8,128)(2,1)} %copy-done.26), channel_id=1, source_target_pairs={{1,0},{2,1},{3,2},{4,3},{5,4},{6,5},{7,6},{9,8},{10,9},{11,10},{12... | collective-permute-start | bytes 393224 | tf_op jit(solution)/shard_map/ppermute | solution.py:516
  (17 other events, 158.0 us)

commit v2 on v1

v2 whole, which is shorter than its diff:
```python
import functools

import jax
import jax.numpy as jnp
from jax import lax
from jax.experimental import pallas as pl
from jax.experimental.pallas import tpu as pltpu
from jax.sharding import PartitionSpec as P

f32 = jnp.float32
bf16 = jnp.bfloat16
BLOCK = 64
PAIR = 2 * BLOCK
STEP = 8
CHUNK = 512
NEVER = -1e30
DIGIT = 64.0
VMEM = pl.BlockSpec(memory_space=pltpu.VMEM)
SMEM = pl.BlockSpec(memory_space=pltpu.SMEM)
ANY = pl.BlockSpec(memory_space=pl.ANY)
PARAMS = pltpu.CompilerParams(vmem_limit_bytes=32 * 1024 * 1024)


def dot(a, b):
    return jnp.dot(a, b, preferred_element_type=f32)


def dot_nt(a, b):
    return lax.dot_general(a, b, (((1,), (1,)), ((), ())), preferred_element_type=f32)


def dot_tn(a, b):
    return lax.dot_general(a, b, (((0,), (0,)), ((), ())), preferred_element_type=f32)


def pick(condition):
    return jnp.where(condition, 1.0, 0.0).astype(bf16)


def pick16(values, places):
    return jnp.where(values == places, jnp.ones((), bf16), jnp.zeros((), bf16))


def call(kernel, out_shape, args, in_specs=None, scratch=()):
    many = isinstance(out_shape, (list, tuple))
    return pl.pallas_call(
        kernel,
        out_shape=out_shape,
        in_specs=in_specs or [VMEM] * len(args),
        out_specs=[VMEM] * len(out_shape) if many else VMEM,
        scratch_shapes=list(scratch),
        compiler_params=PARAMS,
    )(*args)


def shape(rows, columns, dtype):
    return jax.ShapeDtypeStruct((rows, columns), dtype)


def slot_columns(nbr, mask, halo_rows, even):
    rows = nbr.shape[1]
    block = lax.broadcasted_iota(jnp.int32, nbr.shape, 1) // BLOCK
    halo = lax.rem(block, halo_rows // BLOCK) * BLOCK
    lower = jnp.where(even, 2 * BLOCK, BLOCK)
    column = jnp.where(
        nbr < rows,
        nbr - block * BLOCK,
        jnp.where(
            nbr < rows + halo_rows,
            lower + nbr - rows - halo,
            3 * BLOCK - lower + nbr - rows - halo_rows - halo,
        ),
    )
    return jnp.where(mask > 0, column, 3 * BLOCK).astype(f32)


def selector(columns_t):
    first = lax.broadcasted_iota(jnp.int32, (BLOCK, 128), 1).astype(bf16)
    second = (lax.broadcasted_iota(jnp.int32, (BLOCK, 128), 1) + 128).astype(bf16)
    parts = []
    for k in range(8):
        wide = jnp.broadcast_to(columns_t[:, k : k + 1], (BLOCK, 128)).astype(bf16)
        parts.append(jnp.concatenate([pick16(wide, first), pick16(wide, second)], 1))
    return jnp.concatenate(parts, 0)


def selector_t(columns, rolled, half):
    lane = lax.broadcasted_iota(jnp.int32, (1, 128), 1)
    place = lax.broadcasted_iota(jnp.int32, (3 * BLOCK, 128), 0).astype(bf16)
    parts = []
    for j in range(4):
        left, right = (columns, rolled) if half == 0 else (rolled, columns)
        row = jnp.where(lane < BLOCK, left[2 * j : 2 * j + 1], right[2 * j + 1 : 2 * j + 2])
        wide = jnp.broadcast_to(row, (3 * BLOCK, 128)).astype(bf16)
        parts.append(pick16(wide, place))
    own_row = lax.broadcasted_iota(jnp.int32, (BLOCK, 128), 0)
    own_lane = lax.broadcasted_iota(jnp.int32, (BLOCK, 128), 1)
    own = pick(lax.rem(own_lane, BLOCK) == own_row)
    return jnp.concatenate([jnp.concatenate(parts, 1), jnp.concatenate([own] * 4, 1)], 0)


def window_of(far, halo, place):
    halo_rows = halo.shape[0] // 2
    start = place * BLOCK
    return jnp.concatenate(
        [
            far,
            halo[start : start + BLOCK, :],
            halo[halo_rows + start : halo_rows + start + BLOCK, :],
            jnp.full((BLOCK, far.shape[1]), NEVER, bf16),
        ],
        0,
    )


def chunk_of(index, count):
    return pl.ds(pl.multiple_of(index * count, count), count)


def level_terms(h_ref, halo_refs, self_ref, other_ref, own, far, halo):
    halo_rows = halo_refs[0].shape[0]
    other = other_ref[...] * 0.5
    h = h_ref[...]
    own[...] = dot(h, self_ref[...] * 0.5)
    far[...] = dot(h, other).astype(bf16)
    halo[:halo_rows, :] = dot(halo_refs[0][...], other).astype(bf16)
    halo[halo_rows:, :] = dot(halo_refs[1][...], other).astype(bf16)


def edges(own_rows, far_rows, slots, halo):
    places = halo.shape[0] // (2 * BLOCK)
    assert STEP % places == 0
    tables = []
    for n in range(STEP):
        part = slice(n * BLOCK, (n + 1) * BLOCK)
        window = window_of(far_rows[part], halo, n % places)
        tables.append(dot(selector(slots[part]), window))
    sums, slopes = [], []
    for n, picked in enumerate(tables):
        own = own_rows[n * BLOCK : (n + 1) * BLOCK]
        total, pieces = None, []
        for k in range(8):
            y = picked[k * BLOCK : (k + 1) * BLOCK] + own
            t = jnp.tanh(y)
            bent = y * t
            total = y + bent if total is None else total + (y + bent)
            pieces.append(((1.0 + t) * (1.0 + (y - bent))).astype(bf16))
        sums.append(total)
        slopes.append(jnp.concatenate(pieces, 0))
    return jnp.concatenate(sums, 0).astype(bf16), slopes


def edges_back(slopes, grad_sum, columns, halo_grad):
    places = halo_grad.shape[0] // (2 * BLOCK)
    halo_rows = halo_grad.shape[0] // 2
    windows = []
    for n, slope in enumerate(slopes):
        part = grad_sum[n * BLOCK : (n + 1) * BLOCK]
        grad = jnp.concatenate(
            [slope[k * BLOCK : (k + 1) * BLOCK] * part for k in range(8)], 0
        )
        mine = columns[:, n // 2 * PAIR : (n // 2 + 1) * PAIR]
        windows.append(dot(selector_t(mine, pltpu.roll(mine, BLOCK, 1), n % 2), grad))
    for place in range(places):
        for side in range(2):
            start = side * halo_rows + place * BLOCK
            total = halo_grad[start : start + BLOCK, :]
            for window in windows[place::places]:
                total = total + window[(side + 1) * BLOCK : (side + 2) * BLOCK]
            halo_grad[start : start + BLOCK, :] = total
    local = jnp.concatenate([window[:BLOCK] for window in windows], 0)
    down = jnp.concatenate([window[3 * BLOCK :] for window in windows], 0)
    return jnp.concatenate([down, local], 1).astype(bf16)


def gather_kernel(
    even_ref, lo_hbm, hi_hbm, x_hbm, first_ref, second_ref, x, wide, up, down, lo, hi, sems
):
    copies = [
        pltpu.make_async_copy(src, dst, sems.at[n])
        for n, (src, dst) in enumerate([(x_hbm, x), (lo_hbm, lo), (hi_hbm, hi)])
    ]
    for copy in copies:
        copy.start()
    for copy in copies:
        copy.wait()
    wide[...] = x[...].astype(f32)

    def step(r, carry):
        up[pl.ds(r, 1), :] = wide[pl.ds(hi[r], 1), :]
        down[pl.ds(r, 1), :] = wide[pl.ds(lo[r], 1), :]
        return carry

    lax.fori_loop(0, up.shape[0], step, None, unroll=16)
    even = even_ref[0] > 0
    first_ref[...] = jnp.where(even, up[...], down[...]).astype(bf16)
    second_ref[...] = jnp.where(even, down[...], up[...]).astype(bf16)


def gather_rows(even, x, send_lo, send_hi):
    rows, features = x.shape
    count = send_lo.shape[0]
    out = shape(count, features, bf16)
    return call(
        gather_kernel,
        [out, out],
        [even, send_lo, send_hi, x],
        [SMEM, ANY, ANY, ANY],
        [
            pltpu.VMEM((rows, features), bf16),
            pltpu.VMEM((rows, features), f32),
            pltpu.VMEM((count, features), f32),
            pltpu.VMEM((count, features), f32),
            pltpu.SMEM((count,), jnp.int32),
            pltpu.SMEM((count,), jnp.int32),
            pltpu.SemaphoreType.DMA((3,)),
        ],
    )


def owner_sums(owner_ref, tile, values):
    place = lax.broadcasted_iota(jnp.int32, (128, 128), 0) + tile * 128
    groups = owner_ref.shape[0]
    rows = jnp.concatenate(
        [pick(owner_ref[q : q + 1, :] == place) for q in range(groups)], 1
    )
    return dot(rows, values)


def prepare_kernel(
    even_ref,
    owner_ref,
    g_ref,
    nbr_ref,
    mask_ref,
    coarse_nbr_ref,
    coarse_mask_ref,
    after_ref,
    sums_ref,
    counts_ref,
    columns_ref,
    columns_t_ref,
    coarse_columns_ref,
    coarse_columns_t_ref,
    *,
    halo_rows,
    coarse_halo,
):
    even = even_ref[0] > 0
    columns_ref[...] = slot_columns(nbr_ref[...], mask_ref[...], halo_rows, even)
    columns_t_ref[...] = columns_ref[...].T
    coarse_columns_ref[...] = slot_columns(
        coarse_nbr_ref[...], coarse_mask_ref[...], coarse_halo, even
    )
    coarse_columns_t_ref[...] = coarse_columns_ref[...].T
    tiles = sums_ref.shape[0] // 128

    def step(tile, carry):
        sums_ref[chunk_of(tile, 128), :] = owner_sums(owner_ref, tile, g_ref[...]).astype(bf16)
        return carry

    lax.fori_loop(0, tiles, step, None)
    owner = owner_ref[...]
    high, low = owner // 128, lax.rem(owner, 128)
    groups = owner.shape[0]
    place = lax.broadcasted_iota(jnp.int32, (128, 128), 0)
    high_rows = jnp.concatenate(
        [pick(high[q : q + 1, :] == place[:tiles]) for q in range(groups)], 1
    )
    low_rows = jnp.concatenate(
        [pick(low[q : q + 1, :] == place) for q in range(groups)], 1
    )
    counts = dot_nt(high_rows, low_rows)
    most = jnp.floor(counts * (1 / DIGIT))
    counts_ref[...] = jnp.concatenate([most, counts - DIGIT * most], 0).astype(bf16)


def fine_forward_kernel(
    h_ref,
    first_ref,
    second_ref,
    self_ref,
    other_ref,
    node_ref,
    columns_t_ref,
    owner_ref,
    counts_ref,
    summed_ref,
    slope_ref,
    totals_ref,
    own,
    far,
    halo,
    new,
):
    level_terms(h_ref, (first_ref, second_ref), self_ref, other_ref, own, far, halo)

    def step(index, carry):
        here = chunk_of(index, STEP * BLOCK)
        total, slopes = edges(own[here, :], far[here, :], columns_t_ref[here, :], halo)
        summed_ref[here, :] = total
        slope_ref[chunk_of(index, 8 * STEP * BLOCK), :] = jnp.concatenate(slopes, 0)
        return carry

    lax.fori_loop(0, h_ref.shape[0] // (STEP * BLOCK), step, None)
    new[...] = (h_ref[...].astype(f32) + dot(summed_ref[...], node_ref[...])).astype(bf16)
    coarse_rows = totals_ref.shape[0] - counts_ref.shape[0]

    def tile_step(tile, carry):
        totals_ref[chunk_of(tile, 128), :] = owner_sums(owner_ref, tile, new[...]).astype(bf16)
        return carry

    lax.fori_loop(0, coarse_rows // 128, tile_step, None)
    totals_ref[coarse_rows:, :] = counts_ref[...]


def coarse_input_kernel(
    even_ref,
    totals_ref,
    more_totals_ref,
    sums_ref,
    more_sums_ref,
    lo_ref,
    hi_ref,
    cin_ref,
    first_ref,
    second_ref,
    chip_sums_ref,
    counts_ref,
):
    coarse_rows = cin_ref.shape[0]
    tiles = coarse_rows // 128
    chip_sums_ref[...] = (sums_ref[...].astype(f32) + more_sums_ref[...].astype(f32)).astype(bf16)
    totals = totals_ref[...].astype(f32) + more_totals_ref[...].astype(f32)
    digits = totals[coarse_rows:]
    counts_ref[...] = DIGIT * digits[:tiles] + digits[tiles:]
    per_row = counts_ref[...].T
    for tile in range(tiles):
        here = slice(tile * 128, (tile + 1) * 128)
        cin_ref[here, :] = (totals[here] / per_row[:, tile : tile + 1]).astype(bf16)
    cin = cin_ref[...]
    place = lax.broadcasted_iota(jnp.int32, (coarse_rows, lo_ref.shape[1]), 0)
    even = even_ref[0] > 0
    first = jnp.where(even, hi_ref[...], lo_ref[...])
    second = jnp.where(even, lo_ref[...], hi_ref[...])
    first_ref[...] = dot_tn(pick(first == place), cin).astype(bf16)
    second_ref[...] = dot_tn(pick(second == place), cin).astype(bf16)


def coarse_kernel(
    cin_ref,
    first_ref,
    second_ref,
    chip_sums_ref,
    more_sums_ref,
    self_ref,
    other_ref,
    node_ref,
    prolong_ref,
    columns_ref,
    columns_t_ref,
    part_ref,
    first_grad_ref,
    second_grad_ref,
    sums_ref,
    summed_ref,
    ups_ref,
    downs_ref,
    own,
    far,
    halo,
    grad_sum,
    halo_grad,
):
    halo_rows = first_ref.shape[0]
    level_terms(cin_ref, (first_ref, second_ref), self_ref, other_ref, own, far, halo)
    halo_grad[...] = jnp.zeros_like(halo_grad)
    sums_ref[...] = (chip_sums_ref[...].astype(f32) + more_sums_ref[...].astype(f32)).astype(bf16)
    part_ref[...] = dot_nt(sums_ref[...], prolong_ref[...])
    ups_ref[...] = part_ref[...].astype(bf16)
    grad_sum[...] = (dot_nt(ups_ref[...], node_ref[...]) * 0.5).astype(bf16)

    def step(index, carry):
        here = chunk_of(index, STEP * BLOCK)
        total, slopes = edges(own[here, :], far[here, :], columns_t_ref[here, :], halo)
        summed_ref[here, :] = total
        downs_ref[here, :] = edges_back(
            slopes, grad_sum[here, :], columns_ref[:, here], halo_grad
        )
        return carry

    lax.fori_loop(0, cin_ref.shape[0] // (STEP * BLOCK), step, None)
    first_grad_ref[...] = halo_grad[:halo_rows, :].astype(bf16)
    second_grad_ref[...] = halo_grad[halo_rows:, :].astype(bf16)


def coarse_tail_kernel(
    cin_ref,
    first_ref,
    second_ref,
    sums_ref,
    node_ref,
    prolong_ref,
    first_grad_ref,
    second_grad_ref,
    summed_ref,
    ups_ref,
    downs_ref,
    fine_ref,
    weights_ref,
    *,
    scale,
):
    cin = cin_ref[...]
    out = (cin.astype(f32) + dot(summed_ref[...], node_ref[...])).astype(bf16)
    fine_ref[...] = dot(out, prolong_ref[...]).astype(bf16)
    pair_grad = dot_tn(cin, downs_ref[...])
    other_grad = (
        pair_grad[:, 128:]
        + dot_tn(first_ref[...], first_grad_ref[...])
        + dot_tn(second_ref[...], second_grad_ref[...])
    )
    weights_ref[0:128, :] = (pair_grad[:, :128] * scale).astype(bf16)
    weights_ref[128:256, :] = (other_grad * scale).astype(bf16)
    weights_ref[256:384, :] = (dot_tn(summed_ref[...], ups_ref[...]) * scale).astype(bf16)
    weights_ref[384:512, :] = (dot_tn(out, sums_ref[...]) * scale).astype(bf16)


def owner_columns(owner_ref):
    owner = owner_ref[...].astype(f32)
    row = jnp.concatenate([owner[q : q + 1, :] for q in range(owner.shape[0])], 1)
    return jnp.broadcast_to(row, (8, row.shape[1])).T


def owner_rows(owners, values):
    count = owners.shape[0]
    wide = jnp.broadcast_to(owners[:, 0:1], (count, 128))
    lane = lax.broadcasted_iota(jnp.int32, (count, 128), 1).astype(f32)
    tiles = values.shape[0] // 128
    rows = jnp.concatenate([pick(wide == lane + 128.0 * tile) for tile in range(tiles)], 1)
    return dot(rows, values)


def result_kernel(h_ref, summed_ref, node_ref, owner_ref, fine_ref, out_ref, owners):
    owners[...] = owner_columns(owner_ref)

    def step(index, carry):
        here = chunk_of(index, CHUNK)
        updated = h_ref[here, :].astype(f32) + dot(summed_ref[here, :], node_ref[...])
        out_ref[here, :] = (updated + owner_rows(owners[here, :], fine_ref[...])).astype(bf16)
        return carry

    lax.fori_loop(0, h_ref.shape[0] // CHUNK, step, None)


def fine_backward_kernel(
    even_ref,
    h_ref,
    first_ref,
    second_ref,
    g_ref,
    summed_ref,
    slope_ref,
    node_ref,
    columns_ref,
    owner_ref,
    part_ref,
    counts_ref,
    coarse_downs_ref,
    first_back_ref,
    second_back_ref,
    lo_ref,
    hi_ref,
    coarse_self_ref,
    coarse_other_ref,
    coarse_weights_ref,
    ups_ref,
    downs_ref,
    first_grad_ref,
    second_grad_ref,
    weights_ref,
    owners,
    grad_sum,
    halo_grad,
    mean,
):
    halo_rows = first_ref.shape[0]
    coarse_rows = part_ref.shape[0]
    halo_grad[...] = jnp.zeros_like(halo_grad)
    owners[...] = owner_columns(owner_ref)

    even = even_ref[0] > 0
    first = jnp.where(even, hi_ref[...], lo_ref[...])
    second = jnp.where(even, lo_ref[...], hi_ref[...])
    place = lax.broadcasted_iota(jnp.int32, (coarse_rows, lo_ref.shape[1]), 0)
    sends = jnp.concatenate([pick(first == place), pick(second == place)], 1)
    back = jnp.concatenate([first_back_ref[...], second_back_ref[...]], 0)
    back = dot_nt(back, coarse_other_ref[...]).astype(bf16)
    plain = jnp.concatenate([coarse_self_ref[...], coarse_other_ref[...]], 1)
    grad_in = part_ref[...] + dot_nt(coarse_downs_ref[...], plain) + dot(sends, back)
    per_row = counts_ref[...].T
    for tile in range(coarse_rows // 128):
        here = slice(tile * 128, (tile + 1) * 128)
        mean[here, :] = (grad_in[here, :] / per_row[:, tile : tile + 1]).astype(bf16)

    count = STEP * BLOCK
    steps = h_ref.shape[0] // count

    def owner_step(index):
        here = chunk_of(index, count)
        grad_up = g_ref[here, :].astype(f32) + owner_rows(owners[here, :], mean[...])
        ups = grad_up.astype(bf16)
        ups_ref[here, :] = ups
        grad_sum[here, :] = (dot_nt(ups, node_ref[...]) * 0.5).astype(bf16)

    owner_step(0)

    def step(index, carry):
        here = chunk_of(index, count)
        slope = slope_ref[chunk_of(index, 8 * count), :]
        slopes = [slope[n * 8 * BLOCK : (n + 1) * 8 * BLOCK] for n in range(STEP)]
        downs_ref[here, :] = edges_back(
            slopes, grad_sum[here, :], columns_ref[:, here], halo_grad
        )
        owner_step(jnp.minimum(index + 1, steps - 1))
        return carry

    lax.fori_loop(0, steps, step, None)
    first_grad = halo_grad[:halo_rows, :].astype(bf16)
    second_grad = halo_grad[halo_rows:, :].astype(bf16)
    first_grad_ref[...] = first_grad
    second_grad_ref[...] = second_grad
    pair_grad = dot_tn(h_ref[...], downs_ref[...])
    weights_ref[0:128, :] = pair_grad[:, :128].astype(bf16)
    weights_ref[128:256, :] = (
        pair_grad[:, 128:]
        + dot_tn(first_ref[...], first_grad)
        + dot_tn(second_ref[...], second_grad)
    ).astype(bf16)
    weights_ref[256:384, :] = dot_tn(summed_ref[...], ups_ref[...]).astype(bf16)
    weights_ref[384:896, :] = coarse_weights_ref[...]
    weights_ref[896:1024, :] = jnp.zeros((128, 128), bf16)


def finish_kernel(
    even_ref,
    ups_ref,
    downs_ref,
    first_back_ref,
    second_back_ref,
    lo_ref,
    hi_ref,
    self_ref,
    other_ref,
    out_ref,
):
    other = other_ref[...]
    plain = jnp.concatenate([self_ref[...], other], 1)
    back = jnp.concatenate([first_back_ref[...], second_back_ref[...]], 0)
    back = dot_nt(back, other).astype(bf16)
    even = even_ref[0] > 0
    first = jnp.where(even, hi_ref[...], lo_ref[...])
    second = jnp.where(even, lo_ref[...], hi_ref[...])
    sends = jnp.concatenate([first, second], 1)
    place = lax.broadcasted_iota(jnp.int32, (CHUNK, sends.shape[1]), 0)

    def step(index, carry):
        here = chunk_of(index, CHUNK)
        rows = pick(sends - index * CHUNK == place)
        grad = ups_ref[here, :].astype(f32) + dot_nt(downs_ref[here, :], plain)
        out_ref[here, :] = (grad + dot(rows, back)).astype(bf16)
        return carry

    lax.fori_loop(0, ups_ref.shape[0] // CHUNK, step, None)


def share_kernel(parts_ref, after_ref, out_ref):
    total = parts_ref[0].astype(f32)
    for n in range(1, parts_ref.shape[0]):
        total = total + parts_ref[n].astype(f32)
    out_ref[...] = jnp.broadcast_to(total.astype(bf16)[None], out_ref.shape)


def widen_kernel(x_ref, out_ref):
    out_ref[...] = x_ref[: out_ref.shape[0], :].astype(f32)


def exchange(first, second):
    count = lax.axis_size("sub")
    routes = []
    for start in range(2):
        pairs = [(i, i + 1) for i in range(start, count - 1, 2)]
        routes.append(pairs + [(j, i) for i, j in pairs])
    return lax.ppermute(first, "sub", routes[0]), lax.ppermute(second, "sub", routes[1])


def swapped(block, axis, distance):
    return lax.ppermute(block, axis, [(i, i ^ distance) for i in range(lax.axis_size(axis))])


def total_over_all(block, axes, after):
    devices = lax.axis_size(axes)
    share = block.shape[0] // devices
    parts = lax.all_to_all(block.reshape(devices, share, 128), axes, 0, 0, tiled=False)
    mine = call(
        share_kernel,
        jax.ShapeDtypeStruct((devices, share, 128), bf16),
        [parts, after],
        [VMEM, ANY],
    )
    return lax.all_to_all(mine, axes, 0, 0, tiled=False).reshape(block.shape)


def per_device(
    states,
    cotangent,
    fine_self,
    fine_other,
    fine_node,
    coarse_self,
    coarse_other,
    coarse_node,
    prolong,
    fine_nbr,
    fine_mask,
    fine_send_lo,
    fine_send_hi,
    coarse_nbr,
    coarse_mask,
    coarse_send_lo,
    coarse_send_hi,
    coarse_owner,
):
    rows, features = states.shape
    coarse_rows = coarse_nbr.shape[0]
    halo_rows = fine_send_lo.shape[0]
    coarse_halo = coarse_send_lo.shape[0]
    count_rows = coarse_rows // 128
    owner = coarse_owner.reshape(rows // 128, 128)
    fine_nbr, fine_mask = fine_nbr.T, fine_mask.T
    coarse_nbr, coarse_mask = coarse_nbr.T, coarse_mask.T
    coarse_lo, coarse_hi = coarse_send_lo[None], coarse_send_hi[None]
    even = (1 - lax.rem(lax.axis_index("sub"), 2)).astype(jnp.int32).reshape(1)

    def buffer(count, columns, dtype):
        return pltpu.VMEM((count, columns), dtype)

    to_first, to_second = gather_rows(even, states, fine_send_lo, fine_send_hi)
    first, second = exchange(to_first, to_second)

    sums, counts, columns, columns_t, coarse_columns, coarse_columns_t = call(
        functools.partial(prepare_kernel, halo_rows=halo_rows, coarse_halo=coarse_halo),
        [
            shape(coarse_rows, features, bf16),
            shape(2 * count_rows, features, bf16),
            shape(8, rows, f32),
            shape(rows, 8, f32),
            shape(8, coarse_rows, f32),
            shape(coarse_rows, 8, f32),
        ],
        [even, owner, cotangent, fine_nbr, fine_mask, coarse_nbr, coarse_mask, to_first],
        [SMEM] + [VMEM] * 6 + [ANY],
    )
    more_sums = swapped(sums, "grp", 1)

    summed, slope, totals = call(
        fine_forward_kernel,
        [
            shape(rows, features, bf16),
            shape(8 * rows, features, bf16),
            shape(coarse_rows + 2 * count_rows, features, bf16),
        ],
        [states, first, second, fine_self, fine_other, fine_node, columns_t, owner, counts],
        scratch=[
            buffer(rows, features, f32),
            buffer(rows, features, bf16),
            buffer(2 * halo_rows, features, bf16),
            buffer(rows, features, bf16),
        ],
    )
    chip_totals = (totals.astype(f32) + swapped(totals, "grp", 1).astype(f32)).astype(bf16)
    more_totals = swapped(chip_totals, "grp", 2)

    coarse_in, to_first, to_second, chip_sums, counts = call(
        coarse_input_kernel,
        [
            shape(coarse_rows, features, bf16),
            shape(coarse_halo, features, bf16),
            shape(coarse_halo, features, bf16),
            shape(coarse_rows, features, bf16),
            shape(count_rows, features, f32),
        ],
        [even, chip_totals, more_totals, sums, more_sums, coarse_lo, coarse_hi],
        [SMEM] + [VMEM] * 6,
    )
    coarse_first, coarse_second = exchange(to_first, to_second)
    more_sums = swapped(chip_sums, "grp", 2)

    coarse_part, first_grad, second_grad, sums, coarse_sum, coarse_ups, coarse_downs = call(
        coarse_kernel,
        [
            shape(coarse_rows, features, f32),
            shape(coarse_halo, features, bf16),
            shape(coarse_halo, features, bf16),
            shape(coarse_rows, features, bf16),
            shape(coarse_rows, features, bf16),
            shape(coarse_rows, features, bf16),
            shape(coarse_rows, 2 * features, bf16),
        ],
        [
            coarse_in, coarse_first, coarse_second, chip_sums, more_sums,
            coarse_self, coarse_other, coarse_node, prolong, coarse_columns, coarse_columns_t,
        ],
        scratch=[
            buffer(coarse_rows, features, f32),
            buffer(coarse_rows, features, bf16),
            buffer(2 * coarse_halo, features, bf16),
            buffer(coarse_rows, features, bf16),
            buffer(2 * coarse_halo, features, f32),
        ],
    )
    first_back, second_back = exchange(first_grad, second_grad)

    fine_term, coarse_weights = call(
        functools.partial(coarse_tail_kernel, scale=1.0 / lax.axis_size("grp")),
        [shape(coarse_rows, features, bf16), shape(4 * features, features, bf16)],
        [
            coarse_in, coarse_first, coarse_second, sums, coarse_node, prolong,
            first_grad, second_grad, coarse_sum, coarse_ups, coarse_downs,
        ],
    )
    result = call(
        result_kernel,
        shape(rows, features, bf16),
        [states, summed, fine_node, owner, fine_term],
        scratch=[buffer(rows, 8, f32)],
    )

    ups, downs, first_grad, second_grad, weights = call(
        fine_backward_kernel,
        [
            shape(rows, features, bf16),
            shape(rows, 2 * features, bf16),
            shape(halo_rows, features, bf16),
            shape(halo_rows, features, bf16),
            shape(8 * features, features, bf16),
        ],
        [
            even, states, first, second, cotangent, summed, slope, fine_node, columns, owner,
            coarse_part, counts, coarse_downs, first_back, second_back, coarse_lo, coarse_hi,
            coarse_self, coarse_other, coarse_weights,
        ],
        [SMEM] + [VMEM] * 19,
        [
            buffer(rows, 8, f32),
            buffer(rows, features, bf16),
            buffer(2 * halo_rows, features, f32),
            buffer(coarse_rows, features, bf16),
        ],
    )
    weights = total_over_all(weights, ("grp", "sub"), result)
    first_back, second_back = exchange(first_grad, second_grad)

    grad_states = call(
        finish_kernel,
        shape(rows, features, bf16),
        [
            even, ups, downs, first_back, second_back, fine_send_lo[None], fine_send_hi[None],
            fine_self, fine_other,
        ],
        [SMEM] + [VMEM] * 8,
    )
    grad_weights = call(widen_kernel, shape(7 * features, features, f32), [weights])
    return (result, grad_states, grad_weights.reshape(7, features, features))


def solution(mesh):
    fine = P(("grp", "sub"), None)
    fine_row = P(("grp", "sub"))
    in_specs = (
        (fine, fine)
        + (P(),) * 7
        + (fine, fine, fine_row, fine_row)
        + (P("sub", None), P("sub", None), P("sub"), P("sub"), fine_row)
    )
    return jax.shard_map(
        per_device, mesh=mesh, in_specs=in_specs, out_specs=(fine, fine, P()), check_vma=False
    )
```

time: 135 us -> 121 us (0.90)
  blocking collectives: 14.8 us -> 0 us
  local copies, waits for them, and re-layouts: 6.99 us -> 18 us
  Pallas kernels: 54.7 us -> 50 us
  other arithmetic: 2.49 us -> 0.07 us
  starting transfers between devices: 28.6 us -> 26.3 us
    all_to_all x1 -> x0, blocking collectives: 14.8 us -> none  [total_over_all(): lax.all_to_all(block.astype(bf16).reshape(devices, share, 128), axes, 0,...]
    unnamed x56 -> x68, local copies, waits for them, and re-layouts: 5.26 us -> 18 us
    ppermute x8, starting transfers between devices: 21.7 us -> 12.9 us  [the longest x4 10.2 us: exchange(): lax.ppermute(first, 'sub', routes[0])]
    all_to_all x1 -> x2, starting transfers between devices: 3.31 us -> 10.2 us  [the longest x1 7.46 us: total_over_all(): lax.all_to_all(block.reshape(devices, share, 128), axes, 0, 0, tiled=False)]
    pallas_call x9 -> x11, Pallas kernels: 54.7 us -> 50 us  [call(): pl.pallas_call(kernel, out_shape=out_shape, in_specs=in_specs or [VMEM] *...]
    all_to_all x1 -> x2, waiting for transfers between devices: 0.01 us -> 3.05 us  [the longest x1 3.05 us: total_over_all(): lax.all_to_all(block.reshape(devices, share, 128), axes, 0, 0, tiled=False)]
    ppermute x8, waiting for transfers between devices: 13.8 us -> 10.9 us  [the longest x4 10.9 us: exchange(): lax.ppermute(first, 'sub', routes[0])]
  transfers between devices with their start and end apart: 13 -> 14, of which waited for: 6 -> 7; matrix products, arithmetic and copies ran while one was open for 0% -> 0% of each run, Pallas kernels for 9% -> 14%
where the time goes in v2:
time: 121 us; the launch traced here: 120 us
  Pallas kernels  50 us (41%)
  starting transfers between devices  26.3 us (22%)
  waiting for transfers between devices  24.7 us (20%)
  local copies, waits for them, and re-layouts  18 us (15%)
    pallas_call x11, Pallas kernels, call(): pl.pallas_call(kernel, out_shape=out_shape, in_specs=in_specs or [VMEM] *...  50 us
    unnamed x68, local copies, waits for them, and re-layouts  18 us
    ppermute x4, waiting for transfers between devices, exchange(): lax.ppermute(first, 'sub', routes[0])  10.9 us
    ppermute x4, waiting for transfers between devices, swapped(): lax.ppermute(block, axis, [(i, i ^ distance) for i in range(lax.axis_size...  10.8 us
    ppermute x4, starting transfers between devices, exchange(): lax.ppermute(first, 'sub', routes[0])  10.2 us
    all_to_all x1, starting transfers between devices, total_over_all(): lax.all_to_all(block.reshape(devices, share, 128), axes, 0, 0, tiled=False)  7.46 us
    ppermute x4, starting transfers between devices, swapped(): lax.ppermute(block, axis, [(i, i ^ distance) for i in range(lax.axis_size...  3.18 us
    all_to_all x1, waiting for transfers between devices, total_over_all(): lax.all_to_all(block.reshape(devices, share, 128), axes, 0, 0, tiled=False)  3.05 us
  transfers between devices with their start and end apart: 14, of which 7 were waited for; matrix products, arithmetic and copies ran while one was open for 0% of the time, Pallas kernels for 14%

profile of v2, /device:TPU:0, one launch (start us, length us, event | category | flops | bytes accessed | tf_op | source)
XLA Modules:
  0.0 120.0 jit_solution(5351816144930201583)
XLA Ops:
  3.2 1.7 %shard_map.193 = (bf16[512,128]{1,0:T(8,128)(2,1)S(1)}, bf16[512,128]{1,0:T(8,128)(2,1)S(1)}) custom-call(s32[1]{0:T(128)} %bitcast.even_ref, s32[512]{0:T(512)S(1)} %copy-done.26, s32[512]{0:T(512)S(1)} %copy-done.28, bf16[4096,128]{1,0:T(8,128)(2,1)S(1)} %copy-done), custom_call_target="tpu_custom_call" | custom-call | tf_op jit(solution)/shard_map/pallas_call | solution.py:46
  5.6 5.8 %collective-permute-start = (bf16[512,128]{1,0:T(8,128)(2,1)S(1)}, bf16[512,128]{1,0:T(8,128)(2,1)S(1)}, u32[]{:S(2)}, u32[]{:S(2)}) collective-permute-start(bf16[512,128]{1,0:T(8,128)(2,1)S(1)} %get-tuple-element.33.after_ref), channel_id=1, source_target_pairs={{0,1},{2,3},{4,5},{6,7},{1,0},{3,2},{5,4},{7,6},{8,9},{10,11},{12,... | collective-permute-start | bytes 393224 | tf_op jit(solution)/shard_map/ppermute | solution.py:594
  16.7 4.5 %shard_map.194 = (bf16[1024,128]{1,0:T(8,128)(2,1)S(1)}, bf16[16,128]{1,0:T(8,128)(2,1)S(1)}, f32[8,4096]{1,0:T(8,128)S(1)}, f32[4096,8]{1,0:T(8,128)S(1)}, f32[...) custom-call(s32[1]{0:T(128)} %bitcast.even_ref, s32[32,128]{1,0:T(8,128)S(1)} %bitcast.14, bf16[4096,128]{1,0:T(8,128)(2,1)S(1)} %copy-done.2, ...), custom_call_target="tpu_custom_call" | custom-call | tf_op jit(solution)/shard_map/pallas_call | solution.py:46
  23.6 13.1 %shard_map.195 = (bf16[4096,128]{1,0:T(8,128)(2,1)S(1)}, bf16[32768,128]{1,0:T(8,128)(2,1)S(1)}, bf16[1040,128]{1,0:T(8,128)(2,1)S(1)}) custom-call(bf16[4096,128]{1,0:T(8,128)(2,1)S(1)} %copy-done.1, bf16[512,128]{1,0:T(8,128)(2,1)S(1)} %collective-permute-done.first_ref, bf16[512,128]{1,0:T(8,128)(2,1)S(1)} %collective-permute-done.1.second_ref, ...), custom_call_target="tpu_custom_call" | custom-call | tf_op jit(solution)/shard_map/pallas_call | solution.py:46
  36.8 1.5 %collective-permute-done.2 = bf16[1040,128]{1,0:T(8,128)(2,1)S(1)} collective-permute-done((bf16[1040,128]{1,0:T(8,128)(2,1)S(1)}, bf16[1040,128]{1,0:T(8,128)(2,1)S(1)}, u32[]{:S(2)}, u32[]{:S(2)}) %collective-permute-start.2) | collective-permute-done | bytes 266272 | tf_op jit(solution)/shard_map/ppermute | solution.py:598
  38.4 1.6 %collective-permute-start.3 = (bf16[1040,128]{1,0:T(8,128)(2,1)S(1)}, bf16[1040,128]{1,0:T(8,128)(2,1)S(1)}, u32[]{:S(2)}, u32[]{:S(2)}) collective-permute-start(bf16[1040,128]{1,0:T(8,128)(2,1)S(1)} %add_convert_fusion.totals_ref), channel_id=1, source_target_pairs={{0,16},{8,24},{16,0},{24,8},{1,17},{9,25},{17,1},{25,9},{2,18},{10... | collective-permute-start | bytes 798728 | tf_op jit(solution)/shard_map/ppermute | solution.py:598
  39.9 1.5 %collective-permute-done.4.more_sums_ref = bf16[1024,128]{1,0:T(8,128)(2,1)S(1)} collective-permute-done((bf16[1024,128]{1,0:T(8,128)(2,1)S(1)}, bf16[1024,128]{1,0:T(8,128)(2,1)S(1)}, u32[]{:S(2)}, u32[]{:S(2)}) %collective-permute-start.4) | collective-permute-done | bytes 262176 | tf_op jit(solution)/shard_map/ppermute | solution.py:598
  41.5 5.4 %collective-permute-done.3.more_totals_ref = bf16[1040,128]{1,0:T(8,128)(2,1)S(1)} collective-permute-done((bf16[1040,128]{1,0:T(8,128)(2,1)S(1)}, bf16[1040,128]{1,0:T(8,128)(2,1)S(1)}, u32[]{:S(2)}, u32[]{:S(2)}) %collective-permute-start.3) | collective-permute-done | bytes 266272 | tf_op jit(solution)/shard_map/ppermute | solution.py:598
  47.6 1.6 %collective-permute-start.7 = (bf16[1024,128]{1,0:T(8,128)(2,1)S(1)}, bf16[1024,128]{1,0:T(8,128)(2,1)S(1)}, u32[]{:S(2)}, u32[]{:S(2)}) collective-permute-start(bf16[1024,128]{1,0:T(8,128)(2,1)S(1)} %get-tuple-element.43.chip_sums_ref), channel_id=1, source_target_pairs={{0,16},{8,24},{16,0},{24,8},{1,17},{9,25},{17,1},{25,9},{2,18},{10... | collective-permute-start | bytes 786440 | tf_op jit(solution)/shard_map/ppermute | solution.py:598
  49.8 3.1 %collective-permute-done.5.first_ref = bf16[64,128]{1,0:T(8,128)(2,1)S(1)} collective-permute-done((bf16[64,128]{1,0:T(8,128)(2,1)S(1)}, bf16[64,128]{1,0:T(8,128)(2,1)S(1)}, u32[]{:S(2)}, u32[]{:S(2)}) %collective-permute-start.5) | collective-permute-done | bytes 16416 | tf_op jit(solution)/shard_map/ppermute | solution.py:594
  52.9 2.3 %collective-permute-done.7.more_sums_ref = bf16[1024,128]{1,0:T(8,128)(2,1)S(1)} collective-permute-done((bf16[1024,128]{1,0:T(8,128)(2,1)S(1)}, bf16[1024,128]{1,0:T(8,128)(2,1)S(1)}, u32[]{:S(2)}, u32[]{:S(2)}) %collective-permute-start.7) | collective-permute-done | bytes 262176 | tf_op jit(solution)/shard_map/ppermute | solution.py:598
  55.2 3.9 %shard_map.197 = (f32[1024,128]{1,0:T(8,128)S(1)}, bf16[64,128]{1,0:T(8,128)(2,1)S(1)}, bf16[64,128]{1,0:T(8,128)(2,1)S(1)}, bf16[1024,128]{1,0:T(8,128)(2,1)S(1...) custom-call(bf16[1024,128]{1,0:T(8,128)(2,1)S(1)} %get-tuple-element.40.cin_ref, ...), custom_call_target="tpu_custom_call" | custom-call | tf_op jit(solution)/shard_map/pallas_call | solution.py:46
  59.1 2.6 %collective-permute-start.8 = (bf16[64,128]{1,0:T(8,128)(2,1)S(1)}, bf16[64,128]{1,0:T(8,128)(2,1)S(1)}, u32[]{:S(2)}, u32[]{:S(2)}) collective-permute-start(bf16[64,128]{1,0:T(8,128)(2,1)S(1)} %get-tuple-element.47.first_grad_ref), channel_id=1, source_target_pairs={{0,1},{2,3},{4,5},{6,7},{1,0},{3,2},{5,4},{7,6},{8,9},{10,11},{12,... | collective-permute-start | bytes 49160 | tf_op jit(solution)/shard_map/ppermute | solution.py:594
  63.7 11.9 %shard_map.200 = (bf16[4096,128]{1,0:T(8,128)(2,1)S(1)}, bf16[4096,256]{1,0:T(8,128)(2,1)S(1)}, bf16[512,128]{1,0:T(8,128)(2,1)S(1)}, bf16[512,128]{1,0:T(8,128)(2,1)S(1)}, bf16[1024,128]{1,0:T(8,128)(2,1)S(1)}) custom-call(s32[1]{0:T(128)} %bitcast.even_ref, bf16[4096,128]{1,0:T(8,128)(2,1)S(1)} %copy-done.1, ...), custom_call_target="tpu_custom_call" | custom-call | tf_op jit(solution)/shard_map/pallas_call | solution.py:46
  75.6 1.3 %copy-done.5 = bf16[4096,256]{1,0:T(8,128)(2,1)} copy-done((bf16[4096,256]{1,0:T(8,128)(2,1)}, bf16[4096,256]{1,0:T(8,128)(2,1)S(1)}, u32[]{:S(2)}) %copy-start.5) | copy-done | bytes 2097176
  79.0 7.5 %all-to-all-start = ((bf16[32,32,128]{2,1,0:T(8,128)(2,1)}), bf16[32,32,128]{2,1,0:T(8,128)(2,1)S(1)}, u32[]{:S(2)}, u32[]{:S(2)}) async-start(bf16[32,32,128]{2,1,0:T(8,128)(2,1)} %bitcast.18), calls=%async_computation | async-start | bytes 524288 | tf_op jit(solution)/shard_map/all_to_all | solution.py:604
  87.4 6.6 %shard_map.199.after_ref = bf16[4096,128]{1,0:T(8,128)(2,1)} custom-call(bf16[4096,128]{1,0:T(8,128)(2,1)S(1)} %copy-done.1, bf16[4096,128]{1,0:T(8,128)(2,1)S(1)} %get-tuple-element.37.summed_ref, bf16[128,128]{1,0:T(8,128)(2,1)S(1)} %copy-done.8, s32[32,128]{1,0:T(8,128)S(1)} %bitcast.17, bf16[1024,128]{1,0:T(8,128)(2,1)S(1)} %copy-done.13), custom_call_target="tpu_custom_call" | custom-call | tf_op jit(solution)/shard_map/pallas_call | solution.py:46
  94.0 3.0 %all-to-all-done.parts_ref = bf16[32,32,128]{2,1,0:T(8,128)(2,1)S(1)} async-done(((bf16[32,32,128]{2,1,0:T(8,128)(2,1)}), bf16[32,32,128]{2,1,0:T(8,128)(2,1)S(1)}, u32[]{:S(2)}, u32[]{:S(2)}) %all-to-all-start) | async-done | bytes 262176 | tf_op jit(solution)/shard_map/all_to_all | solution.py:604
  97.1 1.2 %copy-done.4 = bf16[4096,128]{1,0:T(8,128)(2,1)S(1)} copy-done((bf16[4096,128]{1,0:T(8,128)(2,1)S(1)}, bf16[4096,128]{1,0:T(8,128)(2,1)}, u32[]{:S(2)}) %copy-start.4) | copy-done | bytes 1048600
  99.1 2.8 %all-to-all-start.1 = ((bf16[32,32,128]{2,1,0:T(8,128)(2,1)}), bf16[32,32,128]{2,1,0:T(8,128)(2,1)S(1)}, u32[]{:S(2)}, u32[]{:S(2)}) async-start(bf16[32,32,128]{2,1,0:T(8,128)(2,1)} %shard_map.202), calls=%async_computation.1 | async-start | bytes 524288 | tf_op jit(solution)/shard_map/all_to_all | solution.py:611
  101.9 1.8 %collective-permute-start.10 = (bf16[512,128]{1,0:T(8,128)(2,1)}, bf16[512,128]{1,0:T(8,128)(2,1)S(1)}, u32[]{:S(2)}, u32[]{:S(2)}) collective-permute-start(bf16[512,128]{1,0:T(8,128)(2,1)} %copy-done.33), channel_id=1, source_target_pairs={{0,1},{2,3},{4,5},{6,7},{1,0},{3,2},{5,4},{7,6},{8,9},{10,11},{12,... | collective-permute-start | bytes 393224 | tf_op jit(solution)/shard_map/ppermute | solution.py:594
  104.4 7.8 %collective-permute-done.10.first_back_ref = bf16[512,128]{1,0:T(8,128)(2,1)S(1)} collective-permute-done((bf16[512,128]{1,0:T(8,128)(2,1)}, bf16[512,128]{1,0:T(8,128)(2,1)S(1)}, u32[]{:S(2)}, u32[]{:S(2)}) %collective-permute-start.10) | collective-permute-done | bytes 131104 | tf_op jit(solution)/shard_map/ppermute | solution.py:594
  112.2 1.6 %copy-done.6 = bf16[4096,256]{1,0:T(8,128)(2,1)S(1)} copy-done((bf16[4096,256]{1,0:T(8,128)(2,1)S(1)}, bf16[4096,256]{1,0:T(8,128)(2,1)}, u32[]{:S(2)}) %copy-start.6) | copy-done | bytes 2097176
  113.8 5.4 %shard_map.201 = bf16[4096,128]{1,0:T(8,128)(2,1)} custom-call(s32[1]{0:T(128)} %bitcast.even_ref, bf16[4096,128]{1,0:T(8,128)(2,1)S(1)} %get-tuple-element.58.ups_ref, bf16[4096,256]{1,0:T(8,128)(2,1)S(1)} %copy-done.6, bf16[512,128]{1,0:T(8,128)(2,1)S(1)} %collective-permute-done.10.first_back_ref, ...), custom_call_target="tpu_custom_call" | custom-call | tf_op jit(solution)/shard_map/pallas_call | solution.py:46
  (84 shorter events, 19.5 us)
Async XLA Ops:
  4.9 16.3 %collective-permute-start.1 = (bf16[512,128]{1,0:T(8,128)(2,1)S(1)}, bf16[512,128]{1,0:T(8,128)(2,1)S(1)}, u32[]{:S(2)}, u32[]{:S(2)}) collective-permute-start(bf16[512,128]{1,0:T(8,128)(2,1)S(1)} %get-tuple-element.34), channel_id=1, source_target_pairs={{1,2},{3,4},{5,6},{2,1},{4,3},{6,5},{9,10},{11,12},{13,14},{10,9},... | collective-permute-start | bytes 393224 | tf_op jit(solution)/shard_map/ppermute | solution.py:594
  5.6 15.6 %collective-permute-start = (bf16[512,128]{1,0:T(8,128)(2,1)S(1)}, bf16[512,128]{1,0:T(8,128)(2,1)S(1)}, u32[]{:S(2)}, u32[]{:S(2)}) collective-permute-start(bf16[512,128]{1,0:T(8,128)(2,1)S(1)} %get-tuple-element.33.after_ref), channel_id=1, source_target_pairs={{0,1},{2,3},{4,5},{6,7},{1,0},{3,2},{5,4},{7,6},{8,9},{10,11},{12,... | collective-permute-start | bytes 393224 | tf_op jit(solution)/shard_map/ppermute | solution.py:594
  23.5 23.3 %copy-start.30 = (s32[64]{0:T(128)S(1)}, s32[64]{0:T(128)}, u32[]{:S(2)}) copy-start(s32[64]{0:T(128)} %param.33) | copy-start | bytes 772
  23.5 23.3 %copy-start.31 = (s32[64]{0:T(128)S(1)}, s32[64]{0:T(128)}, u32[]{:S(2)}) copy-start(s32[64]{0:T(128)} %param.34) | copy-start | bytes 772
  23.5 31.6 %copy-start.18 = (bf16[128,128]{1,0:T(8,128)(2,1)S(1)}, bf16[128,128]{1,0:T(8,128)(2,1)}, u32[]{:S(2)}) copy-start(bf16[128,128]{1,0:T(8,128)(2,1)} %coarse_self_ref.1) | copy-start | bytes 98308
  23.5 31.6 %copy-start.19 = (bf16[128,128]{1,0:T(8,128)(2,1)S(1)}, bf16[128,128]{1,0:T(8,128)(2,1)}, u32[]{:S(2)}) copy-start(bf16[128,128]{1,0:T(8,128)(2,1)} %coarse_other_ref.1) | copy-start | bytes 98308
  23.5 31.6 %copy-start.22 = (bf16[128,128]{1,0:T(8,128)(2,1)S(1)}, bf16[128,128]{1,0:T(8,128)(2,1)}, u32[]{:S(2)}) copy-start(bf16[128,128]{1,0:T(8,128)(2,1)} %node_ref.7) | copy-start | bytes 98308
  23.6 31.6 %copy-start.23 = (bf16[128,128]{1,0:T(8,128)(2,1)S(1)}, bf16[128,128]{1,0:T(8,128)(2,1)}, u32[]{:S(2)}) copy-start(bf16[128,128]{1,0:T(8,128)(2,1)} %prolong_ref.3) | copy-start | bytes 98308
  36.7 1.6 %collective-permute-start.2 = (bf16[1040,128]{1,0:T(8,128)(2,1)S(1)}, bf16[1040,128]{1,0:T(8,128)(2,1)S(1)}, u32[]{:S(2)}, u32[]{:S(2)}) collective-permute-start(bf16[1040,128]{1,0:T(8,128)(2,1)S(1)} %get-tuple-element.38), channel_id=1, source_target_pairs={{0,8},{8,0},{16,24},{24,16},{1,9},{9,1},{17,25},{25,17},{2,10},{10... | collective-permute-start | bytes 798728 | tf_op jit(solution)/shard_map/ppermute | solution.py:598
  38.4 8.5 %collective-permute-start.3 = (bf16[1040,128]{1,0:T(8,128)(2,1)S(1)}, bf16[1040,128]{1,0:T(8,128)(2,1)S(1)}, u32[]{:S(2)}, u32[]{:S(2)}) collective-permute-start(bf16[1040,128]{1,0:T(8,128)(2,1)S(1)} %add_convert_fusion.totals_ref), channel_id=1, source_target_pairs={{0,16},{8,24},{16,0},{24,8},{1,17},{9,25},{17,1},{25,9},{2,18},{10... | collective-permute-start | bytes 798728 | tf_op jit(solution)/shard_map/ppermute | solution.py:598
  39.9 1.5 %collective-permute-start.4 = (bf16[1024,128]{1,0:T(8,128)(2,1)S(1)}, bf16[1024,128]{1,0:T(8,128)(2,1)S(1)}, u32[]{:S(2)}, u32[]{:S(2)}) collective-permute-start(bf16[1024,128]{1,0:T(8,128)(2,1)S(1)} %get-tuple-element.39.sums_ref), channel_id=1, source_target_pairs={{0,8},{8,0},{16,24},{24,16},{1,9},{9,1},{17,25},{25,17},{2,10},{10... | collective-permute-start | bytes 786440 | tf_op jit(solution)/shard_map/ppermute | solution.py:598
  47.6 7.6 %collective-permute-start.7 = (bf16[1024,128]{1,0:T(8,128)(2,1)S(1)}, bf16[1024,128]{1,0:T(8,128)(2,1)S(1)}, u32[]{:S(2)}, u32[]{:S(2)}) collective-permute-start(bf16[1024,128]{1,0:T(8,128)(2,1)S(1)} %get-tuple-element.43.chip_sums_ref), channel_id=1, source_target_pairs={{0,16},{8,24},{16,0},{24,8},{1,17},{9,25},{17,1},{25,9},{2,18},{10... | collective-permute-start | bytes 786440 | tf_op jit(solution)/shard_map/ppermute | solution.py:598
  49.1 3.7 %collective-permute-start.5 = (bf16[64,128]{1,0:T(8,128)(2,1)S(1)}, bf16[64,128]{1,0:T(8,128)(2,1)S(1)}, u32[]{:S(2)}, u32[]{:S(2)}) collective-permute-start(bf16[64,128]{1,0:T(8,128)(2,1)S(1)} %get-tuple-element.41), channel_id=1, source_target_pairs={{0,1},{2,3},{4,5},{6,7},{1,0},{3,2},{5,4},{7,6},{8,9},{10,11},{12,... | collective-permute-start | bytes 49160 | tf_op jit(solution)/shard_map/ppermute | solution.py:594
  49.2 3.7 %collective-permute-start.6 = (bf16[64,128]{1,0:T(8,128)(2,1)S(1)}, bf16[64,128]{1,0:T(8,128)(2,1)S(1)}, u32[]{:S(2)}, u32[]{:S(2)}) collective-permute-start(bf16[64,128]{1,0:T(8,128)(2,1)S(1)} %get-tuple-element.42), channel_id=1, source_target_pairs={{1,2},{3,4},{5,6},{2,1},{4,3},{6,5},{9,10},{11,12},{13,14},{10,9},... | collective-permute-start | bytes 49160 | tf_op jit(solution)/shard_map/ppermute | solution.py:594
  59.1 4.6 %collective-permute-start.8 = (bf16[64,128]{1,0:T(8,128)(2,1)S(1)}, bf16[64,128]{1,0:T(8,128)(2,1)S(1)}, u32[]{:S(2)}, u32[]{:S(2)}) collective-permute-start(bf16[64,128]{1,0:T(8,128)(2,1)S(1)} %get-tuple-element.47.first_grad_ref), channel_id=1, source_target_pairs={{0,1},{2,3},{4,5},{6,7},{1,0},{3,2},{5,4},{7,6},{8,9},{10,11},{12,... | collective-permute-start | bytes 49160 | tf_op jit(solution)/shard_map/ppermute | solution.py:594
  61.7 2.0 %collective-permute-start.9 = (bf16[64,128]{1,0:T(8,128)(2,1)S(1)}, bf16[64,128]{1,0:T(8,128)(2,1)S(1)}, u32[]{:S(2)}, u32[]{:S(2)}) collective-permute-start(bf16[64,128]{1,0:T(8,128)(2,1)S(1)} %get-tuple-element.48.second_grad_ref), channel_id=1, source_target_pairs={{1,2},{3,4},{5,6},{2,1},{4,3},{6,5},{9,10},{11,12},{13,14},{10,9},... | collective-permute-start | bytes 49160 | tf_op jit(solution)/shard_map/ppermute | solution.py:594
  79.0 18.1 %all-to-all-start = ((bf16[32,32,128]{2,1,0:T(8,128)(2,1)}), bf16[32,32,128]{2,1,0:T(8,128)(2,1)S(1)}, u32[]{:S(2)}, u32[]{:S(2)}) async-start(bf16[32,32,128]{2,1,0:T(8,128)(2,1)} %bitcast.18), calls=%async_computation | async-start | bytes 524288 | tf_op jit(solution)/shard_map/all_to_all | solution.py:604
  87.4 24.8 %copy-start.15 = (bf16[128,128]{1,0:T(8,128)(2,1)S(1)}, bf16[128,128]{1,0:T(8,128)(2,1)}, u32[]{:S(2)}) copy-start(bf16[128,128]{1,0:T(8,128)(2,1)} %self_ref.5) | copy-start | bytes 98308
  87.4 24.8 %copy-start.17 = (bf16[128,128]{1,0:T(8,128)(2,1)S(1)}, bf16[128,128]{1,0:T(8,128)(2,1)}, u32[]{:S(2)}) copy-start(bf16[128,128]{1,0:T(8,128)(2,1)} %other_ref.5) | copy-start | bytes 98308
  87.4 24.8 %copy-start.27 = (s32[512]{0:T(512)S(1)}, s32[512]{0:T(512)}, u32[]{:S(2)}) copy-start(s32[512]{0:T(512)} %lo_hbm.1) | copy-start | bytes 6148
  87.4 24.8 %copy-start.29 = (s32[512]{0:T(512)S(1)}, s32[512]{0:T(512)}, u32[]{:S(2)}) copy-start(s32[512]{0:T(512)} %hi_hbm.1) | copy-start | bytes 6148
  99.1 20.1 %all-to-all-start.1 = ((bf16[32,32,128]{2,1,0:T(8,128)(2,1)}), bf16[32,32,128]{2,1,0:T(8,128)(2,1)S(1)}, u32[]{:S(2)}, u32[]{:S(2)}) async-start(bf16[32,32,128]{2,1,0:T(8,128)(2,1)} %shard_map.202), calls=%async_computation.1 | async-start | bytes 524288 | tf_op jit(solution)/shard_map/all_to_all | solution.py:611
  101.9 10.3 %collective-permute-start.10 = (bf16[512,128]{1,0:T(8,128)(2,1)}, bf16[512,128]{1,0:T(8,128)(2,1)S(1)}, u32[]{:S(2)}, u32[]{:S(2)}) collective-permute-start(bf16[512,128]{1,0:T(8,128)(2,1)} %copy-done.33), channel_id=1, source_target_pairs={{0,1},{2,3},{4,5},{6,7},{1,0},{3,2},{5,4},{7,6},{8,9},{10,11},{12,... | collective-permute-start | bytes 393224 | tf_op jit(solution)/shard_map/ppermute | solution.py:594
  103.7 8.5 %collective-permute-start.11 = (bf16[512,128]{1,0:T(8,128)(2,1)}, bf16[512,128]{1,0:T(8,128)(2,1)S(1)}, u32[]{:S(2)}, u32[]{:S(2)}) collective-permute-start(bf16[512,128]{1,0:T(8,128)(2,1)} %copy-done.32), channel_id=1, source_target_pairs={{1,2},{3,4},{5,6},{2,1},{4,3},{6,5},{9,10},{11,12},{13,14},{10,9},... | collective-permute-start | bytes 393224 | tf_op jit(solution)/shard_map/ppermute | solution.py:594
  (24 other events, 90.2 us)

commit v3 on v2

--- a/solution.py
+++ b/solution.py
@@ -18,6 +18,7 @@
 VMEM = pl.BlockSpec(memory_space=pltpu.VMEM)
 SMEM = pl.BlockSpec(memory_space=pltpu.SMEM)
 ANY = pl.BlockSpec(memory_space=pl.ANY)
+HBM = pl.BlockSpec(memory_space=pltpu.HBM)
 PARAMS = pltpu.CompilerParams(vmem_limit_bytes=32 * 1024 * 1024)
 
 
@@ -41,13 +42,18 @@
     return jnp.where(values == places, jnp.ones((), bf16), jnp.zeros((), bf16))
 
 
-def call(kernel, out_shape, args, in_specs=None, scratch=()):
+def call(kernel, out_shape, args, in_specs=None, scratch=(), out_specs=None):
     many = isinstance(out_shape, (list, tuple))
+    in_specs = in_specs or [VMEM] * len(args)
+    args = [
+        pltpu.with_memory_space_constraint(arg, pltpu.HBM) if spec is HBM else arg
+        for arg, spec in zip(args, in_specs)
+    ]
     return pl.pallas_call(
         kernel,
         out_shape=out_shape,
-        in_specs=in_specs or [VMEM] * len(args),
-        out_specs=[VMEM] * len(out_shape) if many else VMEM,
+        in_specs=in_specs,
+        out_specs=out_specs or ([VMEM] * len(out_shape) if many else VMEM),
         scratch_shapes=list(scratch),
         compiler_params=PARAMS,
     )(*args)
@@ -117,11 +123,15 @@
     return pl.ds(pl.multiple_of(index * count, count), count)
 
 
-def level_terms(h_ref, halo_refs, self_ref, other_ref, own, far, halo):
+def matrix(weights_ref, n):
+    return weights_ref[128 * n : 128 * (n + 1), :]
+
+
+def level_terms(h_ref, halo_refs, self_weight, other_weight, own, far, halo):
     halo_rows = halo_refs[0].shape[0]
-    other = other_ref[...] * 0.5
+    other = other_weight * 0.5
     h = h_ref[...]
-    own[...] = dot(h, self_ref[...] * 0.5)
+    own[...] = dot(h, self_weight * 0.5)
     far[...] = dot(h, other).astype(bf16)
     halo[:halo_rows, :] = dot(halo_refs[0][...], other).astype(bf16)
     halo[halo_rows:, :] = dot(halo_refs[1][...], other).astype(bf16)
@@ -173,18 +183,19 @@
     return jnp.concatenate([down, local], 1).astype(bf16)
 
 
-def gather_kernel(
-    even_ref, lo_hbm, hi_hbm, x_hbm, first_ref, second_ref, x, wide, up, down, lo, hi, sems
-):
-    copies = [
-        pltpu.make_async_copy(src, dst, sems.at[n])
-        for n, (src, dst) in enumerate([(x_hbm, x), (lo_hbm, lo), (hi_hbm, hi)])
-    ]
+def fetch(pairs, sems):
+    copies = [pltpu.make_async_copy(src, dst, sems.at[n]) for n, (src, dst) in enumerate(pairs)]
     for copy in copies:
         copy.start()
     for copy in copies:
         copy.wait()
-    wide[...] = x[...].astype(f32)
+
+
+def gather_kernel(
+    even_ref, lo_hbm, hi_hbm, x_hbm, first_ref, second_ref, x_ref, wide, up, down, lo, hi, sems
+):
+    fetch([(x_hbm, x_ref), (lo_hbm, lo), (hi_hbm, hi)], sems)
+    wide[...] = x_ref[...].astype(f32)
 
     def step(r, carry):
         up[pl.ds(r, 1), :] = wide[pl.ds(hi[r], 1), :]
@@ -203,11 +214,10 @@
     out = shape(count, features, bf16)
     return call(
         gather_kernel,
-        [out, out],
+        [out, out, shape(rows, features, bf16)],
         [even, send_lo, send_hi, x],
-        [SMEM, ANY, ANY, ANY],
-        [
-            pltpu.VMEM((rows, features), bf16),
+        [SMEM, HBM, HBM, HBM],
+        [
             pltpu.VMEM((rows, features), f32),
             pltpu.VMEM((count, features), f32),
             pltpu.VMEM((count, features), f32),
@@ -229,24 +239,70 @@
 
 def prepare_kernel(
     even_ref,
-    owner_ref,
-    g_ref,
-    nbr_ref,
-    mask_ref,
-    coarse_nbr_ref,
-    coarse_mask_ref,
-    after_ref,
-    sums_ref,
-    counts_ref,
-    columns_ref,
-    columns_t_ref,
-    coarse_columns_ref,
-    coarse_columns_t_ref,
-    *,
+    g_hbm,
+    owner_hbm,
+    nbr_hbm,
+    mask_hbm,
+    coarse_nbr_hbm,
+    coarse_mask_hbm,
+    lo_hbm,
+    hi_hbm,
+    coarse_lo_hbm,
+    coarse_hi_hbm,
+    *rest,
     halo_rows,
     coarse_halo,
 ):
+    weight_hbms, rest = rest[:7], rest[7:]
+    (
+        after_ref,
+        sums_ref,
+        counts_ref,
+        columns_ref,
+        columns_t_ref,
+        coarse_columns_ref,
+        coarse_columns_t_ref,
+        owners_t_ref,
+        g_ref,
+        weights_ref,
+        sends_ref,
+        coarse_sends_ref,
+        owner_ref,
+        nbr_ref,
+        mask_ref,
+        coarse_nbr_ref,
+        coarse_mask_ref,
+        lo_ref,
+        hi_ref,
+        coarse_lo_ref,
+        coarse_hi_ref,
+        sems,
+    ) = rest
+    fetch(
+        [
+            (g_hbm, g_ref),
+            (owner_hbm, owner_ref),
+            (nbr_hbm, nbr_ref),
+            (mask_hbm, mask_ref),
+            (coarse_nbr_hbm, coarse_nbr_ref),
+            (coarse_mask_hbm, coarse_mask_ref),
+            (lo_hbm, lo_ref),
+            (hi_hbm, hi_ref),
+            (coarse_lo_hbm, coarse_lo_ref),
+            (coarse_hi_hbm, coarse_hi_ref),
+        ]
+        + [(w, weights_ref.at[pl.ds(128 * n, 128), :]) for n, w in enumerate(weight_hbms)],
+        sems,
+    )
     even = even_ref[0] > 0
+    for low, high, out in (
+        (lo_ref, hi_ref, sends_ref),
+        (coarse_lo_ref, coarse_hi_ref, coarse_sends_ref),
+    ):
+        first = jnp.where(even, high[...], low[...])
+        second = jnp.where(even, low[...], high[...])
+        out[...] = jnp.concatenate([first, second], 1)
+    owners_t_ref[...] = owner_columns(owner_ref)
     columns_ref[...] = slot_columns(nbr_ref[...], mask_ref[...], halo_rows, even)
     columns_t_ref[...] = columns_ref[...].T
     coarse_columns_ref[...] = slot_columns(
@@ -279,9 +335,7 @@
     h_ref,
     first_ref,
     second_ref,
-    self_ref,
-    other_ref,
-    node_ref,
+    weights_ref,
     columns_t_ref,
     owner_ref,
     counts_ref,
@@ -293,7 +347,8 @@
     halo,
     new,
 ):
-    level_terms(h_ref, (first_ref, second_ref), self_ref, other_ref, own, far, halo)
+    self_weight, other_weight = matrix(weights_ref, 0), matrix(weights_ref, 1)
+    level_terms(h_ref, (first_ref, second_ref), self_weight, other_weight, own, far, halo)
 
     def step(index, carry):
         here = chunk_of(index, STEP * BLOCK)
@@ -303,7 +358,9 @@
         return carry
 
     lax.fori_loop(0, h_ref.shape[0] // (STEP * BLOCK), step, None)
-    new[...] = (h_ref[...].astype(f32) + dot(summed_ref[...], node_ref[...])).astype(bf16)
+    new[...] = (
+        h_ref[...].astype(f32) + dot(summed_ref[...], matrix(weights_ref, 2))
+    ).astype(bf16)
     coarse_rows = totals_ref.shape[0] - counts_ref.shape[0]
 
     def tile_step(tile, carry):
@@ -315,13 +372,11 @@
 
 
 def coarse_input_kernel(
-    even_ref,
     totals_ref,
     more_totals_ref,
     sums_ref,
     more_sums_ref,
-    lo_ref,
-    hi_ref,
+    sends_ref,
     cin_ref,
     first_ref,
     second_ref,
@@ -339,12 +394,11 @@
         here = slice(tile * 128, (tile + 1) * 128)
         cin_ref[here, :] = (totals[here] / per_row[:, tile : tile + 1]).astype(bf16)
     cin = cin_ref[...]
-    place = lax.broadcasted_iota(jnp.int32, (coarse_rows, lo_ref.shape[1]), 0)
-    even = even_ref[0] > 0
-    first = jnp.where(even, hi_ref[...], lo_ref[...])
-    second = jnp.where(even, lo_ref[...], hi_ref[...])
-    first_ref[...] = dot_tn(pick(first == place), cin).astype(bf16)
-    second_ref[...] = dot_tn(pick(second == place), cin).astype(bf16)
+    place = lax.broadcasted_iota(jnp.int32, (coarse_rows, sends_ref.shape[1]), 0)
+    sent = dot_tn(pick(sends_ref[...] == place), cin).astype(bf16)
+    halo_rows = first_ref.shape[0]
+    first_ref[...] = sent[:halo_rows]
+    second_ref[...] = sent[halo_rows:]
 
 
 def coarse_kernel(
@@ -353,10 +407,7 @@
     second_ref,
     chip_sums_ref,
     more_sums_ref,
-    self_ref,
-    other_ref,
-    node_ref,
-    prolong_ref,
+    weights_ref,
     columns_ref,
     columns_t_ref,
     part_ref,
@@ -373,12 +424,13 @@
     halo_grad,
 ):
     halo_rows = first_ref.shape[0]
-    level_terms(cin_ref, (first_ref, second_ref), self_ref, other_ref, own, far, halo)
+    self_weight, other_weight = matrix(weights_ref, 3), matrix(weights_ref, 4)
+    level_terms(cin_ref, (first_ref, second_ref), self_weight, other_weight, own, far, halo)
     halo_grad[...] = jnp.zeros_like(halo_grad)
     sums_ref[...] = (chip_sums_ref[...].astype(f32) + more_sums_ref[...].astype(f32)).astype(bf16)
-    part_ref[...] = dot_nt(sums_ref[...], prolong_ref[...])
+    part_ref[...] = dot_nt(sums_ref[...], matrix(weights_ref, 6))
     ups_ref[...] = part_ref[...].astype(bf16)
-    grad_sum[...] = (dot_nt(ups_ref[...], node_ref[...]) * 0.5).astype(bf16)
+    grad_sum[...] = (dot_nt(ups_ref[...], matrix(weights_ref, 5)) * 0.5).astype(bf16)
 
     def step(index, carry):
         here = chunk_of(index, STEP * BLOCK)
@@ -399,8 +451,7 @@
     first_ref,
     second_ref,
     sums_ref,
-    node_ref,
-    prolong_ref,
+    matrices_ref,
     first_grad_ref,
     second_grad_ref,
     summed_ref,
@@ -412,8 +463,8 @@
     scale,
 ):
     cin = cin_ref[...]
-    out = (cin.astype(f32) + dot(summed_ref[...], node_ref[...])).astype(bf16)
-    fine_ref[...] = dot(out, prolong_ref[...]).astype(bf16)
+    out = (cin.astype(f32) + dot(summed_ref[...], matrix(matrices_ref, 5))).astype(bf16)
+    fine_ref[...] = dot(out, matrix(matrices_ref, 6)).astype(bf16)
     pair_grad = dot_tn(cin, downs_ref[...])
     other_grad = (
         pair_grad[:, 128:]
@@ -441,62 +492,54 @@
     return dot(rows, values)
 
 
-def result_kernel(h_ref, summed_ref, node_ref, owner_ref, fine_ref, out_ref, owners):
-    owners[...] = owner_columns(owner_ref)
-
+def result_kernel(h_ref, summed_ref, weights_ref, owners_ref, fine_ref, out_ref):
     def step(index, carry):
         here = chunk_of(index, CHUNK)
-        updated = h_ref[here, :].astype(f32) + dot(summed_ref[here, :], node_ref[...])
-        out_ref[here, :] = (updated + owner_rows(owners[here, :], fine_ref[...])).astype(bf16)
+        updated = h_ref[here, :].astype(f32) + dot(summed_ref[here, :], matrix(weights_ref, 2))
+        out_ref[here, :] = (updated + owner_rows(owners_ref[here, :], fine_ref[...])).astype(bf16)
         return carry
 
     lax.fori_loop(0, h_ref.shape[0] // CHUNK, step, None)
 
 
 def fine_backward_kernel(
-    even_ref,
     h_ref,
     first_ref,
     second_ref,
     g_ref,
     summed_ref,
     slope_ref,
-    node_ref,
+    matrices_ref,
     columns_ref,
-    owner_ref,
+    owners_ref,
     part_ref,
     counts_ref,
     coarse_downs_ref,
     first_back_ref,
     second_back_ref,
-    lo_ref,
-    hi_ref,
-    coarse_self_ref,
-    coarse_other_ref,
+    sends_ref,
     coarse_weights_ref,
-    ups_ref,
-    downs_ref,
+    ups_hbm,
+    downs_hbm,
     first_grad_ref,
     second_grad_ref,
     weights_ref,
-    owners,
+    ups_ref,
+    downs_ref,
     grad_sum,
     halo_grad,
     mean,
+    sems,
 ):
     halo_rows = first_ref.shape[0]
     coarse_rows = part_ref.shape[0]
     halo_grad[...] = jnp.zeros_like(halo_grad)
-    owners[...] = owner_columns(owner_ref)
-
-    even = even_ref[0] > 0
-    first = jnp.where(even, hi_ref[...], lo_ref[...])
-    second = jnp.where(even, lo_ref[...], hi_ref[...])
-    place = lax.broadcasted_iota(jnp.int32, (coarse_rows, lo_ref.shape[1]), 0)
-    sends = jnp.concatenate([pick(first == place), pick(second == place)], 1)
+
+    place = lax.broadcasted_iota(jnp.int32, (coarse_rows, sends_ref.shape[1]), 0)
+    sends = pick(sends_ref[...] == place)
     back = jnp.concatenate([first_back_ref[...], second_back_ref[...]], 0)
-    back = dot_nt(back, coarse_other_ref[...]).astype(bf16)
-    plain = jnp.concatenate([coarse_self_ref[...], coarse_other_ref[...]], 1)
+    back = dot_nt(back, matrix(matrices_ref, 4)).astype(bf16)
+    plain = jnp.concatenate([matrix(matrices_ref, 3), matrix(matrices_ref, 4)], 1)
     grad_in = part_ref[...] + dot_nt(coarse_downs_ref[...], plain) + dot(sends, back)
     per_row = counts_ref[...].T
     for tile in range(coarse_rows // 128):
@@ -508,24 +551,34 @@
 
     def owner_step(index):
         here = chunk_of(index, count)
-        grad_up = g_ref[here, :].astype(f32) + owner_rows(owners[here, :], mean[...])
+        grad_up = g_ref[here, :].astype(f32) + owner_rows(owners_ref[here, :], mean[...])
         ups = grad_up.astype(bf16)
         ups_ref[here, :] = ups
-        grad_sum[here, :] = (dot_nt(ups, node_ref[...]) * 0.5).astype(bf16)
-
-    owner_step(0)
-
-    def step(index, carry):
+        grad_sum[here, :] = (dot_nt(ups, matrix(matrices_ref, 2)) * 0.5).astype(bf16)
+
+    def edge_step(index):
         here = chunk_of(index, count)
         slope = slope_ref[chunk_of(index, 8 * count), :]
         slopes = [slope[n * 8 * BLOCK : (n + 1) * 8 * BLOCK] for n in range(STEP)]
         downs_ref[here, :] = edges_back(
             slopes, grad_sum[here, :], columns_ref[:, here], halo_grad
         )
-        owner_step(jnp.minimum(index + 1, steps - 1))
+
+    owner_step(0)
+
+    def step(index, carry):
+        edge_step(index)
+        owner_step(index + 1)
         return carry
 
-    lax.fori_loop(0, steps, step, None)
+    lax.fori_loop(0, steps - 1, step, None)
+    edge_step(steps - 1)
+    copies = [
+        pltpu.make_async_copy(ups_ref, ups_hbm, sems.at[0]),
+        pltpu.make_async_copy(downs_ref, downs_hbm, sems.at[1]),
+    ]
+    for copy in copies:
+        copy.start()
     first_grad = halo_grad[:halo_rows, :].astype(bf16)
     second_grad = halo_grad[halo_rows:, :].astype(bf16)
     first_grad_ref[...] = first_grad
@@ -540,29 +593,36 @@
     weights_ref[256:384, :] = dot_tn(summed_ref[...], ups_ref[...]).astype(bf16)
     weights_ref[384:896, :] = coarse_weights_ref[...]
     weights_ref[896:1024, :] = jnp.zeros((128, 128), bf16)
+    for copy in copies:
+        copy.wait()
 
 
 def finish_kernel(
-    even_ref,
+    ups_hbm,
+    downs_hbm,
+    first_back_ref,
+    second_back_ref,
+    sends_ref,
+    matrices_ref,
+    out_ref,
     ups_ref,
     downs_ref,
-    first_back_ref,
-    second_back_ref,
-    lo_ref,
-    hi_ref,
-    self_ref,
-    other_ref,
-    out_ref,
+    sems,
 ):
-    other = other_ref[...]
-    plain = jnp.concatenate([self_ref[...], other], 1)
+    copies = [
+        pltpu.make_async_copy(ups_hbm, ups_ref, sems.at[0]),
+        pltpu.make_async_copy(downs_hbm, downs_ref, sems.at[1]),
+    ]
+    for copy in copies:
+        copy.start()
+    other = matrix(matrices_ref, 1)
+    plain = jnp.concatenate([matrix(matrices_ref, 0), other], 1)
     back = jnp.concatenate([first_back_ref[...], second_back_ref[...]], 0)
     back = dot_nt(back, other).astype(bf16)
-    even = even_ref[0] > 0
-    first = jnp.where(even, hi_ref[...], lo_ref[...])
-    second = jnp.where(even, lo_ref[...], hi_ref[...])
-    sends = jnp.concatenate([first, second], 1)
+    sends = sends_ref[...]
     place = lax.broadcasted_iota(jnp.int32, (CHUNK, sends.shape[1]), 0)
+    for copy in copies:
+        copy.wait()
 
     def step(index, carry):
         here = chunk_of(index, CHUNK)
@@ -606,7 +666,7 @@
         share_kernel,
         jax.ShapeDtypeStruct((devices, share, 128), bf16),
         [parts, after],
-        [VMEM, ANY],
+        [VMEM, HBM],
     )
     return lax.all_to_all(mine, axes, 0, 0, tiled=False).reshape(block.shape)
 
@@ -637,18 +697,18 @@
     coarse_halo = coarse_send_lo.shape[0]
     count_rows = coarse_rows // 128
     owner = coarse_owner.reshape(rows // 128, 128)
-    fine_nbr, fine_mask = fine_nbr.T, fine_mask.T
-    coarse_nbr, coarse_mask = coarse_nbr.T, coarse_mask.T
-    coarse_lo, coarse_hi = coarse_send_lo[None], coarse_send_hi[None]
     even = (1 - lax.rem(lax.axis_index("sub"), 2)).astype(jnp.int32).reshape(1)
 
     def buffer(count, columns, dtype):
         return pltpu.VMEM((count, columns), dtype)
 
-    to_first, to_second = gather_rows(even, states, fine_send_lo, fine_send_hi)
+    to_first, to_second, states = gather_rows(even, states, fine_send_lo, fine_send_hi)
     first, second = exchange(to_first, to_second)
 
-    sums, counts, columns, columns_t, coarse_columns, coarse_columns_t = call(
+    (
+        sums, counts, columns, columns_t, coarse_columns, coarse_columns_t, owners_t, cotangent,
+        matrices, sends, coarse_sends, owner,
+    ) = call(
         functools.partial(prepare_kernel, halo_rows=halo_rows, coarse_halo=coarse_halo),
         [
             shape(coarse_rows, features, bf16),
@@ -657,9 +717,25 @@
             shape(rows, 8, f32),
             shape(8, coarse_rows, f32),
             shape(coarse_rows, 8, f32),
-        ],
-        [even, owner, cotangent, fine_nbr, fine_mask, coarse_nbr, coarse_mask, to_first],
-        [SMEM] + [VMEM] * 6 + [ANY],
+            shape(rows, 8, f32),
+            shape(rows, features, bf16),
+            shape(7 * features, features, bf16),
+            shape(1, 2 * halo_rows, jnp.int32),
+            shape(1, 2 * coarse_halo, jnp.int32),
+            shape(rows // 128, 128, jnp.int32),
+        ],
+        [
+            even, cotangent, owner, fine_nbr.T, fine_mask.T, coarse_nbr.T, coarse_mask.T,
+            fine_send_lo[None], fine_send_hi[None], coarse_send_lo[None], coarse_send_hi[None],
+            fine_self, fine_other, fine_node, coarse_self, coarse_other, coarse_node, prolong,
+            to_first,
+        ],
+        [SMEM] + [HBM] * 17 + [ANY],
+        [buffer(8, rows, jnp.int32)] * 2
+        + [buffer(8, coarse_rows, jnp.int32)] * 2
+        + [buffer(1, halo_rows, jnp.int32)] * 2
+        + [buffer(1, coarse_halo, jnp.int32)] * 2
+        + [pltpu.SemaphoreType.DMA((17,))],
     )
     more_sums = swapped(sums, "grp", 1)
 
@@ -670,7 +746,7 @@
             shape(8 * rows, features, bf16),
             shape(coarse_rows + 2 * count_rows, features, bf16),
         ],
-        [states, first, second, fine_self, fine_other, fine_node, columns_t, owner, counts],
+        [states, first, second, matrices, columns_t, owner, counts],
         scratch=[
             buffer(rows, features, f32),
             buffer(rows, features, bf16),
@@ -690,8 +766,7 @@
             shape(coarse_rows, features, bf16),
             shape(count_rows, features, f32),
         ],
-        [even, chip_totals, more_totals, sums, more_sums, coarse_lo, coarse_hi],
-        [SMEM] + [VMEM] * 6,
+        [chip_totals, more_totals, sums, more_sums, coarse_sends],
     )
     coarse_first, coarse_second = exchange(to_first, to_second)
     more_sums = swapped(chip_sums, "grp", 2)
@@ -708,8 +783,8 @@
             shape(coarse_rows, 2 * features, bf16),
         ],
         [
-            coarse_in, coarse_first, coarse_second, chip_sums, more_sums,
-            coarse_self, coarse_other, coarse_node, prolong, coarse_columns, coarse_columns_t,
+            coarse_in, coarse_first, coarse_second, chip_sums, more_sums, matrices,
+            coarse_columns, coarse_columns_t,
         ],
         scratch=[
             buffer(coarse_rows, features, f32),
@@ -725,51 +800,54 @@
         functools.partial(coarse_tail_kernel, scale=1.0 / lax.axis_size("grp")),
         [shape(coarse_rows, features, bf16), shape(4 * features, features, bf16)],
         [
-            coarse_in, coarse_first, coarse_second, sums, coarse_node, prolong,
+            coarse_in, coarse_first, coarse_second, sums, matrices,
             first_grad, second_grad, coarse_sum, coarse_ups, coarse_downs,
         ],
     )
     result = call(
         result_kernel,
         shape(rows, features, bf16),
-        [states, summed, fine_node, owner, fine_term],
-        scratch=[buffer(rows, 8, f32)],
+        [states, summed, matrices, owners_t, fine_term],
     )
 
     ups, downs, first_grad, second_grad, weights = call(
         fine_backward_kernel,
         [
-            shape(rows, features, bf16),
-            shape(rows, 2 * features, bf16),
+            pltpu.HBM((rows, features), bf16),
+            pltpu.HBM((rows, 2 * features), bf16),
             shape(halo_rows, features, bf16),
             shape(halo_rows, features, bf16),
             shape(8 * features, features, bf16),
         ],
         [
-            even, states, first, second, cotangent, summed, slope, fine_node, columns, owner,
-            coarse_part, counts, coarse_downs, first_back, second_back, coarse_lo, coarse_hi,
-            coarse_self, coarse_other, coarse_weights,
-        ],
-        [SMEM] + [VMEM] * 19,
-        [
-            buffer(rows, 8, f32),
+            states, first, second, cotangent, summed, slope, matrices, columns, owners_t,
+            coarse_part, counts, coarse_downs, first_back, second_back, coarse_sends,
+            coarse_weights,
+        ],
+        scratch=[
+            buffer(rows, features, bf16),
+            buffer(rows, 2 * features, bf16),
             buffer(rows, features, bf16),
             buffer(2 * halo_rows, features, f32),
             buffer(coarse_rows, features, bf16),
-        ],
-    )
-    weights = total_over_all(weights, ("grp", "sub"), result)
+            pltpu.SemaphoreType.DMA((2,)),
+        ],
+        out_specs=[HBM, HBM, VMEM, VMEM, VMEM],
+    )
     first_back, second_back = exchange(first_grad, second_grad)
 
     grad_states = call(
         finish_kernel,
         shape(rows, features, bf16),
-        [
-            even, ups, downs, first_back, second_back, fine_send_lo[None], fine_send_hi[None],
-            fine_self, fine_other,
-        ],
-        [SMEM] + [VMEM] * 8,
-    )
+        [ups, downs, first_back, second_back, sends, matrices],
+        [HBM, HBM] + [VMEM] * 4,
+        [
+            buffer(rows, features, bf16),
+            buffer(rows, 2 * features, bf16),
+            pltpu.SemaphoreType.DMA((2,)),
+        ],
+    )
+    weights = total_over_all(weights, ("grp", "sub"), grad_states)
     grad_weights = call(widen_kernel, shape(7 * features, features, f32), [weights])
     return (result, grad_states, grad_weights.reshape(7, features, features))
 

time: 121 us -> 114 us (0.942)
  local copies, waits for them, and re-layouts: 18 us -> 4.94 us
  Pallas kernels: 50 us -> 54.2 us
  starting transfers between devices: 26.3 us -> 30 us
  waiting for transfers between devices: 24.7 us -> 23.4 us
    unnamed x68 -> x14, local copies, waits for them, and re-layouts: 18 us -> 4.94 us
    pallas_call x11, Pallas kernels: 50 us -> 54.2 us  [call(): pl.pallas_call(kernel, out_shape=out_shape, in_specs=in_specs, out_specs=...]
    all_to_all x1, waiting for transfers between devices: 3.05 us -> 0.01 us  [total_over_all(): lax.all_to_all(block.reshape(devices, share, 128), axes, 0, 0, tiled=False)]
    all_to_all x1, starting transfers between devices: 2.79 us -> 5.55 us  [total_over_all(): return lax.all_to_all(mine, axes, 0, 0, tiled=False).reshape(block.shape)]
    all_to_all x1, waiting for transfers between devices: 0.01 us -> 2.42 us  [total_over_all(): return lax.all_to_all(mine, axes, 0, 0, tiled=False).reshape(block.shape)]
  transfers between devices with their start and end apart: 14 -> 14, of which waited for: 7 -> 7; matrix products, arithmetic and copies ran while one was open for 0% -> 0% of each run, Pallas kernels for 14% -> 18%
where the time goes in v3:
time: 114 us; the launch traced here: 113 us
  Pallas kernels  54.2 us (48%)
  starting transfers between devices  30 us (26%)
  waiting for transfers between devices  23.4 us (21%)
  local copies, waits for them, and re-layouts  4.94 us (4%)
    pallas_call x11, Pallas kernels, call(): pl.pallas_call(kernel, out_shape=out_shape, in_specs=in_specs, out_specs=...  54.2 us
    ppermute x4, starting transfers between devices, exchange(): lax.ppermute(first, 'sub', routes[0])  10.9 us
    ppermute x4, waiting for transfers between devices, swapped(): lax.ppermute(block, axis, [(i, i ^ distance) for i in range(lax.axis_size...  10.8 us
    ppermute x4, waiting for transfers between devices, exchange(): lax.ppermute(first, 'sub', routes[0])  10.2 us
    all_to_all x1, starting transfers between devices, total_over_all(): lax.all_to_all(block.reshape(devices, share, 128), axes, 0, 0, tiled=False)  7.79 us
    all_to_all x1, starting transfers between devices, total_over_all(): return lax.all_to_all(mine, axes, 0, 0, tiled=False).reshape(block.shape)  5.55 us
    unnamed x14, local copies, waits for them, and re-layouts  4.94 us
    ppermute x4, starting transfers between devices, swapped(): lax.ppermute(block, axis, [(i, i ^ distance) for i in range(lax.axis_size...  3.17 us
  transfers between devices with their start and end apart: 14, of which 7 were waited for; matrix products, arithmetic and copies ran while one was open for 0% of the time, Pallas kernels for 18%

profile of v3, /device:TPU:0, one launch (start us, length us, event | category | flops | bytes accessed | tf_op | source)
XLA Modules:
  0.0 113.4 jit_solution(12063420638012938462)
XLA Ops:
  0.6 2.3 %shard_map.193 = (bf16[512,128]{1,0:T(8,128)(2,1)S(1)}, bf16[512,128]{1,0:T(8,128)(2,1)S(1)}, bf16[4096,128]{1,0:T(8,128)(2,1)S(1)}) custom-call(s32[1]{0:T(128)} %bitcast.even_ref, s32[512]{0:T(512)} %lo_hbm.1, s32[512]{0:T(512)} %hi_hbm.1, bf16[4096,128]{1,0:T(8,128)(2,1)} %x_hbm.1), custom_call_target="tpu_custom_call" | custom-call | tf_op jit(solution)/shard_map/pallas_call | solution.py:52
  3.6 5.8 %collective-permute-start = (bf16[512,128]{1,0:T(8,128)(2,1)S(1)}, bf16[512,128]{1,0:T(8,128)(2,1)S(1)}, u32[]{:S(2)}, u32[]{:S(2)}) collective-permute-start(bf16[512,128]{1,0:T(8,128)(2,1)S(1)} %get-tuple-element.41.rest_7_), channel_id=1, source_target_pairs={{0,1},{2,3},{4,5},{6,7},{1,0},{3,2},{5,4},{7,6},{8,9},{10,11},{12,... | collective-permute-start | bytes 393224 | tf_op jit(solution)/shard_map/ppermute | solution.py:654
  9.4 6.6 %shard_map.194 = (bf16[1024,128]{1,0:T(8,128)(2,1)S(1)}, bf16[16,128]{1,0:T(8,128)(2,1)S(1)}, f32[8,4096]{1,0:T(8,128)S(1)}, f32[4096,8]{1,0:T(8,128)S(1)}, f32[...) custom-call(s32[1]{0:T(128)} %bitcast.even_ref, ...), custom_call_target="tpu_custom_call" | custom-call | tf_op jit(solution)/shard_map/pallas_call | solution.py:52
  16.0 13.0 %shard_map.195 = (bf16[4096,128]{1,0:T(8,128)(2,1)S(1)}, bf16[32768,128]{1,0:T(8,128)(2,1)S(1)}, bf16[1040,128]{1,0:T(8,128)(2,1)S(1)}) custom-call(bf16[4096,128]{1,0:T(8,128)(2,1)S(1)} %get-tuple-element.40.h_ref, bf16[512,128]{1,0:T(8,128)(2,1)S(1)} %collective-permute-done.first_ref, bf16[512,128]{1,0:T(8,128)(2,1)S(1)} %collective-permute-done.1.second_ref, ...), custom_call_target="tpu_custom_call" | custom-call | tf_op jit(solution)/shard_map/pallas_call | solution.py:52
  29.0 1.5 %collective-permute-done.2 = bf16[1040,128]{1,0:T(8,128)(2,1)S(1)} collective-permute-done((bf16[1040,128]{1,0:T(8,128)(2,1)S(1)}, bf16[1040,128]{1,0:T(8,128)(2,1)S(1)}, u32[]{:S(2)}, u32[]{:S(2)}) %collective-permute-start.2) | collective-permute-done | bytes 266272 | tf_op jit(solution)/shard_map/ppermute | solution.py:658
  30.7 1.6 %collective-permute-start.3 = (bf16[1040,128]{1,0:T(8,128)(2,1)S(1)}, bf16[1040,128]{1,0:T(8,128)(2,1)S(1)}, u32[]{:S(2)}, u32[]{:S(2)}) collective-permute-start(bf16[1040,128]{1,0:T(8,128)(2,1)S(1)} %add_convert_fusion.totals_ref), channel_id=1, source_target_pairs={{0,16},{8,24},{16,0},{24,8},{1,17},{9,25},{17,1},{25,9},{2,18},{10... | collective-permute-start | bytes 798728 | tf_op jit(solution)/shard_map/ppermute | solution.py:658
  32.2 1.5 %collective-permute-done.4.more_sums_ref = bf16[1024,128]{1,0:T(8,128)(2,1)S(1)} collective-permute-done((bf16[1024,128]{1,0:T(8,128)(2,1)S(1)}, bf16[1024,128]{1,0:T(8,128)(2,1)S(1)}, u32[]{:S(2)}, u32[]{:S(2)}) %collective-permute-start.4) | collective-permute-done | bytes 262176 | tf_op jit(solution)/shard_map/ppermute | solution.py:658
  33.7 5.4 %collective-permute-done.3.more_totals_ref = bf16[1040,128]{1,0:T(8,128)(2,1)S(1)} collective-permute-done((bf16[1040,128]{1,0:T(8,128)(2,1)S(1)}, bf16[1040,128]{1,0:T(8,128)(2,1)S(1)}, u32[]{:S(2)}, u32[]{:S(2)}) %collective-permute-start.3) | collective-permute-done | bytes 266272 | tf_op jit(solution)/shard_map/ppermute | solution.py:658
  39.8 1.5 %collective-permute-start.7 = (bf16[1024,128]{1,0:T(8,128)(2,1)S(1)}, bf16[1024,128]{1,0:T(8,128)(2,1)S(1)}, u32[]{:S(2)}, u32[]{:S(2)}) collective-permute-start(bf16[1024,128]{1,0:T(8,128)(2,1)S(1)} %get-tuple-element.55.chip_sums_ref), channel_id=1, source_target_pairs={{0,16},{8,24},{16,0},{24,8},{1,17},{9,25},{17,1},{25,9},{2,18},{10... | collective-permute-start | bytes 786440 | tf_op jit(solution)/shard_map/ppermute | solution.py:658
  42.8 2.3 %collective-permute-done.5.first_ref = bf16[64,128]{1,0:T(8,128)(2,1)S(1)} collective-permute-done((bf16[64,128]{1,0:T(8,128)(2,1)S(1)}, bf16[64,128]{1,0:T(8,128)(2,1)S(1)}, u32[]{:S(2)}, u32[]{:S(2)}) %collective-permute-start.5) | collective-permute-done | bytes 16416 | tf_op jit(solution)/shard_map/ppermute | solution.py:654
  45.1 2.3 %collective-permute-done.7.more_sums_ref = bf16[1024,128]{1,0:T(8,128)(2,1)S(1)} collective-permute-done((bf16[1024,128]{1,0:T(8,128)(2,1)S(1)}, bf16[1024,128]{1,0:T(8,128)(2,1)S(1)}, u32[]{:S(2)}, u32[]{:S(2)}) %collective-permute-start.7) | collective-permute-done | bytes 262176 | tf_op jit(solution)/shard_map/ppermute | solution.py:658
  47.4 3.9 %shard_map.197 = (f32[1024,128]{1,0:T(8,128)S(1)}, bf16[64,128]{1,0:T(8,128)(2,1)S(1)}, bf16[64,128]{1,0:T(8,128)(2,1)S(1)}, bf16[1024,128]{1,0:T(8,128)(2,1)S(1...) custom-call(bf16[1024,128]{1,0:T(8,128)(2,1)S(1)} %get-tuple-element.52.cin_ref, ...), custom_call_target="tpu_custom_call" | custom-call | tf_op jit(solution)/shard_map/pallas_call | solution.py:52
  51.3 2.6 %collective-permute-start.8 = (bf16[64,128]{1,0:T(8,128)(2,1)S(1)}, bf16[64,128]{1,0:T(8,128)(2,1)S(1)}, u32[]{:S(2)}, u32[]{:S(2)}) collective-permute-start(bf16[64,128]{1,0:T(8,128)(2,1)S(1)} %get-tuple-element.59.first_grad_ref), channel_id=1, source_target_pairs={{0,1},{2,3},{4,5},{6,7},{1,0},{3,2},{5,4},{7,6},{8,9},{10,11},{12,... | collective-permute-start | bytes 49160 | tf_op jit(solution)/shard_map/ppermute | solution.py:654
  55.8 11.4 %shard_map.200 = (bf16[4096,128]{1,0:T(8,128)(2,1)}, bf16[4096,256]{1,0:T(8,128)(2,1)}, bf16[512,128]{1,0:T(8,128)(2,1)S(1)}, bf16[512,128]{1,0:T(8,128)(2,1)S(1)}, bf16[1024,128]{1,0:T(8,128)(2,1)S(1)}) custom-call(bf16[4096,128]{1,0:T(8,128)(2,1)S(1)} %get-tuple-element.40.h_ref, bf16[512,128]{1,0:T(8,128)(2,1)S(1)} %collective-permute-done.first_ref, ...), custom_call_target="tpu_custom_call" | custom-call | tf_op jit(solution)/shard_map/pallas_call | solution.py:52
  68.6 7.8 %all-to-all-start = ((bf16[32,32,128]{2,1,0:T(8,128)(2,1)}), bf16[32,32,128]{2,1,0:T(8,128)(2,1)}, u32[]{:S(2)}, u32[]{:S(2)}) async-start(bf16[32,32,128]{2,1,0:T(8,128)(2,1)} %bitcast.13), calls=%async_computation | async-start | bytes 524288 | tf_op jit(solution)/shard_map/all_to_all | solution.py:664
  76.4 1.8 %collective-permute-start.10 = (bf16[512,128]{1,0:T(8,128)(2,1)}, bf16[512,128]{1,0:T(8,128)(2,1)S(1)}, u32[]{:S(2)}, u32[]{:S(2)}) collective-permute-start(bf16[512,128]{1,0:T(8,128)(2,1)} %copy-done.6), channel_id=1, source_target_pairs={{0,1},{2,3},{4,5},{6,7},{1,0},{3,2},{5,4},{7,6},{8,9},{10,11},{12,... | collective-permute-start | bytes 393224 | tf_op jit(solution)/shard_map/ppermute | solution.py:654
  78.8 7.8 %collective-permute-done.10.first_back_ref = bf16[512,128]{1,0:T(8,128)(2,1)S(1)} collective-permute-done((bf16[512,128]{1,0:T(8,128)(2,1)}, bf16[512,128]{1,0:T(8,128)(2,1)S(1)}, u32[]{:S(2)}, u32[]{:S(2)}) %collective-permute-start.10) | collective-permute-done | bytes 131104 | tf_op jit(solution)/shard_map/ppermute | solution.py:654
  86.7 7.1 %shard_map.201.after_ref = bf16[4096,128]{1,0:T(8,128)(2,1)} custom-call(bf16[4096,128]{1,0:T(8,128)(2,1)} %get-tuple-element.71.ups_hbm, bf16[4096,256]{1,0:T(8,128)(2,1)} %get-tuple-element.72.downs_hbm, bf16[512,128]{1,0:T(8,128)(2,1)S(1)} %collective-permute-done.10.first_back_ref, bf16[512,128]{1,0:T(8,128)(2,1)S(1)} %collective-permute-done.11.second_back_ref, ...), custom_call_target="tpu_custom_call" | custom-call | tf_op jit(solution)/shard_map/pallas_call | solution.py:52
  93.8 1.0 shard_map.202
  95.5 5.5 %all-to-all-start.1 = ((bf16[32,32,128]{2,1,0:T(8,128)(2,1)}), bf16[32,32,128]{2,1,0:T(8,128)(2,1)}, u32[]{:S(2)}, u32[]{:S(2)}) async-start(bf16[32,32,128]{2,1,0:T(8,128)(2,1)} %copy-done.2), calls=%async_computation.1 | async-start | bytes 524288 | tf_op jit(solution)/shard_map/all_to_all | solution.py:671
  101.0 1.2 %copy-done.1 = bf16[4096,128]{1,0:T(8,128)(2,1)S(1)} copy-done((bf16[4096,128]{1,0:T(8,128)(2,1)S(1)}, bf16[4096,128]{1,0:T(8,128)(2,1)}, u32[]{:S(2)}) %copy-start.1) | copy-done | bytes 1048600
  103.2 6.0 %shard_map.199 = bf16[4096,128]{1,0:T(8,128)(2,1)} custom-call(bf16[4096,128]{1,0:T(8,128)(2,1)S(1)} %get-tuple-element.40.h_ref, bf16[4096,128]{1,0:T(8,128)(2,1)S(1)} %copy-done.1, bf16[896,128]{1,0:T(8,128)(2,1)S(1)} %get-tuple-element.43.weights_ref.matrices_ref, f32[4096,8]{1,0:T(8,128)S(1)} %get-tuple-element.48.owners_ref, bf16[1024,128]{1,0:T(8,128)(2,1)S(1)} %copy-done.4), custom_call_target="tpu_custom_call" | custom-call | tf_op jit(solution)/shard_map/pallas_call | solution.py:52
  109.2 2.4 %all-to-all-done.1 = bf16[32,32,128]{2,1,0:T(8,128)(2,1)} async-done(((bf16[32,32,128]{2,1,0:T(8,128)(2,1)}), bf16[32,32,128]{2,1,0:T(8,128)(2,1)}, u32[]{:S(2)}, u32[]{:S(2)}) %all-to-all-start.1) | async-done | bytes 262176 | tf_op jit(solution)/shard_map/all_to_all | solution.py:671
  111.7 1.7 %shard_map.203 = f32[896,128]{1,0:T(8,128)} custom-call(bf16[1024,128]{1,0:T(8,128)(2,1)} %bitcast.11.x_ref), custom_call_target="tpu_custom_call" | custom-call | tf_op jit(solution)/shard_map/pallas_call | solution.py:52
  (30 shorter events, 8.5 us)
Async XLA Ops:
  2.9 13.0 %collective-permute-start.1 = (bf16[512,128]{1,0:T(8,128)(2,1)S(1)}, bf16[512,128]{1,0:T(8,128)(2,1)S(1)}, u32[]{:S(2)}, u32[]{:S(2)}) collective-permute-start(bf16[512,128]{1,0:T(8,128)(2,1)S(1)} %get-tuple-element.42), channel_id=1, source_target_pairs={{1,2},{3,4},{5,6},{2,1},{4,3},{6,5},{9,10},{11,12},{13,14},{10,9},... | collective-permute-start | bytes 393224 | tf_op jit(solution)/shard_map/ppermute | solution.py:654
  3.6 12.4 %collective-permute-start = (bf16[512,128]{1,0:T(8,128)(2,1)S(1)}, bf16[512,128]{1,0:T(8,128)(2,1)S(1)}, u32[]{:S(2)}, u32[]{:S(2)}) collective-permute-start(bf16[512,128]{1,0:T(8,128)(2,1)S(1)} %get-tuple-element.41.rest_7_), channel_id=1, source_target_pairs={{0,1},{2,3},{4,5},{6,7},{1,0},{3,2},{5,4},{7,6},{8,9},{10,11},{12,... | collective-permute-start | bytes 393224 | tf_op jit(solution)/shard_map/ppermute | solution.py:654
  29.0 26.9 %copy-start = (bf16[4096,128]{1,0:T(8,128)(2,1)}, bf16[4096,128]{1,0:T(8,128)(2,1)S(1)}, u32[]{:S(2)}) copy-start(bf16[4096,128]{1,0:T(8,128)(2,1)S(1)} %get-tuple-element.47.summed_ref) | copy-start | bytes 3145732
  29.0 1.6 %collective-permute-start.2 = (bf16[1040,128]{1,0:T(8,128)(2,1)S(1)}, bf16[1040,128]{1,0:T(8,128)(2,1)S(1)}, u32[]{:S(2)}, u32[]{:S(2)}) collective-permute-start(bf16[1040,128]{1,0:T(8,128)(2,1)S(1)} %get-tuple-element.49), channel_id=1, source_target_pairs={{0,8},{8,0},{16,24},{24,16},{1,9},{9,1},{17,25},{25,17},{2,10},{10... | collective-permute-start | bytes 798728 | tf_op jit(solution)/shard_map/ppermute | solution.py:658
  30.7 8.5 %collective-permute-start.3 = (bf16[1040,128]{1,0:T(8,128)(2,1)S(1)}, bf16[1040,128]{1,0:T(8,128)(2,1)S(1)}, u32[]{:S(2)}, u32[]{:S(2)}) collective-permute-start(bf16[1040,128]{1,0:T(8,128)(2,1)S(1)} %add_convert_fusion.totals_ref), channel_id=1, source_target_pairs={{0,16},{8,24},{16,0},{24,8},{1,17},{9,25},{17,1},{25,9},{2,18},{10... | collective-permute-start | bytes 798728 | tf_op jit(solution)/shard_map/ppermute | solution.py:658
  32.2 1.5 %collective-permute-start.4 = (bf16[1024,128]{1,0:T(8,128)(2,1)S(1)}, bf16[1024,128]{1,0:T(8,128)(2,1)S(1)}, u32[]{:S(2)}, u32[]{:S(2)}) collective-permute-start(bf16[1024,128]{1,0:T(8,128)(2,1)S(1)} %get-tuple-element.50.sums_ref), channel_id=1, source_target_pairs={{0,8},{8,0},{16,24},{24,16},{1,9},{9,1},{17,25},{25,17},{2,10},{10... | collective-permute-start | bytes 786440 | tf_op jit(solution)/shard_map/ppermute | solution.py:658
  39.8 7.6 %collective-permute-start.7 = (bf16[1024,128]{1,0:T(8,128)(2,1)S(1)}, bf16[1024,128]{1,0:T(8,128)(2,1)S(1)}, u32[]{:S(2)}, u32[]{:S(2)}) collective-permute-start(bf16[1024,128]{1,0:T(8,128)(2,1)S(1)} %get-tuple-element.55.chip_sums_ref), channel_id=1, source_target_pairs={{0,16},{8,24},{16,0},{24,8},{1,17},{9,25},{17,1},{25,9},{2,18},{10... | collective-permute-start | bytes 786440 | tf_op jit(solution)/shard_map/ppermute | solution.py:658
  41.3 3.7 %collective-permute-start.5 = (bf16[64,128]{1,0:T(8,128)(2,1)S(1)}, bf16[64,128]{1,0:T(8,128)(2,1)S(1)}, u32[]{:S(2)}, u32[]{:S(2)}) collective-permute-start(bf16[64,128]{1,0:T(8,128)(2,1)S(1)} %get-tuple-element.53), channel_id=1, source_target_pairs={{0,1},{2,3},{4,5},{6,7},{1,0},{3,2},{5,4},{7,6},{8,9},{10,11},{12,... | collective-permute-start | bytes 49160 | tf_op jit(solution)/shard_map/ppermute | solution.py:654
  42.1 3.0 %collective-permute-start.6 = (bf16[64,128]{1,0:T(8,128)(2,1)S(1)}, bf16[64,128]{1,0:T(8,128)(2,1)S(1)}, u32[]{:S(2)}, u32[]{:S(2)}) collective-permute-start(bf16[64,128]{1,0:T(8,128)(2,1)S(1)} %get-tuple-element.54), channel_id=1, source_target_pairs={{1,2},{3,4},{5,6},{2,1},{4,3},{6,5},{9,10},{11,12},{13,14},{10,9},... | collective-permute-start | bytes 49160 | tf_op jit(solution)/shard_map/ppermute | solution.py:654
  51.3 4.6 %collective-permute-start.8 = (bf16[64,128]{1,0:T(8,128)(2,1)S(1)}, bf16[64,128]{1,0:T(8,128)(2,1)S(1)}, u32[]{:S(2)}, u32[]{:S(2)}) collective-permute-start(bf16[64,128]{1,0:T(8,128)(2,1)S(1)} %get-tuple-element.59.first_grad_ref), channel_id=1, source_target_pairs={{0,1},{2,3},{4,5},{6,7},{1,0},{3,2},{5,4},{7,6},{8,9},{10,11},{12,... | collective-permute-start | bytes 49160 | tf_op jit(solution)/shard_map/ppermute | solution.py:654
  53.8 2.0 %collective-permute-start.9 = (bf16[64,128]{1,0:T(8,128)(2,1)S(1)}, bf16[64,128]{1,0:T(8,128)(2,1)S(1)}, u32[]{:S(2)}, u32[]{:S(2)}) collective-permute-start(bf16[64,128]{1,0:T(8,128)(2,1)S(1)} %get-tuple-element.60.second_grad_ref), channel_id=1, source_target_pairs={{1,2},{3,4},{5,6},{2,1},{4,3},{6,5},{9,10},{11,12},{13,14},{10,9},... | collective-permute-start | bytes 49160 | tf_op jit(solution)/shard_map/ppermute | solution.py:654
  55.1 0.7 copy-start.3
  67.2 0.7 copy-start.6
  67.9 0.7 copy-start.5
  68.6 25.1 %all-to-all-start = ((bf16[32,32,128]{2,1,0:T(8,128)(2,1)}), bf16[32,32,128]{2,1,0:T(8,128)(2,1)}, u32[]{:S(2)}, u32[]{:S(2)}) async-start(bf16[32,32,128]{2,1,0:T(8,128)(2,1)} %bitcast.13), calls=%async_computation | async-start | bytes 524288 | tf_op jit(solution)/shard_map/all_to_all | solution.py:664
  76.4 10.3 %collective-permute-start.10 = (bf16[512,128]{1,0:T(8,128)(2,1)}, bf16[512,128]{1,0:T(8,128)(2,1)S(1)}, u32[]{:S(2)}, u32[]{:S(2)}) collective-permute-start(bf16[512,128]{1,0:T(8,128)(2,1)} %copy-done.6), channel_id=1, source_target_pairs={{0,1},{2,3},{4,5},{6,7},{1,0},{3,2},{5,4},{7,6},{8,9},{10,11},{12,... | collective-permute-start | bytes 393224 | tf_op jit(solution)/shard_map/ppermute | solution.py:654
  78.2 8.5 %collective-permute-start.11 = (bf16[512,128]{1,0:T(8,128)(2,1)S(1)}, bf16[512,128]{1,0:T(8,128)(2,1)S(1)}, u32[]{:S(2)}, u32[]{:S(2)}) collective-permute-start(bf16[512,128]{1,0:T(8,128)(2,1)S(1)} %get-tuple-element.74), channel_id=1, source_target_pairs={{1,2},{3,4},{5,6},{2,1},{4,3},{6,5},{9,10},{11,12},{13,14},{10,9},... | collective-permute-start | bytes 393224 | tf_op jit(solution)/shard_map/ppermute | solution.py:654
  94.8 0.7 copy-start.2
  95.5 16.2 %all-to-all-start.1 = ((bf16[32,32,128]{2,1,0:T(8,128)(2,1)}), bf16[32,32,128]{2,1,0:T(8,128)(2,1)}, u32[]{:S(2)}, u32[]{:S(2)}) async-start(bf16[32,32,128]{2,1,0:T(8,128)(2,1)} %copy-done.2), calls=%async_computation.1 | async-start | bytes 524288 | tf_op jit(solution)/shard_map/all_to_all | solution.py:671
  101.0 1.2 %copy-start.1 = (bf16[4096,128]{1,0:T(8,128)(2,1)S(1)}, bf16[4096,128]{1,0:T(8,128)(2,1)}, u32[]{:S(2)}) copy-start(bf16[4096,128]{1,0:T(8,128)(2,1)} %copy-done) | copy-start | bytes 3145732
  102.3 0.9 copy-start.4

commit v4 on v3

--- a/solution.py
+++ b/solution.py
@@ -99,10 +99,7 @@
         row = jnp.where(lane < BLOCK, left[2 * j : 2 * j + 1], right[2 * j + 1 : 2 * j + 2])
         wide = jnp.broadcast_to(row, (3 * BLOCK, 128)).astype(bf16)
         parts.append(pick16(wide, place))
-    own_row = lax.broadcasted_iota(jnp.int32, (BLOCK, 128), 0)
-    own_lane = lax.broadcasted_iota(jnp.int32, (BLOCK, 128), 1)
-    own = pick(lax.rem(own_lane, BLOCK) == own_row)
-    return jnp.concatenate([jnp.concatenate(parts, 1), jnp.concatenate([own] * 4, 1)], 0)
+    return jnp.concatenate(parts, 1)
 
 
 def window_of(far, halo, place):
@@ -148,29 +145,31 @@
     sums, slopes = [], []
     for n, picked in enumerate(tables):
         own = own_rows[n * BLOCK : (n + 1) * BLOCK]
-        total, pieces = None, []
+        values, pieces = [], []
         for k in range(8):
-            y = picked[k * BLOCK : (k + 1) * BLOCK] + own
+            y = (picked[k * BLOCK : (k + 1) * BLOCK] + own).astype(bf16)
             t = jnp.tanh(y)
             bent = y * t
-            total = y + bent if total is None else total + (y + bent)
-            pieces.append(((1.0 + t) * (1.0 + (y - bent))).astype(bf16))
-        sums.append(total)
+            values.append(y + bent)
+            pieces.append((1 + t) * (1 + (y - bent)))
+        while len(values) > 1:
+            values = [left + right for left, right in zip(values[::2], values[1::2])]
+        sums.append(values[0])
         slopes.append(jnp.concatenate(pieces, 0))
-    return jnp.concatenate(sums, 0).astype(bf16), slopes
+    return jnp.concatenate(sums, 0), slopes
 
 
 def edges_back(slopes, grad_sum, columns, halo_grad):
     places = halo_grad.shape[0] // (2 * BLOCK)
     halo_rows = halo_grad.shape[0] // 2
-    windows = []
+    windows, downs = [], []
     for n, slope in enumerate(slopes):
         part = grad_sum[n * BLOCK : (n + 1) * BLOCK]
-        grad = jnp.concatenate(
-            [slope[k * BLOCK : (k + 1) * BLOCK] * part for k in range(8)], 0
-        )
+        grads = [slope[k * BLOCK : (k + 1) * BLOCK] * part for k in range(8)]
+        downs.append(sum(grad.astype(f32) for grad in grads))
         mine = columns[:, n // 2 * PAIR : (n // 2 + 1) * PAIR]
-        windows.append(dot(selector_t(mine, pltpu.roll(mine, BLOCK, 1), n % 2), grad))
+        selected = selector_t(mine, pltpu.roll(mine, BLOCK, 1), n % 2)
+        windows.append(dot(selected, jnp.concatenate(grads, 0)))
     for place in range(places):
         for side in range(2):
             start = side * halo_rows + place * BLOCK
@@ -179,7 +178,7 @@
                 total = total + window[(side + 1) * BLOCK : (side + 2) * BLOCK]
             halo_grad[start : start + BLOCK, :] = total
     local = jnp.concatenate([window[:BLOCK] for window in windows], 0)
-    down = jnp.concatenate([window[3 * BLOCK :] for window in windows], 0)
+    down = jnp.concatenate(downs, 0)
     return jnp.concatenate([down, local], 1).astype(bf16)
 
 
@@ -229,10 +228,14 @@
 
 
 def owner_sums(owner_ref, tile, values):
-    place = lax.broadcasted_iota(jnp.int32, (128, 128), 0) + tile * 128
-    groups = owner_ref.shape[0]
+    place = lax.broadcasted_iota(jnp.int32, (256, 128), 0).astype(bf16)
+    owner = (owner_ref[...] - tile * 256).astype(f32)
     rows = jnp.concatenate(
-        [pick(owner_ref[q : q + 1, :] == place) for q in range(groups)], 1
+        [
+            pick16(jnp.broadcast_to(owner[q : q + 1], (256, 128)).astype(bf16), place)
+            for q in range(owner.shape[0])
+        ],
+        1,
     )
     return dot(rows, values)
 
@@ -256,13 +259,11 @@
     weight_hbms, rest = rest[:7], rest[7:]
     (
         after_ref,
-        sums_ref,
         counts_ref,
         columns_ref,
         columns_t_ref,
         coarse_columns_ref,
         coarse_columns_t_ref,
-        owners_t_ref,
         g_ref,
         weights_ref,
         sends_ref,
@@ -302,20 +303,13 @@
         first = jnp.where(even, high[...], low[...])
         second = jnp.where(even, low[...], high[...])
         out[...] = jnp.concatenate([first, second], 1)
-    owners_t_ref[...] = owner_columns(owner_ref)
     columns_ref[...] = slot_columns(nbr_ref[...], mask_ref[...], halo_rows, even)
     columns_t_ref[...] = columns_ref[...].T
     coarse_columns_ref[...] = slot_columns(
         coarse_nbr_ref[...], coarse_mask_ref[...], coarse_halo, even
     )
     coarse_columns_t_ref[...] = coarse_columns_ref[...].T
-    tiles = sums_ref.shape[0] // 128
-
-    def step(tile, carry):
-        sums_ref[chunk_of(tile, 128), :] = owner_sums(owner_ref, tile, g_ref[...]).astype(bf16)
-        return carry
-
-    lax.fori_loop(0, tiles, step, None)
+    tiles = counts_ref.shape[0] // 2
     owner = owner_ref[...]
     high, low = owner // 128, lax.rem(owner, 128)
     groups = owner.shape[0]
@@ -329,6 +323,18 @@
     counts = dot_nt(high_rows, low_rows)
     most = jnp.floor(counts * (1 / DIGIT))
     counts_ref[...] = jnp.concatenate([most, counts - DIGIT * most], 0).astype(bf16)
+
+
+def sums_kernel(owner_ref, g_ref, after_ref, sums_ref):
+    def step(tile, carry):
+        sums_ref[chunk_of(tile, 256), :] = owner_sums(owner_ref, tile, g_ref[...]).astype(bf16)
+        return carry
+
+    lax.fori_loop(0, sums_ref.shape[0] // 256, step, None)
+
+
+def owners_kernel(owner_ref, after_ref, owners_ref):
+    owners_ref[...] = owner_columns(owner_ref)
 
 
 def fine_forward_kernel(
@@ -364,10 +370,10 @@
     coarse_rows = totals_ref.shape[0] - counts_ref.shape[0]
 
     def tile_step(tile, carry):
-        totals_ref[chunk_of(tile, 128), :] = owner_sums(owner_ref, tile, new[...]).astype(bf16)
+        totals_ref[chunk_of(tile, 256), :] = owner_sums(owner_ref, tile, new[...]).astype(bf16)
         return carry
 
-    lax.fori_loop(0, coarse_rows // 128, tile_step, None)
+    lax.fori_loop(0, coarse_rows // 256, tile_step, None)
     totals_ref[coarse_rows:, :] = counts_ref[...]
 
 
@@ -377,6 +383,7 @@
     sums_ref,
     more_sums_ref,
     sends_ref,
+    after_ref,
     cin_ref,
     first_ref,
     second_ref,
@@ -486,20 +493,25 @@
 def owner_rows(owners, values):
     count = owners.shape[0]
     wide = jnp.broadcast_to(owners[:, 0:1], (count, 128))
-    lane = lax.broadcasted_iota(jnp.int32, (count, 128), 1).astype(f32)
-    tiles = values.shape[0] // 128
-    rows = jnp.concatenate([pick(wide == lane + 128.0 * tile) for tile in range(tiles)], 1)
-    return dot(rows, values)
-
-
-def result_kernel(h_ref, summed_ref, weights_ref, owners_ref, fine_ref, out_ref):
+    lane = lax.broadcasted_iota(jnp.int32, (count, 128), 1)
+    first, second = lane.astype(bf16), (lane + 128).astype(bf16)
+    rows = []
+    for tile in range(values.shape[0] // 256):
+        here = (wide - 256.0 * tile).astype(bf16)
+        rows += [pick16(here, first), pick16(here, second)]
+    return dot(jnp.concatenate(rows, 1), values)
+
+
+def result_kernel(h_ref, summed_ref, weights_ref, owners_ref, fine_ref, out_hbm, out_ref, sem):
     def step(index, carry):
         here = chunk_of(index, CHUNK)
         updated = h_ref[here, :].astype(f32) + dot(summed_ref[here, :], matrix(weights_ref, 2))
         out_ref[here, :] = (updated + owner_rows(owners_ref[here, :], fine_ref[...])).astype(bf16)
+        pltpu.make_async_copy(out_ref.at[here, :], out_hbm.at[here, :], sem).start()
         return carry
 
     lax.fori_loop(0, h_ref.shape[0] // CHUNK, step, None)
+    pltpu.make_async_copy(out_ref, out_hbm, sem).wait()
 
 
 def fine_backward_kernel(
@@ -604,37 +616,54 @@
     second_back_ref,
     sends_ref,
     matrices_ref,
-    out_ref,
+    out_hbm,
     ups_ref,
     downs_ref,
-    sems,
+    out_ref,
+    ups_sems,
+    downs_sems,
+    out_sem,
 ):
-    copies = [
-        pltpu.make_async_copy(ups_hbm, ups_ref, sems.at[0]),
-        pltpu.make_async_copy(downs_hbm, downs_ref, sems.at[1]),
-    ]
-    for copy in copies:
-        copy.start()
+    chunks = ups_ref.shape[0] // CHUNK
+
+    def copies(index):
+        here = chunk_of(index, CHUNK)
+        return (
+            pltpu.make_async_copy(ups_hbm.at[here, :], ups_ref.at[here, :], ups_sems.at[index]),
+            pltpu.make_async_copy(
+                downs_hbm.at[here, :], downs_ref.at[here, :], downs_sems.at[index]
+            ),
+        )
+
+    for index in range(chunks):
+        for copy in copies(index):
+            copy.start()
     other = matrix(matrices_ref, 1)
     plain = jnp.concatenate([matrix(matrices_ref, 0), other], 1)
     back = jnp.concatenate([first_back_ref[...], second_back_ref[...]], 0)
     back = dot_nt(back, other).astype(bf16)
     sends = sends_ref[...]
-    place = lax.broadcasted_iota(jnp.int32, (CHUNK, sends.shape[1]), 0)
-    for copy in copies:
-        copy.wait()
+    place = lax.broadcasted_iota(jnp.int32, (256, sends.shape[1]), 0).astype(bf16)
 
     def step(index, carry):
         here = chunk_of(index, CHUNK)
-        rows = pick(sends - index * CHUNK == place)
+        rows = []
+        for part in range(CHUNK // 256):
+            local = (sends - (index * CHUNK + 256 * part)).astype(f32)
+            rows.append(pick16(jnp.broadcast_to(local, place.shape).astype(bf16), place))
+        spread = dot(jnp.concatenate(rows, 0), back)
+        for copy in copies(index):
+            copy.wait()
         grad = ups_ref[here, :].astype(f32) + dot_nt(downs_ref[here, :], plain)
-        out_ref[here, :] = (grad + dot(rows, back)).astype(bf16)
+        out_ref[here, :] = (grad + spread).astype(bf16)
+        pltpu.make_async_copy(out_ref.at[here, :], out_hbm.at[here, :], out_sem).start()
         return carry
 
-    lax.fori_loop(0, ups_ref.shape[0] // CHUNK, step, None)
-
-
-def share_kernel(parts_ref, after_ref, out_ref):
+    lax.fori_loop(0, chunks, step, None)
+    pltpu.make_async_copy(out_ref, out_hbm, out_sem).wait()
+
+
+def share_kernel(parts_ref, result_ref, first_ref, second_ref, out_ref):
     total = parts_ref[0].astype(f32)
     for n in range(1, parts_ref.shape[0]):
         total = total + parts_ref[n].astype(f32)
@@ -665,8 +694,8 @@
     mine = call(
         share_kernel,
         jax.ShapeDtypeStruct((devices, share, 128), bf16),
-        [parts, after],
-        [VMEM, HBM],
+        [parts, *after],
+        [VMEM, HBM, ANY, ANY],
     )
     return lax.all_to_all(mine, axes, 0, 0, tiled=False).reshape(block.shape)
 
@@ -706,18 +735,16 @@
     first, second = exchange(to_first, to_second)
 
     (
-        sums, counts, columns, columns_t, coarse_columns, coarse_columns_t, owners_t, cotangent,
-        matrices, sends, coarse_sends, owner,
+        counts, columns, columns_t, coarse_columns, coarse_columns_t, cotangent, matrices, sends,
+        coarse_sends, owner,
     ) = call(
         functools.partial(prepare_kernel, halo_rows=halo_rows, coarse_halo=coarse_halo),
         [
-            shape(coarse_rows, features, bf16),
             shape(2 * count_rows, features, bf16),
             shape(8, rows, f32),
             shape(rows, 8, f32),
             shape(8, coarse_rows, f32),
             shape(coarse_rows, 8, f32),
-            shape(rows, 8, f32),
             shape(rows, features, bf16),
             shape(7 * features, features, bf16),
             shape(1, 2 * halo_rows, jnp.int32),
@@ -737,7 +764,6 @@
         + [buffer(1, coarse_halo, jnp.int32)] * 2
         + [pltpu.SemaphoreType.DMA((17,))],
     )
-    more_sums = swapped(sums, "grp", 1)
 
     summed, slope, totals = call(
         fine_forward_kernel,
@@ -756,6 +782,14 @@
     )
     chip_totals = (totals.astype(f32) + swapped(totals, "grp", 1).astype(f32)).astype(bf16)
     more_totals = swapped(chip_totals, "grp", 2)
+    sums = call(
+        sums_kernel,
+        shape(coarse_rows, features, bf16),
+        [owner, cotangent, totals],
+        [VMEM, VMEM, ANY],
+    )
+    more_sums = swapped(sums, "grp", 1)
+    owners_t = call(owners_kernel, shape(rows, 8, f32), [owner, chip_totals], [VMEM, ANY])
 
     coarse_in, to_first, to_second, chip_sums, counts = call(
         coarse_input_kernel,
@@ -766,7 +800,8 @@
             shape(coarse_rows, features, bf16),
             shape(count_rows, features, f32),
         ],
-        [chip_totals, more_totals, sums, more_sums, coarse_sends],
+        [chip_totals, more_totals, sums, more_sums, coarse_sends, owners_t],
+        [VMEM] * 5 + [ANY],
     )
     coarse_first, coarse_second = exchange(to_first, to_second)
     more_sums = swapped(chip_sums, "grp", 2)
@@ -806,8 +841,10 @@
     )
     result = call(
         result_kernel,
-        shape(rows, features, bf16),
+        pltpu.HBM((rows, features), bf16),
         [states, summed, matrices, owners_t, fine_term],
+        scratch=[buffer(rows, features, bf16), pltpu.SemaphoreType.DMA],
+        out_specs=HBM,
     )
 
     ups, downs, first_grad, second_grad, weights = call(
@@ -838,16 +875,20 @@
 
     grad_states = call(
         finish_kernel,
-        shape(rows, features, bf16),
+        pltpu.HBM((rows, features), bf16),
         [ups, downs, first_back, second_back, sends, matrices],
         [HBM, HBM] + [VMEM] * 4,
         [
             buffer(rows, features, bf16),
             buffer(rows, 2 * features, bf16),
-            pltpu.SemaphoreType.DMA((2,)),
-        ],
-    )
-    weights = total_over_all(weights, ("grp", "sub"), grad_states)
+            buffer(rows, features, bf16),
+            pltpu.SemaphoreType.DMA((rows // CHUNK,)),
+            pltpu.SemaphoreType.DMA((rows // CHUNK,)),
+            pltpu.SemaphoreType.DMA,
+        ],
+        out_specs=HBM,
+    )
+    weights = total_over_all(weights, ("grp", "sub"), (result, first_back, second_back))
     grad_weights = call(widen_kernel, shape(7 * features, features, f32), [weights])
     return (result, grad_states, grad_weights.reshape(7, features, features))
 

time: 114 us -> 105 us (0.921)
  waiting for transfers between devices: 23.4 us -> 14.7 us
  starting transfers between devices: 30 us -> 34.9 us
  Pallas kernels: 54.2 us -> 49.4 us
    ppermute x4, waiting for transfers between devices: 10.2 us -> 4.9 us  [exchange(): lax.ppermute(first, 'sub', routes[0])]
    pallas_call x11 -> x13, Pallas kernels: 54.2 us -> 49.4 us  [call(): pl.pallas_call(kernel, out_shape=out_shape, in_specs=in_specs, out_specs=...]
    ppermute x4, waiting for transfers between devices: 10.8 us -> 6.77 us  [swapped(): lax.ppermute(block, axis, [(i, i ^ distance) for i in range(lax.axis_size...]
    ppermute x4, starting transfers between devices: 10.9 us -> 13.2 us  [exchange(): lax.ppermute(first, 'sub', routes[0])]
    all_to_all x1, starting transfers between devices: 7.79 us -> 9.22 us  [total_over_all(): lax.all_to_all(block.reshape(devices, share, 128), axes, 0, 0, tiled=False)]
    unnamed x14 -> x20, local copies, waits for them, and re-layouts: 4.94 us -> 4.48 us
  transfers between devices with their start and end apart: 14 -> 14, of which waited for: 7 -> 9; matrix products, arithmetic and copies ran while one was open for 0% -> 0% of each run, Pallas kernels for 18% -> 18%
where the time goes in v4:
time: 105 us; the launch traced here: 104 us
  Pallas kernels  49.4 us (47%)
  starting transfers between devices  34.9 us (33%)
  waiting for transfers between devices  14.7 us (14%)
  local copies, waits for them, and re-layouts  4.48 us (4%)
    pallas_call x13, Pallas kernels, call(): pl.pallas_call(kernel, out_shape=out_shape, in_specs=in_specs, out_specs=...  49.4 us
    ppermute x4, starting transfers between devices, exchange(): lax.ppermute(first, 'sub', routes[0])  13.2 us
    all_to_all x1, starting transfers between devices, total_over_all(): lax.all_to_all(block.reshape(devices, share, 128), axes, 0, 0, tiled=False)  9.22 us
    ppermute x4, waiting for transfers between devices, swapped(): lax.ppermute(block, axis, [(i, i ^ distance) for i in range(lax.axis_size...  6.77 us
    all_to_all x1, starting transfers between devices, total_over_all(): return lax.all_to_all(mine, axes, 0, 0, tiled=False).reshape(block.shape)  6.37 us
    ppermute x4, waiting for transfers between devices, exchange(): lax.ppermute(first, 'sub', routes[0])  4.9 us
    unnamed x20, local copies, waits for them, and re-layouts  4.48 us
    ppermute x4, starting transfers between devices, swapped(): lax.ppermute(block, axis, [(i, i ^ distance) for i in range(lax.axis_size...  3.29 us
  transfers between devices with their start and end apart: 14, of which 9 were waited for; matrix products, arithmetic and copies ran while one was open for 0% of the time, Pallas kernels for 18%

profile of v4, /device:TPU:0, one launch (start us, length us, event | category | flops | bytes accessed | tf_op | source)
XLA Modules:
  0.0 104.4 jit_solution(2173408807536195652)
XLA Ops:
  0.6 2.3 %shard_map.193 = (bf16[512,128]{1,0:T(8,128)(2,1)S(1)}, bf16[512,128]{1,0:T(8,128)(2,1)S(1)}, bf16[4096,128]{1,0:T(8,128)(2,1)S(1)}) custom-call(s32[1]{0:T(128)} %bitcast.even_ref, s32[512]{0:T(512)} %lo_hbm.1, s32[512]{0:T(512)} %hi_hbm.1, bf16[4096,128]{1,0:T(8,128)(2,1)} %x_hbm.1), custom_call_target="tpu_custom_call" | custom-call | tf_op jit(solution)/shard_map/pallas_call | solution.py:52
  3.6 5.8 %collective-permute-start = (bf16[512,128]{1,0:T(8,128)(2,1)S(1)}, bf16[512,128]{1,0:T(8,128)(2,1)S(1)}, u32[]{:S(2)}, u32[]{:S(2)}) collective-permute-start(bf16[512,128]{1,0:T(8,128)(2,1)S(1)} %get-tuple-element.39.rest_7_), channel_id=1, source_target_pairs={{0,1},{2,3},{4,5},{6,7},{1,0},{3,2},{5,4},{7,6},{8,9},{10,11},{12,... | collective-permute-start | bytes 393224 | tf_op jit(solution)/shard_map/ppermute | solution.py:683
  9.4 2.2 %shard_map.194 = (bf16[16,128]{1,0:T(8,128)(2,1)S(1)}, f32[8,4096]{1,0:T(8,128)S(1)}, f32[4096,8]{1,0:T(8,128)S(1)}, f32[8,1024]{1,0:T(8,128)S(1)}, f32[1024,8]{...) custom-call(s32[1]{0:T(128)} %bitcast.even_ref, ...), custom_call_target="tpu_custom_call" | custom-call | tf_op jit(solution)/shard_map/pallas_call | solution.py:52
  11.6 2.6 %collective-permute-done.first_ref = bf16[512,128]{1,0:T(8,128)(2,1)S(1)} collective-permute-done((bf16[512,128]{1,0:T(8,128)(2,1)S(1)}, bf16[512,128]{1,0:T(8,128)(2,1)S(1)}, u32[]{:S(2)}, u32[]{:S(2)}) %collective-permute-start) | collective-permute-done | bytes 131104 | tf_op jit(solution)/shard_map/ppermute | solution.py:683
  14.2 11.3 %shard_map.195 = (bf16[4096,128]{1,0:T(8,128)(2,1)S(1)}, bf16[32768,128]{1,0:T(8,128)(2,1)S(1)}, bf16[1040,128]{1,0:T(8,128)(2,1)S(1)}) custom-call(bf16[4096,128]{1,0:T(8,128)(2,1)S(1)} %get-tuple-element.38.h_ref, bf16[512,128]{1,0:T(8,128)(2,1)S(1)} %collective-permute-done.first_ref, bf16[512,128]{1,0:T(8,128)(2,1)S(1)} %collective-permute-done.1.second_ref, ...), custom_call_target="tpu_custom_call" | custom-call | tf_op jit(solution)/shard_map/pallas_call | solution.py:52
  25.6 1.5 %collective-permute-done.2 = bf16[1040,128]{1,0:T(8,128)(2,1)S(1)} collective-permute-done((bf16[1040,128]{1,0:T(8,128)(2,1)S(1)}, bf16[1040,128]{1,0:T(8,128)(2,1)S(1)}, u32[]{:S(2)}, u32[]{:S(2)}) %collective-permute-start.2) | collective-permute-done | bytes 266272 | tf_op jit(solution)/shard_map/ppermute | solution.py:687
  27.2 1.6 %collective-permute-start.3 = (bf16[1040,128]{1,0:T(8,128)(2,1)S(1)}, bf16[1040,128]{1,0:T(8,128)(2,1)S(1)}, u32[]{:S(2)}, u32[]{:S(2)}) collective-permute-start(bf16[1040,128]{1,0:T(8,128)(2,1)S(1)} %add_convert_fusion.after_ref.totals_ref), channel_id=1, source_target_pairs={{0,16},{8,24},{16,0},{24,8},{1,17},{9,25},{17,1},{25,9},{2,18},{10... | collective-permute-start | bytes 798728 | tf_op jit(solution)/shard_map/ppermute | solution.py:687
  28.8 2.8 %shard_map.197.sums_ref = bf16[1024,128]{1,0:T(8,128)(2,1)S(1)} custom-call(s32[32,128]{1,0:T(8,128)S(1)} %get-tuple-element.43.owner_ref, bf16[4096,128]{1,0:T(8,128)(2,1)S(1)} %get-tuple-element.47.g_ref, bf16[1040,128]{1,0:T(8,128)(2,1)S(1)} %get-tuple-element.46.after_ref), custom_call_target="tpu_custom_call" | custom-call | tf_op jit(solution)/shard_map/pallas_call | solution.py:52
  33.2 2.5 %collective-permute-done.3.more_totals_ref = bf16[1040,128]{1,0:T(8,128)(2,1)S(1)} collective-permute-done((bf16[1040,128]{1,0:T(8,128)(2,1)S(1)}, bf16[1040,128]{1,0:T(8,128)(2,1)S(1)}, u32[]{:S(2)}, u32[]{:S(2)}) %collective-permute-start.3) | collective-permute-done | bytes 266272 | tf_op jit(solution)/shard_map/ppermute | solution.py:687
  36.4 1.6 %collective-permute-start.7 = (bf16[1024,128]{1,0:T(8,128)(2,1)S(1)}, bf16[1024,128]{1,0:T(8,128)(2,1)S(1)}, u32[]{:S(2)}, u32[]{:S(2)}) collective-permute-start(bf16[1024,128]{1,0:T(8,128)(2,1)S(1)} %get-tuple-element.52.chip_sums_ref), channel_id=1, source_target_pairs={{0,16},{8,24},{16,0},{24,8},{1,17},{9,25},{17,1},{25,9},{2,18},{10... | collective-permute-start | bytes 786440 | tf_op jit(solution)/shard_map/ppermute | solution.py:687
  37.9 2.5 %collective-permute-start.5 = (bf16[64,128]{1,0:T(8,128)(2,1)S(1)}, bf16[64,128]{1,0:T(8,128)(2,1)S(1)}, u32[]{:S(2)}, u32[]{:S(2)}) collective-permute-start(bf16[64,128]{1,0:T(8,128)(2,1)S(1)} %get-tuple-element.50), channel_id=1, source_target_pairs={{0,1},{2,3},{4,5},{6,7},{1,0},{3,2},{5,4},{7,6},{8,9},{10,11},{12,... | collective-permute-start | bytes 49160 | tf_op jit(solution)/shard_map/ppermute | solution.py:683
  41.1 1.1 %collective-permute-done.5.first_ref = bf16[64,128]{1,0:T(8,128)(2,1)S(1)} collective-permute-done((bf16[64,128]{1,0:T(8,128)(2,1)S(1)}, bf16[64,128]{1,0:T(8,128)(2,1)S(1)}, u32[]{:S(2)}, u32[]{:S(2)}) %collective-permute-start.5) | collective-permute-done | bytes 16416 | tf_op jit(solution)/shard_map/ppermute | solution.py:683
  42.1 1.8 %collective-permute-done.7.more_sums_ref = bf16[1024,128]{1,0:T(8,128)(2,1)S(1)} collective-permute-done((bf16[1024,128]{1,0:T(8,128)(2,1)S(1)}, bf16[1024,128]{1,0:T(8,128)(2,1)S(1)}, u32[]{:S(2)}, u32[]{:S(2)}) %collective-permute-start.7) | collective-permute-done | bytes 262176 | tf_op jit(solution)/shard_map/ppermute | solution.py:687
  44.0 3.4 %shard_map.199 = (f32[1024,128]{1,0:T(8,128)S(1)}, bf16[64,128]{1,0:T(8,128)(2,1)S(1)}, bf16[64,128]{1,0:T(8,128)(2,1)S(1)}, bf16[1024,128]{1,0:T(8,128)(2,1)S(1...) custom-call(bf16[1024,128]{1,0:T(8,128)(2,1)S(1)} %get-tuple-element.49.cin_ref, ...), custom_call_target="tpu_custom_call" | custom-call | tf_op jit(solution)/shard_map/pallas_call | solution.py:52
  47.4 3.2 %collective-permute-start.8 = (bf16[64,128]{1,0:T(8,128)(2,1)S(1)}, bf16[64,128]{1,0:T(8,128)(2,1)S(1)}, u32[]{:S(2)}, u32[]{:S(2)}) collective-permute-start(bf16[64,128]{1,0:T(8,128)(2,1)S(1)} %get-tuple-element.56.first_grad_ref), channel_id=1, source_target_pairs={{0,1},{2,3},{4,5},{6,7},{1,0},{3,2},{5,4},{7,6},{8,9},{10,11},{12,... | collective-permute-start | bytes 49160 | tf_op jit(solution)/shard_map/ppermute | solution.py:683
  52.3 10.7 %shard_map.202 = (bf16[4096,128]{1,0:T(8,128)(2,1)}, bf16[4096,256]{1,0:T(8,128)(2,1)}, bf16[512,128]{1,0:T(8,128)(2,1)S(1)}, bf16[512,128]{1,0:T(8,128)(2,1)S(1)}, bf16[1024,128]{1,0:T(8,128)(2,1)S(1)}) custom-call(bf16[4096,128]{1,0:T(8,128)(2,1)S(1)} %get-tuple-element.38.h_ref, bf16[512,128]{1,0:T(8,128)(2,1)S(1)} %collective-permute-done.first_ref, ...), custom_call_target="tpu_custom_call" | custom-call | tf_op jit(solution)/shard_map/pallas_call | solution.py:52
  63.8 9.2 %all-to-all-start = ((bf16[32,32,128]{2,1,0:T(8,128)(2,1)}), bf16[32,32,128]{2,1,0:T(8,128)(2,1)}, u32[]{:S(2)}, u32[]{:S(2)}) async-start(bf16[32,32,128]{2,1,0:T(8,128)(2,1)} %bitcast.14), calls=%async_computation | async-start | bytes 524288 | tf_op jit(solution)/shard_map/all_to_all | solution.py:693
  73.0 1.8 %collective-permute-start.10 = (bf16[512,128]{1,0:T(8,128)(2,1)}, bf16[512,128]{1,0:T(8,128)(2,1)S(1)}, u32[]{:S(2)}, u32[]{:S(2)}) collective-permute-start(bf16[512,128]{1,0:T(8,128)(2,1)} %copy-done.9), channel_id=1, source_target_pairs={{0,1},{2,3},{4,5},{6,7},{1,0},{3,2},{5,4},{7,6},{8,9},{10,11},{12,... | collective-permute-start | bytes 393224 | tf_op jit(solution)/shard_map/ppermute | solution.py:683
  75.5 1.2 %copy-done.1 = bf16[4096,128]{1,0:T(8,128)(2,1)S(1)} copy-done((bf16[4096,128]{1,0:T(8,128)(2,1)S(1)}, bf16[4096,128]{1,0:T(8,128)(2,1)}, u32[]{:S(2)}) %copy-start.1) | copy-done | bytes 1048600
  77.6 4.7 %shard_map.201.result_ref = bf16[4096,128]{1,0:T(8,128)(2,1)} custom-call(bf16[4096,128]{1,0:T(8,128)(2,1)S(1)} %get-tuple-element.38.h_ref, bf16[4096,128]{1,0:T(8,128)(2,1)S(1)} %copy-done.1, bf16[896,128]{1,0:T(8,128)(2,1)S(1)} %get-tuple-element.41.weights_ref.matrices_ref, f32[4096,8]{1,0:T(8,128)S(1)} %shard_map.196.after_ref.owners_ref, ...), custom_call_target="tpu_custom_call" | custom-call | tf_op jit(solution)/shard_map/pallas_call | solution.py:52
  84.9 1.7 %shard_map.204 = bf16[32,32,128]{2,1,0:T(8,128)(2,1)} custom-call(bf16[32,32,128]{2,1,0:T(8,128)(2,1)} %all-to-all-done.parts_ref, bf16[4096,128]{1,0:T(8,128)(2,1)} %shard_map.201.result_ref, bf16[512,128]{1,0:T(8,128)(2,1)S(1)} %collective-permute-done.10.first_back_ref.first_ref, bf16[512,128]{1,0:T(8,128)(2,1)S(1)} %copy-done.3), custom_call_target="tpu_custom_call" | custom-call | tf_op jit(solution)/shard_map/pallas_call | solution.py:52
  86.6 6.4 %all-to-all-start.1 = ((bf16[32,32,128]{2,1,0:T(8,128)(2,1)}), bf16[32,32,128]{2,1,0:T(8,128)(2,1)S(1)}, u32[]{:S(2)}, u32[]{:S(2)}) async-start(bf16[32,32,128]{2,1,0:T(8,128)(2,1)} %shard_map.204), calls=%async_computation.1 | async-start | bytes 524288 | tf_op jit(solution)/shard_map/all_to_all | solution.py:700
  93.0 7.6 %shard_map.203 = bf16[4096,128]{1,0:T(8,128)(2,1)} custom-call(bf16[4096,128]{1,0:T(8,128)(2,1)} %get-tuple-element.67.ups_hbm, bf16[4096,256]{1,0:T(8,128)(2,1)} %get-tuple-element.68.downs_hbm, bf16[512,128]{1,0:T(8,128)(2,1)S(1)} %collective-permute-done.10.first_back_ref.first_ref, bf16[512,128]{1,0:T(8,128)(2,1)S(1)} %copy-done.4, ...), custom_call_target="tpu_custom_call" | custom-call | tf_op jit(solution)/shard_map/pallas_call | solution.py:52
  100.6 3.1 %all-to-all-done.1 = bf16[32,32,128]{2,1,0:T(8,128)(2,1)S(1)} async-done(((bf16[32,32,128]{2,1,0:T(8,128)(2,1)}), bf16[32,32,128]{2,1,0:T(8,128)(2,1)S(1)}, u32[]{:S(2)}, u32[]{:S(2)}) %all-to-all-start.1) | async-done | bytes 262176 | tf_op jit(solution)/shard_map/all_to_all | solution.py:700
  (38 shorter events, 11.1 us)
Async XLA Ops:
  2.9 8.7 %collective-permute-start.1 = (bf16[512,128]{1,0:T(8,128)(2,1)S(1)}, bf16[512,128]{1,0:T(8,128)(2,1)S(1)}, u32[]{:S(2)}, u32[]{:S(2)}) collective-permute-start(bf16[512,128]{1,0:T(8,128)(2,1)S(1)} %get-tuple-element.40), channel_id=1, source_target_pairs={{1,2},{3,4},{5,6},{2,1},{4,3},{6,5},{9,10},{11,12},{13,14},{10,9},... | collective-permute-start | bytes 393224 | tf_op jit(solution)/shard_map/ppermute | solution.py:683
  3.6 10.6 %collective-permute-start = (bf16[512,128]{1,0:T(8,128)(2,1)S(1)}, bf16[512,128]{1,0:T(8,128)(2,1)S(1)}, u32[]{:S(2)}, u32[]{:S(2)}) collective-permute-start(bf16[512,128]{1,0:T(8,128)(2,1)S(1)} %get-tuple-element.39.rest_7_), channel_id=1, source_target_pairs={{0,1},{2,3},{4,5},{6,7},{1,0},{3,2},{5,4},{7,6},{8,9},{10,11},{12,... | collective-permute-start | bytes 393224 | tf_op jit(solution)/shard_map/ppermute | solution.py:683
  25.5 26.8 %copy-start = (bf16[4096,128]{1,0:T(8,128)(2,1)}, bf16[4096,128]{1,0:T(8,128)(2,1)S(1)}, u32[]{:S(2)}) copy-start(bf16[4096,128]{1,0:T(8,128)(2,1)S(1)} %get-tuple-element.45.summed_ref) | copy-start | bytes 3145732
  25.5 1.6 %collective-permute-start.2 = (bf16[1040,128]{1,0:T(8,128)(2,1)S(1)}, bf16[1040,128]{1,0:T(8,128)(2,1)S(1)}, u32[]{:S(2)}, u32[]{:S(2)}) collective-permute-start(bf16[1040,128]{1,0:T(8,128)(2,1)S(1)} %get-tuple-element.46.after_ref), channel_id=1, source_target_pairs={{0,8},{8,0},{16,24},{24,16},{1,9},{9,1},{17,25},{25,17},{2,10},{10... | collective-permute-start | bytes 798728 | tf_op jit(solution)/shard_map/ppermute | solution.py:687
  27.2 8.5 %collective-permute-start.3 = (bf16[1040,128]{1,0:T(8,128)(2,1)S(1)}, bf16[1040,128]{1,0:T(8,128)(2,1)S(1)}, u32[]{:S(2)}, u32[]{:S(2)}) collective-permute-start(bf16[1040,128]{1,0:T(8,128)(2,1)S(1)} %add_convert_fusion.after_ref.totals_ref), channel_id=1, source_target_pairs={{0,16},{8,24},{16,0},{24,8},{1,17},{9,25},{17,1},{25,9},{2,18},{10... | collective-permute-start | bytes 798728 | tf_op jit(solution)/shard_map/ppermute | solution.py:687
  31.6 1.6 %collective-permute-start.4 = (bf16[1024,128]{1,0:T(8,128)(2,1)S(1)}, bf16[1024,128]{1,0:T(8,128)(2,1)S(1)}, u32[]{:S(2)}, u32[]{:S(2)}) collective-permute-start(bf16[1024,128]{1,0:T(8,128)(2,1)S(1)} %shard_map.197.sums_ref), channel_id=1, source_target_pairs={{0,8},{8,0},{16,24},{24,16},{1,9},{9,1},{17,25},{25,17},{2,10},{10... | collective-permute-start | bytes 786440 | tf_op jit(solution)/shard_map/ppermute | solution.py:687
  36.4 7.6 %collective-permute-start.7 = (bf16[1024,128]{1,0:T(8,128)(2,1)S(1)}, bf16[1024,128]{1,0:T(8,128)(2,1)S(1)}, u32[]{:S(2)}, u32[]{:S(2)}) collective-permute-start(bf16[1024,128]{1,0:T(8,128)(2,1)S(1)} %get-tuple-element.52.chip_sums_ref), channel_id=1, source_target_pairs={{0,16},{8,24},{16,0},{24,8},{1,17},{9,25},{17,1},{25,9},{2,18},{10... | collective-permute-start | bytes 786440 | tf_op jit(solution)/shard_map/ppermute | solution.py:687
  37.9 4.2 %collective-permute-start.5 = (bf16[64,128]{1,0:T(8,128)(2,1)S(1)}, bf16[64,128]{1,0:T(8,128)(2,1)S(1)}, u32[]{:S(2)}, u32[]{:S(2)}) collective-permute-start(bf16[64,128]{1,0:T(8,128)(2,1)S(1)} %get-tuple-element.50), channel_id=1, source_target_pairs={{0,1},{2,3},{4,5},{6,7},{1,0},{3,2},{5,4},{7,6},{8,9},{10,11},{12,... | collective-permute-start | bytes 49160 | tf_op jit(solution)/shard_map/ppermute | solution.py:683
  40.4 1.7 %collective-permute-start.6 = (bf16[64,128]{1,0:T(8,128)(2,1)S(1)}, bf16[64,128]{1,0:T(8,128)(2,1)S(1)}, u32[]{:S(2)}, u32[]{:S(2)}) collective-permute-start(bf16[64,128]{1,0:T(8,128)(2,1)S(1)} %get-tuple-element.51), channel_id=1, source_target_pairs={{1,2},{3,4},{5,6},{2,1},{4,3},{6,5},{9,10},{11,12},{13,14},{10,9},... | collective-permute-start | bytes 49160 | tf_op jit(solution)/shard_map/ppermute | solution.py:683
  47.4 4.9 %collective-permute-start.8 = (bf16[64,128]{1,0:T(8,128)(2,1)S(1)}, bf16[64,128]{1,0:T(8,128)(2,1)S(1)}, u32[]{:S(2)}, u32[]{:S(2)}) collective-permute-start(bf16[64,128]{1,0:T(8,128)(2,1)S(1)} %get-tuple-element.56.first_grad_ref), channel_id=1, source_target_pairs={{0,1},{2,3},{4,5},{6,7},{1,0},{3,2},{5,4},{7,6},{8,9},{10,11},{12,... | collective-permute-start | bytes 49160 | tf_op jit(solution)/shard_map/ppermute | solution.py:683
  50.5 1.7 %collective-permute-start.9 = (bf16[64,128]{1,0:T(8,128)(2,1)S(1)}, bf16[64,128]{1,0:T(8,128)(2,1)S(1)}, u32[]{:S(2)}, u32[]{:S(2)}) collective-permute-start(bf16[64,128]{1,0:T(8,128)(2,1)S(1)} %get-tuple-element.57.second_grad_ref), channel_id=1, source_target_pairs={{1,2},{3,4},{5,6},{2,1},{4,3},{6,5},{9,10},{11,12},{13,14},{10,9},... | collective-permute-start | bytes 49160 | tf_op jit(solution)/shard_map/ppermute | solution.py:683
  52.0 11.0 %copy-start.5 = (bf16[1024,128]{1,0:T(8,128)(2,1)}, bf16[1024,128]{1,0:T(8,128)(2,1)S(1)}, u32[]{:S(2)}) copy-start(bf16[1024,128]{1,0:T(8,128)(2,1)S(1)} %get-tuple-element.61.fine_ref) | copy-start | bytes 786436
  63.0 0.7 copy-start.7
  63.0 0.7 copy-start.8
  63.1 10.0 %copy-start.9 = (bf16[512,128]{1,0:T(8,128)(2,1)}, bf16[512,128]{1,0:T(8,128)(2,1)S(1)}, u32[]{:S(2)}) copy-start(bf16[512,128]{1,0:T(8,128)(2,1)S(1)} %get-tuple-element.69) | copy-start | bytes 393220
  63.8 20.2 %all-to-all-start = ((bf16[32,32,128]{2,1,0:T(8,128)(2,1)}), bf16[32,32,128]{2,1,0:T(8,128)(2,1)}, u32[]{:S(2)}, u32[]{:S(2)}) async-start(bf16[32,32,128]{2,1,0:T(8,128)(2,1)} %bitcast.14), calls=%async_computation | async-start | bytes 524288 | tf_op jit(solution)/shard_map/all_to_all | solution.py:693
  73.0 10.3 %collective-permute-start.10 = (bf16[512,128]{1,0:T(8,128)(2,1)}, bf16[512,128]{1,0:T(8,128)(2,1)S(1)}, u32[]{:S(2)}, u32[]{:S(2)}) collective-permute-start(bf16[512,128]{1,0:T(8,128)(2,1)} %copy-done.9), channel_id=1, source_target_pairs={{0,1},{2,3},{4,5},{6,7},{1,0},{3,2},{5,4},{7,6},{8,9},{10,11},{12,... | collective-permute-start | bytes 393224 | tf_op jit(solution)/shard_map/ppermute | solution.py:683
  74.8 8.5 %collective-permute-start.11 = (bf16[512,128]{1,0:T(8,128)(2,1)}, bf16[512,128]{1,0:T(8,128)(2,1)S(1)}, u32[]{:S(2)}, u32[]{:S(2)}) collective-permute-start(bf16[512,128]{1,0:T(8,128)(2,1)} %copy-done.8), channel_id=1, source_target_pairs={{1,2},{3,4},{5,6},{2,1},{4,3},{6,5},{9,10},{11,12},{13,14},{10,9},... | collective-permute-start | bytes 393224 | tf_op jit(solution)/shard_map/ppermute | solution.py:683
  75.4 1.2 %copy-start.1 = (bf16[4096,128]{1,0:T(8,128)(2,1)S(1)}, bf16[4096,128]{1,0:T(8,128)(2,1)}, u32[]{:S(2)}) copy-start(bf16[4096,128]{1,0:T(8,128)(2,1)} %copy-done) | copy-start | bytes 3145732
  76.7 0.9 copy-start.6
  83.3 0.7 copy-start.2
  84.0 0.9 copy-start.3
  84.9 8.1 %copy-start.4 = (bf16[512,128]{1,0:T(8,128)(2,1)S(1)}, bf16[512,128]{1,0:T(8,128)(2,1)}, u32[]{:S(2)}) copy-start(bf16[512,128]{1,0:T(8,128)(2,1)} %copy-done.2) | copy-start | bytes 393220
  86.6 17.0 %all-to-all-start.1 = ((bf16[32,32,128]{2,1,0:T(8,128)(2,1)}), bf16[32,32,128]{2,1,0:T(8,128)(2,1)S(1)}, u32[]{:S(2)}, u32[]{:S(2)}) async-start(bf16[32,32,128]{2,1,0:T(8,128)(2,1)} %shard_map.204), calls=%async_computation.1 | async-start | bytes 524288 | tf_op jit(solution)/shard_map/all_to_all | solution.py:700

commit v5 on v4

--- a/solution.py
+++ b/solution.py
@@ -454,6 +454,7 @@
 
 
 def coarse_tail_kernel(
+    group_ref,
     cin_ref,
     first_ref,
     second_ref,
@@ -466,8 +467,6 @@
     downs_ref,
     fine_ref,
     weights_ref,
-    *,
-    scale,
 ):
     cin = cin_ref[...]
     out = (cin.astype(f32) + dot(summed_ref[...], matrix(matrices_ref, 5))).astype(bf16)
@@ -478,10 +477,20 @@
         + dot_tn(first_ref[...], first_grad_ref[...])
         + dot_tn(second_ref[...], second_grad_ref[...])
     )
-    weights_ref[0:128, :] = (pair_grad[:, :128] * scale).astype(bf16)
-    weights_ref[128:256, :] = (other_grad * scale).astype(bf16)
-    weights_ref[256:384, :] = (dot_tn(summed_ref[...], ups_ref[...]) * scale).astype(bf16)
-    weights_ref[384:512, :] = (dot_tn(out, sums_ref[...]) * scale).astype(bf16)
+    grads = [
+        pair_grad[:, :128],
+        other_grad,
+        dot_tn(summed_ref[...], ups_ref[...]),
+        dot_tn(out, sums_ref[...]),
+    ]
+    weights_ref[...] = choose(group_ref[0], grads).astype(bf16)
+
+
+def choose(place, values):
+    picked = values[-1]
+    for n, value in enumerate(values[:-1]):
+        picked = jnp.where(place == n, value, picked)
+    return picked
 
 
 def owner_columns(owner_ref):
@@ -603,8 +612,7 @@
         + dot_tn(second_ref[...], second_grad)
     ).astype(bf16)
     weights_ref[256:384, :] = dot_tn(summed_ref[...], ups_ref[...]).astype(bf16)
-    weights_ref[384:896, :] = coarse_weights_ref[...]
-    weights_ref[896:1024, :] = jnp.zeros((128, 128), bf16)
+    weights_ref[384:512, :] = coarse_weights_ref[...]
     for copy in copies:
         copy.wait()
 
@@ -663,15 +671,27 @@
     pltpu.make_async_copy(out_ref, out_hbm, out_sem).wait()
 
 
-def share_kernel(parts_ref, result_ref, first_ref, second_ref, out_ref):
-    total = parts_ref[0].astype(f32)
-    for n in range(1, parts_ref.shape[0]):
-        total = total + parts_ref[n].astype(f32)
-    out_ref[...] = jnp.broadcast_to(total.astype(bf16)[None], out_ref.shape)
-
-
-def widen_kernel(x_ref, out_ref):
-    out_ref[...] = x_ref[: out_ref.shape[0], :].astype(f32)
+def add_kernel(mine_ref, theirs_ref, *rest):
+    out_ref = rest[-1]
+    out_ref[...] = (mine_ref[...].astype(f32) + theirs_ref[...].astype(f32)).astype(bf16)
+
+
+def add_gather_kernel(mine_ref, theirs_ref, out_ref):
+    mine, theirs = mine_ref[...].astype(f32), theirs_ref[...].astype(f32)
+    out_ref[:384, :] = mine[:384] + theirs[:384]
+    out_ref[384:512, :] = mine[384:]
+    out_ref[512:, :] = theirs[384:]
+
+
+def weights_kernel(group_ref, mine_ref, theirs_ref, out_ref):
+    out_ref[:384, :] = mine_ref[:384, :] + theirs_ref[:384, :]
+    group = group_ref[0]
+    low, high = lax.rem(group, 2), group // 2
+    for n in range(4):
+        row = jnp.where(high == n // 2, 384, 512)
+        here = pl.ds(pl.multiple_of(row, 128), 128)
+        value = jnp.where(low == n % 2, mine_ref[here, :], theirs_ref[here, :])
+        out_ref[384 + 128 * n : 512 + 128 * n, :] = value
 
 
 def exchange(first, second):
@@ -687,17 +707,29 @@
     return lax.ppermute(block, axis, [(i, i ^ distance) for i in range(lax.axis_size(axis))])
 
 
-def total_over_all(block, axes, after):
-    devices = lax.axis_size(axes)
-    share = block.shape[0] // devices
-    parts = lax.all_to_all(block.reshape(devices, share, 128), axes, 0, 0, tiled=False)
-    mine = call(
-        share_kernel,
-        jax.ShapeDtypeStruct((devices, share, 128), bf16),
-        [parts, *after],
-        [VMEM, HBM, ANY, ANY],
-    )
-    return lax.all_to_all(mine, axes, 0, 0, tiled=False).reshape(block.shape)
+def total_weights(weights, group, after):
+    distance, number = 1, 0
+    while distance < lax.axis_size("sub"):
+        theirs = swapped(weights, "sub", distance)
+        waits = after[number] if number < len(after) else ()
+        weights = call(
+            add_kernel,
+            shape(*weights.shape, bf16),
+            [weights, theirs, *waits],
+            [VMEM, VMEM] + [HBM] * len(waits),
+        )
+        distance, number = 2 * distance, number + 1
+    weights = call(
+        add_gather_kernel,
+        shape(640, 128, f32),
+        [weights, swapped(weights, "grp", 2)],
+    )
+    return call(
+        weights_kernel,
+        shape(896, 128, f32),
+        [group, weights, swapped(weights, "grp", 1)],
+        [SMEM, VMEM, VMEM],
+    )
 
 
 def per_device(
@@ -727,6 +759,7 @@
     count_rows = coarse_rows // 128
     owner = coarse_owner.reshape(rows // 128, 128)
     even = (1 - lax.rem(lax.axis_index("sub"), 2)).astype(jnp.int32).reshape(1)
+    group = lax.axis_index("grp").astype(jnp.int32).reshape(1)
 
     def buffer(count, columns, dtype):
         return pltpu.VMEM((count, columns), dtype)
@@ -832,12 +865,13 @@
     first_back, second_back = exchange(first_grad, second_grad)
 
     fine_term, coarse_weights = call(
-        functools.partial(coarse_tail_kernel, scale=1.0 / lax.axis_size("grp")),
-        [shape(coarse_rows, features, bf16), shape(4 * features, features, bf16)],
-        [
-            coarse_in, coarse_first, coarse_second, sums, matrices,
+        coarse_tail_kernel,
+        [shape(coarse_rows, features, bf16), shape(features, features, bf16)],
+        [
+            group, coarse_in, coarse_first, coarse_second, sums, matrices,
             first_grad, second_grad, coarse_sum, coarse_ups, coarse_downs,
         ],
+        [SMEM] + [VMEM] * 10,
     )
     result = call(
         result_kernel,
@@ -854,7 +888,7 @@
             pltpu.HBM((rows, 2 * features), bf16),
             shape(halo_rows, features, bf16),
             shape(halo_rows, features, bf16),
-            shape(8 * features, features, bf16),
+            shape(4 * features, features, bf16),
         ],
         [
             states, first, second, cotangent, summed, slope, matrices, columns, owners_t,
@@ -888,8 +922,7 @@
         ],
         out_specs=HBM,
     )
-    weights = total_over_all(weights, ("grp", "sub"), (result, first_back, second_back))
-    grad_weights = call(widen_kernel, shape(7 * features, features, f32), [weights])
+    grad_weights = total_weights(weights, group, ((), (result,), (grad_states,)))
     return (result, grad_states, grad_weights.reshape(7, features, features))
 
 

time: 105 us -> 122 us (1.16)
  local copies, waits for them, and re-layouts: 4.48 us -> 20.9 us
  starting transfers between devices: 34.9 us -> 29.9 us
  waiting for transfers between devices: 14.7 us -> 18.9 us
    unnamed x20 -> x58, local copies, waits for them, and re-layouts: 4.48 us -> 20.9 us
    all_to_all x2 -> x0, starting transfers between devices: 15.6 us -> none  [the longest x1 9.22 us: total_over_all(): lax.all_to_all(block.reshape(devices, share, 128), axes, 0, 0, tiled=False)]
    ppermute x4 -> x9, starting transfers between devices: 3.29 us -> 13.1 us  [swapped(): lax.ppermute(block, axis, [(i, i ^ distance) for i in range(lax.axis_size...]
    ppermute x4 -> x9, waiting for transfers between devices: 6.77 us -> 15.8 us  [swapped(): lax.ppermute(block, axis, [(i, i ^ distance) for i in range(lax.axis_size...]
    all_to_all x2 -> x0, waiting for transfers between devices: 3.05 us -> none  [the longest x1 3.05 us: total_over_all(): return lax.all_to_all(mine, axes, 0, 0, tiled=False).reshape(block.shape)]
    ppermute x4, waiting for transfers between devices: 4.9 us -> 3.09 us  [exchange(): lax.ppermute(first, 'sub', routes[0])]
    pallas_call x13 -> x16, Pallas kernels: 49.4 us -> 50 us  [call(): pl.pallas_call(kernel, out_shape=out_shape, in_specs=in_specs, out_specs=...]
  transfers between devices with their start and end apart: 14 -> 17, of which waited for: 9 -> 9; matrix products, arithmetic and copies ran while one was open for 0% -> 0% of each run, Pallas kernels for 18% -> 16%
where the time goes in v5:
time: 122 us; the launch traced here: 121 us
  Pallas kernels  50 us (41%)
  starting transfers between devices  29.9 us (25%)
  local copies, waits for them, and re-layouts  20.9 us (17%)
  waiting for transfers between devices  18.9 us (15%)
    pallas_call x16, Pallas kernels, call(): pl.pallas_call(kernel, out_shape=out_shape, in_specs=in_specs, out_specs=...  50 us
    unnamed x58, local copies, waits for them, and re-layouts  20.9 us
    ppermute x9, waiting for transfers between devices, swapped(): lax.ppermute(block, axis, [(i, i ^ distance) for i in range(lax.axis_size...  15.8 us
    ppermute x4, starting transfers between devices, exchange(): lax.ppermute(first, 'sub', routes[0])  13.6 us
    ppermute x9, starting transfers between devices, swapped(): lax.ppermute(block, axis, [(i, i ^ distance) for i in range(lax.axis_size...  13.1 us
    ppermute x4, starting transfers between devices, exchange(): lax.ppermute(second, 'sub', routes[1])  3.22 us
    ppermute x4, waiting for transfers between devices, exchange(): lax.ppermute(first, 'sub', routes[0])  3.09 us
  transfers between devices with their start and end apart: 17, of which 9 were waited for; matrix products, arithmetic and copies ran while one was open for 0% of the time, Pallas kernels for 16%

profile of v5, /device:TPU:0, one launch (start us, length us, event | category | flops | bytes accessed | tf_op | source)
XLA Modules:
  0.0 120.7 jit_solution(8525594427209508610)
XLA Ops:
  0.6 2.3 %shard_map.193 = (bf16[512,128]{1,0:T(8,128)(2,1)S(1)}, bf16[512,128]{1,0:T(8,128)(2,1)S(1)}, bf16[4096,128]{1,0:T(8,128)(2,1)S(1)}) custom-call(s32[1]{0:T(128)} %bitcast.even_ref, s32[512]{0:T(512)} %lo_hbm.1, s32[512]{0:T(512)} %hi_hbm.1, bf16[4096,128]{1,0:T(8,128)(2,1)} %x_hbm.1), custom_call_target="tpu_custom_call" | custom-call | tf_op jit(solution)/shard_map/pallas_call | solution.py:52
  3.6 5.8 %collective-permute-start = (bf16[512,128]{1,0:T(8,128)(2,1)S(1)}, bf16[512,128]{1,0:T(8,128)(2,1)S(1)}, u32[]{:S(2)}, u32[]{:S(2)}) collective-permute-start(bf16[512,128]{1,0:T(8,128)(2,1)S(1)} %get-tuple-element.39.rest_7_), channel_id=1, source_target_pairs={{0,1},{2,3},{4,5},{6,7},{1,0},{3,2},{5,4},{7,6},{8,9},{10,11},{12,... | collective-permute-start | bytes 393224 | tf_op jit(solution)/shard_map/ppermute | solution.py:703
  9.4 2.2 %shard_map.194 = (bf16[16,128]{1,0:T(8,128)(2,1)S(1)}, f32[8,4096]{1,0:T(8,128)S(1)}, f32[4096,8]{1,0:T(8,128)S(1)}, f32[8,1024]{1,0:T(8,128)S(1)}, f32[1024,8]{...) custom-call(s32[1]{0:T(128)} %bitcast.even_ref, ...), custom_call_target="tpu_custom_call" | custom-call | tf_op jit(solution)/shard_map/pallas_call | solution.py:52
  12.2 2.0 %collective-permute-done.first_ref = bf16[512,128]{1,0:T(8,128)(2,1)S(1)} collective-permute-done((bf16[512,128]{1,0:T(8,128)(2,1)S(1)}, bf16[512,128]{1,0:T(8,128)(2,1)S(1)}, u32[]{:S(2)}, u32[]{:S(2)}) %collective-permute-start) | collective-permute-done | bytes 131104 | tf_op jit(solution)/shard_map/ppermute | solution.py:703
  14.2 11.3 %shard_map.195 = (bf16[4096,128]{1,0:T(8,128)(2,1)S(1)}, bf16[32768,128]{1,0:T(8,128)(2,1)S(1)}, bf16[1040,128]{1,0:T(8,128)(2,1)S(1)}) custom-call(bf16[4096,128]{1,0:T(8,128)(2,1)S(1)} %get-tuple-element.38.h_ref, bf16[512,128]{1,0:T(8,128)(2,1)S(1)} %collective-permute-done.first_ref, bf16[512,128]{1,0:T(8,128)(2,1)S(1)} %collective-permute-done.1.second_ref, ...), custom_call_target="tpu_custom_call" | custom-call | tf_op jit(solution)/shard_map/pallas_call | solution.py:52
  25.5 3.3 %copy-done = bf16[32768,128]{1,0:T(8,128)(2,1)} copy-done((bf16[32768,128]{1,0:T(8,128)(2,1)}, bf16[32768,128]{1,0:T(8,128)(2,1)S(1)}, u32[]{:S(2)}) %copy-start) | copy-done | bytes 8388632
  30.5 1.6 %collective-permute-start.3 = (bf16[1040,128]{1,0:T(8,128)(2,1)S(1)}, bf16[1040,128]{1,0:T(8,128)(2,1)S(1)}, u32[]{:S(2)}, u32[]{:S(2)}) collective-permute-start(bf16[1040,128]{1,0:T(8,128)(2,1)S(1)} %add_convert_fusion.after_ref.totals_ref), channel_id=1, source_target_pairs={{0,16},{8,24},{16,0},{24,8},{1,17},{9,25},{17,1},{25,9},{2,18},{10... | collective-permute-start | bytes 798728 | tf_op jit(solution)/shard_map/ppermute | solution.py:707
  32.0 2.8 %shard_map.197.sums_ref = bf16[1024,128]{1,0:T(8,128)(2,1)S(1)} custom-call(s32[32,128]{1,0:T(8,128)S(1)} %get-tuple-element.43.owner_ref, bf16[4096,128]{1,0:T(8,128)(2,1)S(1)} %get-tuple-element.47.g_ref, bf16[1040,128]{1,0:T(8,128)(2,1)S(1)} %get-tuple-element.46.after_ref), custom_call_target="tpu_custom_call" | custom-call | tf_op jit(solution)/shard_map/pallas_call | solution.py:52
  36.4 2.5 %collective-permute-done.3.more_totals_ref = bf16[1040,128]{1,0:T(8,128)(2,1)S(1)} collective-permute-done((bf16[1040,128]{1,0:T(8,128)(2,1)S(1)}, bf16[1040,128]{1,0:T(8,128)(2,1)S(1)}, u32[]{:S(2)}, u32[]{:S(2)}) %collective-permute-start.3) | collective-permute-done | bytes 266272 | tf_op jit(solution)/shard_map/ppermute | solution.py:707
  41.7 2.5 %collective-permute-start.5 = (bf16[64,128]{1,0:T(8,128)(2,1)S(1)}, bf16[64,128]{1,0:T(8,128)(2,1)S(1)}, u32[]{:S(2)}, u32[]{:S(2)}) collective-permute-start(bf16[64,128]{1,0:T(8,128)(2,1)S(1)} %get-tuple-element.50), channel_id=1, source_target_pairs={{0,1},{2,3},{4,5},{6,7},{1,0},{3,2},{5,4},{7,6},{8,9},{10,11},{12,... | collective-permute-start | bytes 49160 | tf_op jit(solution)/shard_map/ppermute | solution.py:703
  45.9 1.8 %collective-permute-done.7.more_sums_ref = bf16[1024,128]{1,0:T(8,128)(2,1)S(1)} collective-permute-done((bf16[1024,128]{1,0:T(8,128)(2,1)S(1)}, bf16[1024,128]{1,0:T(8,128)(2,1)S(1)}, u32[]{:S(2)}, u32[]{:S(2)}) %collective-permute-start.7) | collective-permute-done | bytes 262176 | tf_op jit(solution)/shard_map/ppermute | solution.py:707
  47.7 4.0 %shard_map.199 = (f32[1024,128]{1,0:T(8,128)S(1)}, bf16[64,128]{1,0:T(8,128)(2,1)}, bf16[64,128]{1,0:T(8,128)(2,1)}, bf16[1024,128]{1,0:T(8,128)(2,1)S(1)}, bf16...) custom-call(bf16[1024,128]{1,0:T(8,128)(2,1)S(1)} %get-tuple-element.49.cin_ref, ...), custom_call_target="tpu_custom_call" | custom-call | tf_op jit(solution)/shard_map/pallas_call | solution.py:52
  55.5 3.1 %collective-permute-start.8 = (bf16[64,128]{1,0:T(8,128)(2,1)}, bf16[64,128]{1,0:T(8,128)(2,1)S(1)}, u32[]{:S(2)}, u32[]{:S(2)}) collective-permute-start(bf16[64,128]{1,0:T(8,128)(2,1)} %get-tuple-element.56.first_grad_ref), channel_id=1, source_target_pairs={{0,1},{2,3},{4,5},{6,7},{1,0},{3,2},{5,4},{7,6},{8,9},{10,11},{12,... | collective-permute-start | bytes 49160 | tf_op jit(solution)/shard_map/ppermute | solution.py:703
  66.2 3.4 %copy-done.1 = bf16[32768,128]{1,0:T(8,128)(2,1)S(1)} copy-done((bf16[32768,128]{1,0:T(8,128)(2,1)S(1)}, bf16[32768,128]{1,0:T(8,128)(2,1)}, u32[]{:S(2)}) %copy-start.1) | copy-done | bytes 8388632
  74.0 11.5 %shard_map.202 = (bf16[4096,128]{1,0:T(8,128)(2,1)}, bf16[4096,256]{1,0:T(8,128)(2,1)}, bf16[512,128]{1,0:T(8,128)(2,1)S(1)}, bf16[512,128]{1,0:T(8,128)(2,1)S(1)}, bf16[512,128]{1,0:T(8,128)(2,1)S(1)}) custom-call(bf16[4096,128]{1,0:T(8,128)(2,1)S(1)} %get-tuple-element.38.h_ref, bf16[512,128]{1,0:T(8,128)(2,1)S(1)} %copy-done.12, ...), custom_call_target="tpu_custom_call" | custom-call | tf_op jit(solution)/shard_map/pallas_call | solution.py:52
  85.5 4.3 %collective-permute-start.12 = (bf16[512,128]{1,0:T(8,128)(2,1)S(1)}, bf16[512,128]{1,0:T(8,128)(2,1)S(1)}, u32[]{:S(2)}, u32[]{:S(2)}) collective-permute-start(bf16[512,128]{1,0:T(8,128)(2,1)S(1)} %get-tuple-element.72.mine_ref), channel_id=1, source_target_pairs={{0,1},{1,0},{2,3},{3,2},{4,5},{5,4},{6,7},{7,6},{8,9},{9,8},{10,11... | collective-permute-start | bytes 393224 | tf_op jit(solution)/shard_map/ppermute | solution.py:707
  89.8 2.9 %collective-permute-done.12.theirs_ref = bf16[512,128]{1,0:T(8,128)(2,1)S(1)} collective-permute-done((bf16[512,128]{1,0:T(8,128)(2,1)S(1)}, bf16[512,128]{1,0:T(8,128)(2,1)S(1)}, u32[]{:S(2)}, u32[]{:S(2)}) %collective-permute-start.12) | collective-permute-done | bytes 131104 | tf_op jit(solution)/shard_map/ppermute | solution.py:707
  92.8 2.7 %collective-permute-start.13 = (bf16[512,128]{1,0:T(8,128)(2,1)S(1)}, bf16[512,128]{1,0:T(8,128)(2,1)S(1)}, u32[]{:S(2)}, u32[]{:S(2)}) collective-permute-start(bf16[512,128]{1,0:T(8,128)(2,1)S(1)} %shard_map.204.mine_ref), channel_id=1, source_target_pairs={{0,2},{1,3},{2,0},{3,1},{4,6},{5,7},{6,4},{7,5},{8,10},{9,11},{10,... | collective-permute-start | bytes 393224 | tf_op jit(solution)/shard_map/ppermute | solution.py:707
  95.5 2.2 %collective-permute-start.10 = (bf16[512,128]{1,0:T(8,128)(2,1)S(1)}, bf16[512,128]{1,0:T(8,128)(2,1)S(1)}, u32[]{:S(2)}, u32[]{:S(2)}) collective-permute-start(bf16[512,128]{1,0:T(8,128)(2,1)S(1)} %get-tuple-element.69), channel_id=1, source_target_pairs={{0,1},{2,3},{4,5},{6,7},{1,0},{3,2},{5,4},{7,6},{8,9},{10,11},{12,... | collective-permute-start | bytes 393224 | tf_op jit(solution)/shard_map/ppermute | solution.py:703
  98.4 4.7 %shard_map.201.rest_0_ = bf16[4096,128]{1,0:T(8,128)(2,1)} custom-call(bf16[4096,128]{1,0:T(8,128)(2,1)S(1)} %get-tuple-element.38.h_ref, bf16[4096,128]{1,0:T(8,128)(2,1)S(1)} %copy-done.6, bf16[896,128]{1,0:T(8,128)(2,1)S(1)} %get-tuple-element.41.weights_ref.matrices_ref, f32[4096,8]{1,0:T(8,128)S(1)} %shard_map.196.after_ref.owners_ref, ...), custom_call_target="tpu_custom_call" | custom-call | tf_op jit(solution)/shard_map/pallas_call | solution.py:52
  103.2 2.3 %collective-permute-start.14 = (bf16[512,128]{1,0:T(8,128)(2,1)S(1)}, bf16[512,128]{1,0:T(8,128)(2,1)S(1)}, u32[]{:S(2)}, u32[]{:S(2)}) collective-permute-start(bf16[512,128]{1,0:T(8,128)(2,1)S(1)} %shard_map.205.mine_ref), channel_id=1, source_target_pairs={{0,4},{1,5},{2,6},{3,7},{4,0},{5,1},{6,2},{7,3},{8,12},{9,13},{10,... | collective-permute-start | bytes 393224 | tf_op jit(solution)/shard_map/ppermute | solution.py:707
  105.5 7.6 %shard_map.203.rest_0_ = bf16[4096,128]{1,0:T(8,128)(2,1)} custom-call(bf16[4096,128]{1,0:T(8,128)(2,1)} %get-tuple-element.67.ups_hbm, bf16[4096,256]{1,0:T(8,128)(2,1)} %get-tuple-element.68.downs_hbm, bf16[512,128]{1,0:T(8,128)(2,1)S(1)} %collective-permute-done.10.first_back_ref, bf16[512,128]{1,0:T(8,128)(2,1)S(1)} %collective-permute-done.11.second_back_ref, ...), custom_call_target="tpu_custom_call" | custom-call | tf_op jit(solution)/shard_map/pallas_call | solution.py:52
  113.7 4.5 %collective-permute-done.15.theirs_ref = bf16[512,128]{1,0:T(8,128)(2,1)S(1)} collective-permute-done((bf16[512,128]{1,0:T(8,128)(2,1)S(1)}, bf16[512,128]{1,0:T(8,128)(2,1)S(1)}, u32[]{:S(2)}, u32[]{:S(2)}) %collective-permute-start.15) | collective-permute-done | bytes 131104 | tf_op jit(solution)/shard_map/ppermute | solution.py:707
  118.3 1.6 %collective-permute-done.16.theirs_ref = f32[640,128]{1,0:T(8,128)S(1)} collective-permute-done((f32[640,128]{1,0:T(8,128)S(1)}, f32[640,128]{1,0:T(8,128)S(1)}, u32[]{:S(2)}, u32[]{:S(2)}) %collective-permute-start.16) | collective-permute-done | bytes 327712 | tf_op jit(solution)/shard_map/ppermute | solution.py:707
  (85 shorter events, 26.8 us)
Async XLA Ops:
  2.9 9.3 %collective-permute-start.1 = (bf16[512,128]{1,0:T(8,128)(2,1)S(1)}, bf16[512,128]{1,0:T(8,128)(2,1)S(1)}, u32[]{:S(2)}, u32[]{:S(2)}) collective-permute-start(bf16[512,128]{1,0:T(8,128)(2,1)S(1)} %get-tuple-element.40), channel_id=1, source_target_pairs={{1,2},{3,4},{5,6},{2,1},{4,3},{6,5},{9,10},{11,12},{13,14},{10,9},... | collective-permute-start | bytes 393224 | tf_op jit(solution)/shard_map/ppermute | solution.py:703
  3.6 10.6 %collective-permute-start = (bf16[512,128]{1,0:T(8,128)(2,1)S(1)}, bf16[512,128]{1,0:T(8,128)(2,1)S(1)}, u32[]{:S(2)}, u32[]{:S(2)}) collective-permute-start(bf16[512,128]{1,0:T(8,128)(2,1)S(1)} %get-tuple-element.39.rest_7_), channel_id=1, source_target_pairs={{0,1},{2,3},{4,5},{6,7},{1,0},{3,2},{5,4},{7,6},{8,9},{10,11},{12,... | collective-permute-start | bytes 393224 | tf_op jit(solution)/shard_map/ppermute | solution.py:703
  12.2 18.3 %copy-start.21 = (f32[8,4096]{1,0:T(8,128)}, f32[8,4096]{1,0:T(8,128)S(1)}, u32[]{:S(2)}) copy-start(f32[8,4096]{1,0:T(8,128)S(1)} %get-tuple-element.63.columns_ref) | copy-start | bytes 393220
  12.2 19.8 %copy-start.2 = (bf16[4096,128]{1,0:T(8,128)(2,1)}, bf16[4096,128]{1,0:T(8,128)(2,1)S(1)}, u32[]{:S(2)}) copy-start(bf16[4096,128]{1,0:T(8,128)(2,1)S(1)} %get-tuple-element.47.g_ref) | copy-start | bytes 3145732
  12.2 26.8 %copy-start.27 = (s32[1,128]{1,0:T(1,128)}, s32[1,128]{1,0:T(1,128)S(1)}, u32[]{:S(2)}) copy-start(s32[1,128]{1,0:T(1,128)S(1)} %get-tuple-element.48.sends_ref) | copy-start | bytes 1540
  14.2 16.2 %copy-start.11 = (bf16[512,128]{1,0:T(8,128)(2,1)}, bf16[512,128]{1,0:T(8,128)(2,1)S(1)}, u32[]{:S(2)}) copy-start(bf16[512,128]{1,0:T(8,128)(2,1)S(1)} %collective-permute-done.first_ref) | copy-start | bytes 393220
  28.8 1.5 %collective-permute-start.2 = (bf16[1040,128]{1,0:T(8,128)(2,1)S(1)}, bf16[1040,128]{1,0:T(8,128)(2,1)S(1)}, u32[]{:S(2)}, u32[]{:S(2)}) collective-permute-start(bf16[1040,128]{1,0:T(8,128)(2,1)S(1)} %get-tuple-element.46.after_ref), channel_id=1, source_target_pairs={{0,8},{8,0},{16,24},{24,16},{1,9},{9,1},{17,25},{25,17},{2,10},{10... | collective-permute-start | bytes 798728 | tf_op jit(solution)/shard_map/ppermute | solution.py:707
  30.5 8.5 %collective-permute-start.3 = (bf16[1040,128]{1,0:T(8,128)(2,1)S(1)}, bf16[1040,128]{1,0:T(8,128)(2,1)S(1)}, u32[]{:S(2)}, u32[]{:S(2)}) collective-permute-start(bf16[1040,128]{1,0:T(8,128)(2,1)S(1)} %add_convert_fusion.after_ref.totals_ref), channel_id=1, source_target_pairs={{0,16},{8,24},{16,0},{24,8},{1,17},{9,25},{17,1},{25,9},{2,18},{10... | collective-permute-start | bytes 798728 | tf_op jit(solution)/shard_map/ppermute | solution.py:707
  34.8 1.6 %collective-permute-start.4 = (bf16[1024,128]{1,0:T(8,128)(2,1)S(1)}, bf16[1024,128]{1,0:T(8,128)(2,1)S(1)}, u32[]{:S(2)}, u32[]{:S(2)}) collective-permute-start(bf16[1024,128]{1,0:T(8,128)(2,1)S(1)} %shard_map.197.sums_ref), channel_id=1, source_target_pairs={{0,8},{8,0},{16,24},{24,16},{1,9},{9,1},{17,25},{25,17},{2,10},{10... | collective-permute-start | bytes 786440 | tf_op jit(solution)/shard_map/ppermute | solution.py:707
  40.2 11.6 %copy-start.9 = (bf16[1024,128]{1,0:T(8,128)(2,1)}, bf16[1024,128]{1,0:T(8,128)(2,1)S(1)}, u32[]{:S(2)}) copy-start(bf16[1024,128]{1,0:T(8,128)(2,1)S(1)} %get-tuple-element.49.cin_ref) | copy-start | bytes 786436
  40.2 7.5 %collective-permute-start.7 = (bf16[1024,128]{1,0:T(8,128)(2,1)S(1)}, bf16[1024,128]{1,0:T(8,128)(2,1)S(1)}, u32[]{:S(2)}, u32[]{:S(2)}) collective-permute-start(bf16[1024,128]{1,0:T(8,128)(2,1)S(1)} %get-tuple-element.52.chip_sums_ref), channel_id=1, source_target_pairs={{0,16},{8,24},{16,0},{24,8},{1,17},{9,25},{17,1},{25,9},{2,18},{10... | collective-permute-start | bytes 786440 | tf_op jit(solution)/shard_map/ppermute | solution.py:707
  41.7 4.2 %collective-permute-start.5 = (bf16[64,128]{1,0:T(8,128)(2,1)S(1)}, bf16[64,128]{1,0:T(8,128)(2,1)S(1)}, u32[]{:S(2)}, u32[]{:S(2)}) collective-permute-start(bf16[64,128]{1,0:T(8,128)(2,1)S(1)} %get-tuple-element.50), channel_id=1, source_target_pairs={{0,1},{2,3},{4,5},{6,7},{1,0},{3,2},{5,4},{7,6},{8,9},{10,11},{12,... | collective-permute-start | bytes 49160 | tf_op jit(solution)/shard_map/ppermute | solution.py:703
  44.2 1.7 %collective-permute-start.6 = (bf16[64,128]{1,0:T(8,128)(2,1)S(1)}, bf16[64,128]{1,0:T(8,128)(2,1)S(1)}, u32[]{:S(2)}, u32[]{:S(2)}) collective-permute-start(bf16[64,128]{1,0:T(8,128)(2,1)S(1)} %get-tuple-element.51), channel_id=1, source_target_pairs={{1,2},{3,4},{5,6},{2,1},{4,3},{6,5},{9,10},{11,12},{13,14},{10,9},... | collective-permute-start | bytes 49160 | tf_op jit(solution)/shard_map/ppermute | solution.py:703
  55.5 10.7 %collective-permute-start.8 = (bf16[64,128]{1,0:T(8,128)(2,1)}, bf16[64,128]{1,0:T(8,128)(2,1)S(1)}, u32[]{:S(2)}, u32[]{:S(2)}) collective-permute-start(bf16[64,128]{1,0:T(8,128)(2,1)} %get-tuple-element.56.first_grad_ref), channel_id=1, source_target_pairs={{0,1},{2,3},{4,5},{6,7},{1,0},{3,2},{5,4},{7,6},{8,9},{10,11},{12,... | collective-permute-start | bytes 49160 | tf_op jit(solution)/shard_map/ppermute | solution.py:703
  58.6 7.6 %collective-permute-start.9 = (bf16[64,128]{1,0:T(8,128)(2,1)}, bf16[64,128]{1,0:T(8,128)(2,1)}, u32[]{:S(2)}, u32[]{:S(2)}) collective-permute-start(bf16[64,128]{1,0:T(8,128)(2,1)} %get-tuple-element.57.second_grad_ref), channel_id=1, source_target_pairs={{1,2},{3,4},{5,6},{2,1},{4,3},{6,5},{9,10},{11,12},{13,14},{10,9},... | collective-permute-start | bytes 49160 | tf_op jit(solution)/shard_map/ppermute | solution.py:703
  74.0 24.4 %copy-start.6 = (bf16[4096,128]{1,0:T(8,128)(2,1)S(1)}, bf16[4096,128]{1,0:T(8,128)(2,1)}, u32[]{:S(2)}) copy-start(bf16[4096,128]{1,0:T(8,128)(2,1)} %copy-done.4) | copy-start | bytes 3145732
  85.5 7.3 %collective-permute-start.12 = (bf16[512,128]{1,0:T(8,128)(2,1)S(1)}, bf16[512,128]{1,0:T(8,128)(2,1)S(1)}, u32[]{:S(2)}, u32[]{:S(2)}) collective-permute-start(bf16[512,128]{1,0:T(8,128)(2,1)S(1)} %get-tuple-element.72.mine_ref), channel_id=1, source_target_pairs={{0,1},{1,0},{2,3},{3,2},{4,5},{5,4},{6,7},{7,6},{8,9},{9,8},{10,11... | collective-permute-start | bytes 393224 | tf_op jit(solution)/shard_map/ppermute | solution.py:707
  92.8 10.3 %collective-permute-start.13 = (bf16[512,128]{1,0:T(8,128)(2,1)S(1)}, bf16[512,128]{1,0:T(8,128)(2,1)S(1)}, u32[]{:S(2)}, u32[]{:S(2)}) collective-permute-start(bf16[512,128]{1,0:T(8,128)(2,1)S(1)} %shard_map.204.mine_ref), channel_id=1, source_target_pairs={{0,2},{1,3},{2,0},{3,1},{4,6},{5,7},{6,4},{7,5},{8,10},{9,11},{10,... | collective-permute-start | bytes 393224 | tf_op jit(solution)/shard_map/ppermute | solution.py:707
  95.5 10.0 %collective-permute-start.10 = (bf16[512,128]{1,0:T(8,128)(2,1)S(1)}, bf16[512,128]{1,0:T(8,128)(2,1)S(1)}, u32[]{:S(2)}, u32[]{:S(2)}) collective-permute-start(bf16[512,128]{1,0:T(8,128)(2,1)S(1)} %get-tuple-element.69), channel_id=1, source_target_pairs={{0,1},{2,3},{4,5},{6,7},{1,0},{3,2},{5,4},{7,6},{8,9},{10,11},{12,... | collective-permute-start | bytes 393224 | tf_op jit(solution)/shard_map/ppermute | solution.py:703
  97.7 7.8 %collective-permute-start.11 = (bf16[512,128]{1,0:T(8,128)(2,1)S(1)}, bf16[512,128]{1,0:T(8,128)(2,1)S(1)}, u32[]{:S(2)}, u32[]{:S(2)}) collective-permute-start(bf16[512,128]{1,0:T(8,128)(2,1)S(1)} %get-tuple-element.70), channel_id=1, source_target_pairs={{1,2},{3,4},{5,6},{2,1},{4,3},{6,5},{9,10},{11,12},{13,14},{10,9},... | collective-permute-start | bytes 393224 | tf_op jit(solution)/shard_map/ppermute | solution.py:703
  98.4 7.1 %copy-start.26 = (s32[1,1024]{1,0:T(1,128)S(1)}, s32[1,1024]{1,0:T(1,128)}, u32[]{:S(2)}) copy-start(s32[1,1024]{1,0:T(1,128)} %copy-done.25) | copy-start | bytes 12292
  103.2 9.9 %collective-permute-start.14 = (bf16[512,128]{1,0:T(8,128)(2,1)S(1)}, bf16[512,128]{1,0:T(8,128)(2,1)S(1)}, u32[]{:S(2)}, u32[]{:S(2)}) collective-permute-start(bf16[512,128]{1,0:T(8,128)(2,1)S(1)} %shard_map.205.mine_ref), channel_id=1, source_target_pairs={{0,4},{1,5},{2,6},{3,7},{4,0},{5,1},{6,2},{7,3},{8,12},{9,13},{10,... | collective-permute-start | bytes 393224 | tf_op jit(solution)/shard_map/ppermute | solution.py:707
  113.2 5.0 %collective-permute-start.15 = (bf16[512,128]{1,0:T(8,128)(2,1)S(1)}, bf16[512,128]{1,0:T(8,128)(2,1)S(1)}, u32[]{:S(2)}, u32[]{:S(2)}) collective-permute-start(bf16[512,128]{1,0:T(8,128)(2,1)S(1)} %shard_map.206.mine_ref), channel_id=1, source_target_pairs={{0,16},{8,24},{16,0},{24,8},{1,17},{9,25},{17,1},{25,9},{2,18},{10... | collective-permute-start | bytes 393224 | tf_op jit(solution)/shard_map/ppermute | solution.py:707
  118.2 1.7 %collective-permute-start.16 = (f32[640,128]{1,0:T(8,128)S(1)}, f32[640,128]{1,0:T(8,128)S(1)}, u32[]{:S(2)}, u32[]{:S(2)}) collective-permute-start(f32[640,128]{1,0:T(8,128)S(1)} %shard_map.207.mine_ref), channel_id=1, source_target_pairs={{0,8},{8,0},{16,24},{24,16},{1,9},{9,1},{17,25},{25,17},{2,10},{10... | collective-permute-start | bytes 983048 | tf_op jit(solution)/shard_map/ppermute | solution.py:707
  (22 other events, 34.7 us)

commit v6 on v5

--- a/solution.py
+++ b/solution.py
@@ -11,15 +11,15 @@
 bf16 = jnp.bfloat16
 BLOCK = 64
 PAIR = 2 * BLOCK
-STEP = 8
-CHUNK = 512
+STEP = 16
+CHUNK = 1024
 NEVER = -1e30
 DIGIT = 64.0
 VMEM = pl.BlockSpec(memory_space=pltpu.VMEM)
 SMEM = pl.BlockSpec(memory_space=pltpu.SMEM)
 ANY = pl.BlockSpec(memory_space=pl.ANY)
 HBM = pl.BlockSpec(memory_space=pltpu.HBM)
-PARAMS = pltpu.CompilerParams(vmem_limit_bytes=32 * 1024 * 1024)
+MIB = 1024 * 1024
 
 
 def dot(a, b):
@@ -42,7 +42,7 @@
     return jnp.where(values == places, jnp.ones((), bf16), jnp.zeros((), bf16))
 
 
-def call(kernel, out_shape, args, in_specs=None, scratch=(), out_specs=None):
+def call(kernel, out_shape, args, in_specs=None, scratch=(), out_specs=None, mib=16):
     many = isinstance(out_shape, (list, tuple))
     in_specs = in_specs or [VMEM] * len(args)
     args = [
@@ -55,7 +55,7 @@
         in_specs=in_specs,
         out_specs=out_specs or ([VMEM] * len(out_shape) if many else VMEM),
         scratch_shapes=list(scratch),
-        compiler_params=PARAMS,
+        compiler_params=pltpu.CompilerParams(vmem_limit_bytes=mib * MIB),
     )(*args)
 
 
@@ -346,12 +346,14 @@
     owner_ref,
     counts_ref,
     summed_ref,
-    slope_ref,
+    slope_hbm,
     totals_ref,
     own,
     far,
     halo,
     new,
+    slope_ref,
+    sem,
 ):
     self_weight, other_weight = matrix(weights_ref, 0), matrix(weights_ref, 1)
     level_terms(h_ref, (first_ref, second_ref), self_weight, other_weight, own, far, halo)
@@ -360,7 +362,9 @@
         here = chunk_of(index, STEP * BLOCK)
         total, slopes = edges(own[here, :], far[here, :], columns_t_ref[here, :], halo)
         summed_ref[here, :] = total
-        slope_ref[chunk_of(index, 8 * STEP * BLOCK), :] = jnp.concatenate(slopes, 0)
+        edge = chunk_of(index, 8 * STEP * BLOCK)
+        slope_ref[edge, :] = jnp.concatenate(slopes, 0)
+        pltpu.make_async_copy(slope_ref.at[edge, :], slope_hbm.at[edge, :], sem).start()
         return carry
 
     lax.fori_loop(0, h_ref.shape[0] // (STEP * BLOCK), step, None)
@@ -375,6 +379,7 @@
 
     lax.fori_loop(0, coarse_rows // 256, tile_step, None)
     totals_ref[coarse_rows:, :] = counts_ref[...]
+    pltpu.make_async_copy(slope_ref, slope_hbm, sem).wait()
 
 
 def coarse_input_kernel(
@@ -529,7 +534,7 @@
     second_ref,
     g_ref,
     summed_ref,
-    slope_ref,
+    slope_hbm,
     matrices_ref,
     columns_ref,
     owners_ref,
@@ -550,8 +555,21 @@
     grad_sum,
     halo_grad,
     mean,
+    slope_ref,
+    slope_sems,
     sems,
 ):
+    count = STEP * BLOCK
+    steps = h_ref.shape[0] // count
+
+    def slope_copy(index):
+        edge = chunk_of(index, 8 * count)
+        return pltpu.make_async_copy(
+            slope_hbm.at[edge, :], slope_ref.at[edge, :], slope_sems.at[index]
+        )
+
+    for index in range(steps):
+        slope_copy(index).start()
     halo_rows = first_ref.shape[0]
     coarse_rows = part_ref.shape[0]
     halo_grad[...] = jnp.zeros_like(halo_grad)
@@ -567,9 +585,6 @@
         here = slice(tile * 128, (tile + 1) * 128)
         mean[here, :] = (grad_in[here, :] / per_row[:, tile : tile + 1]).astype(bf16)
 
-    count = STEP * BLOCK
-    steps = h_ref.shape[0] // count
-
     def owner_step(index):
         here = chunk_of(index, count)
         grad_up = g_ref[here, :].astype(f32) + owner_rows(owners_ref[here, :], mean[...])
@@ -579,6 +594,7 @@
 
     def edge_step(index):
         here = chunk_of(index, count)
+        slope_copy(index).wait()
         slope = slope_ref[chunk_of(index, 8 * count), :]
         slopes = [slope[n * 8 * BLOCK : (n + 1) * 8 * BLOCK] for n in range(STEP)]
         downs_ref[here, :] = edges_back(
@@ -802,7 +818,7 @@
         fine_forward_kernel,
         [
             shape(rows, features, bf16),
-            shape(8 * rows, features, bf16),
+            pltpu.HBM((8 * rows, features), bf16),
             shape(coarse_rows + 2 * count_rows, features, bf16),
         ],
         [states, first, second, matrices, columns_t, owner, counts],
@@ -811,7 +827,11 @@
             buffer(rows, features, bf16),
             buffer(2 * halo_rows, features, bf16),
             buffer(rows, features, bf16),
-        ],
+            buffer(8 * rows, features, bf16),
+            pltpu.SemaphoreType.DMA,
+        ],
+        out_specs=[VMEM, HBM, VMEM],
+        mib=32,
     )
     chip_totals = (totals.astype(f32) + swapped(totals, "grp", 1).astype(f32)).astype(bf16)
     more_totals = swapped(chip_totals, "grp", 2)
@@ -895,15 +915,19 @@
             coarse_part, counts, coarse_downs, first_back, second_back, coarse_sends,
             coarse_weights,
         ],
-        scratch=[
+        [VMEM] * 5 + [HBM] + [VMEM] * 10,
+        [
             buffer(rows, features, bf16),
             buffer(rows, 2 * features, bf16),
             buffer(rows, features, bf16),
             buffer(2 * halo_rows, features, f32),
             buffer(coarse_rows, features, bf16),
+            buffer(8 * rows, features, bf16),
+            pltpu.SemaphoreType.DMA((rows // (STEP * BLOCK),)),
             pltpu.SemaphoreType.DMA((2,)),
         ],
         out_specs=[HBM, HBM, VMEM, VMEM, VMEM],
+        mib=32,
     )
     first_back, second_back = exchange(first_grad, second_grad)
 

time: 122 us -> 113 us (0.926)
  local copies, waits for them, and re-layouts: 20.9 us -> 15.2 us
  Pallas kernels: 50 us -> 46.3 us
    unnamed x58 -> x54, local copies, waits for them, and re-layouts: 20.9 us -> 15.2 us
    pallas_call x16, Pallas kernels: 50 us -> 46.3 us  [call(): pl.pallas_call(kernel, out_shape=out_shape, in_specs=in_specs, out_specs=...]
  transfers between devices with their start and end apart: 17 -> 17, of which waited for: 9 -> 9; matrix products, arithmetic and copies ran while one was open for 0% -> 0% of each run, Pallas kernels for 16% -> 15%
where the time goes in v6:
time: 113 us; the launch traced here: 111 us
  Pallas kernels  46.3 us (41%)
  starting transfers between devices  30 us (27%)
  waiting for transfers between devices  18.9 us (17%)
  local copies, waits for them, and re-layouts  15.2 us (13%)
    pallas_call x16, Pallas kernels, call(): pl.pallas_call(kernel, out_shape=out_shape, in_specs=in_specs, out_specs=...  46.3 us
    ppermute x9, waiting for transfers between devices, swapped(): lax.ppermute(block, axis, [(i, i ^ distance) for i in range(lax.axis_size...  15.8 us
    unnamed x54, local copies, waits for them, and re-layouts  15.2 us
    ppermute x4, starting transfers between devices, exchange(): lax.ppermute(first, 'sub', routes[0])  13.6 us
    ppermute x9, starting transfers between devices, swapped(): lax.ppermute(block, axis, [(i, i ^ distance) for i in range(lax.axis_size...  13.2 us
    ppermute x4, starting transfers between devices, exchange(): lax.ppermute(second, 'sub', routes[1])  3.23 us
    ppermute x4, waiting for transfers between devices, exchange(): lax.ppermute(first, 'sub', routes[0])  3.09 us
  transfers between devices with their start and end apart: 17, of which 9 were waited for; matrix products, arithmetic and copies ran while one was open for 0% of the time, Pallas kernels for 15%

profile of v6, /device:TPU:0, one launch (start us, length us, event | category | flops | bytes accessed | tf_op | source)
XLA Modules:
  0.0 111.4 jit_solution(3486158972226360878)
XLA Ops:
  0.6 2.3 %shard_map.193 = (bf16[512,128]{1,0:T(8,128)(2,1)S(1)}, bf16[512,128]{1,0:T(8,128)(2,1)S(1)}, bf16[4096,128]{1,0:T(8,128)(2,1)S(1)}) custom-call(s32[1]{0:T(128)} %bitcast.even_ref, s32[512]{0:T(512)} %lo_hbm.1, s32[512]{0:T(512)} %hi_hbm.1, bf16[4096,128]{1,0:T(8,128)(2,1)} %x_hbm.1), custom_call_target="tpu_custom_call" | custom-call | tf_op jit(solution)/shard_map/pallas_call | solution.py:52
  3.6 5.8 %collective-permute-start = (bf16[512,128]{1,0:T(8,128)(2,1)S(1)}, bf16[512,128]{1,0:T(8,128)(2,1)S(1)}, u32[]{:S(2)}, u32[]{:S(2)}) collective-permute-start(bf16[512,128]{1,0:T(8,128)(2,1)S(1)} %get-tuple-element.39.rest_7_), channel_id=1, source_target_pairs={{0,1},{2,3},{4,5},{6,7},{1,0},{3,2},{5,4},{7,6},{8,9},{10,11},{12,... | collective-permute-start | bytes 393224 | tf_op jit(solution)/shard_map/ppermute | solution.py:719
  9.4 2.2 %shard_map.194 = (bf16[16,128]{1,0:T(8,128)(2,1)S(1)}, f32[8,4096]{1,0:T(8,128)S(1)}, f32[4096,8]{1,0:T(8,128)S(1)}, f32[8,1024]{1,0:T(8,128)S(1)}, f32[1024,8]{...) custom-call(s32[1]{0:T(128)} %bitcast.even_ref, ...), custom_call_target="tpu_custom_call" | custom-call | tf_op jit(solution)/shard_map/pallas_call | solution.py:52
  12.2 2.0 %collective-permute-done.first_ref = bf16[512,128]{1,0:T(8,128)(2,1)S(1)} collective-permute-done((bf16[512,128]{1,0:T(8,128)(2,1)S(1)}, bf16[512,128]{1,0:T(8,128)(2,1)S(1)}, u32[]{:S(2)}, u32[]{:S(2)}) %collective-permute-start) | collective-permute-done | bytes 131104 | tf_op jit(solution)/shard_map/ppermute | solution.py:719
  14.2 10.7 %shard_map.195 = (bf16[4096,128]{1,0:T(8,128)(2,1)S(1)}, bf16[32768,128]{1,0:T(8,128)(2,1)}, bf16[1040,128]{1,0:T(8,128)(2,1)S(1)}) custom-call(bf16[4096,128]{1,0:T(8,128)(2,1)S(1)} %get-tuple-element.38.h_ref, bf16[512,128]{1,0:T(8,128)(2,1)S(1)} %collective-permute-done.first_ref, bf16[512,128]{1,0:T(8,128)(2,1)S(1)} %collective-permute-done.1.second_ref, ...), custom_call_target="tpu_custom_call" | custom-call | tf_op jit(solution)/shard_map/pallas_call | solution.py:52
  25.1 1.5 %collective-permute-done.2 = bf16[1040,128]{1,0:T(8,128)(2,1)S(1)} collective-permute-done((bf16[1040,128]{1,0:T(8,128)(2,1)S(1)}, bf16[1040,128]{1,0:T(8,128)(2,1)S(1)}, u32[]{:S(2)}, u32[]{:S(2)}) %collective-permute-start.2) | collective-permute-done | bytes 266272 | tf_op jit(solution)/shard_map/ppermute | solution.py:723
  26.7 1.6 %collective-permute-start.3 = (bf16[1040,128]{1,0:T(8,128)(2,1)S(1)}, bf16[1040,128]{1,0:T(8,128)(2,1)S(1)}, u32[]{:S(2)}, u32[]{:S(2)}) collective-permute-start(bf16[1040,128]{1,0:T(8,128)(2,1)S(1)} %add_convert_fusion.after_ref.totals_ref), channel_id=1, source_target_pairs={{0,16},{8,24},{16,0},{24,8},{1,17},{9,25},{17,1},{25,9},{2,18},{10... | collective-permute-start | bytes 798728 | tf_op jit(solution)/shard_map/ppermute | solution.py:723
  28.2 2.8 %shard_map.197.sums_ref = bf16[1024,128]{1,0:T(8,128)(2,1)S(1)} custom-call(s32[32,128]{1,0:T(8,128)S(1)} %get-tuple-element.43.owner_ref, bf16[4096,128]{1,0:T(8,128)(2,1)S(1)} %get-tuple-element.47.g_ref, bf16[1040,128]{1,0:T(8,128)(2,1)S(1)} %get-tuple-element.46.after_ref), custom_call_target="tpu_custom_call" | custom-call | tf_op jit(solution)/shard_map/pallas_call | solution.py:52
  32.6 2.5 %collective-permute-done.3.more_totals_ref = bf16[1040,128]{1,0:T(8,128)(2,1)S(1)} collective-permute-done((bf16[1040,128]{1,0:T(8,128)(2,1)S(1)}, bf16[1040,128]{1,0:T(8,128)(2,1)S(1)}, u32[]{:S(2)}, u32[]{:S(2)}) %collective-permute-start.3) | collective-permute-done | bytes 266272 | tf_op jit(solution)/shard_map/ppermute | solution.py:723
  36.4 1.5 %collective-permute-start.7 = (bf16[1024,128]{1,0:T(8,128)(2,1)S(1)}, bf16[1024,128]{1,0:T(8,128)(2,1)S(1)}, u32[]{:S(2)}, u32[]{:S(2)}) collective-permute-start(bf16[1024,128]{1,0:T(8,128)(2,1)S(1)} %get-tuple-element.52.chip_sums_ref), channel_id=1, source_target_pairs={{0,16},{8,24},{16,0},{24,8},{1,17},{9,25},{17,1},{25,9},{2,18},{10... | collective-permute-start | bytes 786440 | tf_op jit(solution)/shard_map/ppermute | solution.py:723
  37.9 2.5 %collective-permute-start.5 = (bf16[64,128]{1,0:T(8,128)(2,1)S(1)}, bf16[64,128]{1,0:T(8,128)(2,1)S(1)}, u32[]{:S(2)}, u32[]{:S(2)}) collective-permute-start(bf16[64,128]{1,0:T(8,128)(2,1)S(1)} %get-tuple-element.50), channel_id=1, source_target_pairs={{0,1},{2,3},{4,5},{6,7},{1,0},{3,2},{5,4},{7,6},{8,9},{10,11},{12,... | collective-permute-start | bytes 49160 | tf_op jit(solution)/shard_map/ppermute | solution.py:719
  42.1 1.8 %collective-permute-done.7.more_sums_ref = bf16[1024,128]{1,0:T(8,128)(2,1)S(1)} collective-permute-done((bf16[1024,128]{1,0:T(8,128)(2,1)S(1)}, bf16[1024,128]{1,0:T(8,128)(2,1)S(1)}, u32[]{:S(2)}, u32[]{:S(2)}) %collective-permute-start.7) | collective-permute-done | bytes 262176 | tf_op jit(solution)/shard_map/ppermute | solution.py:723
  43.9 3.5 %shard_map.199 = (f32[1024,128]{1,0:T(8,128)S(1)}, bf16[64,128]{1,0:T(8,128)(2,1)}, bf16[64,128]{1,0:T(8,128)(2,1)}, bf16[1024,128]{1,0:T(8,128)(2,1)S(1)}, bf16...) custom-call(bf16[1024,128]{1,0:T(8,128)(2,1)S(1)} %get-tuple-element.49.cin_ref, ...), custom_call_target="tpu_custom_call" | custom-call | tf_op jit(solution)/shard_map/pallas_call | solution.py:52
  51.2 3.1 %collective-permute-start.8 = (bf16[64,128]{1,0:T(8,128)(2,1)}, bf16[64,128]{1,0:T(8,128)(2,1)S(1)}, u32[]{:S(2)}, u32[]{:S(2)}) collective-permute-start(bf16[64,128]{1,0:T(8,128)(2,1)} %get-tuple-element.56.first_grad_ref), channel_id=1, source_target_pairs={{0,1},{2,3},{4,5},{6,7},{1,0},{3,2},{5,4},{7,6},{8,9},{10,11},{12,... | collective-permute-start | bytes 49160 | tf_op jit(solution)/shard_map/ppermute | solution.py:719
  67.3 11.2 %shard_map.202 = (bf16[4096,128]{1,0:T(8,128)(2,1)}, bf16[4096,256]{1,0:T(8,128)(2,1)}, bf16[512,128]{1,0:T(8,128)(2,1)S(1)}, bf16[512,128]{1,0:T(8,128)(2,1)S(1)}, bf16[512,128]{1,0:T(8,128)(2,1)S(1)}) custom-call(bf16[4096,128]{1,0:T(8,128)(2,1)S(1)} %get-tuple-element.38.h_ref, bf16[512,128]{1,0:T(8,128)(2,1)S(1)} %copy-done.10, ...), custom_call_target="tpu_custom_call" | custom-call | tf_op jit(solution)/shard_map/pallas_call | solution.py:52
  78.5 4.3 %collective-permute-start.12 = (bf16[512,128]{1,0:T(8,128)(2,1)S(1)}, bf16[512,128]{1,0:T(8,128)(2,1)S(1)}, u32[]{:S(2)}, u32[]{:S(2)}) collective-permute-start(bf16[512,128]{1,0:T(8,128)(2,1)S(1)} %get-tuple-element.72.mine_ref), channel_id=1, source_target_pairs={{0,1},{1,0},{2,3},{3,2},{4,5},{5,4},{6,7},{7,6},{8,9},{9,8},{10,11... | collective-permute-start | bytes 393224 | tf_op jit(solution)/shard_map/ppermute | solution.py:723
  82.8 2.9 %collective-permute-done.12.theirs_ref = bf16[512,128]{1,0:T(8,128)(2,1)S(1)} collective-permute-done((bf16[512,128]{1,0:T(8,128)(2,1)S(1)}, bf16[512,128]{1,0:T(8,128)(2,1)S(1)}, u32[]{:S(2)}, u32[]{:S(2)}) %collective-permute-start.12) | collective-permute-done | bytes 131104 | tf_op jit(solution)/shard_map/ppermute | solution.py:723
  85.8 2.7 %collective-permute-start.13 = (bf16[512,128]{1,0:T(8,128)(2,1)S(1)}, bf16[512,128]{1,0:T(8,128)(2,1)S(1)}, u32[]{:S(2)}, u32[]{:S(2)}) collective-permute-start(bf16[512,128]{1,0:T(8,128)(2,1)S(1)} %shard_map.204.mine_ref), channel_id=1, source_target_pairs={{0,2},{1,3},{2,0},{3,1},{4,6},{5,7},{6,4},{7,5},{8,10},{9,11},{10,... | collective-permute-start | bytes 393224 | tf_op jit(solution)/shard_map/ppermute | solution.py:723
  88.5 2.2 %collective-permute-start.10 = (bf16[512,128]{1,0:T(8,128)(2,1)S(1)}, bf16[512,128]{1,0:T(8,128)(2,1)S(1)}, u32[]{:S(2)}, u32[]{:S(2)}) collective-permute-start(bf16[512,128]{1,0:T(8,128)(2,1)S(1)} %get-tuple-element.69), channel_id=1, source_target_pairs={{0,1},{2,3},{4,5},{6,7},{1,0},{3,2},{5,4},{7,6},{8,9},{10,11},{12,... | collective-permute-start | bytes 393224 | tf_op jit(solution)/shard_map/ppermute | solution.py:719
  91.4 3.9 %shard_map.201.rest_0_ = bf16[4096,128]{1,0:T(8,128)(2,1)} custom-call(bf16[4096,128]{1,0:T(8,128)(2,1)S(1)} %get-tuple-element.38.h_ref, bf16[4096,128]{1,0:T(8,128)(2,1)S(1)} %copy-done.3, bf16[896,128]{1,0:T(8,128)(2,1)S(1)} %get-tuple-element.41.weights_ref.matrices_ref, f32[4096,8]{1,0:T(8,128)S(1)} %shard_map.196.after_ref.owners_ref, ...), custom_call_target="tpu_custom_call" | custom-call | tf_op jit(solution)/shard_map/pallas_call | solution.py:52
  95.4 2.3 %collective-permute-start.14 = (bf16[512,128]{1,0:T(8,128)(2,1)S(1)}, bf16[512,128]{1,0:T(8,128)(2,1)S(1)}, u32[]{:S(2)}, u32[]{:S(2)}) collective-permute-start(bf16[512,128]{1,0:T(8,128)(2,1)S(1)} %shard_map.205.mine_ref), channel_id=1, source_target_pairs={{0,4},{1,5},{2,6},{3,7},{4,0},{5,1},{6,2},{7,3},{8,12},{9,13},{10,... | collective-permute-start | bytes 393224 | tf_op jit(solution)/shard_map/ppermute | solution.py:723
  97.7 6.1 %shard_map.203.rest_0_ = bf16[4096,128]{1,0:T(8,128)(2,1)} custom-call(bf16[4096,128]{1,0:T(8,128)(2,1)} %get-tuple-element.67.ups_hbm, bf16[4096,256]{1,0:T(8,128)(2,1)} %get-tuple-element.68.downs_hbm, bf16[512,128]{1,0:T(8,128)(2,1)S(1)} %collective-permute-done.10.first_back_ref, bf16[512,128]{1,0:T(8,128)(2,1)S(1)} %collective-permute-done.11.second_back_ref, ...), custom_call_target="tpu_custom_call" | custom-call | tf_op jit(solution)/shard_map/pallas_call | solution.py:52
  104.4 4.5 %collective-permute-done.15.theirs_ref = bf16[512,128]{1,0:T(8,128)(2,1)S(1)} collective-permute-done((bf16[512,128]{1,0:T(8,128)(2,1)S(1)}, bf16[512,128]{1,0:T(8,128)(2,1)S(1)}, u32[]{:S(2)}, u32[]{:S(2)}) %collective-permute-start.15) | collective-permute-done | bytes 131104 | tf_op jit(solution)/shard_map/ppermute | solution.py:723
  109.0 1.6 %collective-permute-done.16.theirs_ref = f32[640,128]{1,0:T(8,128)S(1)} collective-permute-done((f32[640,128]{1,0:T(8,128)S(1)}, f32[640,128]{1,0:T(8,128)S(1)}, u32[]{:S(2)}, u32[]{:S(2)}) %collective-permute-start.16) | collective-permute-done | bytes 327712 | tf_op jit(solution)/shard_map/ppermute | solution.py:723
  (81 shorter events, 24.9 us)
Async XLA Ops:
  2.9 9.3 %collective-permute-start.1 = (bf16[512,128]{1,0:T(8,128)(2,1)S(1)}, bf16[512,128]{1,0:T(8,128)(2,1)S(1)}, u32[]{:S(2)}, u32[]{:S(2)}) collective-permute-start(bf16[512,128]{1,0:T(8,128)(2,1)S(1)} %get-tuple-element.40), channel_id=1, source_target_pairs={{1,2},{3,4},{5,6},{2,1},{4,3},{6,5},{9,10},{11,12},{13,14},{10,9},... | collective-permute-start | bytes 393224 | tf_op jit(solution)/shard_map/ppermute | solution.py:719
  3.6 10.6 %collective-permute-start = (bf16[512,128]{1,0:T(8,128)(2,1)S(1)}, bf16[512,128]{1,0:T(8,128)(2,1)S(1)}, u32[]{:S(2)}, u32[]{:S(2)}) collective-permute-start(bf16[512,128]{1,0:T(8,128)(2,1)S(1)} %get-tuple-element.39.rest_7_), channel_id=1, source_target_pairs={{0,1},{2,3},{4,5},{6,7},{1,0},{3,2},{5,4},{7,6},{8,9},{10,11},{12,... | collective-permute-start | bytes 393224 | tf_op jit(solution)/shard_map/ppermute | solution.py:719
  12.2 14.5 %copy-start.19 = (f32[8,4096]{1,0:T(8,128)}, f32[8,4096]{1,0:T(8,128)S(1)}, u32[]{:S(2)}) copy-start(f32[8,4096]{1,0:T(8,128)S(1)} %get-tuple-element.63.columns_ref) | copy-start | bytes 393220
  12.2 16.0 %copy-start = (bf16[4096,128]{1,0:T(8,128)(2,1)}, bf16[4096,128]{1,0:T(8,128)(2,1)S(1)}, u32[]{:S(2)}) copy-start(bf16[4096,128]{1,0:T(8,128)(2,1)S(1)} %get-tuple-element.47.g_ref) | copy-start | bytes 3145732
  12.2 23.0 %copy-start.25 = (s32[1,128]{1,0:T(1,128)}, s32[1,128]{1,0:T(1,128)S(1)}, u32[]{:S(2)}) copy-start(s32[1,128]{1,0:T(1,128)S(1)} %get-tuple-element.48.sends_ref) | copy-start | bytes 1540
  14.2 12.4 %copy-start.9 = (bf16[512,128]{1,0:T(8,128)(2,1)}, bf16[512,128]{1,0:T(8,128)(2,1)S(1)}, u32[]{:S(2)}) copy-start(bf16[512,128]{1,0:T(8,128)(2,1)S(1)} %collective-permute-done.first_ref) | copy-start | bytes 393220
  25.0 6.8 %copy-start.2 = (bf16[4096,128]{1,0:T(8,128)(2,1)}, bf16[4096,128]{1,0:T(8,128)(2,1)S(1)}, u32[]{:S(2)}) copy-start(bf16[4096,128]{1,0:T(8,128)(2,1)S(1)} %get-tuple-element.45.summed_ref) | copy-start | bytes 3145732
  25.0 1.6 %collective-permute-start.2 = (bf16[1040,128]{1,0:T(8,128)(2,1)S(1)}, bf16[1040,128]{1,0:T(8,128)(2,1)S(1)}, u32[]{:S(2)}, u32[]{:S(2)}) collective-permute-start(bf16[1040,128]{1,0:T(8,128)(2,1)S(1)} %get-tuple-element.46.after_ref), channel_id=1, source_target_pairs={{0,8},{8,0},{16,24},{24,16},{1,9},{9,1},{17,25},{25,17},{2,10},{10... | collective-permute-start | bytes 798728 | tf_op jit(solution)/shard_map/ppermute | solution.py:723
  26.7 8.5 %collective-permute-start.3 = (bf16[1040,128]{1,0:T(8,128)(2,1)S(1)}, bf16[1040,128]{1,0:T(8,128)(2,1)S(1)}, u32[]{:S(2)}, u32[]{:S(2)}) collective-permute-start(bf16[1040,128]{1,0:T(8,128)(2,1)S(1)} %add_convert_fusion.after_ref.totals_ref), channel_id=1, source_target_pairs={{0,16},{8,24},{16,0},{24,8},{1,17},{9,25},{17,1},{25,9},{2,18},{10... | collective-permute-start | bytes 798728 | tf_op jit(solution)/shard_map/ppermute | solution.py:723
  31.0 1.6 %collective-permute-start.4 = (bf16[1024,128]{1,0:T(8,128)(2,1)S(1)}, bf16[1024,128]{1,0:T(8,128)(2,1)S(1)}, u32[]{:S(2)}, u32[]{:S(2)}) collective-permute-start(bf16[1024,128]{1,0:T(8,128)(2,1)S(1)} %shard_map.197.sums_ref), channel_id=1, source_target_pairs={{0,8},{8,0},{16,24},{24,16},{1,9},{9,1},{17,25},{25,17},{2,10},{10... | collective-permute-start | bytes 786440 | tf_op jit(solution)/shard_map/ppermute | solution.py:723
  36.4 11.0 %copy-start.7 = (bf16[1024,128]{1,0:T(8,128)(2,1)}, bf16[1024,128]{1,0:T(8,128)(2,1)S(1)}, u32[]{:S(2)}) copy-start(bf16[1024,128]{1,0:T(8,128)(2,1)S(1)} %get-tuple-element.49.cin_ref) | copy-start | bytes 786436
  36.4 7.5 %collective-permute-start.7 = (bf16[1024,128]{1,0:T(8,128)(2,1)S(1)}, bf16[1024,128]{1,0:T(8,128)(2,1)S(1)}, u32[]{:S(2)}, u32[]{:S(2)}) collective-permute-start(bf16[1024,128]{1,0:T(8,128)(2,1)S(1)} %get-tuple-element.52.chip_sums_ref), channel_id=1, source_target_pairs={{0,16},{8,24},{16,0},{24,8},{1,17},{9,25},{17,1},{25,9},{2,18},{10... | collective-permute-start | bytes 786440 | tf_op jit(solution)/shard_map/ppermute | solution.py:723
  37.9 4.2 %collective-permute-start.5 = (bf16[64,128]{1,0:T(8,128)(2,1)S(1)}, bf16[64,128]{1,0:T(8,128)(2,1)S(1)}, u32[]{:S(2)}, u32[]{:S(2)}) collective-permute-start(bf16[64,128]{1,0:T(8,128)(2,1)S(1)} %get-tuple-element.50), channel_id=1, source_target_pairs={{0,1},{2,3},{4,5},{6,7},{1,0},{3,2},{5,4},{7,6},{8,9},{10,11},{12,... | collective-permute-start | bytes 49160 | tf_op jit(solution)/shard_map/ppermute | solution.py:719
  40.4 1.7 %collective-permute-start.6 = (bf16[64,128]{1,0:T(8,128)(2,1)S(1)}, bf16[64,128]{1,0:T(8,128)(2,1)S(1)}, u32[]{:S(2)}, u32[]{:S(2)}) collective-permute-start(bf16[64,128]{1,0:T(8,128)(2,1)S(1)} %get-tuple-element.51), channel_id=1, source_target_pairs={{1,2},{3,4},{5,6},{2,1},{4,3},{6,5},{9,10},{11,12},{13,14},{10,9},... | collective-permute-start | bytes 49160 | tf_op jit(solution)/shard_map/ppermute | solution.py:719
  51.2 10.7 %collective-permute-start.8 = (bf16[64,128]{1,0:T(8,128)(2,1)}, bf16[64,128]{1,0:T(8,128)(2,1)S(1)}, u32[]{:S(2)}, u32[]{:S(2)}) collective-permute-start(bf16[64,128]{1,0:T(8,128)(2,1)} %get-tuple-element.56.first_grad_ref), channel_id=1, source_target_pairs={{0,1},{2,3},{4,5},{6,7},{1,0},{3,2},{5,4},{7,6},{8,9},{10,11},{12,... | collective-permute-start | bytes 49160 | tf_op jit(solution)/shard_map/ppermute | solution.py:719
  54.3 7.6 %collective-permute-start.9 = (bf16[64,128]{1,0:T(8,128)(2,1)}, bf16[64,128]{1,0:T(8,128)(2,1)}, u32[]{:S(2)}, u32[]{:S(2)}) collective-permute-start(bf16[64,128]{1,0:T(8,128)(2,1)} %get-tuple-element.57.second_grad_ref), channel_id=1, source_target_pairs={{1,2},{3,4},{5,6},{2,1},{4,3},{6,5},{9,10},{11,12},{13,14},{10,9},... | collective-permute-start | bytes 49160 | tf_op jit(solution)/shard_map/ppermute | solution.py:719
  55.5 6.4 %copy-start.1 = (bf16[4096,128]{1,0:T(8,128)(2,1)S(1)}, bf16[4096,128]{1,0:T(8,128)(2,1)}, u32[]{:S(2)}) copy-start(bf16[4096,128]{1,0:T(8,128)(2,1)} %copy-done) | copy-start | bytes 3145732
  78.5 7.3 %collective-permute-start.12 = (bf16[512,128]{1,0:T(8,128)(2,1)S(1)}, bf16[512,128]{1,0:T(8,128)(2,1)S(1)}, u32[]{:S(2)}, u32[]{:S(2)}) collective-permute-start(bf16[512,128]{1,0:T(8,128)(2,1)S(1)} %get-tuple-element.72.mine_ref), channel_id=1, source_target_pairs={{0,1},{1,0},{2,3},{3,2},{4,5},{5,4},{6,7},{7,6},{8,9},{9,8},{10,11... | collective-permute-start | bytes 393224 | tf_op jit(solution)/shard_map/ppermute | solution.py:723
  85.8 9.5 %collective-permute-start.13 = (bf16[512,128]{1,0:T(8,128)(2,1)S(1)}, bf16[512,128]{1,0:T(8,128)(2,1)S(1)}, u32[]{:S(2)}, u32[]{:S(2)}) collective-permute-start(bf16[512,128]{1,0:T(8,128)(2,1)S(1)} %shard_map.204.mine_ref), channel_id=1, source_target_pairs={{0,2},{1,3},{2,0},{3,1},{4,6},{5,7},{6,4},{7,5},{8,10},{9,11},{10,... | collective-permute-start | bytes 393224 | tf_op jit(solution)/shard_map/ppermute | solution.py:723
  88.5 9.2 %collective-permute-start.10 = (bf16[512,128]{1,0:T(8,128)(2,1)S(1)}, bf16[512,128]{1,0:T(8,128)(2,1)S(1)}, u32[]{:S(2)}, u32[]{:S(2)}) collective-permute-start(bf16[512,128]{1,0:T(8,128)(2,1)S(1)} %get-tuple-element.69), channel_id=1, source_target_pairs={{0,1},{2,3},{4,5},{6,7},{1,0},{3,2},{5,4},{7,6},{8,9},{10,11},{12,... | collective-permute-start | bytes 393224 | tf_op jit(solution)/shard_map/ppermute | solution.py:719
  90.7 7.0 %collective-permute-start.11 = (bf16[512,128]{1,0:T(8,128)(2,1)S(1)}, bf16[512,128]{1,0:T(8,128)(2,1)S(1)}, u32[]{:S(2)}, u32[]{:S(2)}) collective-permute-start(bf16[512,128]{1,0:T(8,128)(2,1)S(1)} %get-tuple-element.70), channel_id=1, source_target_pairs={{1,2},{3,4},{5,6},{2,1},{4,3},{6,5},{9,10},{11,12},{13,14},{10,9},... | collective-permute-start | bytes 393224 | tf_op jit(solution)/shard_map/ppermute | solution.py:719
  95.4 8.4 %collective-permute-start.14 = (bf16[512,128]{1,0:T(8,128)(2,1)S(1)}, bf16[512,128]{1,0:T(8,128)(2,1)S(1)}, u32[]{:S(2)}, u32[]{:S(2)}) collective-permute-start(bf16[512,128]{1,0:T(8,128)(2,1)S(1)} %shard_map.205.mine_ref), channel_id=1, source_target_pairs={{0,4},{1,5},{2,6},{3,7},{4,0},{5,1},{6,2},{7,3},{8,12},{9,13},{10,... | collective-permute-start | bytes 393224 | tf_op jit(solution)/shard_map/ppermute | solution.py:723
  103.9 5.0 %collective-permute-start.15 = (bf16[512,128]{1,0:T(8,128)(2,1)S(1)}, bf16[512,128]{1,0:T(8,128)(2,1)S(1)}, u32[]{:S(2)}, u32[]{:S(2)}) collective-permute-start(bf16[512,128]{1,0:T(8,128)(2,1)S(1)} %shard_map.206.mine_ref), channel_id=1, source_target_pairs={{0,16},{8,24},{16,0},{24,8},{1,17},{9,25},{17,1},{25,9},{2,18},{10... | collective-permute-start | bytes 393224 | tf_op jit(solution)/shard_map/ppermute | solution.py:723
  108.9 1.7 %collective-permute-start.16 = (f32[640,128]{1,0:T(8,128)S(1)}, f32[640,128]{1,0:T(8,128)S(1)}, u32[]{:S(2)}, u32[]{:S(2)}) collective-permute-start(f32[640,128]{1,0:T(8,128)S(1)} %shard_map.207.mine_ref), channel_id=1, source_target_pairs={{0,8},{8,0},{16,24},{24,16},{1,9},{9,1},{17,25},{25,17},{2,10},{10... | collective-permute-start | bytes 983048 | tf_op jit(solution)/shard_map/ppermute | solution.py:723
  (20 other events, 23.0 us)

commit v7 on v6

--- a/solution.py
+++ b/solution.py
@@ -191,7 +191,7 @@
 
 
 def gather_kernel(
-    even_ref, lo_hbm, hi_hbm, x_hbm, first_ref, second_ref, x_ref, wide, up, down, lo, hi, sems
+    place_ref, lo_hbm, hi_hbm, x_hbm, first_ref, second_ref, x_ref, wide, up, down, lo, hi, sems
 ):
     fetch([(x_hbm, x_ref), (lo_hbm, lo), (hi_hbm, hi)], sems)
     wide[...] = x_ref[...].astype(f32)
@@ -202,19 +202,19 @@
         return carry
 
     lax.fori_loop(0, up.shape[0], step, None, unroll=16)
-    even = even_ref[0] > 0
+    even = place_ref[0] > 0
     first_ref[...] = jnp.where(even, up[...], down[...]).astype(bf16)
     second_ref[...] = jnp.where(even, down[...], up[...]).astype(bf16)
 
 
-def gather_rows(even, x, send_lo, send_hi):
+def gather_rows(place, x, send_lo, send_hi):
     rows, features = x.shape
     count = send_lo.shape[0]
     out = shape(count, features, bf16)
     return call(
         gather_kernel,
         [out, out, shape(rows, features, bf16)],
-        [even, send_lo, send_hi, x],
+        [place, send_lo, send_hi, x],
         [SMEM, HBM, HBM, HBM],
         [
             pltpu.VMEM((rows, features), f32),
@@ -241,7 +241,7 @@
 
 
 def prepare_kernel(
-    even_ref,
+    place_ref,
     g_hbm,
     owner_hbm,
     nbr_hbm,
@@ -295,7 +295,7 @@
         + [(w, weights_ref.at[pl.ds(128 * n, 128), :]) for n, w in enumerate(weight_hbms)],
         sems,
     )
-    even = even_ref[0] > 0
+    even = place_ref[0] > 0
     for low, high, out in (
         (lo_ref, hi_ref, sends_ref),
         (coarse_lo_ref, coarse_hi_ref, coarse_sends_ref),
@@ -459,7 +459,7 @@
 
 
 def coarse_tail_kernel(
-    group_ref,
+    place_ref,
     cin_ref,
     first_ref,
     second_ref,
@@ -488,7 +488,7 @@
         dot_tn(summed_ref[...], ups_ref[...]),
         dot_tn(out, sums_ref[...]),
     ]
-    weights_ref[...] = choose(group_ref[0], grads).astype(bf16)
+    weights_ref[...] = choose(place_ref[1], grads).astype(bf16)
 
 
 def choose(place, values):
@@ -699,9 +699,9 @@
     out_ref[512:, :] = theirs[384:]
 
 
-def weights_kernel(group_ref, mine_ref, theirs_ref, out_ref):
+def weights_kernel(place_ref, mine_ref, theirs_ref, out_ref):
     out_ref[:384, :] = mine_ref[:384, :] + theirs_ref[:384, :]
-    group = group_ref[0]
+    group = place_ref[1]
     low, high = lax.rem(group, 2), group // 2
     for n in range(4):
         row = jnp.where(high == n // 2, 384, 512)
@@ -723,7 +723,7 @@
     return lax.ppermute(block, axis, [(i, i ^ distance) for i in range(lax.axis_size(axis))])
 
 
-def total_weights(weights, group, after):
+def total_weights(weights, place, after):
     distance, number = 1, 0
     while distance < lax.axis_size("sub"):
         theirs = swapped(weights, "sub", distance)
@@ -743,7 +743,7 @@
     return call(
         weights_kernel,
         shape(896, 128, f32),
-        [group, weights, swapped(weights, "grp", 1)],
+        [place, weights, swapped(weights, "grp", 1)],
         [SMEM, VMEM, VMEM],
     )
 
@@ -774,13 +774,12 @@
     coarse_halo = coarse_send_lo.shape[0]
     count_rows = coarse_rows // 128
     owner = coarse_owner.reshape(rows // 128, 128)
-    even = (1 - lax.rem(lax.axis_index("sub"), 2)).astype(jnp.int32).reshape(1)
-    group = lax.axis_index("grp").astype(jnp.int32).reshape(1)
+    place = jnp.stack([1 - lax.rem(lax.axis_index("sub"), 2), lax.axis_index("grp")])
 
     def buffer(count, columns, dtype):
         return pltpu.VMEM((count, columns), dtype)
 
-    to_first, to_second, states = gather_rows(even, states, fine_send_lo, fine_send_hi)
+    to_first, to_second, states = gather_rows(place, states, fine_send_lo, fine_send_hi)
     first, second = exchange(to_first, to_second)
 
     (
@@ -801,7 +800,7 @@
             shape(rows // 128, 128, jnp.int32),
         ],
         [
-            even, cotangent, owner, fine_nbr.T, fine_mask.T, coarse_nbr.T, coarse_mask.T,
+            place, cotangent, owner, fine_nbr.T, fine_mask.T, coarse_nbr.T, coarse_mask.T,
             fine_send_lo[None], fine_send_hi[None], coarse_send_lo[None], coarse_send_hi[None],
             fine_self, fine_other, fine_node, coarse_self, coarse_other, coarse_node, prolong,
             to_first,
@@ -833,7 +832,9 @@
         out_specs=[VMEM, HBM, VMEM],
         mib=32,
     )
-    chip_totals = (totals.astype(f32) + swapped(totals, "grp", 1).astype(f32)).astype(bf16)
+    chip_totals = call(
+        add_kernel, shape(*totals.shape, bf16), [totals, swapped(totals, "grp", 1)]
+    )
     more_totals = swapped(chip_totals, "grp", 2)
     sums = call(
         sums_kernel,
@@ -888,7 +889,7 @@
         coarse_tail_kernel,
         [shape(coarse_rows, features, bf16), shape(features, features, bf16)],
         [
-            group, coarse_in, coarse_first, coarse_second, sums, matrices,
+            place, coarse_in, coarse_first, coarse_second, sums, matrices,
             first_grad, second_grad, coarse_sum, coarse_ups, coarse_downs,
         ],
         [SMEM] + [VMEM] * 10,
@@ -946,7 +947,7 @@
         ],
         out_specs=HBM,
     )
-    grad_weights = total_weights(weights, group, ((), (result,), (grad_states,)))
+    grad_weights = total_weights(weights, place, ((), (result,), (grad_states,)))
     return (result, grad_states, grad_weights.reshape(7, features, features))
 
 

time: 113 us -> 98.9 us (0.88)
  local copies, waits for them, and re-layouts: 15.2 us -> 0 us
  starting transfers between devices: 30 us -> 32.4 us
    unnamed x54 -> x0, local copies, waits for them, and re-layouts: 15.2 us -> none
    ppermute x9, starting transfers between devices: 13.2 us -> 16.7 us  [swapped(): lax.ppermute(block, axis, [(i, i ^ distance) for i in range(lax.axis_size...]
    pallas_call x16 -> x17, Pallas kernels: 46.3 us -> 46.7 us  [call(): pl.pallas_call(kernel, out_shape=out_shape, in_specs=in_specs, out_specs=...]
  transfers between devices with their start and end apart: 17 -> 17, of which waited for: 9 -> 9; matrix products, arithmetic and copies ran while one was open for 0% -> 0% of each run, Pallas kernels for 15% -> 18%
where the time goes in v7:
time: 98.9 us; the launch traced here: 98.3 us
  Pallas kernels  46.7 us (47%)
  starting transfers between devices  32.4 us (33%)
  waiting for transfers between devices  18.2 us (18%)
    pallas_call x17, Pallas kernels, call(): pl.pallas_call(kernel, out_shape=out_shape, in_specs=in_specs, out_specs=...  46.7 us
    ppermute x9, starting transfers between devices, swapped(): lax.ppermute(block, axis, [(i, i ^ distance) for i in range(lax.axis_size...  16.7 us
    ppermute x9, waiting for transfers between devices, swapped(): lax.ppermute(block, axis, [(i, i ^ distance) for i in range(lax.axis_size...  15.1 us
    ppermute x4, starting transfers between devices, exchange(): lax.ppermute(first, 'sub', routes[0])  13 us
    ppermute x4, waiting for transfers between devices, exchange(): lax.ppermute(first, 'sub', routes[0])  3.14 us
    ppermute x4, starting transfers between devices, exchange(): lax.ppermute(second, 'sub', routes[1])  2.81 us
  transfers between devices with their start and end apart: 17, of which 9 were waited for; matrix products, arithmetic and copies ran while one was open for 0% of the time, Pallas kernels for 18%

profile of v7, /device:TPU:0, one launch (start us, length us, event | category | flops | bytes accessed | tf_op | source)
XLA Modules:
  0.0 98.3 jit_solution(611751309627558979)
XLA Ops:
  0.7 2.8 %shard_map.193 = (bf16[512,128]{1,0:T(8,128)(2,1)S(1)}, bf16[512,128]{1,0:T(8,128)(2,1)S(1)}, bf16[4096,128]{1,0:T(8,128)(2,1)S(1)}) custom-call(s32[2]{0:T(128)S(1)} %pad_add_fusion.place_ref, s32[512]{0:T(512)} %lo_hbm.1, s32[512]{0:T(512)} %hi_hbm.1, bf16[4096,128]{1,0:T(8,128)(2,1)} %x_hbm.1), custom_call_target="tpu_custom_call" | custom-call | tf_op jit(solution)/shard_map/pallas_call | solution.py:52
  4.2 5.8 %collective-permute-start = (bf16[512,128]{1,0:T(8,128)(2,1)S(1)}, bf16[512,128]{1,0:T(8,128)(2,1)S(1)}, u32[]{:S(2)}, u32[]{:S(2)}) collective-permute-start(bf16[512,128]{1,0:T(8,128)(2,1)S(1)} %get-tuple-element.39.rest_7_), channel_id=1, source_target_pairs={{0,1},{2,3},{4,5},{6,7},{1,0},{3,2},{5,4},{7,6},{8,9},{10,11},{12,... | collective-permute-start | bytes 393224 | tf_op jit(solution)/shard_map/ppermute | solution.py:719
  10.0 2.8 %shard_map.194 = (bf16[16,128]{1,0:T(8,128)(2,1)S(1)}, f32[8,4096]{1,0:T(8,128)S(1)}, f32[4096,8]{1,0:T(8,128)S(1)}, f32[8,1024]{1,0:T(8,128)S(1)}, f32[1024,8]{...) custom-call(s32[2]{0:T(128)S(1)} %pad_add_fusion.place_ref, ...), custom_call_target="tpu_custom_call" | custom-call | tf_op jit(solution)/shard_map/pallas_call | solution.py:52
  12.8 2.1 %collective-permute-done.first_ref = bf16[512,128]{1,0:T(8,128)(2,1)S(1)} collective-permute-done((bf16[512,128]{1,0:T(8,128)(2,1)S(1)}, bf16[512,128]{1,0:T(8,128)(2,1)S(1)}, u32[]{:S(2)}, u32[]{:S(2)}) %collective-permute-start) | collective-permute-done | bytes 131104 | tf_op jit(solution)/shard_map/ppermute | solution.py:719
  14.9 10.7 %shard_map.195 = (bf16[4096,128]{1,0:T(8,128)(2,1)S(1)}, bf16[32768,128]{1,0:T(8,128)(2,1)}, bf16[1040,128]{1,0:T(8,128)(2,1)S(1)}) custom-call(bf16[4096,128]{1,0:T(8,128)(2,1)S(1)} %get-tuple-element.38.h_ref, bf16[512,128]{1,0:T(8,128)(2,1)S(1)} %collective-permute-done.first_ref, bf16[512,128]{1,0:T(8,128)(2,1)S(1)} %collective-permute-done.1.second_ref, ...), custom_call_target="tpu_custom_call" | custom-call | tf_op jit(solution)/shard_map/pallas_call | solution.py:52
  25.7 1.5 %collective-permute-done.2.theirs_ref = bf16[1040,128]{1,0:T(8,128)(2,1)S(1)} collective-permute-done((bf16[1040,128]{1,0:T(8,128)(2,1)S(1)}, bf16[1040,128]{1,0:T(8,128)(2,1)S(1)}, u32[]{:S(2)}, u32[]{:S(2)}) %collective-permute-start.2) | collective-permute-done | bytes 266272 | tf_op jit(solution)/shard_map/ppermute | solution.py:723
  27.3 1.6 %collective-permute-start.3 = (bf16[1040,128]{1,0:T(8,128)(2,1)S(1)}, bf16[1040,128]{1,0:T(8,128)(2,1)S(1)}, u32[]{:S(2)}, u32[]{:S(2)}) collective-permute-start(bf16[1040,128]{1,0:T(8,128)(2,1)S(1)} %shard_map.196.after_ref.totals_ref), channel_id=1, source_target_pairs={{0,16},{8,24},{16,0},{24,8},{1,17},{9,25},{17,1},{25,9},{2,18},{10... | collective-permute-start | bytes 798728 | tf_op jit(solution)/shard_map/ppermute | solution.py:723
  28.8 2.8 %shard_map.198.sums_ref = bf16[1024,128]{1,0:T(8,128)(2,1)S(1)} custom-call(s32[32,128]{1,0:T(8,128)S(1)} %get-tuple-element.43.owner_ref, bf16[4096,128]{1,0:T(8,128)(2,1)S(1)} %get-tuple-element.47.g_ref, bf16[1040,128]{1,0:T(8,128)(2,1)S(1)} %get-tuple-element.46.mine_ref.after_ref), custom_call_target="tpu_custom_call" | custom-call | tf_op jit(solution)/shard_map/pallas_call | solution.py:52
  33.2 2.5 %collective-permute-done.3.more_totals_ref = bf16[1040,128]{1,0:T(8,128)(2,1)S(1)} collective-permute-done((bf16[1040,128]{1,0:T(8,128)(2,1)S(1)}, bf16[1040,128]{1,0:T(8,128)(2,1)S(1)}, u32[]{:S(2)}, u32[]{:S(2)}) %collective-permute-start.3) | collective-permute-done | bytes 266272 | tf_op jit(solution)/shard_map/ppermute | solution.py:723
  36.4 1.6 %collective-permute-start.7 = (bf16[1024,128]{1,0:T(8,128)(2,1)S(1)}, bf16[1024,128]{1,0:T(8,128)(2,1)S(1)}, u32[]{:S(2)}, u32[]{:S(2)}) collective-permute-start(bf16[1024,128]{1,0:T(8,128)(2,1)S(1)} %get-tuple-element.52.chip_sums_ref), channel_id=1, source_target_pairs={{0,16},{8,24},{16,0},{24,8},{1,17},{9,25},{17,1},{25,9},{2,18},{10... | collective-permute-start | bytes 786440 | tf_op jit(solution)/shard_map/ppermute | solution.py:723
  38.0 2.5 %collective-permute-start.5 = (bf16[64,128]{1,0:T(8,128)(2,1)S(1)}, bf16[64,128]{1,0:T(8,128)(2,1)S(1)}, u32[]{:S(2)}, u32[]{:S(2)}) collective-permute-start(bf16[64,128]{1,0:T(8,128)(2,1)S(1)} %get-tuple-element.50), channel_id=1, source_target_pairs={{0,1},{2,3},{4,5},{6,7},{1,0},{3,2},{5,4},{7,6},{8,9},{10,11},{12,... | collective-permute-start | bytes 49160 | tf_op jit(solution)/shard_map/ppermute | solution.py:719
  42.2 1.8 %collective-permute-done.7.more_sums_ref = bf16[1024,128]{1,0:T(8,128)(2,1)S(1)} collective-permute-done((bf16[1024,128]{1,0:T(8,128)(2,1)S(1)}, bf16[1024,128]{1,0:T(8,128)(2,1)S(1)}, u32[]{:S(2)}, u32[]{:S(2)}) %collective-permute-start.7) | collective-permute-done | bytes 262176 | tf_op jit(solution)/shard_map/ppermute | solution.py:723
  44.0 2.9 %shard_map.200 = (f32[1024,128]{1,0:T(8,128)S(1)}, bf16[64,128]{1,0:T(8,128)(2,1)S(1)}, bf16[64,128]{1,0:T(8,128)(2,1)S(1)}, bf16[1024,128]{1,0:T(8,128)(2,1)S(1...) custom-call(bf16[1024,128]{1,0:T(8,128)(2,1)S(1)} %get-tuple-element.49.cin_ref, ...), custom_call_target="tpu_custom_call" | custom-call | tf_op jit(solution)/shard_map/pallas_call | solution.py:52
  46.9 3.2 %collective-permute-start.8 = (bf16[64,128]{1,0:T(8,128)(2,1)S(1)}, bf16[64,128]{1,0:T(8,128)(2,1)S(1)}, u32[]{:S(2)}, u32[]{:S(2)}) collective-permute-start(bf16[64,128]{1,0:T(8,128)(2,1)S(1)} %get-tuple-element.56.first_grad_ref), channel_id=1, source_target_pairs={{0,1},{2,3},{4,5},{6,7},{1,0},{3,2},{5,4},{7,6},{8,9},{10,11},{12,... | collective-permute-start | bytes 49160 | tf_op jit(solution)/shard_map/ppermute | solution.py:719
  52.1 10.8 %shard_map.203 = (bf16[4096,128]{1,0:T(8,128)(2,1)}, bf16[4096,256]{1,0:T(8,128)(2,1)}, bf16[512,128]{1,0:T(8,128)(2,1)S(1)}, bf16[512,128]{1,0:T(8,128)(2,1)S(1)}, bf16[512,128]{1,0:T(8,128)(2,1)S(1)}) custom-call(bf16[4096,128]{1,0:T(8,128)(2,1)S(1)} %get-tuple-element.38.h_ref, bf16[512,128]{1,0:T(8,128)(2,1)S(1)} %collective-permute-done.first_ref, ...), custom_call_target="tpu_custom_call" | custom-call | tf_op jit(solution)/shard_map/pallas_call | solution.py:52
  62.8 5.1 %collective-permute-start.12 = (bf16[512,128]{1,0:T(8,128)(2,1)S(1)}, bf16[512,128]{1,0:T(8,128)(2,1)S(1)}, u32[]{:S(2)}, u32[]{:S(2)}) collective-permute-start(bf16[512,128]{1,0:T(8,128)(2,1)S(1)} %get-tuple-element.72.mine_ref), channel_id=1, source_target_pairs={{0,1},{1,0},{2,3},{3,2},{4,5},{5,4},{6,7},{7,6},{8,9},{9,8},{10,11... | collective-permute-start | bytes 393224 | tf_op jit(solution)/shard_map/ppermute | solution.py:723
  67.9 2.9 %collective-permute-done.12.theirs_ref = bf16[512,128]{1,0:T(8,128)(2,1)S(1)} collective-permute-done((bf16[512,128]{1,0:T(8,128)(2,1)S(1)}, bf16[512,128]{1,0:T(8,128)(2,1)S(1)}, u32[]{:S(2)}, u32[]{:S(2)}) %collective-permute-start.12) | collective-permute-done | bytes 131104 | tf_op jit(solution)/shard_map/ppermute | solution.py:723
  70.9 4.1 %collective-permute-start.13 = (bf16[512,128]{1,0:T(8,128)(2,1)S(1)}, bf16[512,128]{1,0:T(8,128)(2,1)S(1)}, u32[]{:S(2)}, u32[]{:S(2)}) collective-permute-start(bf16[512,128]{1,0:T(8,128)(2,1)S(1)} %shard_map.205.mine_ref), channel_id=1, source_target_pairs={{0,2},{1,3},{2,0},{3,1},{4,6},{5,7},{6,4},{7,5},{8,10},{9,11},{10,... | collective-permute-start | bytes 393224 | tf_op jit(solution)/shard_map/ppermute | solution.py:723
  75.0 1.5 %collective-permute-start.10 = (bf16[512,128]{1,0:T(8,128)(2,1)S(1)}, bf16[512,128]{1,0:T(8,128)(2,1)S(1)}, u32[]{:S(2)}, u32[]{:S(2)}) collective-permute-start(bf16[512,128]{1,0:T(8,128)(2,1)S(1)} %get-tuple-element.69), channel_id=1, source_target_pairs={{0,1},{2,3},{4,5},{6,7},{1,0},{3,2},{5,4},{7,6},{8,9},{10,11},{12,... | collective-permute-start | bytes 393224 | tf_op jit(solution)/shard_map/ppermute | solution.py:719
  77.2 4.0 %shard_map.202.rest_0_ = bf16[4096,128]{1,0:T(8,128)(2,1)} custom-call(bf16[4096,128]{1,0:T(8,128)(2,1)S(1)} %get-tuple-element.38.h_ref, bf16[4096,128]{1,0:T(8,128)(2,1)S(1)} %get-tuple-element.45.summed_ref, bf16[896,128]{1,0:T(8,128)(2,1)S(1)} %get-tuple-element.41.weights_ref.matrices_ref, f32[4096,8]{1,0:T(8,128)S(1)} %shard_map.197.after_ref.owners_ref, ...), custom_call_target="tpu_custom_call" | custom-call | tf_op jit(solution)/shard_map/pallas_call | solution.py:52
  81.2 2.8 %collective-permute-start.14 = (bf16[512,128]{1,0:T(8,128)(2,1)S(1)}, bf16[512,128]{1,0:T(8,128)(2,1)S(1)}, u32[]{:S(2)}, u32[]{:S(2)}) collective-permute-start(bf16[512,128]{1,0:T(8,128)(2,1)S(1)} %shard_map.206.mine_ref), channel_id=1, source_target_pairs={{0,4},{1,5},{2,6},{3,7},{4,0},{5,1},{6,2},{7,3},{8,12},{9,13},{10,... | collective-permute-start | bytes 393224 | tf_op jit(solution)/shard_map/ppermute | solution.py:723
  84.0 6.1 %shard_map.204.rest_0_ = bf16[4096,128]{1,0:T(8,128)(2,1)} custom-call(bf16[4096,128]{1,0:T(8,128)(2,1)} %get-tuple-element.67.ups_hbm, bf16[4096,256]{1,0:T(8,128)(2,1)} %get-tuple-element.68.downs_hbm, bf16[512,128]{1,0:T(8,128)(2,1)S(1)} %collective-permute-done.10.first_back_ref, bf16[512,128]{1,0:T(8,128)(2,1)S(1)} %collective-permute-done.11.second_back_ref, ...), custom_call_target="tpu_custom_call" | custom-call | tf_op jit(solution)/shard_map/pallas_call | solution.py:52
  91.5 3.7 %collective-permute-done.15.theirs_ref = bf16[512,128]{1,0:T(8,128)(2,1)S(1)} collective-permute-done((bf16[512,128]{1,0:T(8,128)(2,1)S(1)}, bf16[512,128]{1,0:T(8,128)(2,1)S(1)}, u32[]{:S(2)}, u32[]{:S(2)}) %collective-permute-start.15) | collective-permute-done | bytes 131104 | tf_op jit(solution)/shard_map/ppermute | solution.py:723
  95.3 1.6 %collective-permute-done.16.theirs_ref = f32[640,128]{1,0:T(8,128)S(1)} collective-permute-done((f32[640,128]{1,0:T(8,128)S(1)}, f32[640,128]{1,0:T(8,128)S(1)}, u32[]{:S(2)}, u32[]{:S(2)}) %collective-permute-start.16) | collective-permute-done | bytes 327712 | tf_op jit(solution)/shard_map/ppermute | solution.py:723
  (28 shorter events, 10.4 us)
Async XLA Ops:
  3.5 9.2 %collective-permute-start.1 = (bf16[512,128]{1,0:T(8,128)(2,1)S(1)}, bf16[512,128]{1,0:T(8,128)(2,1)S(1)}, u32[]{:S(2)}, u32[]{:S(2)}) collective-permute-start(bf16[512,128]{1,0:T(8,128)(2,1)S(1)} %get-tuple-element.40), channel_id=1, source_target_pairs={{1,2},{3,4},{5,6},{2,1},{4,3},{6,5},{9,10},{11,12},{13,14},{10,9},... | collective-permute-start | bytes 393224 | tf_op jit(solution)/shard_map/ppermute | solution.py:719
  4.2 10.6 %collective-permute-start = (bf16[512,128]{1,0:T(8,128)(2,1)S(1)}, bf16[512,128]{1,0:T(8,128)(2,1)S(1)}, u32[]{:S(2)}, u32[]{:S(2)}) collective-permute-start(bf16[512,128]{1,0:T(8,128)(2,1)S(1)} %get-tuple-element.39.rest_7_), channel_id=1, source_target_pairs={{0,1},{2,3},{4,5},{6,7},{1,0},{3,2},{5,4},{7,6},{8,9},{10,11},{12,... | collective-permute-start | bytes 393224 | tf_op jit(solution)/shard_map/ppermute | solution.py:719
  25.6 1.6 %collective-permute-start.2 = (bf16[1040,128]{1,0:T(8,128)(2,1)S(1)}, bf16[1040,128]{1,0:T(8,128)(2,1)S(1)}, u32[]{:S(2)}, u32[]{:S(2)}) collective-permute-start(bf16[1040,128]{1,0:T(8,128)(2,1)S(1)} %get-tuple-element.46.mine_ref.after_ref), channel_id=1, source_target_pairs={{0,8},{8,0},{16,24},{24,16},{1,9},{9,1},{17,25},{25,17},{2,10},{10... | collective-permute-start | bytes 798728 | tf_op jit(solution)/shard_map/ppermute | solution.py:723
  27.3 8.5 %collective-permute-start.3 = (bf16[1040,128]{1,0:T(8,128)(2,1)S(1)}, bf16[1040,128]{1,0:T(8,128)(2,1)S(1)}, u32[]{:S(2)}, u32[]{:S(2)}) collective-permute-start(bf16[1040,128]{1,0:T(8,128)(2,1)S(1)} %shard_map.196.after_ref.totals_ref), channel_id=1, source_target_pairs={{0,16},{8,24},{16,0},{24,8},{1,17},{9,25},{17,1},{25,9},{2,18},{10... | collective-permute-start | bytes 798728 | tf_op jit(solution)/shard_map/ppermute | solution.py:723
  31.6 1.6 %collective-permute-start.4 = (bf16[1024,128]{1,0:T(8,128)(2,1)S(1)}, bf16[1024,128]{1,0:T(8,128)(2,1)S(1)}, u32[]{:S(2)}, u32[]{:S(2)}) collective-permute-start(bf16[1024,128]{1,0:T(8,128)(2,1)S(1)} %shard_map.198.sums_ref), channel_id=1, source_target_pairs={{0,8},{8,0},{16,24},{24,16},{1,9},{9,1},{17,25},{25,17},{2,10},{10... | collective-permute-start | bytes 786440 | tf_op jit(solution)/shard_map/ppermute | solution.py:723
  36.4 7.6 %collective-permute-start.7 = (bf16[1024,128]{1,0:T(8,128)(2,1)S(1)}, bf16[1024,128]{1,0:T(8,128)(2,1)S(1)}, u32[]{:S(2)}, u32[]{:S(2)}) collective-permute-start(bf16[1024,128]{1,0:T(8,128)(2,1)S(1)} %get-tuple-element.52.chip_sums_ref), channel_id=1, source_target_pairs={{0,16},{8,24},{16,0},{24,8},{1,17},{9,25},{17,1},{25,9},{2,18},{10... | collective-permute-start | bytes 786440 | tf_op jit(solution)/shard_map/ppermute | solution.py:723
  38.0 4.2 %collective-permute-start.5 = (bf16[64,128]{1,0:T(8,128)(2,1)S(1)}, bf16[64,128]{1,0:T(8,128)(2,1)S(1)}, u32[]{:S(2)}, u32[]{:S(2)}) collective-permute-start(bf16[64,128]{1,0:T(8,128)(2,1)S(1)} %get-tuple-element.50), channel_id=1, source_target_pairs={{0,1},{2,3},{4,5},{6,7},{1,0},{3,2},{5,4},{7,6},{8,9},{10,11},{12,... | collective-permute-start | bytes 49160 | tf_op jit(solution)/shard_map/ppermute | solution.py:719
  40.4 1.7 %collective-permute-start.6 = (bf16[64,128]{1,0:T(8,128)(2,1)S(1)}, bf16[64,128]{1,0:T(8,128)(2,1)S(1)}, u32[]{:S(2)}, u32[]{:S(2)}) collective-permute-start(bf16[64,128]{1,0:T(8,128)(2,1)S(1)} %get-tuple-element.51), channel_id=1, source_target_pairs={{1,2},{3,4},{5,6},{2,1},{4,3},{6,5},{9,10},{11,12},{13,14},{10,9},... | collective-permute-start | bytes 49160 | tf_op jit(solution)/shard_map/ppermute | solution.py:719
  46.9 5.2 %collective-permute-start.8 = (bf16[64,128]{1,0:T(8,128)(2,1)S(1)}, bf16[64,128]{1,0:T(8,128)(2,1)S(1)}, u32[]{:S(2)}, u32[]{:S(2)}) collective-permute-start(bf16[64,128]{1,0:T(8,128)(2,1)S(1)} %get-tuple-element.56.first_grad_ref), channel_id=1, source_target_pairs={{0,1},{2,3},{4,5},{6,7},{1,0},{3,2},{5,4},{7,6},{8,9},{10,11},{12,... | collective-permute-start | bytes 49160 | tf_op jit(solution)/shard_map/ppermute | solution.py:719
  50.0 2.0 %collective-permute-start.9 = (bf16[64,128]{1,0:T(8,128)(2,1)S(1)}, bf16[64,128]{1,0:T(8,128)(2,1)S(1)}, u32[]{:S(2)}, u32[]{:S(2)}) collective-permute-start(bf16[64,128]{1,0:T(8,128)(2,1)S(1)} %get-tuple-element.57.second_grad_ref), channel_id=1, source_target_pairs={{1,2},{3,4},{5,6},{2,1},{4,3},{6,5},{9,10},{11,12},{13,14},{10,9},... | collective-permute-start | bytes 49160 | tf_op jit(solution)/shard_map/ppermute | solution.py:719
  62.8 8.0 %collective-permute-start.12 = (bf16[512,128]{1,0:T(8,128)(2,1)S(1)}, bf16[512,128]{1,0:T(8,128)(2,1)S(1)}, u32[]{:S(2)}, u32[]{:S(2)}) collective-permute-start(bf16[512,128]{1,0:T(8,128)(2,1)S(1)} %get-tuple-element.72.mine_ref), channel_id=1, source_target_pairs={{0,1},{1,0},{2,3},{3,2},{4,5},{5,4},{6,7},{7,6},{8,9},{9,8},{10,11... | collective-permute-start | bytes 393224 | tf_op jit(solution)/shard_map/ppermute | solution.py:723
  70.9 10.3 %collective-permute-start.13 = (bf16[512,128]{1,0:T(8,128)(2,1)S(1)}, bf16[512,128]{1,0:T(8,128)(2,1)S(1)}, u32[]{:S(2)}, u32[]{:S(2)}) collective-permute-start(bf16[512,128]{1,0:T(8,128)(2,1)S(1)} %shard_map.205.mine_ref), channel_id=1, source_target_pairs={{0,2},{1,3},{2,0},{3,1},{4,6},{5,7},{6,4},{7,5},{8,10},{9,11},{10,... | collective-permute-start | bytes 393224 | tf_op jit(solution)/shard_map/ppermute | solution.py:723
  75.0 9.0 %collective-permute-start.10 = (bf16[512,128]{1,0:T(8,128)(2,1)S(1)}, bf16[512,128]{1,0:T(8,128)(2,1)S(1)}, u32[]{:S(2)}, u32[]{:S(2)}) collective-permute-start(bf16[512,128]{1,0:T(8,128)(2,1)S(1)} %get-tuple-element.69), channel_id=1, source_target_pairs={{0,1},{2,3},{4,5},{6,7},{1,0},{3,2},{5,4},{7,6},{8,9},{10,11},{12,... | collective-permute-start | bytes 393224 | tf_op jit(solution)/shard_map/ppermute | solution.py:719
  76.5 7.5 %collective-permute-start.11 = (bf16[512,128]{1,0:T(8,128)(2,1)S(1)}, bf16[512,128]{1,0:T(8,128)(2,1)S(1)}, u32[]{:S(2)}, u32[]{:S(2)}) collective-permute-start(bf16[512,128]{1,0:T(8,128)(2,1)S(1)} %get-tuple-element.70), channel_id=1, source_target_pairs={{1,2},{3,4},{5,6},{2,1},{4,3},{6,5},{9,10},{11,12},{13,14},{10,9},... | collective-permute-start | bytes 393224 | tf_op jit(solution)/shard_map/ppermute | solution.py:719
  81.2 8.9 %collective-permute-start.14 = (bf16[512,128]{1,0:T(8,128)(2,1)S(1)}, bf16[512,128]{1,0:T(8,128)(2,1)S(1)}, u32[]{:S(2)}, u32[]{:S(2)}) collective-permute-start(bf16[512,128]{1,0:T(8,128)(2,1)S(1)} %shard_map.206.mine_ref), channel_id=1, source_target_pairs={{0,4},{1,5},{2,6},{3,7},{4,0},{5,1},{6,2},{7,3},{8,12},{9,13},{10,... | collective-permute-start | bytes 393224 | tf_op jit(solution)/shard_map/ppermute | solution.py:723
  90.2 5.0 %collective-permute-start.15 = (bf16[512,128]{1,0:T(8,128)(2,1)S(1)}, bf16[512,128]{1,0:T(8,128)(2,1)S(1)}, u32[]{:S(2)}, u32[]{:S(2)}) collective-permute-start(bf16[512,128]{1,0:T(8,128)(2,1)S(1)} %shard_map.207.mine_ref), channel_id=1, source_target_pairs={{0,16},{8,24},{16,0},{24,8},{1,17},{9,25},{17,1},{25,9},{2,18},{10... | collective-permute-start | bytes 393224 | tf_op jit(solution)/shard_map/ppermute | solution.py:723
  95.2 1.7 %collective-permute-start.16 = (f32[640,128]{1,0:T(8,128)S(1)}, f32[640,128]{1,0:T(8,128)S(1)}, u32[]{:S(2)}, u32[]{:S(2)}) collective-permute-start(f32[640,128]{1,0:T(8,128)S(1)} %shard_map.208.mine_ref), channel_id=1, source_target_pairs={{0,8},{8,0},{16,24},{24,16},{1,9},{9,1},{17,25},{25,17},{2,10},{10... | collective-permute-start | bytes 983048 | tf_op jit(solution)/shard_map/ppermute | solution.py:723

commit v8 on v7

--- a/solution.py
+++ b/solution.py
@@ -127,9 +127,9 @@
 def level_terms(h_ref, halo_refs, self_weight, other_weight, own, far, halo):
     halo_rows = halo_refs[0].shape[0]
     other = other_weight * 0.5
-    h = h_ref[...]
-    own[...] = dot(h, self_weight * 0.5)
-    far[...] = dot(h, other).astype(bf16)
+    terms = dot(h_ref[...], jnp.concatenate([self_weight * 0.5, other], 1))
+    own[...] = terms[:, :128]
+    far[...] = terms[:, 128:].astype(bf16)
     halo[:halo_rows, :] = dot(halo_refs[0][...], other).astype(bf16)
     halo[halo_rows:, :] = dot(halo_refs[1][...], other).astype(bf16)
 
@@ -368,13 +368,13 @@
         return carry
 
     lax.fori_loop(0, h_ref.shape[0] // (STEP * BLOCK), step, None)
-    new[...] = (
-        h_ref[...].astype(f32) + dot(summed_ref[...], matrix(weights_ref, 2))
-    ).astype(bf16)
+    new[...] = jnp.concatenate([h_ref[...], summed_ref[...]], 1)
     coarse_rows = totals_ref.shape[0] - counts_ref.shape[0]
 
     def tile_step(tile, carry):
-        totals_ref[chunk_of(tile, 256), :] = owner_sums(owner_ref, tile, new[...]).astype(bf16)
+        sums = owner_sums(owner_ref, tile, new[...])
+        totals = sums[:, :128] + dot(sums[:, 128:].astype(bf16), matrix(weights_ref, 2))
+        totals_ref[chunk_of(tile, 256), :] = totals.astype(bf16)
         return carry
 
     lax.fori_loop(0, coarse_rows // 256, tile_step, None)
@@ -545,19 +545,16 @@
     second_back_ref,
     sends_ref,
     coarse_weights_ref,
-    ups_hbm,
-    downs_hbm,
+    ups_ref,
+    downs_ref,
     first_grad_ref,
     second_grad_ref,
     weights_ref,
-    ups_ref,
-    downs_ref,
     grad_sum,
     halo_grad,
     mean,
     slope_ref,
     slope_sems,
-    sems,
 ):
     count = STEP * BLOCK
     steps = h_ref.shape[0] // count
@@ -610,12 +607,6 @@
 
     lax.fori_loop(0, steps - 1, step, None)
     edge_step(steps - 1)
-    copies = [
-        pltpu.make_async_copy(ups_ref, ups_hbm, sems.at[0]),
-        pltpu.make_async_copy(downs_ref, downs_hbm, sems.at[1]),
-    ]
-    for copy in copies:
-        copy.start()
     first_grad = halo_grad[:halo_rows, :].astype(bf16)
     second_grad = halo_grad[halo_rows:, :].astype(bf16)
     first_grad_ref[...] = first_grad
@@ -629,39 +620,19 @@
     ).astype(bf16)
     weights_ref[256:384, :] = dot_tn(summed_ref[...], ups_ref[...]).astype(bf16)
     weights_ref[384:512, :] = coarse_weights_ref[...]
-    for copy in copies:
-        copy.wait()
 
 
 def finish_kernel(
-    ups_hbm,
-    downs_hbm,
+    ups_ref,
+    downs_ref,
     first_back_ref,
     second_back_ref,
     sends_ref,
     matrices_ref,
     out_hbm,
-    ups_ref,
-    downs_ref,
     out_ref,
-    ups_sems,
-    downs_sems,
-    out_sem,
+    sem,
 ):
-    chunks = ups_ref.shape[0] // CHUNK
-
-    def copies(index):
-        here = chunk_of(index, CHUNK)
-        return (
-            pltpu.make_async_copy(ups_hbm.at[here, :], ups_ref.at[here, :], ups_sems.at[index]),
-            pltpu.make_async_copy(
-                downs_hbm.at[here, :], downs_ref.at[here, :], downs_sems.at[index]
-            ),
-        )
-
-    for index in range(chunks):
-        for copy in copies(index):
-            copy.start()
     other = matrix(matrices_ref, 1)
     plain = jnp.concatenate([matrix(matrices_ref, 0), other], 1)
     back = jnp.concatenate([first_back_ref[...], second_back_ref[...]], 0)
@@ -675,16 +646,13 @@
         for part in range(CHUNK // 256):
             local = (sends - (index * CHUNK + 256 * part)).astype(f32)
             rows.append(pick16(jnp.broadcast_to(local, place.shape).astype(bf16), place))
-        spread = dot(jnp.concatenate(rows, 0), back)
-        for copy in copies(index):
-            copy.wait()
         grad = ups_ref[here, :].astype(f32) + dot_nt(downs_ref[here, :], plain)
-        out_ref[here, :] = (grad + spread).astype(bf16)
-        pltpu.make_async_copy(out_ref.at[here, :], out_hbm.at[here, :], out_sem).start()
+        out_ref[here, :] = (grad + dot(jnp.concatenate(rows, 0), back)).astype(bf16)
+        pltpu.make_async_copy(out_ref.at[here, :], out_hbm.at[here, :], sem).start()
         return carry
 
-    lax.fori_loop(0, chunks, step, None)
-    pltpu.make_async_copy(out_ref, out_hbm, out_sem).wait()
+    lax.fori_loop(0, ups_ref.shape[0] // CHUNK, step, None)
+    pltpu.make_async_copy(out_ref, out_hbm, sem).wait()
 
 
 def add_kernel(mine_ref, theirs_ref, *rest):
@@ -692,7 +660,7 @@
     out_ref[...] = (mine_ref[...].astype(f32) + theirs_ref[...].astype(f32)).astype(bf16)
 
 
-def add_gather_kernel(mine_ref, theirs_ref, out_ref):
+def add_gather_kernel(mine_ref, theirs_ref, after_ref, out_ref):
     mine, theirs = mine_ref[...].astype(f32), theirs_ref[...].astype(f32)
     out_ref[:384, :] = mine[:384] + theirs[:384]
     out_ref[384:512, :] = mine[384:]
@@ -723,7 +691,7 @@
     return lax.ppermute(block, axis, [(i, i ^ distance) for i in range(lax.axis_size(axis))])
 
 
-def total_weights(weights, place, after):
+def total_weights(weights, place, after, last):
     distance, number = 1, 0
     while distance < lax.axis_size("sub"):
         theirs = swapped(weights, "sub", distance)
@@ -738,7 +706,8 @@
     weights = call(
         add_gather_kernel,
         shape(640, 128, f32),
-        [weights, swapped(weights, "grp", 2)],
+        [weights, swapped(weights, "grp", 2), last],
+        [VMEM, VMEM, HBM],
     )
     return call(
         weights_kernel,
@@ -825,7 +794,7 @@
             buffer(rows, features, f32),
             buffer(rows, features, bf16),
             buffer(2 * halo_rows, features, bf16),
-            buffer(rows, features, bf16),
+            buffer(rows, 2 * features, bf16),
             buffer(8 * rows, features, bf16),
             pltpu.SemaphoreType.DMA,
         ],
@@ -905,8 +874,8 @@
     ups, downs, first_grad, second_grad, weights = call(
         fine_backward_kernel,
         [
-            pltpu.HBM((rows, features), bf16),
-            pltpu.HBM((rows, 2 * features), bf16),
+            shape(rows, features, bf16),
+            shape(rows, 2 * features, bf16),
             shape(halo_rows, features, bf16),
             shape(halo_rows, features, bf16),
             shape(4 * features, features, bf16),
@@ -918,16 +887,12 @@
         ],
         [VMEM] * 5 + [HBM] + [VMEM] * 10,
         [
-            buffer(rows, features, bf16),
-            buffer(rows, 2 * features, bf16),
             buffer(rows, features, bf16),
             buffer(2 * halo_rows, features, f32),
             buffer(coarse_rows, features, bf16),
             buffer(8 * rows, features, bf16),
             pltpu.SemaphoreType.DMA((rows // (STEP * BLOCK),)),
-            pltpu.SemaphoreType.DMA((2,)),
-        ],
-        out_specs=[HBM, HBM, VMEM, VMEM, VMEM],
+        ],
         mib=32,
     )
     first_back, second_back = exchange(first_grad, second_grad)
@@ -936,18 +901,10 @@
         finish_kernel,
         pltpu.HBM((rows, features), bf16),
         [ups, downs, first_back, second_back, sends, matrices],
-        [HBM, HBM] + [VMEM] * 4,
-        [
-            buffer(rows, features, bf16),
-            buffer(rows, 2 * features, bf16),
-            buffer(rows, features, bf16),
-            pltpu.SemaphoreType.DMA((rows // CHUNK,)),
-            pltpu.SemaphoreType.DMA((rows // CHUNK,)),
-            pltpu.SemaphoreType.DMA,
-        ],
+        scratch=[buffer(rows, features, bf16), pltpu.SemaphoreType.DMA],
         out_specs=HBM,
     )
-    grad_weights = total_weights(weights, place, ((), (result,), (grad_states,)))
+    grad_weights = total_weights(weights, place, ((), (), (grad_states,)), result)
     return (result, grad_states, grad_weights.reshape(7, features, features))
 
 

time: 98.9 us -> 94.2 us (0.952)
  Pallas kernels: 46.7 us -> 44 us
  waiting for transfers between devices: 18.2 us -> 17 us
    pallas_call x17, Pallas kernels: 46.7 us -> 44 us  [call(): pl.pallas_call(kernel, out_shape=out_shape, in_specs=in_specs, out_specs=...]
    ppermute x9, waiting for transfers between devices: 15.1 us -> 13.8 us  [swapped(): lax.ppermute(block, axis, [(i, i ^ distance) for i in range(lax.axis_size...]
  transfers between devices with their start and end apart: 17 -> 17, of which waited for: 9 -> 10; matrix products, arithmetic and copies ran while one was open for 0% -> 0% of each run, Pallas kernels for 18% -> 17%
where the time goes in v8:
time: 94.2 us; the launch traced here: 93.8 us
  Pallas kernels  44 us (47%)
  starting transfers between devices  32 us (34%)
  waiting for transfers between devices  17 us (18%)
    pallas_call x17, Pallas kernels, call(): pl.pallas_call(kernel, out_shape=out_shape, in_specs=in_specs, out_specs=...  44 us
    ppermute x9, starting transfers between devices, swapped(): lax.ppermute(block, axis, [(i, i ^ distance) for i in range(lax.axis_size...  16.2 us
    ppermute x9, waiting for transfers between devices, swapped(): lax.ppermute(block, axis, [(i, i ^ distance) for i in range(lax.axis_size...  13.8 us
    ppermute x4, starting transfers between devices, exchange(): lax.ppermute(first, 'sub', routes[0])  13 us
    ppermute x4, waiting for transfers between devices, exchange(): lax.ppermute(first, 'sub', routes[0])  3.14 us
    ppermute x4, starting transfers between devices, exchange(): lax.ppermute(second, 'sub', routes[1])  2.81 us
  transfers between devices with their start and end apart: 17, of which 10 were waited for; matrix products, arithmetic and copies ran while one was open for 0% of the time, Pallas kernels for 17%

profile of v8, /device:TPU:0, one launch (start us, length us, event | category | flops | bytes accessed | tf_op | source)
XLA Modules:
  0.0 93.8 jit_solution(5375556154457823453)
XLA Ops:
  0.7 2.8 %shard_map.193 = (bf16[512,128]{1,0:T(8,128)(2,1)S(1)}, bf16[512,128]{1,0:T(8,128)(2,1)S(1)}, bf16[4096,128]{1,0:T(8,128)(2,1)S(1)}) custom-call(s32[2]{0:T(128)S(1)} %pad_add_fusion.place_ref, s32[512]{0:T(512)} %lo_hbm.1, s32[512]{0:T(512)} %hi_hbm.1, bf16[4096,128]{1,0:T(8,128)(2,1)} %x_hbm.1), custom_call_target="tpu_custom_call" | custom-call | tf_op jit(solution)/shard_map/pallas_call | solution.py:52
  4.2 5.8 %collective-permute-start = (bf16[512,128]{1,0:T(8,128)(2,1)S(1)}, bf16[512,128]{1,0:T(8,128)(2,1)S(1)}, u32[]{:S(2)}, u32[]{:S(2)}) collective-permute-start(bf16[512,128]{1,0:T(8,128)(2,1)S(1)} %get-tuple-element.39.rest_7_), channel_id=1, source_target_pairs={{0,1},{2,3},{4,5},{6,7},{1,0},{3,2},{5,4},{7,6},{8,9},{10,11},{12,... | collective-permute-start | bytes 393224 | tf_op jit(solution)/shard_map/ppermute | solution.py:687
  10.0 2.8 %shard_map.194 = (bf16[16,128]{1,0:T(8,128)(2,1)S(1)}, f32[8,4096]{1,0:T(8,128)S(1)}, f32[4096,8]{1,0:T(8,128)S(1)}, f32[8,1024]{1,0:T(8,128)S(1)}, f32[1024,8]{...) custom-call(s32[2]{0:T(128)S(1)} %pad_add_fusion.place_ref, ...), custom_call_target="tpu_custom_call" | custom-call | tf_op jit(solution)/shard_map/pallas_call | solution.py:52
  12.8 2.1 %collective-permute-done.first_ref = bf16[512,128]{1,0:T(8,128)(2,1)S(1)} collective-permute-done((bf16[512,128]{1,0:T(8,128)(2,1)S(1)}, bf16[512,128]{1,0:T(8,128)(2,1)S(1)}, u32[]{:S(2)}, u32[]{:S(2)}) %collective-permute-start) | collective-permute-done | bytes 131104 | tf_op jit(solution)/shard_map/ppermute | solution.py:687
  14.9 11.2 %shard_map.195 = (bf16[4096,128]{1,0:T(8,128)(2,1)S(1)}, bf16[32768,128]{1,0:T(8,128)(2,1)}, bf16[1040,128]{1,0:T(8,128)(2,1)S(1)}) custom-call(bf16[4096,128]{1,0:T(8,128)(2,1)S(1)} %get-tuple-element.38.h_ref, bf16[512,128]{1,0:T(8,128)(2,1)S(1)} %collective-permute-done.first_ref, bf16[512,128]{1,0:T(8,128)(2,1)S(1)} %collective-permute-done.1.second_ref, ...), custom_call_target="tpu_custom_call" | custom-call | tf_op jit(solution)/shard_map/pallas_call | solution.py:52
  26.2 1.5 %collective-permute-done.2.theirs_ref = bf16[1040,128]{1,0:T(8,128)(2,1)S(1)} collective-permute-done((bf16[1040,128]{1,0:T(8,128)(2,1)S(1)}, bf16[1040,128]{1,0:T(8,128)(2,1)S(1)}, u32[]{:S(2)}, u32[]{:S(2)}) %collective-permute-start.2) | collective-permute-done | bytes 266272 | tf_op jit(solution)/shard_map/ppermute | solution.py:691
  27.8 1.6 %collective-permute-start.3 = (bf16[1040,128]{1,0:T(8,128)(2,1)S(1)}, bf16[1040,128]{1,0:T(8,128)(2,1)S(1)}, u32[]{:S(2)}, u32[]{:S(2)}) collective-permute-start(bf16[1040,128]{1,0:T(8,128)(2,1)S(1)} %shard_map.196.after_ref.totals_ref), channel_id=1, source_target_pairs={{0,16},{8,24},{16,0},{24,8},{1,17},{9,25},{17,1},{25,9},{2,18},{10... | collective-permute-start | bytes 798728 | tf_op jit(solution)/shard_map/ppermute | solution.py:691
  29.3 2.8 %shard_map.198.sums_ref = bf16[1024,128]{1,0:T(8,128)(2,1)S(1)} custom-call(s32[32,128]{1,0:T(8,128)S(1)} %get-tuple-element.43.owner_ref, bf16[4096,128]{1,0:T(8,128)(2,1)S(1)} %get-tuple-element.47.g_ref, bf16[1040,128]{1,0:T(8,128)(2,1)S(1)} %get-tuple-element.46.mine_ref.after_ref), custom_call_target="tpu_custom_call" | custom-call | tf_op jit(solution)/shard_map/pallas_call | solution.py:52
  33.8 2.5 %collective-permute-done.3.more_totals_ref = bf16[1040,128]{1,0:T(8,128)(2,1)S(1)} collective-permute-done((bf16[1040,128]{1,0:T(8,128)(2,1)S(1)}, bf16[1040,128]{1,0:T(8,128)(2,1)S(1)}, u32[]{:S(2)}, u32[]{:S(2)}) %collective-permute-start.3) | collective-permute-done | bytes 266272 | tf_op jit(solution)/shard_map/ppermute | solution.py:691
  36.9 1.6 %collective-permute-start.7 = (bf16[1024,128]{1,0:T(8,128)(2,1)S(1)}, bf16[1024,128]{1,0:T(8,128)(2,1)S(1)}, u32[]{:S(2)}, u32[]{:S(2)}) collective-permute-start(bf16[1024,128]{1,0:T(8,128)(2,1)S(1)} %get-tuple-element.52.chip_sums_ref), channel_id=1, source_target_pairs={{0,16},{8,24},{16,0},{24,8},{1,17},{9,25},{17,1},{25,9},{2,18},{10... | collective-permute-start | bytes 786440 | tf_op jit(solution)/shard_map/ppermute | solution.py:691
  38.5 2.5 %collective-permute-start.5 = (bf16[64,128]{1,0:T(8,128)(2,1)S(1)}, bf16[64,128]{1,0:T(8,128)(2,1)S(1)}, u32[]{:S(2)}, u32[]{:S(2)}) collective-permute-start(bf16[64,128]{1,0:T(8,128)(2,1)S(1)} %get-tuple-element.50), channel_id=1, source_target_pairs={{0,1},{2,3},{4,5},{6,7},{1,0},{3,2},{5,4},{7,6},{8,9},{10,11},{12,... | collective-permute-start | bytes 49160 | tf_op jit(solution)/shard_map/ppermute | solution.py:687
  42.7 1.8 %collective-permute-done.7.more_sums_ref = bf16[1024,128]{1,0:T(8,128)(2,1)S(1)} collective-permute-done((bf16[1024,128]{1,0:T(8,128)(2,1)S(1)}, bf16[1024,128]{1,0:T(8,128)(2,1)S(1)}, u32[]{:S(2)}, u32[]{:S(2)}) %collective-permute-start.7) | collective-permute-done | bytes 262176 | tf_op jit(solution)/shard_map/ppermute | solution.py:691
  44.5 2.8 %shard_map.200 = (f32[1024,128]{1,0:T(8,128)S(1)}, bf16[64,128]{1,0:T(8,128)(2,1)S(1)}, bf16[64,128]{1,0:T(8,128)(2,1)S(1)}, bf16[1024,128]{1,0:T(8,128)(2,1)S(1...) custom-call(bf16[1024,128]{1,0:T(8,128)(2,1)S(1)} %get-tuple-element.49.cin_ref, ...), custom_call_target="tpu_custom_call" | custom-call | tf_op jit(solution)/shard_map/pallas_call | solution.py:52
  47.3 3.2 %collective-permute-start.8 = (bf16[64,128]{1,0:T(8,128)(2,1)S(1)}, bf16[64,128]{1,0:T(8,128)(2,1)S(1)}, u32[]{:S(2)}, u32[]{:S(2)}) collective-permute-start(bf16[64,128]{1,0:T(8,128)(2,1)S(1)} %get-tuple-element.56.first_grad_ref), channel_id=1, source_target_pairs={{0,1},{2,3},{4,5},{6,7},{1,0},{3,2},{5,4},{7,6},{8,9},{10,11},{12,... | collective-permute-start | bytes 49160 | tf_op jit(solution)/shard_map/ppermute | solution.py:687
  52.5 9.3 %shard_map.203 = (bf16[4096,128]{1,0:T(8,128)(2,1)S(1)}, bf16[4096,256]{1,0:T(8,128)(2,1)S(1)}, bf16[512,128]{1,0:T(8,128)(2,1)S(1)}, bf16[512,128]{1,0:T(8,128)(2,1)S(1)}, bf16[512,128]{1,0:T(8,128)(2,1)S(1)}) custom-call(bf16[4096,128]{1,0:T(8,128)(2,1)S(1)} %get-tuple-element.38.h_ref, bf16[512,128]{1,0:T(8,128)(2,1)S(1)} %collective-permute-done.first_ref, ...), custom_call_target="tpu_custom_call" | custom-call | tf_op jit(solution)/shard_map/pallas_call | solution.py:52
  61.8 5.1 %collective-permute-start.12 = (bf16[512,128]{1,0:T(8,128)(2,1)S(1)}, bf16[512,128]{1,0:T(8,128)(2,1)S(1)}, u32[]{:S(2)}, u32[]{:S(2)}) collective-permute-start(bf16[512,128]{1,0:T(8,128)(2,1)S(1)} %get-tuple-element.72.mine_ref), channel_id=1, source_target_pairs={{0,1},{1,0},{2,3},{3,2},{4,5},{5,4},{6,7},{7,6},{8,9},{9,8},{10,11... | collective-permute-start | bytes 393224 | tf_op jit(solution)/shard_map/ppermute | solution.py:691
  66.9 2.9 %collective-permute-done.12.theirs_ref = bf16[512,128]{1,0:T(8,128)(2,1)S(1)} collective-permute-done((bf16[512,128]{1,0:T(8,128)(2,1)S(1)}, bf16[512,128]{1,0:T(8,128)(2,1)S(1)}, u32[]{:S(2)}, u32[]{:S(2)}) %collective-permute-start.12) | collective-permute-done | bytes 131104 | tf_op jit(solution)/shard_map/ppermute | solution.py:691
  69.9 4.1 %collective-permute-start.13 = (bf16[512,128]{1,0:T(8,128)(2,1)S(1)}, bf16[512,128]{1,0:T(8,128)(2,1)S(1)}, u32[]{:S(2)}, u32[]{:S(2)}) collective-permute-start(bf16[512,128]{1,0:T(8,128)(2,1)S(1)} %shard_map.205.mine_ref), channel_id=1, source_target_pairs={{0,2},{1,3},{2,0},{3,1},{4,6},{5,7},{6,4},{7,5},{8,10},{9,11},{10,... | collective-permute-start | bytes 393224 | tf_op jit(solution)/shard_map/ppermute | solution.py:691
  74.0 1.5 %collective-permute-start.10 = (bf16[512,128]{1,0:T(8,128)(2,1)S(1)}, bf16[512,128]{1,0:T(8,128)(2,1)S(1)}, u32[]{:S(2)}, u32[]{:S(2)}) collective-permute-start(bf16[512,128]{1,0:T(8,128)(2,1)S(1)} %get-tuple-element.69), channel_id=1, source_target_pairs={{0,1},{2,3},{4,5},{6,7},{1,0},{3,2},{5,4},{7,6},{8,9},{10,11},{12,... | collective-permute-start | bytes 393224 | tf_op jit(solution)/shard_map/ppermute | solution.py:687
  76.2 1.8 %collective-permute-done.13.theirs_ref = bf16[512,128]{1,0:T(8,128)(2,1)S(1)} collective-permute-done((bf16[512,128]{1,0:T(8,128)(2,1)S(1)}, bf16[512,128]{1,0:T(8,128)(2,1)S(1)}, u32[]{:S(2)}, u32[]{:S(2)}) %collective-permute-start.13) | collective-permute-done | bytes 131104 | tf_op jit(solution)/shard_map/ppermute | solution.py:691
  78.0 2.3 %collective-permute-start.14 = (bf16[512,128]{1,0:T(8,128)(2,1)S(1)}, bf16[512,128]{1,0:T(8,128)(2,1)S(1)}, u32[]{:S(2)}, u32[]{:S(2)}) collective-permute-start(bf16[512,128]{1,0:T(8,128)(2,1)S(1)} %shard_map.206.mine_ref), channel_id=1, source_target_pairs={{0,4},{1,5},{2,6},{3,7},{4,0},{5,1},{6,2},{7,3},{8,12},{9,13},{10,... | collective-permute-start | bytes 393224 | tf_op jit(solution)/shard_map/ppermute | solution.py:691
  80.4 4.4 %shard_map.204.rest_0_ = bf16[4096,128]{1,0:T(8,128)(2,1)} custom-call(bf16[4096,128]{1,0:T(8,128)(2,1)S(1)} %get-tuple-element.67.ups_ref, bf16[4096,256]{1,0:T(8,128)(2,1)S(1)} %get-tuple-element.68.downs_ref, bf16[512,128]{1,0:T(8,128)(2,1)S(1)} %collective-permute-done.10.first_back_ref, bf16[512,128]{1,0:T(8,128)(2,1)S(1)} %collective-permute-done.11.second_back_ref, ...), custom_call_target="tpu_custom_call" | custom-call | tf_op jit(solution)/shard_map/pallas_call | solution.py:52
  86.7 4.0 %shard_map.202.after_ref = bf16[4096,128]{1,0:T(8,128)(2,1)} custom-call(bf16[4096,128]{1,0:T(8,128)(2,1)S(1)} %get-tuple-element.38.h_ref, bf16[4096,128]{1,0:T(8,128)(2,1)S(1)} %get-tuple-element.45.summed_ref, bf16[896,128]{1,0:T(8,128)(2,1)S(1)} %get-tuple-element.41.weights_ref.matrices_ref, f32[4096,8]{1,0:T(8,128)S(1)} %shard_map.197.after_ref.owners_ref, ...), custom_call_target="tpu_custom_call" | custom-call | tf_op jit(solution)/shard_map/pallas_call | solution.py:52
  90.8 1.6 %collective-permute-done.16.theirs_ref = f32[640,128]{1,0:T(8,128)S(1)} collective-permute-done((f32[640,128]{1,0:T(8,128)S(1)}, f32[640,128]{1,0:T(8,128)S(1)}, u32[]{:S(2)}, u32[]{:S(2)}) %collective-permute-start.16) | collective-permute-done | bytes 327712 | tf_op jit(solution)/shard_map/ppermute | solution.py:691
  (28 shorter events, 11.0 us)
Async XLA Ops:
  3.5 9.2 %collective-permute-start.1 = (bf16[512,128]{1,0:T(8,128)(2,1)S(1)}, bf16[512,128]{1,0:T(8,128)(2,1)S(1)}, u32[]{:S(2)}, u32[]{:S(2)}) collective-permute-start(bf16[512,128]{1,0:T(8,128)(2,1)S(1)} %get-tuple-element.40), channel_id=1, source_target_pairs={{1,2},{3,4},{5,6},{2,1},{4,3},{6,5},{9,10},{11,12},{13,14},{10,9},... | collective-permute-start | bytes 393224 | tf_op jit(solution)/shard_map/ppermute | solution.py:687
  4.2 10.6 %collective-permute-start = (bf16[512,128]{1,0:T(8,128)(2,1)S(1)}, bf16[512,128]{1,0:T(8,128)(2,1)S(1)}, u32[]{:S(2)}, u32[]{:S(2)}) collective-permute-start(bf16[512,128]{1,0:T(8,128)(2,1)S(1)} %get-tuple-element.39.rest_7_), channel_id=1, source_target_pairs={{0,1},{2,3},{4,5},{6,7},{1,0},{3,2},{5,4},{7,6},{8,9},{10,11},{12,... | collective-permute-start | bytes 393224 | tf_op jit(solution)/shard_map/ppermute | solution.py:687
  26.1 1.6 %collective-permute-start.2 = (bf16[1040,128]{1,0:T(8,128)(2,1)S(1)}, bf16[1040,128]{1,0:T(8,128)(2,1)S(1)}, u32[]{:S(2)}, u32[]{:S(2)}) collective-permute-start(bf16[1040,128]{1,0:T(8,128)(2,1)S(1)} %get-tuple-element.46.mine_ref.after_ref), channel_id=1, source_target_pairs={{0,8},{8,0},{16,24},{24,16},{1,9},{9,1},{17,25},{25,17},{2,10},{10... | collective-permute-start | bytes 798728 | tf_op jit(solution)/shard_map/ppermute | solution.py:691
  27.8 8.5 %collective-permute-start.3 = (bf16[1040,128]{1,0:T(8,128)(2,1)S(1)}, bf16[1040,128]{1,0:T(8,128)(2,1)S(1)}, u32[]{:S(2)}, u32[]{:S(2)}) collective-permute-start(bf16[1040,128]{1,0:T(8,128)(2,1)S(1)} %shard_map.196.after_ref.totals_ref), channel_id=1, source_target_pairs={{0,16},{8,24},{16,0},{24,8},{1,17},{9,25},{17,1},{25,9},{2,18},{10... | collective-permute-start | bytes 798728 | tf_op jit(solution)/shard_map/ppermute | solution.py:691
  32.1 1.6 %collective-permute-start.4 = (bf16[1024,128]{1,0:T(8,128)(2,1)S(1)}, bf16[1024,128]{1,0:T(8,128)(2,1)S(1)}, u32[]{:S(2)}, u32[]{:S(2)}) collective-permute-start(bf16[1024,128]{1,0:T(8,128)(2,1)S(1)} %shard_map.198.sums_ref), channel_id=1, source_target_pairs={{0,8},{8,0},{16,24},{24,16},{1,9},{9,1},{17,25},{25,17},{2,10},{10... | collective-permute-start | bytes 786440 | tf_op jit(solution)/shard_map/ppermute | solution.py:691
  36.9 7.6 %collective-permute-start.7 = (bf16[1024,128]{1,0:T(8,128)(2,1)S(1)}, bf16[1024,128]{1,0:T(8,128)(2,1)S(1)}, u32[]{:S(2)}, u32[]{:S(2)}) collective-permute-start(bf16[1024,128]{1,0:T(8,128)(2,1)S(1)} %get-tuple-element.52.chip_sums_ref), channel_id=1, source_target_pairs={{0,16},{8,24},{16,0},{24,8},{1,17},{9,25},{17,1},{25,9},{2,18},{10... | collective-permute-start | bytes 786440 | tf_op jit(solution)/shard_map/ppermute | solution.py:691
  38.5 4.2 %collective-permute-start.5 = (bf16[64,128]{1,0:T(8,128)(2,1)S(1)}, bf16[64,128]{1,0:T(8,128)(2,1)S(1)}, u32[]{:S(2)}, u32[]{:S(2)}) collective-permute-start(bf16[64,128]{1,0:T(8,128)(2,1)S(1)} %get-tuple-element.50), channel_id=1, source_target_pairs={{0,1},{2,3},{4,5},{6,7},{1,0},{3,2},{5,4},{7,6},{8,9},{10,11},{12,... | collective-permute-start | bytes 49160 | tf_op jit(solution)/shard_map/ppermute | solution.py:687
  41.0 1.7 %collective-permute-start.6 = (bf16[64,128]{1,0:T(8,128)(2,1)S(1)}, bf16[64,128]{1,0:T(8,128)(2,1)S(1)}, u32[]{:S(2)}, u32[]{:S(2)}) collective-permute-start(bf16[64,128]{1,0:T(8,128)(2,1)S(1)} %get-tuple-element.51), channel_id=1, source_target_pairs={{1,2},{3,4},{5,6},{2,1},{4,3},{6,5},{9,10},{11,12},{13,14},{10,9},... | collective-permute-start | bytes 49160 | tf_op jit(solution)/shard_map/ppermute | solution.py:687
  47.3 5.2 %collective-permute-start.8 = (bf16[64,128]{1,0:T(8,128)(2,1)S(1)}, bf16[64,128]{1,0:T(8,128)(2,1)S(1)}, u32[]{:S(2)}, u32[]{:S(2)}) collective-permute-start(bf16[64,128]{1,0:T(8,128)(2,1)S(1)} %get-tuple-element.56.first_grad_ref), channel_id=1, source_target_pairs={{0,1},{2,3},{4,5},{6,7},{1,0},{3,2},{5,4},{7,6},{8,9},{10,11},{12,... | collective-permute-start | bytes 49160 | tf_op jit(solution)/shard_map/ppermute | solution.py:687
  50.5 2.0 %collective-permute-start.9 = (bf16[64,128]{1,0:T(8,128)(2,1)S(1)}, bf16[64,128]{1,0:T(8,128)(2,1)S(1)}, u32[]{:S(2)}, u32[]{:S(2)}) collective-permute-start(bf16[64,128]{1,0:T(8,128)(2,1)S(1)} %get-tuple-element.57.second_grad_ref), channel_id=1, source_target_pairs={{1,2},{3,4},{5,6},{2,1},{4,3},{6,5},{9,10},{11,12},{13,14},{10,9},... | collective-permute-start | bytes 49160 | tf_op jit(solution)/shard_map/ppermute | solution.py:687
  61.8 8.0 %collective-permute-start.12 = (bf16[512,128]{1,0:T(8,128)(2,1)S(1)}, bf16[512,128]{1,0:T(8,128)(2,1)S(1)}, u32[]{:S(2)}, u32[]{:S(2)}) collective-permute-start(bf16[512,128]{1,0:T(8,128)(2,1)S(1)} %get-tuple-element.72.mine_ref), channel_id=1, source_target_pairs={{0,1},{1,0},{2,3},{3,2},{4,5},{5,4},{6,7},{7,6},{8,9},{9,8},{10,11... | collective-permute-start | bytes 393224 | tf_op jit(solution)/shard_map/ppermute | solution.py:691
  69.9 8.1 %collective-permute-start.13 = (bf16[512,128]{1,0:T(8,128)(2,1)S(1)}, bf16[512,128]{1,0:T(8,128)(2,1)S(1)}, u32[]{:S(2)}, u32[]{:S(2)}) collective-permute-start(bf16[512,128]{1,0:T(8,128)(2,1)S(1)} %shard_map.205.mine_ref), channel_id=1, source_target_pairs={{0,2},{1,3},{2,0},{3,1},{4,6},{5,7},{6,4},{7,5},{8,10},{9,11},{10,... | collective-permute-start | bytes 393224 | tf_op jit(solution)/shard_map/ppermute | solution.py:691
  74.0 6.4 %collective-permute-start.10 = (bf16[512,128]{1,0:T(8,128)(2,1)S(1)}, bf16[512,128]{1,0:T(8,128)(2,1)S(1)}, u32[]{:S(2)}, u32[]{:S(2)}) collective-permute-start(bf16[512,128]{1,0:T(8,128)(2,1)S(1)} %get-tuple-element.69), channel_id=1, source_target_pairs={{0,1},{2,3},{4,5},{6,7},{1,0},{3,2},{5,4},{7,6},{8,9},{10,11},{12,... | collective-permute-start | bytes 393224 | tf_op jit(solution)/shard_map/ppermute | solution.py:687
  75.5 4.9 %collective-permute-start.11 = (bf16[512,128]{1,0:T(8,128)(2,1)S(1)}, bf16[512,128]{1,0:T(8,128)(2,1)S(1)}, u32[]{:S(2)}, u32[]{:S(2)}) collective-permute-start(bf16[512,128]{1,0:T(8,128)(2,1)S(1)} %get-tuple-element.70), channel_id=1, source_target_pairs={{1,2},{3,4},{5,6},{2,1},{4,3},{6,5},{9,10},{11,12},{13,14},{10,9},... | collective-permute-start | bytes 393224 | tf_op jit(solution)/shard_map/ppermute | solution.py:687
  78.0 7.3 %collective-permute-start.14 = (bf16[512,128]{1,0:T(8,128)(2,1)S(1)}, bf16[512,128]{1,0:T(8,128)(2,1)S(1)}, u32[]{:S(2)}, u32[]{:S(2)}) collective-permute-start(bf16[512,128]{1,0:T(8,128)(2,1)S(1)} %shard_map.206.mine_ref), channel_id=1, source_target_pairs={{0,4},{1,5},{2,6},{3,7},{4,0},{5,1},{6,2},{7,3},{8,12},{9,13},{10,... | collective-permute-start | bytes 393224 | tf_op jit(solution)/shard_map/ppermute | solution.py:691
  85.4 5.3 %collective-permute-start.15 = (bf16[512,128]{1,0:T(8,128)(2,1)S(1)}, bf16[512,128]{1,0:T(8,128)(2,1)S(1)}, u32[]{:S(2)}, u32[]{:S(2)}) collective-permute-start(bf16[512,128]{1,0:T(8,128)(2,1)S(1)} %shard_map.207.mine_ref), channel_id=1, source_target_pairs={{0,16},{8,24},{16,0},{24,8},{1,17},{9,25},{17,1},{25,9},{2,18},{10... | collective-permute-start | bytes 393224 | tf_op jit(solution)/shard_map/ppermute | solution.py:691
  90.8 1.7 %collective-permute-start.16 = (f32[640,128]{1,0:T(8,128)S(1)}, f32[640,128]{1,0:T(8,128)S(1)}, u32[]{:S(2)}, u32[]{:S(2)}) collective-permute-start(f32[640,128]{1,0:T(8,128)S(1)} %shard_map.208.mine_ref), channel_id=1, source_target_pairs={{0,8},{8,0},{16,24},{24,16},{1,9},{9,1},{17,25},{25,17},{2,10},{10... | collective-permute-start | bytes 983048 | tf_op jit(solution)/shard_map/ppermute | solution.py:691

commit v9 on v8

--- a/solution.py
+++ b/solution.py
@@ -337,7 +337,20 @@
     owners_ref[...] = owner_columns(owner_ref)
 
 
+def half_totals(owner_ref, new_ref, counts_ref, half, out_ref):
+    tiles = (out_ref.shape[0] - counts_ref.shape[0]) // 256
+    for tile in range(tiles):
+        totals = owner_sums(owner_ref, half * tiles + tile, new_ref[...])
+        out_ref[256 * tile : 256 * (tile + 1), :] = totals.astype(bf16)
+    out_ref[256 * tiles :, :] = counts_ref[...]
+
+
+def keep_kernel(place_ref, owner_ref, new_ref, counts_ref, out_ref):
+    half_totals(owner_ref, new_ref, counts_ref, lax.rem(place_ref[1], 2), out_ref)
+
+
 def fine_forward_kernel(
+    place_ref,
     h_ref,
     first_ref,
     second_ref,
@@ -347,11 +360,11 @@
     counts_ref,
     summed_ref,
     slope_hbm,
-    totals_ref,
+    new_ref,
+    give_ref,
     own,
     far,
     halo,
-    new,
     slope_ref,
     sem,
 ):
@@ -368,92 +381,110 @@
         return carry
 
     lax.fori_loop(0, h_ref.shape[0] // (STEP * BLOCK), step, None)
-    new[...] = jnp.concatenate([h_ref[...], summed_ref[...]], 1)
-    coarse_rows = totals_ref.shape[0] - counts_ref.shape[0]
-
-    def tile_step(tile, carry):
-        sums = owner_sums(owner_ref, tile, new[...])
-        totals = sums[:, :128] + dot(sums[:, 128:].astype(bf16), matrix(weights_ref, 2))
-        totals_ref[chunk_of(tile, 256), :] = totals.astype(bf16)
-        return carry
-
-    lax.fori_loop(0, coarse_rows // 256, tile_step, None)
-    totals_ref[coarse_rows:, :] = counts_ref[...]
+    new_ref[...] = (
+        h_ref[...].astype(f32) + dot(summed_ref[...], matrix(weights_ref, 2))
+    ).astype(bf16)
+    half_totals(owner_ref, new_ref, counts_ref, 1 - lax.rem(place_ref[1], 2), give_ref)
     pltpu.make_async_copy(slope_ref, slope_hbm, sem).wait()
 
 
+def half_kernel(place_ref, totals_ref, more_totals_ref, after_ref, half_ref, counts_ref):
+    half_rows = half_ref.shape[0]
+    totals = totals_ref[...].astype(f32) + more_totals_ref[...].astype(f32)
+    digits = totals[half_rows:]
+    tiles = counts_ref.shape[0]
+    counts_ref[...] = DIGIT * digits[:tiles] + digits[tiles:]
+    per_row = counts_ref[...].T
+    first = lax.rem(place_ref[1], 2) == 0
+    for tile in range(tiles // 2):
+        here = slice(tile * 128, (tile + 1) * 128)
+        later = tile + tiles // 2
+        count = jnp.where(first, per_row[:, tile : tile + 1], per_row[:, later : later + 1])
+        half_ref[here, :] = (totals[here] / count).astype(bf16)
+
+
 def coarse_input_kernel(
-    totals_ref,
-    more_totals_ref,
+    place_ref,
+    half_ref,
+    their_half_ref,
     sums_ref,
     more_sums_ref,
     sends_ref,
-    after_ref,
     cin_ref,
     first_ref,
     second_ref,
     chip_sums_ref,
-    counts_ref,
 ):
-    coarse_rows = cin_ref.shape[0]
-    tiles = coarse_rows // 128
-    chip_sums_ref[...] = (sums_ref[...].astype(f32) + more_sums_ref[...].astype(f32)).astype(bf16)
-    totals = totals_ref[...].astype(f32) + more_totals_ref[...].astype(f32)
-    digits = totals[coarse_rows:]
-    counts_ref[...] = DIGIT * digits[:tiles] + digits[tiles:]
-    per_row = counts_ref[...].T
-    for tile in range(tiles):
-        here = slice(tile * 128, (tile + 1) * 128)
-        cin_ref[here, :] = (totals[here] / per_row[:, tile : tile + 1]).astype(bf16)
-    cin = cin_ref[...]
-    place = lax.broadcasted_iota(jnp.int32, (coarse_rows, sends_ref.shape[1]), 0)
+    mine, theirs = half_ref[...], their_half_ref[...]
+    first = lax.rem(place_ref[1], 2) == 0
+    cin = jnp.concatenate([jnp.where(first, mine, theirs), jnp.where(first, theirs, mine)], 0)
+    cin_ref[...] = cin
+    place = lax.broadcasted_iota(jnp.int32, (cin.shape[0], sends_ref.shape[1]), 0)
     sent = dot_tn(pick(sends_ref[...] == place), cin).astype(bf16)
     halo_rows = first_ref.shape[0]
     first_ref[...] = sent[:halo_rows]
     second_ref[...] = sent[halo_rows:]
-
-
-def coarse_kernel(
+    chip_sums_ref[...] = (sums_ref[...].astype(f32) + more_sums_ref[...].astype(f32)).astype(bf16)
+
+
+def coarse_forward_kernel(
     cin_ref,
     first_ref,
     second_ref,
+    weights_ref,
+    columns_t_ref,
+    summed_ref,
+    slope_ref,
+    own,
+    far,
+    halo,
+):
+    self_weight, other_weight = matrix(weights_ref, 3), matrix(weights_ref, 4)
+    level_terms(cin_ref, (first_ref, second_ref), self_weight, other_weight, own, far, halo)
+
+    def step(index, carry):
+        here = chunk_of(index, STEP * BLOCK)
+        total, slopes = edges(own[here, :], far[here, :], columns_t_ref[here, :], halo)
+        summed_ref[here, :] = total
+        slope_ref[chunk_of(index, 8 * STEP * BLOCK), :] = jnp.concatenate(slopes, 0)
+        return carry
+
+    lax.fori_loop(0, cin_ref.shape[0] // (STEP * BLOCK), step, None)
+
+
+def coarse_backward_kernel(
+    slope_ref,
     chip_sums_ref,
     more_sums_ref,
     weights_ref,
     columns_ref,
-    columns_t_ref,
     part_ref,
     first_grad_ref,
     second_grad_ref,
     sums_ref,
-    summed_ref,
     ups_ref,
     downs_ref,
-    own,
-    far,
-    halo,
     grad_sum,
     halo_grad,
 ):
-    halo_rows = first_ref.shape[0]
-    self_weight, other_weight = matrix(weights_ref, 3), matrix(weights_ref, 4)
-    level_terms(cin_ref, (first_ref, second_ref), self_weight, other_weight, own, far, halo)
+    halo_rows = first_grad_ref.shape[0]
     halo_grad[...] = jnp.zeros_like(halo_grad)
     sums_ref[...] = (chip_sums_ref[...].astype(f32) + more_sums_ref[...].astype(f32)).astype(bf16)
     part_ref[...] = dot_nt(sums_ref[...], matrix(weights_ref, 6))
     ups_ref[...] = part_ref[...].astype(bf16)
     grad_sum[...] = (dot_nt(ups_ref[...], matrix(weights_ref, 5)) * 0.5).astype(bf16)
+    count = STEP * BLOCK
 
     def step(index, carry):
-        here = chunk_of(index, STEP * BLOCK)
-        total, slopes = edges(own[here, :], far[here, :], columns_t_ref[here, :], halo)
-        summed_ref[here, :] = total
+        here = chunk_of(index, count)
+        slope = slope_ref[chunk_of(index, 8 * count), :]
+        slopes = [slope[n * 8 * BLOCK : (n + 1) * 8 * BLOCK] for n in range(STEP)]
         downs_ref[here, :] = edges_back(
             slopes, grad_sum[here, :], columns_ref[:, here], halo_grad
         )
         return carry
 
-    lax.fori_loop(0, cin_ref.shape[0] // (STEP * BLOCK), step, None)
+    lax.fori_loop(0, part_ref.shape[0] // count, step, None)
     first_grad_ref[...] = halo_grad[:halo_rows, :].astype(bf16)
     second_grad_ref[...] = halo_grad[halo_rows:, :].astype(bf16)
 
@@ -782,72 +813,88 @@
         + [pltpu.SemaphoreType.DMA((17,))],
     )
 
-    summed, slope, totals = call(
+    half_rows = coarse_rows // 2 + 2 * count_rows
+    summed, slope, new, give = call(
         fine_forward_kernel,
         [
             shape(rows, features, bf16),
             pltpu.HBM((8 * rows, features), bf16),
-            shape(coarse_rows + 2 * count_rows, features, bf16),
-        ],
-        [states, first, second, matrices, columns_t, owner, counts],
-        scratch=[
+            shape(rows, features, bf16),
+            shape(half_rows, features, bf16),
+        ],
+        [place, states, first, second, matrices, columns_t, owner, counts],
+        [SMEM] + [VMEM] * 7,
+        [
             buffer(rows, features, f32),
             buffer(rows, features, bf16),
             buffer(2 * halo_rows, features, bf16),
-            buffer(rows, 2 * features, bf16),
             buffer(8 * rows, features, bf16),
             pltpu.SemaphoreType.DMA,
         ],
-        out_specs=[VMEM, HBM, VMEM],
+        [VMEM, HBM, VMEM, VMEM],
         mib=32,
     )
-    chip_totals = call(
-        add_kernel, shape(*totals.shape, bf16), [totals, swapped(totals, "grp", 1)]
-    )
+    theirs = swapped(give, "grp", 1)
+    keep = call(
+        keep_kernel,
+        shape(half_rows, features, bf16),
+        [place, owner, new, counts],
+        [SMEM] + [VMEM] * 3,
+    )
+    chip_totals = call(add_kernel, shape(half_rows, features, bf16), [keep, theirs])
     more_totals = swapped(chip_totals, "grp", 2)
     sums = call(
         sums_kernel,
         shape(coarse_rows, features, bf16),
-        [owner, cotangent, totals],
+        [owner, cotangent, chip_totals],
         [VMEM, VMEM, ANY],
     )
     more_sums = swapped(sums, "grp", 1)
-    owners_t = call(owners_kernel, shape(rows, 8, f32), [owner, chip_totals], [VMEM, ANY])
-
-    coarse_in, to_first, to_second, chip_sums, counts = call(
+    owners_t = call(owners_kernel, shape(rows, 8, f32), [owner, sums], [VMEM, ANY])
+
+    half, counts = call(
+        half_kernel,
+        [shape(coarse_rows // 2, features, bf16), shape(count_rows, features, f32)],
+        [place, chip_totals, more_totals, sums],
+        [SMEM, VMEM, VMEM, ANY],
+    )
+    their_half = swapped(half, "grp", 1)
+    coarse_in, to_first, to_second, chip_sums = call(
         coarse_input_kernel,
         [
             shape(coarse_rows, features, bf16),
             shape(coarse_halo, features, bf16),
             shape(coarse_halo, features, bf16),
             shape(coarse_rows, features, bf16),
-            shape(count_rows, features, f32),
-        ],
-        [chip_totals, more_totals, sums, more_sums, coarse_sends, owners_t],
-        [VMEM] * 5 + [ANY],
+        ],
+        [place, half, their_half, sums, more_sums, coarse_sends],
+        [SMEM] + [VMEM] * 5,
     )
     coarse_first, coarse_second = exchange(to_first, to_second)
     more_sums = swapped(chip_sums, "grp", 2)
 
-    coarse_part, first_grad, second_grad, sums, coarse_sum, coarse_ups, coarse_downs = call(
-        coarse_kernel,
+    coarse_sum, coarse_slope = call(
+        coarse_forward_kernel,
+        [shape(coarse_rows, features, bf16), shape(8 * coarse_rows, features, bf16)],
+        [coarse_in, coarse_first, coarse_second, matrices, coarse_columns_t],
+        scratch=[
+            buffer(coarse_rows, features, f32),
+            buffer(coarse_rows, features, bf16),
+            buffer(2 * coarse_halo, features, bf16),
+        ],
+    )
+    coarse_part, first_grad, second_grad, sums, coarse_ups, coarse_downs = call(
+        coarse_backward_kernel,
         [
             shape(coarse_rows, features, f32),
             shape(coarse_halo, features, bf16),
             shape(coarse_halo, features, bf16),
             shape(coarse_rows, features, bf16),
             shape(coarse_rows, features, bf16),
-            shape(coarse_rows, features, bf16),
             shape(coarse_rows, 2 * features, bf16),
         ],
-        [
-            coarse_in, coarse_first, coarse_second, chip_sums, more_sums, matrices,
-            coarse_columns, coarse_columns_t,
-        ],
+        [coarse_slope, chip_sums, more_sums, matrices, coarse_columns],
         scratch=[
-            buffer(coarse_rows, features, f32),
-            buffer(coarse_rows, features, bf16),
-            buffer(2 * coarse_halo, features, bf16),
             buffer(coarse_rows, features, bf16),
             buffer(2 * coarse_halo, features, f32),
         ],

time: 94.2 us -> 94.1 us (level)
  waiting for transfers between devices: 17 us -> 14.3 us
  Pallas kernels: 44 us -> 46 us
    ppermute x9 -> x10, waiting for transfers between devices: 13.8 us -> 11.2 us  [swapped(): lax.ppermute(block, axis, [(i, i ^ distance) for i in range(lax.axis_size...]
    pallas_call x17 -> x20, Pallas kernels: 44 us -> 46 us  [call(): pl.pallas_call(kernel, out_shape=out_shape, in_specs=in_specs, out_specs=...]
    ppermute x4, starting transfers between devices: 13 us -> 14 us  [exchange(): lax.ppermute(first, 'sub', routes[0])]
    ppermute x9 -> x10, starting transfers between devices: 16.2 us -> 15.8 us  [swapped(): lax.ppermute(block, axis, [(i, i ^ distance) for i in range(lax.axis_size...]
  transfers between devices with their start and end apart: 17 -> 18, of which waited for: 10 -> 10; matrix products, arithmetic and copies ran while one was open for 0% -> 0% of each run, Pallas kernels for 17% -> 21%
where the time goes in v9:
time: 94.1 us; the launch traced here: 93.9 us
  Pallas kernels  46 us (49%)
  starting transfers between devices  32.6 us (35%)
  waiting for transfers between devices  14.3 us (15%)
    pallas_call x20, Pallas kernels, call(): pl.pallas_call(kernel, out_shape=out_shape, in_specs=in_specs, out_specs=...  46 us
    ppermute x10, starting transfers between devices, swapped(): lax.ppermute(block, axis, [(i, i ^ distance) for i in range(lax.axis_size...  15.8 us
    ppermute x4, starting transfers between devices, exchange(): lax.ppermute(first, 'sub', routes[0])  14 us
    ppermute x10, waiting for transfers between devices, swapped(): lax.ppermute(block, axis, [(i, i ^ distance) for i in range(lax.axis_size...  11.2 us
    ppermute x4, waiting for transfers between devices, exchange(): lax.ppermute(first, 'sub', routes[0])  3.14 us
    ppermute x4, starting transfers between devices, exchange(): lax.ppermute(second, 'sub', routes[1])  2.81 us
  transfers between devices with their start and end apart: 18, of which 10 were waited for; matrix products, arithmetic and copies ran while one was open for 0% of the time, Pallas kernels for 21%

profile of v9, /device:TPU:0, one launch (start us, length us, event | category | flops | bytes accessed | tf_op | source)
XLA Modules:
  0.0 93.9 jit_solution(17079782078451949461)
XLA Ops:
  0.7 2.8 %shard_map.193 = (bf16[512,128]{1,0:T(8,128)(2,1)S(1)}, bf16[512,128]{1,0:T(8,128)(2,1)S(1)}, bf16[4096,128]{1,0:T(8,128)(2,1)S(1)}) custom-call(s32[2]{0:T(128)S(1)} %pad_add_fusion.place_ref, s32[512]{0:T(512)} %lo_hbm.1, s32[512]{0:T(512)} %hi_hbm.1, bf16[4096,128]{1,0:T(8,128)(2,1)} %x_hbm.1), custom_call_target="tpu_custom_call" | custom-call | tf_op jit(solution)/shard_map/pallas_call | solution.py:52
  4.2 5.8 %collective-permute-start = (bf16[512,128]{1,0:T(8,128)(2,1)S(1)}, bf16[512,128]{1,0:T(8,128)(2,1)S(1)}, u32[]{:S(2)}, u32[]{:S(2)}) collective-permute-start(bf16[512,128]{1,0:T(8,128)(2,1)S(1)} %get-tuple-element.42.rest_7_), channel_id=1, source_target_pairs={{0,1},{2,3},{4,5},{6,7},{1,0},{3,2},{5,4},{7,6},{8,9},{10,11},{12,... | collective-permute-start | bytes 393224 | tf_op jit(solution)/shard_map/ppermute | solution.py:718
  10.0 2.8 %shard_map.194 = (bf16[16,128]{1,0:T(8,128)(2,1)S(1)}, f32[8,4096]{1,0:T(8,128)S(1)}, f32[4096,8]{1,0:T(8,128)S(1)}, f32[8,1024]{1,0:T(8,128)S(1)}, f32[1024,8]{...) custom-call(s32[2]{0:T(128)S(1)} %pad_add_fusion.place_ref, ...), custom_call_target="tpu_custom_call" | custom-call | tf_op jit(solution)/shard_map/pallas_call | solution.py:52
  12.8 2.1 %collective-permute-done.first_ref = bf16[512,128]{1,0:T(8,128)(2,1)S(1)} collective-permute-done((bf16[512,128]{1,0:T(8,128)(2,1)S(1)}, bf16[512,128]{1,0:T(8,128)(2,1)S(1)}, u32[]{:S(2)}, u32[]{:S(2)}) %collective-permute-start) | collective-permute-done | bytes 131104 | tf_op jit(solution)/shard_map/ppermute | solution.py:718
  14.9 9.7 %shard_map.195 = (bf16[4096,128]{1,0:T(8,128)(2,1)S(1)}, bf16[32768,128]{1,0:T(8,128)(2,1)}, bf16[4096,128]{1,0:T(8,128)(2,1)S(1)}, bf16[528,128]{1,0:T(8,128)(2,1)S(1)}) custom-call(s32[2]{0:T(128)S(1)} %pad_add_fusion.place_ref, bf16[4096,128]{1,0:T(8,128)(2,1)S(1)} %get-tuple-element.41.h_ref, bf16[512,128]{1,0:T(8,128)(2,1)S(1)} %collective-permute-done.first_ref, ...), custom_call_target="tpu_custom_call" | custom-call | tf_op jit(solution)/shard_map/pallas_call | solution.py:52
  24.7 1.8 %shard_map.196.mine_ref = bf16[528,128]{1,0:T(8,128)(2,1)S(1)} custom-call(s32[2]{0:T(128)S(1)} %pad_add_fusion.place_ref, s32[32,128]{1,0:T(8,128)S(1)} %get-tuple-element.46.owner_ref, bf16[4096,128]{1,0:T(8,128)(2,1)S(1)} %get-tuple-element.50.new_ref, bf16[16,128]{1,0:T(8,128)(2,1)S(1)} %get-tuple-element.47.counts_ref), custom_call_target="tpu_custom_call" | custom-call | tf_op jit(solution)/shard_map/pallas_call | solution.py:52
  26.5 1.6 %collective-permute-start.3 = (bf16[528,128]{1,0:T(8,128)(2,1)S(1)}, bf16[528,128]{1,0:T(8,128)(2,1)S(1)}, u32[]{:S(2)}, u32[]{:S(2)}) collective-permute-start(bf16[528,128]{1,0:T(8,128)(2,1)S(1)} %shard_map.197.after_ref.totals_ref), channel_id=1, source_target_pairs={{0,16},{8,24},{16,0},{24,8},{1,17},{9,25},{17,1},{25,9},{2,18},{10... | collective-permute-start | bytes 405512 | tf_op jit(solution)/shard_map/ppermute | solution.py:722
  28.1 2.8 %shard_map.198.after_ref.sums_ref = bf16[1024,128]{1,0:T(8,128)(2,1)S(1)} custom-call(s32[32,128]{1,0:T(8,128)S(1)} %get-tuple-element.46.owner_ref, bf16[4096,128]{1,0:T(8,128)(2,1)S(1)} %get-tuple-element.49.g_ref, bf16[528,128]{1,0:T(8,128)(2,1)S(1)} %shard_map.197.after_ref.totals_ref), custom_call_target="tpu_custom_call" | custom-call | tf_op jit(solution)/shard_map/pallas_call | solution.py:52
  31.2 1.4 %collective-permute-done.3.more_totals_ref = bf16[528,128]{1,0:T(8,128)(2,1)S(1)} collective-permute-done((bf16[528,128]{1,0:T(8,128)(2,1)S(1)}, bf16[528,128]{1,0:T(8,128)(2,1)S(1)}, u32[]{:S(2)}, u32[]{:S(2)}) %collective-permute-start.3) | collective-permute-done | bytes 135200 | tf_op jit(solution)/shard_map/ppermute | solution.py:722
  35.7 1.6 %collective-permute-start.8 = (bf16[1024,128]{1,0:T(8,128)(2,1)S(1)}, bf16[1024,128]{1,0:T(8,128)(2,1)S(1)}, u32[]{:S(2)}, u32[]{:S(2)}) collective-permute-start(bf16[1024,128]{1,0:T(8,128)(2,1)S(1)} %get-tuple-element.59.chip_sums_ref), channel_id=1, source_target_pairs={{0,16},{8,24},{16,0},{24,8},{1,17},{9,25},{17,1},{25,9},{2,18},{10... | collective-permute-start | bytes 786440 | tf_op jit(solution)/shard_map/ppermute | solution.py:722
  37.3 2.5 %collective-permute-start.6 = (bf16[64,128]{1,0:T(8,128)(2,1)S(1)}, bf16[64,128]{1,0:T(8,128)(2,1)S(1)}, u32[]{:S(2)}, u32[]{:S(2)}) collective-permute-start(bf16[64,128]{1,0:T(8,128)(2,1)S(1)} %get-tuple-element.55), channel_id=1, source_target_pairs={{0,1},{2,3},{4,5},{6,7},{1,0},{3,2},{5,4},{7,6},{8,9},{10,11},{12,... | collective-permute-start | bytes 49160 | tf_op jit(solution)/shard_map/ppermute | solution.py:718
  41.5 1.9 %shard_map.202 = (bf16[1024,128]{1,0:T(8,128)(2,1)S(1)}, bf16[8192,128]{1,0:T(8,128)(2,1)S(1)}) custom-call(bf16[1024,128]{1,0:T(8,128)(2,1)S(1)} %get-tuple-element.54.cin_ref, bf16[64,128]{1,0:T(8,128)(2,1)S(1)} %collective-permute-done.6.first_ref, bf16[64,128]{1,0:T(8,128)(2,1)S(1)} %collective-permute-done.7.second_ref, ...), custom_call_target="tpu_custom_call" | custom-call | tf_op jit(solution)/shard_map/pallas_call | solution.py:52
  44.2 1.6 %shard_map.203 = (f32[1024,128]{1,0:T(8,128)S(1)}, bf16[64,128]{1,0:T(8,128)(2,1)S(1)}, bf16[64,128]{1,0:T(8,128)(2,1)S(1)}, bf16[1024,128]{1,0:T(8,128)(2,1)S(1...) custom-call(bf16[8192,128]{1,0:T(8,128)(2,1)S(1)} %get-tuple-element.58.slope_ref, ...), custom_call_target="tpu_custom_call" | custom-call | tf_op jit(solution)/shard_map/pallas_call | solution.py:52
  45.7 4.2 %collective-permute-start.9 = (bf16[64,128]{1,0:T(8,128)(2,1)S(1)}, bf16[64,128]{1,0:T(8,128)(2,1)S(1)}, u32[]{:S(2)}, u32[]{:S(2)}) collective-permute-start(bf16[64,128]{1,0:T(8,128)(2,1)S(1)} %get-tuple-element.62.first_grad_ref), channel_id=1, source_target_pairs={{0,1},{2,3},{4,5},{6,7},{1,0},{3,2},{5,4},{7,6},{8,9},{10,11},{12,... | collective-permute-start | bytes 49160 | tf_op jit(solution)/shard_map/ppermute | solution.py:718
  52.6 9.3 %shard_map.206 = (bf16[4096,128]{1,0:T(8,128)(2,1)S(1)}, bf16[4096,256]{1,0:T(8,128)(2,1)S(1)}, bf16[512,128]{1,0:T(8,128)(2,1)S(1)}, bf16[512,128]{1,0:T(8,128)(2,1)S(1)}, bf16[512,128]{1,0:T(8,128)(2,1)S(1)}) custom-call(bf16[4096,128]{1,0:T(8,128)(2,1)S(1)} %get-tuple-element.41.h_ref, bf16[512,128]{1,0:T(8,128)(2,1)S(1)} %collective-permute-done.first_ref, ...), custom_call_target="tpu_custom_call" | custom-call | tf_op jit(solution)/shard_map/pallas_call | solution.py:52
  61.9 4.7 %collective-permute-start.13 = (bf16[512,128]{1,0:T(8,128)(2,1)S(1)}, bf16[512,128]{1,0:T(8,128)(2,1)S(1)}, u32[]{:S(2)}, u32[]{:S(2)}) collective-permute-start(bf16[512,128]{1,0:T(8,128)(2,1)S(1)} %get-tuple-element.78.mine_ref), channel_id=1, source_target_pairs={{0,1},{1,0},{2,3},{3,2},{4,5},{5,4},{6,7},{7,6},{8,9},{9,8},{10,11... | collective-permute-start | bytes 393224 | tf_op jit(solution)/shard_map/ppermute | solution.py:722
  66.7 2.9 %collective-permute-done.13.theirs_ref = bf16[512,128]{1,0:T(8,128)(2,1)S(1)} collective-permute-done((bf16[512,128]{1,0:T(8,128)(2,1)S(1)}, bf16[512,128]{1,0:T(8,128)(2,1)S(1)}, u32[]{:S(2)}, u32[]{:S(2)}) %collective-permute-start.13) | collective-permute-done | bytes 131104 | tf_op jit(solution)/shard_map/ppermute | solution.py:722
  69.6 4.6 %collective-permute-start.14 = (bf16[512,128]{1,0:T(8,128)(2,1)S(1)}, bf16[512,128]{1,0:T(8,128)(2,1)S(1)}, u32[]{:S(2)}, u32[]{:S(2)}) collective-permute-start(bf16[512,128]{1,0:T(8,128)(2,1)S(1)} %shard_map.208.mine_ref), channel_id=1, source_target_pairs={{0,2},{1,3},{2,0},{3,1},{4,6},{5,7},{6,4},{7,5},{8,10},{9,11},{10,... | collective-permute-start | bytes 393224 | tf_op jit(solution)/shard_map/ppermute | solution.py:722
  74.2 1.5 %collective-permute-start.11 = (bf16[512,128]{1,0:T(8,128)(2,1)S(1)}, bf16[512,128]{1,0:T(8,128)(2,1)S(1)}, u32[]{:S(2)}, u32[]{:S(2)}) collective-permute-start(bf16[512,128]{1,0:T(8,128)(2,1)S(1)} %get-tuple-element.75), channel_id=1, source_target_pairs={{0,1},{2,3},{4,5},{6,7},{1,0},{3,2},{5,4},{7,6},{8,9},{10,11},{12,... | collective-permute-start | bytes 393224 | tf_op jit(solution)/shard_map/ppermute | solution.py:718
  76.4 1.9 %collective-permute-done.14.theirs_ref = bf16[512,128]{1,0:T(8,128)(2,1)S(1)} collective-permute-done((bf16[512,128]{1,0:T(8,128)(2,1)S(1)}, bf16[512,128]{1,0:T(8,128)(2,1)S(1)}, u32[]{:S(2)}, u32[]{:S(2)}) %collective-permute-start.14) | collective-permute-done | bytes 131104 | tf_op jit(solution)/shard_map/ppermute | solution.py:722
  78.4 2.3 %collective-permute-start.15 = (bf16[512,128]{1,0:T(8,128)(2,1)S(1)}, bf16[512,128]{1,0:T(8,128)(2,1)S(1)}, u32[]{:S(2)}, u32[]{:S(2)}) collective-permute-start(bf16[512,128]{1,0:T(8,128)(2,1)S(1)} %shard_map.209.mine_ref), channel_id=1, source_target_pairs={{0,4},{1,5},{2,6},{3,7},{4,0},{5,1},{6,2},{7,3},{8,12},{9,13},{10,... | collective-permute-start | bytes 393224 | tf_op jit(solution)/shard_map/ppermute | solution.py:722
  80.7 4.4 %shard_map.207.rest_0_ = bf16[4096,128]{1,0:T(8,128)(2,1)} custom-call(bf16[4096,128]{1,0:T(8,128)(2,1)S(1)} %get-tuple-element.73.ups_ref, bf16[4096,256]{1,0:T(8,128)(2,1)S(1)} %get-tuple-element.74.downs_ref, bf16[512,128]{1,0:T(8,128)(2,1)S(1)} %collective-permute-done.11.first_back_ref, bf16[512,128]{1,0:T(8,128)(2,1)S(1)} %collective-permute-done.12.second_back_ref, ...), custom_call_target="tpu_custom_call" | custom-call | tf_op jit(solution)/shard_map/pallas_call | solution.py:52
  86.3 3.9 %shard_map.205.after_ref = bf16[4096,128]{1,0:T(8,128)(2,1)} custom-call(bf16[4096,128]{1,0:T(8,128)(2,1)S(1)} %get-tuple-element.41.h_ref, bf16[4096,128]{1,0:T(8,128)(2,1)S(1)} %get-tuple-element.48.summed_ref, bf16[896,128]{1,0:T(8,128)(2,1)S(1)} %get-tuple-element.44.weights_ref.matrices_ref, f32[4096,8]{1,0:T(8,128)S(1)} %shard_map.199.owners_ref, ...), custom_call_target="tpu_custom_call" | custom-call | tf_op jit(solution)/shard_map/pallas_call | solution.py:52
  90.9 1.6 %collective-permute-done.17.theirs_ref = f32[640,128]{1,0:T(8,128)S(1)} collective-permute-done((f32[640,128]{1,0:T(8,128)S(1)}, f32[640,128]{1,0:T(8,128)S(1)}, u32[]{:S(2)}, u32[]{:S(2)}) %collective-permute-start.17) | collective-permute-done | bytes 327712 | tf_op jit(solution)/shard_map/ppermute | solution.py:722
  (33 shorter events, 13.3 us)
Async XLA Ops:
  3.5 9.2 %collective-permute-start.1 = (bf16[512,128]{1,0:T(8,128)(2,1)S(1)}, bf16[512,128]{1,0:T(8,128)(2,1)S(1)}, u32[]{:S(2)}, u32[]{:S(2)}) collective-permute-start(bf16[512,128]{1,0:T(8,128)(2,1)S(1)} %get-tuple-element.43), channel_id=1, source_target_pairs={{1,2},{3,4},{5,6},{2,1},{4,3},{6,5},{9,10},{11,12},{13,14},{10,9},... | collective-permute-start | bytes 393224 | tf_op jit(solution)/shard_map/ppermute | solution.py:718
  4.2 10.6 %collective-permute-start = (bf16[512,128]{1,0:T(8,128)(2,1)S(1)}, bf16[512,128]{1,0:T(8,128)(2,1)S(1)}, u32[]{:S(2)}, u32[]{:S(2)}) collective-permute-start(bf16[512,128]{1,0:T(8,128)(2,1)S(1)} %get-tuple-element.42.rest_7_), channel_id=1, source_target_pairs={{0,1},{2,3},{4,5},{6,7},{1,0},{3,2},{5,4},{7,6},{8,9},{10,11},{12,... | collective-permute-start | bytes 393224 | tf_op jit(solution)/shard_map/ppermute | solution.py:718
  24.6 1.9 %collective-permute-start.2 = (bf16[528,128]{1,0:T(8,128)(2,1)S(1)}, bf16[528,128]{1,0:T(8,128)(2,1)S(1)}, u32[]{:S(2)}, u32[]{:S(2)}) collective-permute-start(bf16[528,128]{1,0:T(8,128)(2,1)S(1)} %get-tuple-element.51), channel_id=1, source_target_pairs={{0,8},{8,0},{16,24},{24,16},{1,9},{9,1},{17,25},{25,17},{2,10},{10... | collective-permute-start | bytes 405512 | tf_op jit(solution)/shard_map/ppermute | solution.py:722
  26.5 6.0 %collective-permute-start.3 = (bf16[528,128]{1,0:T(8,128)(2,1)S(1)}, bf16[528,128]{1,0:T(8,128)(2,1)S(1)}, u32[]{:S(2)}, u32[]{:S(2)}) collective-permute-start(bf16[528,128]{1,0:T(8,128)(2,1)S(1)} %shard_map.197.after_ref.totals_ref), channel_id=1, source_target_pairs={{0,16},{8,24},{16,0},{24,8},{1,17},{9,25},{17,1},{25,9},{2,18},{10... | collective-permute-start | bytes 405512 | tf_op jit(solution)/shard_map/ppermute | solution.py:722
  30.9 2.6 %collective-permute-start.5 = (bf16[1024,128]{1,0:T(8,128)(2,1)S(1)}, bf16[1024,128]{1,0:T(8,128)(2,1)S(1)}, u32[]{:S(2)}, u32[]{:S(2)}) collective-permute-start(bf16[1024,128]{1,0:T(8,128)(2,1)S(1)} %shard_map.198.after_ref.sums_ref), channel_id=1, source_target_pairs={{0,8},{8,0},{16,24},{24,16},{1,9},{9,1},{17,25},{25,17},{2,10},{10... | collective-permute-start | bytes 786440 | tf_op jit(solution)/shard_map/ppermute | solution.py:722
  33.4 1.4 %collective-permute-start.4 = (bf16[512,128]{1,0:T(8,128)(2,1)S(1)}, bf16[512,128]{1,0:T(8,128)(2,1)S(1)}, u32[]{:S(2)}, u32[]{:S(2)}) collective-permute-start(bf16[512,128]{1,0:T(8,128)(2,1)S(1)} %get-tuple-element.52.half_ref), channel_id=1, source_target_pairs={{0,8},{8,0},{16,24},{24,16},{1,9},{9,1},{17,25},{25,17},{2,10},{10... | collective-permute-start | bytes 393224 | tf_op jit(solution)/shard_map/ppermute | solution.py:722
  35.7 8.4 %collective-permute-start.8 = (bf16[1024,128]{1,0:T(8,128)(2,1)S(1)}, bf16[1024,128]{1,0:T(8,128)(2,1)S(1)}, u32[]{:S(2)}, u32[]{:S(2)}) collective-permute-start(bf16[1024,128]{1,0:T(8,128)(2,1)S(1)} %get-tuple-element.59.chip_sums_ref), channel_id=1, source_target_pairs={{0,16},{8,24},{16,0},{24,8},{1,17},{9,25},{17,1},{25,9},{2,18},{10... | collective-permute-start | bytes 786440 | tf_op jit(solution)/shard_map/ppermute | solution.py:722
  37.3 4.2 %collective-permute-start.6 = (bf16[64,128]{1,0:T(8,128)(2,1)S(1)}, bf16[64,128]{1,0:T(8,128)(2,1)S(1)}, u32[]{:S(2)}, u32[]{:S(2)}) collective-permute-start(bf16[64,128]{1,0:T(8,128)(2,1)S(1)} %get-tuple-element.55), channel_id=1, source_target_pairs={{0,1},{2,3},{4,5},{6,7},{1,0},{3,2},{5,4},{7,6},{8,9},{10,11},{12,... | collective-permute-start | bytes 49160 | tf_op jit(solution)/shard_map/ppermute | solution.py:718
  39.8 1.7 %collective-permute-start.7 = (bf16[64,128]{1,0:T(8,128)(2,1)S(1)}, bf16[64,128]{1,0:T(8,128)(2,1)S(1)}, u32[]{:S(2)}, u32[]{:S(2)}) collective-permute-start(bf16[64,128]{1,0:T(8,128)(2,1)S(1)} %get-tuple-element.56), channel_id=1, source_target_pairs={{1,2},{3,4},{5,6},{2,1},{4,3},{6,5},{9,10},{11,12},{13,14},{10,9},... | collective-permute-start | bytes 49160 | tf_op jit(solution)/shard_map/ppermute | solution.py:718
  45.7 6.8 %collective-permute-start.9 = (bf16[64,128]{1,0:T(8,128)(2,1)S(1)}, bf16[64,128]{1,0:T(8,128)(2,1)S(1)}, u32[]{:S(2)}, u32[]{:S(2)}) collective-permute-start(bf16[64,128]{1,0:T(8,128)(2,1)S(1)} %get-tuple-element.62.first_grad_ref), channel_id=1, source_target_pairs={{0,1},{2,3},{4,5},{6,7},{1,0},{3,2},{5,4},{7,6},{8,9},{10,11},{12,... | collective-permute-start | bytes 49160 | tf_op jit(solution)/shard_map/ppermute | solution.py:718
  49.9 2.6 %collective-permute-start.10 = (bf16[64,128]{1,0:T(8,128)(2,1)S(1)}, bf16[64,128]{1,0:T(8,128)(2,1)S(1)}, u32[]{:S(2)}, u32[]{:S(2)}) collective-permute-start(bf16[64,128]{1,0:T(8,128)(2,1)S(1)} %get-tuple-element.63.second_grad_ref), channel_id=1, source_target_pairs={{1,2},{3,4},{5,6},{2,1},{4,3},{6,5},{9,10},{11,12},{13,14},{10,9},... | collective-permute-start | bytes 49160 | tf_op jit(solution)/shard_map/ppermute | solution.py:718
  61.9 7.7 %collective-permute-start.13 = (bf16[512,128]{1,0:T(8,128)(2,1)S(1)}, bf16[512,128]{1,0:T(8,128)(2,1)S(1)}, u32[]{:S(2)}, u32[]{:S(2)}) collective-permute-start(bf16[512,128]{1,0:T(8,128)(2,1)S(1)} %get-tuple-element.78.mine_ref), channel_id=1, source_target_pairs={{0,1},{1,0},{2,3},{3,2},{4,5},{5,4},{6,7},{7,6},{8,9},{9,8},{10,11... | collective-permute-start | bytes 393224 | tf_op jit(solution)/shard_map/ppermute | solution.py:722
  69.6 8.7 %collective-permute-start.14 = (bf16[512,128]{1,0:T(8,128)(2,1)S(1)}, bf16[512,128]{1,0:T(8,128)(2,1)S(1)}, u32[]{:S(2)}, u32[]{:S(2)}) collective-permute-start(bf16[512,128]{1,0:T(8,128)(2,1)S(1)} %shard_map.208.mine_ref), channel_id=1, source_target_pairs={{0,2},{1,3},{2,0},{3,1},{4,6},{5,7},{6,4},{7,5},{8,10},{9,11},{10,... | collective-permute-start | bytes 393224 | tf_op jit(solution)/shard_map/ppermute | solution.py:722
  74.2 6.4 %collective-permute-start.11 = (bf16[512,128]{1,0:T(8,128)(2,1)S(1)}, bf16[512,128]{1,0:T(8,128)(2,1)S(1)}, u32[]{:S(2)}, u32[]{:S(2)}) collective-permute-start(bf16[512,128]{1,0:T(8,128)(2,1)S(1)} %get-tuple-element.75), channel_id=1, source_target_pairs={{0,1},{2,3},{4,5},{6,7},{1,0},{3,2},{5,4},{7,6},{8,9},{10,11},{12,... | collective-permute-start | bytes 393224 | tf_op jit(solution)/shard_map/ppermute | solution.py:718
  75.8 4.9 %collective-permute-start.12 = (bf16[512,128]{1,0:T(8,128)(2,1)S(1)}, bf16[512,128]{1,0:T(8,128)(2,1)S(1)}, u32[]{:S(2)}, u32[]{:S(2)}) collective-permute-start(bf16[512,128]{1,0:T(8,128)(2,1)S(1)} %get-tuple-element.76), channel_id=1, source_target_pairs={{1,2},{3,4},{5,6},{2,1},{4,3},{6,5},{9,10},{11,12},{13,14},{10,9},... | collective-permute-start | bytes 393224 | tf_op jit(solution)/shard_map/ppermute | solution.py:718
  78.4 7.3 %collective-permute-start.15 = (bf16[512,128]{1,0:T(8,128)(2,1)S(1)}, bf16[512,128]{1,0:T(8,128)(2,1)S(1)}, u32[]{:S(2)}, u32[]{:S(2)}) collective-permute-start(bf16[512,128]{1,0:T(8,128)(2,1)S(1)} %shard_map.209.mine_ref), channel_id=1, source_target_pairs={{0,4},{1,5},{2,6},{3,7},{4,0},{5,1},{6,2},{7,3},{8,12},{9,13},{10,... | collective-permute-start | bytes 393224 | tf_op jit(solution)/shard_map/ppermute | solution.py:722
  85.7 5.0 %collective-permute-start.16 = (bf16[512,128]{1,0:T(8,128)(2,1)S(1)}, bf16[512,128]{1,0:T(8,128)(2,1)S(1)}, u32[]{:S(2)}, u32[]{:S(2)}) collective-permute-start(bf16[512,128]{1,0:T(8,128)(2,1)S(1)} %shard_map.210.mine_ref), channel_id=1, source_target_pairs={{0,16},{8,24},{16,0},{24,8},{1,17},{9,25},{17,1},{25,9},{2,18},{10... | collective-permute-start | bytes 393224 | tf_op jit(solution)/shard_map/ppermute | solution.py:722
  90.8 1.7 %collective-permute-start.17 = (f32[640,128]{1,0:T(8,128)S(1)}, f32[640,128]{1,0:T(8,128)S(1)}, u32[]{:S(2)}, u32[]{:S(2)}) collective-permute-start(f32[640,128]{1,0:T(8,128)S(1)} %shard_map.211.mine_ref), channel_id=1, source_target_pairs={{0,8},{8,0},{16,24},{24,16},{1,9},{9,1},{17,25},{25,17},{2,10},{10... | collective-permute-start | bytes 983048 | tf_op jit(solution)/shard_map/ppermute | solution.py:722

commit v10 on v9

--- a/solution.py
+++ b/solution.py
@@ -333,6 +333,10 @@
     lax.fori_loop(0, sums_ref.shape[0] // 256, step, None)
 
 
+def relay_kernel(x_ref, after_ref, also_after_ref, out_ref):
+    out_ref[...] = x_ref[...]
+
+
 def owners_kernel(owner_ref, after_ref, owners_ref):
     owners_ref[...] = owner_columns(owner_ref)
 
@@ -349,7 +353,43 @@
     half_totals(owner_ref, new_ref, counts_ref, lax.rem(place_ref[1], 2), out_ref)
 
 
-def fine_forward_kernel(
+def forward_steps(own, far, halo, columns_t_ref, first_row, summed_ref, slope_ref, slope_hbm, sem):
+    def step(index, carry):
+        here = chunk_of(index, STEP * BLOCK)
+        there = pl.ds(pl.multiple_of(first_row + index * STEP * BLOCK, BLOCK), STEP * BLOCK)
+        total, slopes = edges(own[here, :], far[here, :], columns_t_ref[there, :], halo)
+        summed_ref[there, :] = total
+        edge = chunk_of(index, 8 * STEP * BLOCK)
+        slope_ref[edge, :] = jnp.concatenate(slopes, 0)
+        pltpu.make_async_copy(slope_ref.at[edge, :], slope_hbm.at[edge, :], sem).start()
+        return carry
+
+    lax.fori_loop(0, own.shape[0] // (STEP * BLOCK), step, None)
+
+
+def early_forward_kernel(
+    h_ref,
+    first_ref,
+    second_ref,
+    weights_ref,
+    columns_t_ref,
+    after_ref,
+    summed_ref,
+    slope_hbm,
+    own,
+    far,
+    halo,
+    slope_ref,
+    sem,
+):
+    self_weight, other_weight = matrix(weights_ref, 0), matrix(weights_ref, 1)
+    h = h_ref.at[: own.shape[0], :]
+    level_terms(h, (first_ref, second_ref), self_weight, other_weight, own, far, halo)
+    forward_steps(own, far, halo, columns_t_ref, 0, summed_ref, slope_ref, slope_hbm, sem)
+    pltpu.make_async_copy(slope_ref, slope_hbm, sem).wait()
+
+
+def late_forward_kernel(
     place_ref,
     h_ref,
     first_ref,
@@ -358,6 +398,8 @@
     columns_t_ref,
     owner_ref,
     counts_ref,
+    early_ref,
+    after_ref,
     summed_ref,
     slope_hbm,
     new_ref,
@@ -368,19 +410,12 @@
     slope_ref,
     sem,
 ):
+    half = own.shape[0]
     self_weight, other_weight = matrix(weights_ref, 0), matrix(weights_ref, 1)
-    level_terms(h_ref, (first_ref, second_ref), self_weight, other_weight, own, far, halo)
-
-    def step(index, carry):
-        here = chunk_of(index, STEP * BLOCK)
-        total, slopes = edges(own[here, :], far[here, :], columns_t_ref[here, :], halo)
-        summed_ref[here, :] = total
-        edge = chunk_of(index, 8 * STEP * BLOCK)
-        slope_ref[edge, :] = jnp.concatenate(slopes, 0)
-        pltpu.make_async_copy(slope_ref.at[edge, :], slope_hbm.at[edge, :], sem).start()
-        return carry
-
-    lax.fori_loop(0, h_ref.shape[0] // (STEP * BLOCK), step, None)
+    h = h_ref.at[half:, :]
+    level_terms(h, (first_ref, second_ref), self_weight, other_weight, own, far, halo)
+    summed_ref[:half, :] = early_ref[...]
+    forward_steps(own, far, halo, columns_t_ref, half, summed_ref, slope_ref, slope_hbm, sem)
     new_ref[...] = (
         h_ref[...].astype(f32) + dot(summed_ref[...], matrix(weights_ref, 2))
     ).astype(bf16)
@@ -407,13 +442,10 @@
     place_ref,
     half_ref,
     their_half_ref,
-    sums_ref,
-    more_sums_ref,
     sends_ref,
     cin_ref,
     first_ref,
     second_ref,
-    chip_sums_ref,
 ):
     mine, theirs = half_ref[...], their_half_ref[...]
     first = lax.rem(place_ref[1], 2) == 0
@@ -424,7 +456,6 @@
     halo_rows = first_ref.shape[0]
     first_ref[...] = sent[:halo_rows]
     second_ref[...] = sent[halo_rows:]
-    chip_sums_ref[...] = (sums_ref[...].astype(f32) + more_sums_ref[...].astype(f32)).astype(bf16)
 
 
 def coarse_forward_kernel(
@@ -565,7 +596,8 @@
     second_ref,
     g_ref,
     summed_ref,
-    slope_hbm,
+    early_slope_hbm,
+    late_slope_hbm,
     matrices_ref,
     columns_ref,
     owners_ref,
@@ -590,14 +622,21 @@
     count = STEP * BLOCK
     steps = h_ref.shape[0] // count
 
-    def slope_copy(index):
-        edge = chunk_of(index, 8 * count)
-        return pltpu.make_async_copy(
-            slope_hbm.at[edge, :], slope_ref.at[edge, :], slope_sems.at[index]
-        )
-
+    edge_rows = 8 * count
     for index in range(steps):
-        slope_copy(index).start()
+        late = index >= steps // 2
+        source = (late_slope_hbm if late else early_slope_hbm).at[
+            pl.ds((index - late * (steps // 2)) * edge_rows, edge_rows), :
+        ]
+        target = slope_ref.at[pl.ds(index * edge_rows, edge_rows), :]
+        pltpu.make_async_copy(source, target, slope_sems.at[index]).start()
+
+    def slope_wait(index):
+        edge = chunk_of(index, edge_rows)
+        pltpu.make_async_copy(
+            slope_ref.at[edge, :], slope_ref.at[edge, :], slope_sems.at[index]
+        ).wait()
+
     halo_rows = first_ref.shape[0]
     coarse_rows = part_ref.shape[0]
     halo_grad[...] = jnp.zeros_like(halo_grad)
@@ -622,7 +661,7 @@
 
     def edge_step(index):
         here = chunk_of(index, count)
-        slope_copy(index).wait()
+        slope_wait(index)
         slope = slope_ref[chunk_of(index, 8 * count), :]
         slopes = [slope[n * 8 * BLOCK : (n + 1) * 8 * BLOCK] for n in range(STEP)]
         downs_ref[here, :] = edges_back(
@@ -813,26 +852,59 @@
         + [pltpu.SemaphoreType.DMA((17,))],
     )
 
+    sums = call(
+        sums_kernel,
+        shape(coarse_rows, features, bf16),
+        [owner, cotangent, sends],
+        [VMEM, VMEM, ANY],
+    )
+    sent_sums = call(
+        relay_kernel,
+        shape(coarse_rows, features, bf16),
+        [sums, first, second],
+        [VMEM, ANY, ANY],
+    )
+    more_sums = swapped(sent_sums, "grp", 1)
+
     half_rows = coarse_rows // 2 + 2 * count_rows
-    summed, slope, new, give = call(
-        fine_forward_kernel,
+    forward_scratch = [
+        buffer(rows // 2, features, f32),
+        buffer(rows // 2, features, bf16),
+        buffer(2 * halo_rows, features, bf16),
+        buffer(4 * rows, features, bf16),
+        pltpu.SemaphoreType.DMA,
+    ]
+    summed, early_slope = call(
+        early_forward_kernel,
+        [shape(rows // 2, features, bf16), pltpu.HBM((4 * rows, features), bf16)],
+        [states, first, second, matrices, columns_t, sums],
+        [VMEM] * 5 + [ANY],
+        forward_scratch,
+        [VMEM, HBM],
+        mib=24,
+    )
+    chip_sums = call(
+        add_kernel,
+        shape(coarse_rows, features, bf16),
+        [sums, more_sums, summed],
+        [VMEM, VMEM, ANY],
+    )
+    more_sums = swapped(chip_sums, "grp", 2)
+    summed, late_slope, new, give = call(
+        late_forward_kernel,
         [
             shape(rows, features, bf16),
-            pltpu.HBM((8 * rows, features), bf16),
+            pltpu.HBM((4 * rows, features), bf16),
             shape(rows, features, bf16),
             shape(half_rows, features, bf16),
         ],
-        [place, states, first, second, matrices, columns_t, owner, counts],
-        [SMEM] + [VMEM] * 7,
-        [
-            buffer(rows, features, f32),
-            buffer(rows, features, bf16),
-            buffer(2 * halo_rows, features, bf16),
-            buffer(8 * rows, features, bf16),
-            pltpu.SemaphoreType.DMA,
-        ],
+        [
+            place, states, first, second, matrices, columns_t, owner, counts, summed, chip_sums,
+        ],
+        [SMEM] + [VMEM] * 8 + [ANY],
+        forward_scratch,
         [VMEM, HBM, VMEM, VMEM],
-        mib=32,
+        mib=24,
     )
     theirs = swapped(give, "grp", 1)
     keep = call(
@@ -841,37 +913,33 @@
         [place, owner, new, counts],
         [SMEM] + [VMEM] * 3,
     )
-    chip_totals = call(add_kernel, shape(half_rows, features, bf16), [keep, theirs])
+    chip_totals = call(
+        add_kernel,
+        shape(half_rows, features, bf16),
+        [keep, theirs, more_sums],
+        [VMEM, VMEM, ANY],
+    )
     more_totals = swapped(chip_totals, "grp", 2)
-    sums = call(
-        sums_kernel,
-        shape(coarse_rows, features, bf16),
-        [owner, cotangent, chip_totals],
-        [VMEM, VMEM, ANY],
-    )
-    more_sums = swapped(sums, "grp", 1)
-    owners_t = call(owners_kernel, shape(rows, 8, f32), [owner, sums], [VMEM, ANY])
+    owners_t = call(owners_kernel, shape(rows, 8, f32), [owner, chip_totals], [VMEM, ANY])
 
     half, counts = call(
         half_kernel,
         [shape(coarse_rows // 2, features, bf16), shape(count_rows, features, f32)],
-        [place, chip_totals, more_totals, sums],
+        [place, chip_totals, more_totals, owners_t],
         [SMEM, VMEM, VMEM, ANY],
     )
     their_half = swapped(half, "grp", 1)
-    coarse_in, to_first, to_second, chip_sums = call(
+    coarse_in, to_first, to_second = call(
         coarse_input_kernel,
         [
             shape(coarse_rows, features, bf16),
             shape(coarse_halo, features, bf16),
             shape(coarse_halo, features, bf16),
-            shape(coarse_rows, features, bf16),
-        ],
-        [place, half, their_half, sums, more_sums, coarse_sends],
-        [SMEM] + [VMEM] * 5,
+        ],
+        [place, half, their_half, coarse_sends],
+        [SMEM] + [VMEM] * 3,
     )
     coarse_first, coarse_second = exchange(to_first, to_second)
-    more_sums = swapped(chip_sums, "grp", 2)
 
     coarse_sum, coarse_slope = call(
         coarse_forward_kernel,
@@ -928,11 +996,11 @@
             shape(4 * features, features, bf16),
         ],
         [
-            states, first, second, cotangent, summed, slope, matrices, columns, owners_t,
-            coarse_part, counts, coarse_downs, first_back, second_back, coarse_sends,
+            states, first, second, cotangent, summed, early_slope, late_slope, matrices, columns,
+            owners_t, coarse_part, counts, coarse_downs, first_back, second_back, coarse_sends,
             coarse_weights,
         ],
-        [VMEM] * 5 + [HBM] + [VMEM] * 10,
+        [VMEM] * 5 + [HBM] * 2 + [VMEM] * 10,
         [
             buffer(rows, features, bf16),
             buffer(2 * halo_rows, features, f32),
@@ -951,7 +1019,7 @@
         scratch=[buffer(rows, features, bf16), pltpu.SemaphoreType.DMA],
         out_specs=HBM,
     )
-    grad_weights = total_weights(weights, place, ((), (), (grad_states,)), result)
+    grad_weights = total_weights(weights, place, ((), (), (result,)), grad_states)
     return (result, grad_states, grad_weights.reshape(7, features, features))
 
 

time: 94.1 us -> 96.5 us (1.026)
  starting transfers between devices: 32.6 us -> 31.1 us
  waiting for transfers between devices: 14.3 us -> 15.8 us
  Pallas kernels: 46 us -> 47.4 us
    ppermute x10, waiting for transfers between devices: 11.2 us -> 14.7 us  [swapped(): lax.ppermute(block, axis, [(i, i ^ distance) for i in range(lax.axis_size...]
    ppermute x4, waiting for transfers between devices: 3.14 us -> 1.18 us  [exchange(): lax.ppermute(first, 'sub', routes[0])]
    ppermute x10, starting transfers between devices: 15.8 us -> 14.3 us  [swapped(): lax.ppermute(block, axis, [(i, i ^ distance) for i in range(lax.axis_size...]
    pallas_call x20 -> x23, Pallas kernels: 46 us -> 47.4 us  [call(): pl.pallas_call(kernel, out_shape=out_shape, in_specs=in_specs, out_specs=...]
  transfers between devices with their start and end apart: 18 -> 18, of which waited for: 10 -> 7; matrix products, arithmetic and copies ran while one was open for 0% -> 0% of each run, Pallas kernels for 21% -> 30%
where the time goes in v10:
time: 96.5 us; the launch traced here: 95.3 us
  Pallas kernels  47.4 us (49%)
  starting transfers between devices  31.1 us (32%)
  waiting for transfers between devices  15.8 us (16%)
    pallas_call x23, Pallas kernels, call(): pl.pallas_call(kernel, out_shape=out_shape, in_specs=in_specs, out_specs=...  47.4 us
    ppermute x10, waiting for transfers between devices, swapped(): lax.ppermute(block, axis, [(i, i ^ distance) for i in range(lax.axis_size...  14.7 us
    ppermute x10, starting transfers between devices, swapped(): lax.ppermute(block, axis, [(i, i ^ distance) for i in range(lax.axis_size...  14.3 us
    ppermute x4, starting transfers between devices, exchange(): lax.ppermute(first, 'sub', routes[0])  14 us
    ppermute x4, starting transfers between devices, exchange(): lax.ppermute(second, 'sub', routes[1])  2.81 us
  transfers between devices with their start and end apart: 18, of which 7 were waited for; matrix products, arithmetic and copies ran while one was open for 0% of the time, Pallas kernels for 30%

profile of v10, /device:TPU:0, one launch (start us, length us, event | category | flops | bytes accessed | tf_op | source)
XLA Modules:
  0.0 95.3 jit_solution(365158761981197539)
XLA Ops:
  0.7 2.8 %shard_map.193 = (bf16[512,128]{1,0:T(8,128)(2,1)S(1)}, bf16[512,128]{1,0:T(8,128)(2,1)S(1)}, bf16[4096,128]{1,0:T(8,128)(2,1)S(1)}) custom-call(s32[2]{0:T(128)S(1)} %pad_add_fusion.place_ref, s32[512]{0:T(512)} %lo_hbm.1, s32[512]{0:T(512)} %hi_hbm.1, bf16[4096,128]{1,0:T(8,128)(2,1)} %x_hbm.1), custom_call_target="tpu_custom_call" | custom-call | tf_op jit(solution)/shard_map/pallas_call | solution.py:52
  4.2 5.8 %collective-permute-start = (bf16[512,128]{1,0:T(8,128)(2,1)S(1)}, bf16[512,128]{1,0:T(8,128)(2,1)S(1)}, u32[]{:S(2)}, u32[]{:S(2)}) collective-permute-start(bf16[512,128]{1,0:T(8,128)(2,1)S(1)} %get-tuple-element.43.rest_7_), channel_id=1, source_target_pairs={{0,1},{2,3},{4,5},{6,7},{1,0},{3,2},{5,4},{7,6},{8,9},{10,11},{12,... | collective-permute-start | bytes 393224 | tf_op jit(solution)/shard_map/ppermute | solution.py:757
  10.0 2.8 %shard_map.194 = (bf16[16,128]{1,0:T(8,128)(2,1)S(1)}, f32[8,4096]{1,0:T(8,128)S(1)}, f32[4096,8]{1,0:T(8,128)S(1)}, f32[8,1024]{1,0:T(8,128)S(1)}, f32[1024,8]{...) custom-call(s32[2]{0:T(128)S(1)} %pad_add_fusion.place_ref, ...), custom_call_target="tpu_custom_call" | custom-call | tf_op jit(solution)/shard_map/pallas_call | solution.py:52
  12.8 2.8 %shard_map.195.after_ref.x_ref.mine_ref = bf16[1024,128]{1,0:T(8,128)(2,1)S(1)} custom-call(s32[32,128]{1,0:T(8,128)S(1)} %get-tuple-element.47.owner_ref, bf16[4096,128]{1,0:T(8,128)(2,1)S(1)} %get-tuple-element.49.g_ref, s32[1,1024]{1,0:T(1,128)S(1)} %get-tuple-element.50.after_ref.sends_ref), custom_call_target="tpu_custom_call" | custom-call | tf_op jit(solution)/shard_map/pallas_call | solution.py:52
  15.7 5.1 %shard_map.196 = (bf16[2048,128]{1,0:T(8,128)(2,1)S(1)}, bf16[16384,128]{1,0:T(8,128)(2,1)}) custom-call(bf16[4096,128]{1,0:T(8,128)(2,1)S(1)} %get-tuple-element.42.h_ref, bf16[512,128]{1,0:T(8,128)(2,1)S(1)} %collective-permute-done.first_ref.after_ref, bf16[512,128]{1,0:T(8,128)(2,1)S(1)} %collective-permute-done.1.second_ref.also_after_ref, ...), custom_call_target="tpu_custom_call" | custom-call | tf_op jit(solution)/shard_map/pallas_call | solution.py:52
  20.9 1.6 %collective-permute-start.4 = (bf16[1024,128]{1,0:T(8,128)(2,1)S(1)}, bf16[1024,128]{1,0:T(8,128)(2,1)S(1)}, u32[]{:S(2)}, u32[]{:S(2)}) collective-permute-start(bf16[1024,128]{1,0:T(8,128)(2,1)S(1)} %shard_map.198.after_ref.chip_sums_ref), channel_id=1, source_target_pairs={{0,16},{8,24},{16,0},{24,8},{1,17},{9,25},{17,1},{25,9},{2,18},{10... | collective-permute-start | bytes 786440 | tf_op jit(solution)/shard_map/ppermute | solution.py:761
  22.5 6.1 %shard_map.199 = (bf16[4096,128]{1,0:T(8,128)(2,1)S(1)}, bf16[16384,128]{1,0:T(8,128)(2,1)}, bf16[4096,128]{1,0:T(8,128)(2,1)S(1)}, bf16[528,128]{1,0:T(8,128)(2,1)S(1)}) custom-call(s32[2]{0:T(128)S(1)} %pad_add_fusion.place_ref, bf16[4096,128]{1,0:T(8,128)(2,1)S(1)} %get-tuple-element.42.h_ref, ...), custom_call_target="tpu_custom_call" | custom-call | tf_op jit(solution)/shard_map/pallas_call | solution.py:52
  28.8 1.8 %shard_map.200.mine_ref = bf16[528,128]{1,0:T(8,128)(2,1)S(1)} custom-call(s32[2]{0:T(128)S(1)} %pad_add_fusion.place_ref, s32[32,128]{1,0:T(8,128)S(1)} %get-tuple-element.47.owner_ref, bf16[4096,128]{1,0:T(8,128)(2,1)S(1)} %get-tuple-element.53.new_ref, bf16[16,128]{1,0:T(8,128)(2,1)S(1)} %get-tuple-element.48.counts_ref), custom_call_target="tpu_custom_call" | custom-call | tf_op jit(solution)/shard_map/pallas_call | solution.py:52
  31.9 4.6 %collective-permute-done.5.more_totals_ref = bf16[528,128]{1,0:T(8,128)(2,1)S(1)} collective-permute-done((bf16[528,128]{1,0:T(8,128)(2,1)S(1)}, bf16[528,128]{1,0:T(8,128)(2,1)S(1)}, u32[]{:S(2)}, u32[]{:S(2)}) %collective-permute-start.5) | collective-permute-done | bytes 135200 | tf_op jit(solution)/shard_map/ppermute | solution.py:761
  39.6 1.8 %collective-permute-start.7 = (bf16[64,128]{1,0:T(8,128)(2,1)S(1)}, bf16[64,128]{1,0:T(8,128)(2,1)S(1)}, u32[]{:S(2)}, u32[]{:S(2)}) collective-permute-start(bf16[64,128]{1,0:T(8,128)(2,1)S(1)} %get-tuple-element.58), channel_id=1, source_target_pairs={{0,1},{2,3},{4,5},{6,7},{1,0},{3,2},{5,4},{7,6},{8,9},{10,11},{12,... | collective-permute-start | bytes 49160 | tf_op jit(solution)/shard_map/ppermute | solution.py:757
  43.4 1.9 %shard_map.205 = (bf16[1024,128]{1,0:T(8,128)(2,1)S(1)}, bf16[8192,128]{1,0:T(8,128)(2,1)S(1)}) custom-call(bf16[1024,128]{1,0:T(8,128)(2,1)S(1)} %get-tuple-element.57.cin_ref, bf16[64,128]{1,0:T(8,128)(2,1)S(1)} %collective-permute-done.7.first_ref, bf16[64,128]{1,0:T(8,128)(2,1)S(1)} %collective-permute-done.8.second_ref, ...), custom_call_target="tpu_custom_call" | custom-call | tf_op jit(solution)/shard_map/pallas_call | solution.py:52
  45.3 1.5 %shard_map.206 = (f32[1024,128]{1,0:T(8,128)S(1)}, bf16[64,128]{1,0:T(8,128)(2,1)S(1)}, bf16[64,128]{1,0:T(8,128)(2,1)S(1)}, bf16[1024,128]{1,0:T(8,128)(2,1)S(1...) custom-call(bf16[8192,128]{1,0:T(8,128)(2,1)S(1)} %get-tuple-element.61.slope_ref, ...), custom_call_target="tpu_custom_call" | custom-call | tf_op jit(solution)/shard_map/pallas_call | solution.py:52
  46.8 4.9 %collective-permute-start.9 = (bf16[64,128]{1,0:T(8,128)(2,1)S(1)}, bf16[64,128]{1,0:T(8,128)(2,1)S(1)}, u32[]{:S(2)}, u32[]{:S(2)}) collective-permute-start(bf16[64,128]{1,0:T(8,128)(2,1)S(1)} %get-tuple-element.64.first_grad_ref), channel_id=1, source_target_pairs={{0,1},{2,3},{4,5},{6,7},{1,0},{3,2},{5,4},{7,6},{8,9},{10,11},{12,... | collective-permute-start | bytes 49160 | tf_op jit(solution)/shard_map/ppermute | solution.py:757
  53.5 9.3 %shard_map.209 = (bf16[4096,128]{1,0:T(8,128)(2,1)S(1)}, bf16[4096,256]{1,0:T(8,128)(2,1)S(1)}, bf16[512,128]{1,0:T(8,128)(2,1)S(1)}, bf16[512,128]{1,0:T(8,128)(2,1)S(1)}, bf16[512,128]{1,0:T(8,128)(2,1)S(1)}) custom-call(bf16[4096,128]{1,0:T(8,128)(2,1)S(1)} %get-tuple-element.42.h_ref, bf16[512,128]{1,0:T(8,128)(2,1)S(1)} %collective-permute-done.first_ref.after_ref, ...), custom_call_target="tpu_custom_call" | custom-call | tf_op jit(solution)/shard_map/pallas_call | solution.py:52
  62.9 5.1 %collective-permute-start.13 = (bf16[512,128]{1,0:T(8,128)(2,1)S(1)}, bf16[512,128]{1,0:T(8,128)(2,1)S(1)}, u32[]{:S(2)}, u32[]{:S(2)}) collective-permute-start(bf16[512,128]{1,0:T(8,128)(2,1)S(1)} %get-tuple-element.80.mine_ref), channel_id=1, source_target_pairs={{0,1},{1,0},{2,3},{3,2},{4,5},{5,4},{6,7},{7,6},{8,9},{9,8},{10,11... | collective-permute-start | bytes 393224 | tf_op jit(solution)/shard_map/ppermute | solution.py:761
  67.9 2.9 %collective-permute-done.13.theirs_ref = bf16[512,128]{1,0:T(8,128)(2,1)S(1)} collective-permute-done((bf16[512,128]{1,0:T(8,128)(2,1)S(1)}, bf16[512,128]{1,0:T(8,128)(2,1)S(1)}, u32[]{:S(2)}, u32[]{:S(2)}) %collective-permute-start.13) | collective-permute-done | bytes 131104 | tf_op jit(solution)/shard_map/ppermute | solution.py:761
  70.9 3.5 %collective-permute-start.14 = (bf16[512,128]{1,0:T(8,128)(2,1)S(1)}, bf16[512,128]{1,0:T(8,128)(2,1)S(1)}, u32[]{:S(2)}, u32[]{:S(2)}) collective-permute-start(bf16[512,128]{1,0:T(8,128)(2,1)S(1)} %shard_map.211.mine_ref), channel_id=1, source_target_pairs={{0,2},{1,3},{2,0},{3,1},{4,6},{5,7},{6,4},{7,5},{8,10},{9,11},{10,... | collective-permute-start | bytes 393224 | tf_op jit(solution)/shard_map/ppermute | solution.py:761
  74.4 4.1 %collective-permute-done.14.theirs_ref = bf16[512,128]{1,0:T(8,128)(2,1)S(1)} collective-permute-done((bf16[512,128]{1,0:T(8,128)(2,1)S(1)}, bf16[512,128]{1,0:T(8,128)(2,1)S(1)}, u32[]{:S(2)}, u32[]{:S(2)}) %collective-permute-start.14) | collective-permute-done | bytes 131104 | tf_op jit(solution)/shard_map/ppermute | solution.py:761
  78.5 2.5 %collective-permute-start.15 = (bf16[512,128]{1,0:T(8,128)(2,1)S(1)}, bf16[512,128]{1,0:T(8,128)(2,1)S(1)}, u32[]{:S(2)}, u32[]{:S(2)}) collective-permute-start(bf16[512,128]{1,0:T(8,128)(2,1)S(1)} %shard_map.212.mine_ref), channel_id=1, source_target_pairs={{0,4},{1,5},{2,6},{3,7},{4,0},{5,1},{6,2},{7,3},{8,12},{9,13},{10,... | collective-permute-start | bytes 393224 | tf_op jit(solution)/shard_map/ppermute | solution.py:761
  81.0 1.5 %collective-permute-start.11 = (bf16[512,128]{1,0:T(8,128)(2,1)S(1)}, bf16[512,128]{1,0:T(8,128)(2,1)S(1)}, u32[]{:S(2)}, u32[]{:S(2)}) collective-permute-start(bf16[512,128]{1,0:T(8,128)(2,1)S(1)} %get-tuple-element.78), channel_id=1, source_target_pairs={{0,1},{2,3},{4,5},{6,7},{1,0},{3,2},{5,4},{7,6},{8,9},{10,11},{12,... | collective-permute-start | bytes 393224 | tf_op jit(solution)/shard_map/ppermute | solution.py:757
  83.2 4.0 %shard_map.208.rest_0_ = bf16[4096,128]{1,0:T(8,128)(2,1)} custom-call(bf16[4096,128]{1,0:T(8,128)(2,1)S(1)} %get-tuple-element.42.h_ref, bf16[4096,128]{1,0:T(8,128)(2,1)S(1)} %get-tuple-element.52.summed_ref, bf16[896,128]{1,0:T(8,128)(2,1)S(1)} %get-tuple-element.45.weights_ref.matrices_ref, f32[4096,8]{1,0:T(8,128)S(1)} %shard_map.202.after_ref.owners_ref, ...), custom_call_target="tpu_custom_call" | custom-call | tf_op jit(solution)/shard_map/pallas_call | solution.py:52
  87.8 4.4 %shard_map.210.after_ref = bf16[4096,128]{1,0:T(8,128)(2,1)} custom-call(bf16[4096,128]{1,0:T(8,128)(2,1)S(1)} %get-tuple-element.76.ups_ref, bf16[4096,256]{1,0:T(8,128)(2,1)S(1)} %get-tuple-element.77.downs_ref, bf16[512,128]{1,0:T(8,128)(2,1)S(1)} %collective-permute-done.11.first_back_ref, bf16[512,128]{1,0:T(8,128)(2,1)S(1)} %collective-permute-done.12.second_back_ref, ...), custom_call_target="tpu_custom_call" | custom-call | tf_op jit(solution)/shard_map/pallas_call | solution.py:52
  92.3 1.6 %collective-permute-done.17.theirs_ref = f32[640,128]{1,0:T(8,128)S(1)} collective-permute-done((f32[640,128]{1,0:T(8,128)S(1)}, f32[640,128]{1,0:T(8,128)S(1)}, u32[]{:S(2)}, u32[]{:S(2)}) %collective-permute-start.17) | collective-permute-done | bytes 327712 | tf_op jit(solution)/shard_map/ppermute | solution.py:761
  93.9 1.3 %shard_map.215 = f32[896,128]{1,0:T(8,128)} custom-call(s32[2]{0:T(128)S(1)} %pad_add_fusion.place_ref, f32[640,128]{1,0:T(8,128)S(1)} %shard_map.214.mine_ref, f32[640,128]{1,0:T(8,128)S(1)} %collective-permute-done.17.theirs_ref), custom_call_target="tpu_custom_call" | custom-call | tf_op jit(solution)/shard_map/pallas_call | solution.py:52
  (36 shorter events, 10.9 us)
Async XLA Ops:
  3.5 12.0 %collective-permute-start.1 = (bf16[512,128]{1,0:T(8,128)(2,1)S(1)}, bf16[512,128]{1,0:T(8,128)(2,1)S(1)}, u32[]{:S(2)}, u32[]{:S(2)}) collective-permute-start(bf16[512,128]{1,0:T(8,128)(2,1)S(1)} %get-tuple-element.44), channel_id=1, source_target_pairs={{1,2},{3,4},{5,6},{2,1},{4,3},{6,5},{9,10},{11,12},{13,14},{10,9},... | collective-permute-start | bytes 393224 | tf_op jit(solution)/shard_map/ppermute | solution.py:757
  4.2 11.4 %collective-permute-start = (bf16[512,128]{1,0:T(8,128)(2,1)S(1)}, bf16[512,128]{1,0:T(8,128)(2,1)S(1)}, u32[]{:S(2)}, u32[]{:S(2)}) collective-permute-start(bf16[512,128]{1,0:T(8,128)(2,1)S(1)} %get-tuple-element.43.rest_7_), channel_id=1, source_target_pairs={{0,1},{2,3},{4,5},{6,7},{1,0},{3,2},{5,4},{7,6},{8,9},{10,11},{12,... | collective-permute-start | bytes 393224 | tf_op jit(solution)/shard_map/ppermute | solution.py:757
  15.6 5.2 %collective-permute-start.2 = (bf16[1024,128]{1,0:T(8,128)(2,1)S(1)}, bf16[1024,128]{1,0:T(8,128)(2,1)S(1)}, u32[]{:S(2)}, u32[]{:S(2)}) collective-permute-start(bf16[1024,128]{1,0:T(8,128)(2,1)S(1)} %shard_map.197), channel_id=1, source_target_pairs={{0,8},{8,0},{16,24},{24,16},{1,9},{9,1},{17,25},{25,17},{2,10},{10... | collective-permute-start | bytes 786440 | tf_op jit(solution)/shard_map/ppermute | solution.py:761
  20.9 9.7 %collective-permute-start.4 = (bf16[1024,128]{1,0:T(8,128)(2,1)S(1)}, bf16[1024,128]{1,0:T(8,128)(2,1)S(1)}, u32[]{:S(2)}, u32[]{:S(2)}) collective-permute-start(bf16[1024,128]{1,0:T(8,128)(2,1)S(1)} %shard_map.198.after_ref.chip_sums_ref), channel_id=1, source_target_pairs={{0,16},{8,24},{16,0},{24,8},{1,17},{9,25},{17,1},{25,9},{2,18},{10... | collective-permute-start | bytes 786440 | tf_op jit(solution)/shard_map/ppermute | solution.py:761
  28.5 2.1 %collective-permute-start.3 = (bf16[528,128]{1,0:T(8,128)(2,1)S(1)}, bf16[528,128]{1,0:T(8,128)(2,1)S(1)}, u32[]{:S(2)}, u32[]{:S(2)}) collective-permute-start(bf16[528,128]{1,0:T(8,128)(2,1)S(1)} %get-tuple-element.54), channel_id=1, source_target_pairs={{0,8},{8,0},{16,24},{24,16},{1,9},{9,1},{17,25},{25,17},{2,10},{10... | collective-permute-start | bytes 405512 | tf_op jit(solution)/shard_map/ppermute | solution.py:761
  30.6 5.9 %collective-permute-start.5 = (bf16[528,128]{1,0:T(8,128)(2,1)S(1)}, bf16[528,128]{1,0:T(8,128)(2,1)S(1)}, u32[]{:S(2)}, u32[]{:S(2)}) collective-permute-start(bf16[528,128]{1,0:T(8,128)(2,1)S(1)} %shard_map.201.after_ref.totals_ref), channel_id=1, source_target_pairs={{0,16},{8,24},{16,0},{24,8},{1,17},{9,25},{17,1},{25,9},{2,18},{10... | collective-permute-start | bytes 405512 | tf_op jit(solution)/shard_map/ppermute | solution.py:761
  37.4 1.4 %collective-permute-start.6 = (bf16[512,128]{1,0:T(8,128)(2,1)S(1)}, bf16[512,128]{1,0:T(8,128)(2,1)S(1)}, u32[]{:S(2)}, u32[]{:S(2)}) collective-permute-start(bf16[512,128]{1,0:T(8,128)(2,1)S(1)} %get-tuple-element.55.half_ref), channel_id=1, source_target_pairs={{0,8},{8,0},{16,24},{24,16},{1,9},{9,1},{17,25},{25,17},{2,10},{10... | collective-permute-start | bytes 393224 | tf_op jit(solution)/shard_map/ppermute | solution.py:761
  39.6 3.8 %collective-permute-start.7 = (bf16[64,128]{1,0:T(8,128)(2,1)S(1)}, bf16[64,128]{1,0:T(8,128)(2,1)S(1)}, u32[]{:S(2)}, u32[]{:S(2)}) collective-permute-start(bf16[64,128]{1,0:T(8,128)(2,1)S(1)} %get-tuple-element.58), channel_id=1, source_target_pairs={{0,1},{2,3},{4,5},{6,7},{1,0},{3,2},{5,4},{7,6},{8,9},{10,11},{12,... | collective-permute-start | bytes 49160 | tf_op jit(solution)/shard_map/ppermute | solution.py:757
  41.4 2.0 %collective-permute-start.8 = (bf16[64,128]{1,0:T(8,128)(2,1)S(1)}, bf16[64,128]{1,0:T(8,128)(2,1)S(1)}, u32[]{:S(2)}, u32[]{:S(2)}) collective-permute-start(bf16[64,128]{1,0:T(8,128)(2,1)S(1)} %get-tuple-element.59), channel_id=1, source_target_pairs={{1,2},{3,4},{5,6},{2,1},{4,3},{6,5},{9,10},{11,12},{13,14},{10,9},... | collective-permute-start | bytes 49160 | tf_op jit(solution)/shard_map/ppermute | solution.py:757
  46.8 6.7 %collective-permute-start.9 = (bf16[64,128]{1,0:T(8,128)(2,1)S(1)}, bf16[64,128]{1,0:T(8,128)(2,1)S(1)}, u32[]{:S(2)}, u32[]{:S(2)}) collective-permute-start(bf16[64,128]{1,0:T(8,128)(2,1)S(1)} %get-tuple-element.64.first_grad_ref), channel_id=1, source_target_pairs={{0,1},{2,3},{4,5},{6,7},{1,0},{3,2},{5,4},{7,6},{8,9},{10,11},{12,... | collective-permute-start | bytes 49160 | tf_op jit(solution)/shard_map/ppermute | solution.py:757
  51.7 1.8 %collective-permute-start.10 = (bf16[64,128]{1,0:T(8,128)(2,1)S(1)}, bf16[64,128]{1,0:T(8,128)(2,1)S(1)}, u32[]{:S(2)}, u32[]{:S(2)}) collective-permute-start(bf16[64,128]{1,0:T(8,128)(2,1)S(1)} %get-tuple-element.65.second_grad_ref), channel_id=1, source_target_pairs={{1,2},{3,4},{5,6},{2,1},{4,3},{6,5},{9,10},{11,12},{13,14},{10,9},... | collective-permute-start | bytes 49160 | tf_op jit(solution)/shard_map/ppermute | solution.py:757
  62.9 8.0 %collective-permute-start.13 = (bf16[512,128]{1,0:T(8,128)(2,1)S(1)}, bf16[512,128]{1,0:T(8,128)(2,1)S(1)}, u32[]{:S(2)}, u32[]{:S(2)}) collective-permute-start(bf16[512,128]{1,0:T(8,128)(2,1)S(1)} %get-tuple-element.80.mine_ref), channel_id=1, source_target_pairs={{0,1},{1,0},{2,3},{3,2},{4,5},{5,4},{6,7},{7,6},{8,9},{9,8},{10,11... | collective-permute-start | bytes 393224 | tf_op jit(solution)/shard_map/ppermute | solution.py:761
  70.9 7.6 %collective-permute-start.14 = (bf16[512,128]{1,0:T(8,128)(2,1)S(1)}, bf16[512,128]{1,0:T(8,128)(2,1)S(1)}, u32[]{:S(2)}, u32[]{:S(2)}) collective-permute-start(bf16[512,128]{1,0:T(8,128)(2,1)S(1)} %shard_map.211.mine_ref), channel_id=1, source_target_pairs={{0,2},{1,3},{2,0},{3,1},{4,6},{5,7},{6,4},{7,5},{8,10},{9,11},{10,... | collective-permute-start | bytes 393224 | tf_op jit(solution)/shard_map/ppermute | solution.py:761
  78.5 8.6 %collective-permute-start.15 = (bf16[512,128]{1,0:T(8,128)(2,1)S(1)}, bf16[512,128]{1,0:T(8,128)(2,1)S(1)}, u32[]{:S(2)}, u32[]{:S(2)}) collective-permute-start(bf16[512,128]{1,0:T(8,128)(2,1)S(1)} %shard_map.212.mine_ref), channel_id=1, source_target_pairs={{0,4},{1,5},{2,6},{3,7},{4,0},{5,1},{6,2},{7,3},{8,12},{9,13},{10,... | collective-permute-start | bytes 393224 | tf_op jit(solution)/shard_map/ppermute | solution.py:761
  81.0 6.8 %collective-permute-start.11 = (bf16[512,128]{1,0:T(8,128)(2,1)S(1)}, bf16[512,128]{1,0:T(8,128)(2,1)S(1)}, u32[]{:S(2)}, u32[]{:S(2)}) collective-permute-start(bf16[512,128]{1,0:T(8,128)(2,1)S(1)} %get-tuple-element.78), channel_id=1, source_target_pairs={{0,1},{2,3},{4,5},{6,7},{1,0},{3,2},{5,4},{7,6},{8,9},{10,11},{12,... | collective-permute-start | bytes 393224 | tf_op jit(solution)/shard_map/ppermute | solution.py:757
  82.5 5.3 %collective-permute-start.12 = (bf16[512,128]{1,0:T(8,128)(2,1)S(1)}, bf16[512,128]{1,0:T(8,128)(2,1)S(1)}, u32[]{:S(2)}, u32[]{:S(2)}) collective-permute-start(bf16[512,128]{1,0:T(8,128)(2,1)S(1)} %get-tuple-element.79), channel_id=1, source_target_pairs={{1,2},{3,4},{5,6},{2,1},{4,3},{6,5},{9,10},{11,12},{13,14},{10,9},... | collective-permute-start | bytes 393224 | tf_op jit(solution)/shard_map/ppermute | solution.py:757
  87.2 5.0 %collective-permute-start.16 = (bf16[512,128]{1,0:T(8,128)(2,1)S(1)}, bf16[512,128]{1,0:T(8,128)(2,1)S(1)}, u32[]{:S(2)}, u32[]{:S(2)}) collective-permute-start(bf16[512,128]{1,0:T(8,128)(2,1)S(1)} %shard_map.213.mine_ref), channel_id=1, source_target_pairs={{0,16},{8,24},{16,0},{24,8},{1,17},{9,25},{17,1},{25,9},{2,18},{10... | collective-permute-start | bytes 393224 | tf_op jit(solution)/shard_map/ppermute | solution.py:761
  92.3 1.7 %collective-permute-start.17 = (f32[640,128]{1,0:T(8,128)S(1)}, f32[640,128]{1,0:T(8,128)S(1)}, u32[]{:S(2)}, u32[]{:S(2)}) collective-permute-start(f32[640,128]{1,0:T(8,128)S(1)} %shard_map.214.mine_ref), channel_id=1, source_target_pairs={{0,8},{8,0},{16,24},{24,16},{1,9},{9,1},{17,25},{25,17},{2,10},{10... | collective-permute-start | bytes 983048 | tf_op jit(solution)/shard_map/ppermute | solution.py:761

commit v11 on v9

--- a/solution.py
+++ b/solution.py
@@ -407,13 +407,10 @@
     place_ref,
     half_ref,
     their_half_ref,
-    sums_ref,
-    more_sums_ref,
     sends_ref,
     cin_ref,
     first_ref,
     second_ref,
-    chip_sums_ref,
 ):
     mine, theirs = half_ref[...], their_half_ref[...]
     first = lax.rem(place_ref[1], 2) == 0
@@ -424,7 +421,6 @@
     halo_rows = first_ref.shape[0]
     first_ref[...] = sent[:halo_rows]
     second_ref[...] = sent[halo_rows:]
-    chip_sums_ref[...] = (sums_ref[...].astype(f32) + more_sums_ref[...].astype(f32)).astype(bf16)
 
 
 def coarse_forward_kernel(
@@ -560,6 +556,7 @@
 
 
 def fine_backward_kernel(
+    place_ref,
     h_ref,
     first_ref,
     second_ref,
@@ -580,11 +577,13 @@
     downs_ref,
     first_grad_ref,
     second_grad_ref,
-    weights_ref,
+    give_ref,
+    keep_ref,
     grad_sum,
     halo_grad,
     mean,
     slope_ref,
+    weights,
     slope_sems,
 ):
     count = STEP * BLOCK
@@ -643,14 +642,17 @@
     first_grad_ref[...] = first_grad
     second_grad_ref[...] = second_grad
     pair_grad = dot_tn(h_ref[...], downs_ref[...])
-    weights_ref[0:128, :] = pair_grad[:, :128].astype(bf16)
-    weights_ref[128:256, :] = (
+    weights[0:128, :] = pair_grad[:, :128]
+    weights[128:256, :] = (
         pair_grad[:, 128:]
         + dot_tn(first_ref[...], first_grad)
         + dot_tn(second_ref[...], second_grad)
-    ).astype(bf16)
-    weights_ref[256:384, :] = dot_tn(summed_ref[...], ups_ref[...]).astype(bf16)
-    weights_ref[384:512, :] = coarse_weights_ref[...]
+    )
+    weights[256:384, :] = dot_tn(summed_ref[...], ups_ref[...])
+    core = lax.rem(place_ref[1], 2)
+    give_ref[...] = weights[pl.ds(pl.multiple_of((1 - core) * 192, 64), 192), :]
+    keep_ref[:192, :] = weights[pl.ds(pl.multiple_of(core * 192, 64), 192), :]
+    keep_ref[192:, :] = coarse_weights_ref[...].astype(f32)
 
 
 def finish_kernel(
@@ -691,20 +693,28 @@
     out_ref[...] = (mine_ref[...].astype(f32) + theirs_ref[...].astype(f32)).astype(bf16)
 
 
-def add_gather_kernel(mine_ref, theirs_ref, after_ref, out_ref):
-    mine, theirs = mine_ref[...].astype(f32), theirs_ref[...].astype(f32)
-    out_ref[:384, :] = mine[:384] + theirs[:384]
-    out_ref[384:512, :] = mine[384:]
-    out_ref[512:, :] = theirs[384:]
+def add_first_kernel(keep_ref, theirs_ref, out_ref):
+    out_ref[:192, :] = (keep_ref[:192, :] + theirs_ref[...]).astype(bf16)
+    out_ref[192:, :] = keep_ref[192:, :].astype(bf16)
+
+
+def add_gather_kernel(mine_ref, y_ref, x_ref, both_ref, after_ref, out_ref):
+    mine = mine_ref[...].astype(f32) + y_ref[...].astype(f32)
+    theirs = x_ref[...].astype(f32) + both_ref[...].astype(f32)
+    out_ref[:192, :] = mine[:192] + theirs[:192]
+    out_ref[192:320, :] = mine[192:]
+    out_ref[320:, :] = theirs[192:]
 
 
 def weights_kernel(place_ref, mine_ref, theirs_ref, out_ref):
-    out_ref[:384, :] = mine_ref[:384, :] + theirs_ref[:384, :]
     group = place_ref[1]
     low, high = lax.rem(group, 2), group // 2
+    mine, theirs = mine_ref[:192, :], theirs_ref[:192, :]
+    out_ref[:192, :] = jnp.where(low == 0, mine, theirs)
+    out_ref[192:384, :] = jnp.where(low == 0, theirs, mine)
     for n in range(4):
-        row = jnp.where(high == n // 2, 384, 512)
-        here = pl.ds(pl.multiple_of(row, 128), 128)
+        row = jnp.where(high == n // 2, 192, 320)
+        here = pl.ds(pl.multiple_of(row, 64), 128)
         value = jnp.where(low == n % 2, mine_ref[here, :], theirs_ref[here, :])
         out_ref[384 + 128 * n : 512 + 128 * n, :] = value
 
@@ -722,23 +732,38 @@
     return lax.ppermute(block, axis, [(i, i ^ distance) for i in range(lax.axis_size(axis))])
 
 
-def total_weights(weights, place, after, last):
-    distance, number = 1, 0
+def total_weights(give, keep, place, after, last):
+    weights = call(
+        add_first_kernel, shape(320, 128, bf16), [keep, swapped(give, "grp", 1)]
+    )
+    distance, number = 2, 0
     while distance < lax.axis_size("sub"):
         theirs = swapped(weights, "sub", distance)
         waits = after[number] if number < len(after) else ()
         weights = call(
             add_kernel,
-            shape(*weights.shape, bf16),
+            shape(320, 128, bf16),
             [weights, theirs, *waits],
             [VMEM, VMEM] + [HBM] * len(waits),
         )
         distance, number = 2 * distance, number + 1
+    count = lax.axis_size("sub")
+    corners = [
+        (g * count + s, (g ^ 2) * count + (s ^ 1))
+        for g in range(lax.axis_size("grp"))
+        for s in range(count)
+    ]
     weights = call(
         add_gather_kernel,
-        shape(640, 128, f32),
-        [weights, swapped(weights, "grp", 2), last],
-        [VMEM, VMEM, HBM],
+        shape(448, 128, f32),
+        [
+            weights,
+            swapped(weights, "sub", 1),
+            swapped(weights, "grp", 2),
+            lax.ppermute(weights, ("grp", "sub"), corners),
+            last,
+        ],
+        [VMEM] * 4 + [HBM],
     )
     return call(
         weights_kernel,
@@ -859,16 +884,16 @@
         [SMEM, VMEM, VMEM, ANY],
     )
     their_half = swapped(half, "grp", 1)
-    coarse_in, to_first, to_second, chip_sums = call(
+    chip_sums = call(add_kernel, shape(coarse_rows, features, bf16), [sums, more_sums])
+    coarse_in, to_first, to_second = call(
         coarse_input_kernel,
         [
             shape(coarse_rows, features, bf16),
             shape(coarse_halo, features, bf16),
             shape(coarse_halo, features, bf16),
-            shape(coarse_rows, features, bf16),
-        ],
-        [place, half, their_half, sums, more_sums, coarse_sends],
-        [SMEM] + [VMEM] * 5,
+        ],
+        [place, half, their_half, coarse_sends],
+        [SMEM] + [VMEM] * 3,
     )
     coarse_first, coarse_second = exchange(to_first, to_second)
     more_sums = swapped(chip_sums, "grp", 2)
@@ -918,26 +943,28 @@
         out_specs=HBM,
     )
 
-    ups, downs, first_grad, second_grad, weights = call(
+    ups, downs, first_grad, second_grad, give, keep = call(
         fine_backward_kernel,
         [
             shape(rows, features, bf16),
             shape(rows, 2 * features, bf16),
             shape(halo_rows, features, bf16),
             shape(halo_rows, features, bf16),
-            shape(4 * features, features, bf16),
-        ],
-        [
-            states, first, second, cotangent, summed, slope, matrices, columns, owners_t,
+            shape(192, features, f32),
+            shape(320, features, f32),
+        ],
+        [
+            place, states, first, second, cotangent, summed, slope, matrices, columns, owners_t,
             coarse_part, counts, coarse_downs, first_back, second_back, coarse_sends,
             coarse_weights,
         ],
-        [VMEM] * 5 + [HBM] + [VMEM] * 10,
+        [SMEM] + [VMEM] * 5 + [HBM] + [VMEM] * 10,
         [
             buffer(rows, features, bf16),
             buffer(2 * halo_rows, features, f32),
             buffer(coarse_rows, features, bf16),
             buffer(8 * rows, features, bf16),
+            buffer(384, features, f32),
             pltpu.SemaphoreType.DMA((rows // (STEP * BLOCK),)),
         ],
         mib=32,
@@ -951,7 +978,7 @@
         scratch=[buffer(rows, features, bf16), pltpu.SemaphoreType.DMA],
         out_specs=HBM,
     )
-    grad_weights = total_weights(weights, place, ((), (), (grad_states,)), result)
+    grad_weights = total_weights(give, keep, place, ((), (grad_states,)), result)
     return (result, grad_states, grad_weights.reshape(7, features, features))
 
 

time: 94.1 us -> 97 us (1.031)
  starting transfers between devices: 32.6 us -> 34.8 us
    ppermute x0 -> x1, starting transfers between devices: none -> 4.2 us  [total_weights(): lax.ppermute(weights, ('grp', 'sub'), corners)]
    ppermute x10 -> x11, starting transfers between devices: 15.8 us -> 12.9 us  [swapped(): lax.ppermute(block, axis, [(i, i ^ distance) for i in range(lax.axis_size...]
    pallas_call x20 -> x21, Pallas kernels: 46 us -> 46.8 us  [call(): pl.pallas_call(kernel, out_shape=out_shape, in_specs=in_specs, out_specs=...]
    ppermute x10 -> x11, waiting for transfers between devices: 11.2 us -> 10.3 us  [swapped(): lax.ppermute(block, axis, [(i, i ^ distance) for i in range(lax.axis_size...]
  transfers between devices with their start and end apart: 18 -> 20, of which waited for: 10 -> 9; matrix products, arithmetic and copies ran while one was open for 0% -> 0% of each run, Pallas kernels for 21% -> 19%
where the time goes in v11:
time: 97 us; the launch traced here: 96.1 us
  Pallas kernels  46.8 us (48%)
  starting transfers between devices  34.8 us (36%)
  waiting for transfers between devices  13.5 us (14%)
    pallas_call x21, Pallas kernels, call(): pl.pallas_call(kernel, out_shape=out_shape, in_specs=in_specs, out_specs=...  46.8 us
    ppermute x4, starting transfers between devices, exchange(): lax.ppermute(first, 'sub', routes[0])  14.9 us
    ppermute x11, starting transfers between devices, swapped(): lax.ppermute(block, axis, [(i, i ^ distance) for i in range(lax.axis_size...  12.9 us
    ppermute x11, waiting for transfers between devices, swapped(): lax.ppermute(block, axis, [(i, i ^ distance) for i in range(lax.axis_size...  10.3 us
    ppermute x1, starting transfers between devices, total_weights(): lax.ppermute(weights, ('grp', 'sub'), corners)  4.2 us
    ppermute x4, waiting for transfers between devices, exchange(): lax.ppermute(first, 'sub', routes[0])  3.14 us
    ppermute x4, starting transfers between devices, exchange(): lax.ppermute(second, 'sub', routes[1])  2.81 us
  transfers between devices with their start and end apart: 20, of which 9 were waited for; matrix products, arithmetic and copies ran while one was open for 0% of the time, Pallas kernels for 19%

profile of v11, /device:TPU:0, one launch (start us, length us, event | category | flops | bytes accessed | tf_op | source)
XLA Modules:
  0.0 96.1 jit_solution(10259934151624058007)
XLA Ops:
  0.7 2.8 %shard_map.193 = (bf16[512,128]{1,0:T(8,128)(2,1)S(1)}, bf16[512,128]{1,0:T(8,128)(2,1)S(1)}, bf16[4096,128]{1,0:T(8,128)(2,1)S(1)}) custom-call(s32[2]{0:T(128)S(1)} %pad_add_fusion.place_ref, s32[512]{0:T(512)} %lo_hbm.1, s32[512]{0:T(512)} %hi_hbm.1, bf16[4096,128]{1,0:T(8,128)(2,1)} %x_hbm.1), custom_call_target="tpu_custom_call" | custom-call | tf_op jit(solution)/shard_map/pallas_call | solution.py:52
  4.2 5.8 %collective-permute-start = (bf16[512,128]{1,0:T(8,128)(2,1)S(1)}, bf16[512,128]{1,0:T(8,128)(2,1)S(1)}, u32[]{:S(2)}, u32[]{:S(2)}) collective-permute-start(bf16[512,128]{1,0:T(8,128)(2,1)S(1)} %get-tuple-element.42.rest_7_), channel_id=1, source_target_pairs={{0,1},{2,3},{4,5},{6,7},{1,0},{3,2},{5,4},{7,6},{8,9},{10,11},{12,... | collective-permute-start | bytes 393224 | tf_op jit(solution)/shard_map/ppermute | solution.py:728
  10.0 2.8 %shard_map.194 = (bf16[16,128]{1,0:T(8,128)(2,1)S(1)}, f32[8,4096]{1,0:T(8,128)S(1)}, f32[4096,8]{1,0:T(8,128)S(1)}, f32[8,1024]{1,0:T(8,128)S(1)}, f32[1024,8]{...) custom-call(s32[2]{0:T(128)S(1)} %pad_add_fusion.place_ref, ...), custom_call_target="tpu_custom_call" | custom-call | tf_op jit(solution)/shard_map/pallas_call | solution.py:52
  12.8 2.1 %collective-permute-done.first_ref = bf16[512,128]{1,0:T(8,128)(2,1)S(1)} collective-permute-done((bf16[512,128]{1,0:T(8,128)(2,1)S(1)}, bf16[512,128]{1,0:T(8,128)(2,1)S(1)}, u32[]{:S(2)}, u32[]{:S(2)}) %collective-permute-start) | collective-permute-done | bytes 131104 | tf_op jit(solution)/shard_map/ppermute | solution.py:728
  14.9 9.7 %shard_map.195 = (bf16[4096,128]{1,0:T(8,128)(2,1)S(1)}, bf16[32768,128]{1,0:T(8,128)(2,1)}, bf16[4096,128]{1,0:T(8,128)(2,1)S(1)}, bf16[528,128]{1,0:T(8,128)(2,1)S(1)}) custom-call(s32[2]{0:T(128)S(1)} %pad_add_fusion.place_ref, bf16[4096,128]{1,0:T(8,128)(2,1)S(1)} %get-tuple-element.41.h_ref, bf16[512,128]{1,0:T(8,128)(2,1)S(1)} %collective-permute-done.first_ref, ...), custom_call_target="tpu_custom_call" | custom-call | tf_op jit(solution)/shard_map/pallas_call | solution.py:52
  24.7 1.8 %shard_map.196.mine_ref = bf16[528,128]{1,0:T(8,128)(2,1)S(1)} custom-call(s32[2]{0:T(128)S(1)} %pad_add_fusion.place_ref, s32[32,128]{1,0:T(8,128)S(1)} %get-tuple-element.46.owner_ref, bf16[4096,128]{1,0:T(8,128)(2,1)S(1)} %get-tuple-element.50.new_ref, bf16[16,128]{1,0:T(8,128)(2,1)S(1)} %get-tuple-element.47.counts_ref), custom_call_target="tpu_custom_call" | custom-call | tf_op jit(solution)/shard_map/pallas_call | solution.py:52
  26.5 2.8 %shard_map.198.after_ref.mine_ref = bf16[1024,128]{1,0:T(8,128)(2,1)S(1)} custom-call(s32[32,128]{1,0:T(8,128)S(1)} %get-tuple-element.46.owner_ref, bf16[4096,128]{1,0:T(8,128)(2,1)S(1)} %get-tuple-element.49.g_ref, bf16[528,128]{1,0:T(8,128)(2,1)S(1)} %shard_map.197.after_ref.totals_ref), custom_call_target="tpu_custom_call" | custom-call | tf_op jit(solution)/shard_map/pallas_call | solution.py:52
  29.9 1.5 %collective-permute-start.3 = (bf16[528,128]{1,0:T(8,128)(2,1)S(1)}, bf16[528,128]{1,0:T(8,128)(2,1)S(1)}, u32[]{:S(2)}, u32[]{:S(2)}) collective-permute-start(bf16[528,128]{1,0:T(8,128)(2,1)S(1)} %shard_map.197.after_ref.totals_ref), channel_id=1, source_target_pairs={{0,16},{8,24},{16,0},{24,8},{1,17},{9,25},{17,1},{25,9},{2,18},{10... | collective-permute-start | bytes 405512 | tf_op jit(solution)/shard_map/ppermute | solution.py:732
  32.7 3.6 %collective-permute-done.3.more_totals_ref = bf16[528,128]{1,0:T(8,128)(2,1)S(1)} collective-permute-done((bf16[528,128]{1,0:T(8,128)(2,1)S(1)}, bf16[528,128]{1,0:T(8,128)(2,1)S(1)}, u32[]{:S(2)}, u32[]{:S(2)}) %collective-permute-start.3) | collective-permute-done | bytes 135200 | tf_op jit(solution)/shard_map/ppermute | solution.py:732
  37.3 1.3 %collective-permute-done.4.their_half_ref = bf16[512,128]{1,0:T(8,128)(2,1)S(1)} collective-permute-done((bf16[512,128]{1,0:T(8,128)(2,1)S(1)}, bf16[512,128]{1,0:T(8,128)(2,1)S(1)}, u32[]{:S(2)}, u32[]{:S(2)}) %collective-permute-start.4) | collective-permute-done | bytes 131104 | tf_op jit(solution)/shard_map/ppermute | solution.py:732
  39.4 2.6 %collective-permute-start.5 = (bf16[64,128]{1,0:T(8,128)(2,1)S(1)}, bf16[64,128]{1,0:T(8,128)(2,1)S(1)}, u32[]{:S(2)}, u32[]{:S(2)}) collective-permute-start(bf16[64,128]{1,0:T(8,128)(2,1)S(1)} %get-tuple-element.55), channel_id=1, source_target_pairs={{0,1},{2,3},{4,5},{6,7},{1,0},{3,2},{5,4},{7,6},{8,9},{10,11},{12,... | collective-permute-start | bytes 49160 | tf_op jit(solution)/shard_map/ppermute | solution.py:728
  43.7 1.9 %shard_map.202 = (bf16[1024,128]{1,0:T(8,128)(2,1)S(1)}, bf16[8192,128]{1,0:T(8,128)(2,1)S(1)}) custom-call(bf16[1024,128]{1,0:T(8,128)(2,1)S(1)} %get-tuple-element.54.cin_ref, bf16[64,128]{1,0:T(8,128)(2,1)S(1)} %collective-permute-done.5.first_ref, bf16[64,128]{1,0:T(8,128)(2,1)S(1)} %collective-permute-done.6.second_ref, ...), custom_call_target="tpu_custom_call" | custom-call | tf_op jit(solution)/shard_map/pallas_call | solution.py:52
  45.6 1.6 %shard_map.204 = (f32[1024,128]{1,0:T(8,128)S(1)}, bf16[64,128]{1,0:T(8,128)(2,1)S(1)}, bf16[64,128]{1,0:T(8,128)(2,1)S(1)}, bf16[1024,128]{1,0:T(8,128)(2,1)S(1...) custom-call(bf16[8192,128]{1,0:T(8,128)(2,1)S(1)} %get-tuple-element.58.slope_ref, ...), custom_call_target="tpu_custom_call" | custom-call | tf_op jit(solution)/shard_map/pallas_call | solution.py:52
  47.2 5.0 %collective-permute-start.9 = (bf16[64,128]{1,0:T(8,128)(2,1)S(1)}, bf16[64,128]{1,0:T(8,128)(2,1)S(1)}, u32[]{:S(2)}, u32[]{:S(2)}) collective-permute-start(bf16[64,128]{1,0:T(8,128)(2,1)S(1)} %get-tuple-element.61.first_grad_ref), channel_id=1, source_target_pairs={{0,1},{2,3},{4,5},{6,7},{1,0},{3,2},{5,4},{7,6},{8,9},{10,11},{12,... | collective-permute-start | bytes 49160 | tf_op jit(solution)/shard_map/ppermute | solution.py:728
  54.8 10.2 %shard_map.207 = (bf16[4096,128]{1,0:T(8,128)(2,1)S(1)}, bf16[4096,256]{1,0:T(8,128)(2,1)S(1)}, bf16[512,128]{1,0:T(8,128)(2,1)S(1)}, bf16[512,128]{1,0:T(8,128)...) custom-call(s32[2]{0:T(128)S(1)} %pad_add_fusion.place_ref, bf16[4096,128]{1,0:T(8,128)(2,1)S(1)} %get-tuple-element.41.h_ref, ...), custom_call_target="tpu_custom_call" | custom-call | tf_op jit(solution)/shard_map/pallas_call | solution.py:52
  66.4 5.9 %collective-permute-start.14 = (bf16[320,128]{1,0:T(8,128)(2,1)S(1)}, bf16[320,128]{1,0:T(8,128)(2,1)S(1)}, u32[]{:S(2)}, u32[]{:S(2)}) collective-permute-start(bf16[320,128]{1,0:T(8,128)(2,1)S(1)} %shard_map.209.mine_ref), channel_id=1, source_target_pairs={{0,2},{1,3},{2,0},{3,1},{4,6},{5,7},{6,4},{7,5},{8,10},{9,11},{10,... | collective-permute-start | bytes 245768 | tf_op jit(solution)/shard_map/ppermute | solution.py:732
  72.3 1.5 %collective-permute-start.11 = (bf16[512,128]{1,0:T(8,128)(2,1)S(1)}, bf16[512,128]{1,0:T(8,128)(2,1)S(1)}, u32[]{:S(2)}, u32[]{:S(2)}) collective-permute-start(bf16[512,128]{1,0:T(8,128)(2,1)S(1)} %get-tuple-element.74), channel_id=1, source_target_pairs={{0,1},{2,3},{4,5},{6,7},{1,0},{3,2},{5,4},{7,6},{8,9},{10,11},{12,... | collective-permute-start | bytes 393224 | tf_op jit(solution)/shard_map/ppermute | solution.py:728
  75.1 2.8 %collective-permute-start.15 = (bf16[320,128]{1,0:T(8,128)(2,1)S(1)}, bf16[320,128]{1,0:T(8,128)(2,1)S(1)}, u32[]{:S(2)}, u32[]{:S(2)}) collective-permute-start(bf16[320,128]{1,0:T(8,128)(2,1)S(1)} %shard_map.210.mine_ref), channel_id=1, source_target_pairs={{0,4},{1,5},{2,6},{3,7},{4,0},{5,1},{6,2},{7,3},{8,12},{9,13},{10,... | collective-permute-start | bytes 245768 | tf_op jit(solution)/shard_map/ppermute | solution.py:732
  77.9 4.4 %shard_map.208.rest_0_ = bf16[4096,128]{1,0:T(8,128)(2,1)} custom-call(bf16[4096,128]{1,0:T(8,128)(2,1)S(1)} %get-tuple-element.72.ups_ref, bf16[4096,256]{1,0:T(8,128)(2,1)S(1)} %get-tuple-element.73.downs_ref, bf16[512,128]{1,0:T(8,128)(2,1)S(1)} %collective-permute-done.11.first_back_ref, bf16[512,128]{1,0:T(8,128)(2,1)S(1)} %collective-permute-done.12.second_back_ref, ...), custom_call_target="tpu_custom_call" | custom-call | tf_op jit(solution)/shard_map/pallas_call | solution.py:52
  82.2 1.7 %collective-permute-done.15.theirs_ref = bf16[320,128]{1,0:T(8,128)(2,1)S(1)} collective-permute-done((bf16[320,128]{1,0:T(8,128)(2,1)S(1)}, bf16[320,128]{1,0:T(8,128)(2,1)S(1)}, u32[]{:S(2)}, u32[]{:S(2)}) %collective-permute-start.15) | collective-permute-done | bytes 81952 | tf_op jit(solution)/shard_map/ppermute | solution.py:732
  83.9 4.2 %collective-permute-start.18 = (bf16[320,128]{1,0:T(8,128)(2,1)S(1)}, bf16[320,128]{1,0:T(8,128)(2,1)S(1)}, u32[]{:S(2)}, u32[]{:S(2)}) collective-permute-start(bf16[320,128]{1,0:T(8,128)(2,1)S(1)} %shard_map.211.mine_ref), channel_id=1, source_target_pairs={{0,17},{1,16},{2,19},{3,18},{4,21},{5,20},{6,23},{7,22},{8,25},{9,... | collective-permute-start | bytes 245768 | tf_op jit(solution)/shard_map/ppermute | solution.py:763
  88.8 3.9 %shard_map.206.after_ref = bf16[4096,128]{1,0:T(8,128)(2,1)} custom-call(bf16[4096,128]{1,0:T(8,128)(2,1)S(1)} %get-tuple-element.41.h_ref, bf16[4096,128]{1,0:T(8,128)(2,1)S(1)} %get-tuple-element.48.summed_ref, bf16[896,128]{1,0:T(8,128)(2,1)S(1)} %get-tuple-element.44.weights_ref.matrices_ref, f32[4096,8]{1,0:T(8,128)S(1)} %shard_map.199.owners_ref, ...), custom_call_target="tpu_custom_call" | custom-call | tf_op jit(solution)/shard_map/pallas_call | solution.py:52
  93.2 1.5 %collective-permute-done.19.theirs_ref = f32[448,128]{1,0:T(8,128)S(1)} collective-permute-done((f32[448,128]{1,0:T(8,128)S(1)}, f32[448,128]{1,0:T(8,128)S(1)}, u32[]{:S(2)}, u32[]{:S(2)}) %collective-permute-start.19) | collective-permute-done | bytes 229408 | tf_op jit(solution)/shard_map/ppermute | solution.py:732
  94.7 1.3 %shard_map.213 = f32[896,128]{1,0:T(8,128)} custom-call(s32[2]{0:T(128)S(1)} %pad_add_fusion.place_ref, f32[448,128]{1,0:T(8,128)S(1)} %shard_map.212.mine_ref, f32[448,128]{1,0:T(8,128)S(1)} %collective-permute-done.19.theirs_ref), custom_call_target="tpu_custom_call" | custom-call | tf_op jit(solution)/shard_map/pallas_call | solution.py:52
  (38 shorter events, 12.6 us)
Async XLA Ops:
  3.5 9.2 %collective-permute-start.1 = (bf16[512,128]{1,0:T(8,128)(2,1)S(1)}, bf16[512,128]{1,0:T(8,128)(2,1)S(1)}, u32[]{:S(2)}, u32[]{:S(2)}) collective-permute-start(bf16[512,128]{1,0:T(8,128)(2,1)S(1)} %get-tuple-element.43), channel_id=1, source_target_pairs={{1,2},{3,4},{5,6},{2,1},{4,3},{6,5},{9,10},{11,12},{13,14},{10,9},... | collective-permute-start | bytes 393224 | tf_op jit(solution)/shard_map/ppermute | solution.py:728
  4.2 10.6 %collective-permute-start = (bf16[512,128]{1,0:T(8,128)(2,1)S(1)}, bf16[512,128]{1,0:T(8,128)(2,1)S(1)}, u32[]{:S(2)}, u32[]{:S(2)}) collective-permute-start(bf16[512,128]{1,0:T(8,128)(2,1)S(1)} %get-tuple-element.42.rest_7_), channel_id=1, source_target_pairs={{0,1},{2,3},{4,5},{6,7},{1,0},{3,2},{5,4},{7,6},{8,9},{10,11},{12,... | collective-permute-start | bytes 393224 | tf_op jit(solution)/shard_map/ppermute | solution.py:728
  24.6 1.9 %collective-permute-start.2 = (bf16[528,128]{1,0:T(8,128)(2,1)S(1)}, bf16[528,128]{1,0:T(8,128)(2,1)S(1)}, u32[]{:S(2)}, u32[]{:S(2)}) collective-permute-start(bf16[528,128]{1,0:T(8,128)(2,1)S(1)} %get-tuple-element.51), channel_id=1, source_target_pairs={{0,8},{8,0},{16,24},{24,16},{1,9},{9,1},{17,25},{25,17},{2,10},{10... | collective-permute-start | bytes 405512 | tf_op jit(solution)/shard_map/ppermute | solution.py:732
  29.3 2.0 %collective-permute-start.7 = (bf16[1024,128]{1,0:T(8,128)(2,1)S(1)}, bf16[1024,128]{1,0:T(8,128)(2,1)S(1)}, u32[]{:S(2)}, u32[]{:S(2)}) collective-permute-start(bf16[1024,128]{1,0:T(8,128)(2,1)S(1)} %shard_map.198.after_ref.mine_ref), channel_id=1, source_target_pairs={{0,8},{8,0},{16,24},{24,16},{1,9},{9,1},{17,25},{25,17},{2,10},{10... | collective-permute-start | bytes 786440 | tf_op jit(solution)/shard_map/ppermute | solution.py:732
  29.9 6.4 %collective-permute-start.3 = (bf16[528,128]{1,0:T(8,128)(2,1)S(1)}, bf16[528,128]{1,0:T(8,128)(2,1)S(1)}, u32[]{:S(2)}, u32[]{:S(2)}) collective-permute-start(bf16[528,128]{1,0:T(8,128)(2,1)S(1)} %shard_map.197.after_ref.totals_ref), channel_id=1, source_target_pairs={{0,16},{8,24},{16,0},{24,8},{1,17},{9,25},{17,1},{25,9},{2,18},{10... | collective-permute-start | bytes 405512 | tf_op jit(solution)/shard_map/ppermute | solution.py:732
  31.4 14.1 %collective-permute-start.8 = (bf16[1024,128]{1,0:T(8,128)(2,1)S(1)}, bf16[1024,128]{1,0:T(8,128)(2,1)S(1)}, u32[]{:S(2)}, u32[]{:S(2)}) collective-permute-start(bf16[1024,128]{1,0:T(8,128)(2,1)S(1)} %shard_map.203.chip_sums_ref), channel_id=1, source_target_pairs={{0,16},{8,24},{16,0},{24,8},{1,17},{9,25},{17,1},{25,9},{2,18},{10... | collective-permute-start | bytes 786440 | tf_op jit(solution)/shard_map/ppermute | solution.py:732
  37.2 1.4 %collective-permute-start.4 = (bf16[512,128]{1,0:T(8,128)(2,1)S(1)}, bf16[512,128]{1,0:T(8,128)(2,1)S(1)}, u32[]{:S(2)}, u32[]{:S(2)}) collective-permute-start(bf16[512,128]{1,0:T(8,128)(2,1)S(1)} %get-tuple-element.52.half_ref), channel_id=1, source_target_pairs={{0,8},{8,0},{16,24},{24,16},{1,9},{9,1},{17,25},{25,17},{2,10},{10... | collective-permute-start | bytes 393224 | tf_op jit(solution)/shard_map/ppermute | solution.py:732
  39.4 4.3 %collective-permute-start.5 = (bf16[64,128]{1,0:T(8,128)(2,1)S(1)}, bf16[64,128]{1,0:T(8,128)(2,1)S(1)}, u32[]{:S(2)}, u32[]{:S(2)}) collective-permute-start(bf16[64,128]{1,0:T(8,128)(2,1)S(1)} %get-tuple-element.55), channel_id=1, source_target_pairs={{0,1},{2,3},{4,5},{6,7},{1,0},{3,2},{5,4},{7,6},{8,9},{10,11},{12,... | collective-permute-start | bytes 49160 | tf_op jit(solution)/shard_map/ppermute | solution.py:728
  42.0 1.7 %collective-permute-start.6 = (bf16[64,128]{1,0:T(8,128)(2,1)S(1)}, bf16[64,128]{1,0:T(8,128)(2,1)S(1)}, u32[]{:S(2)}, u32[]{:S(2)}) collective-permute-start(bf16[64,128]{1,0:T(8,128)(2,1)S(1)} %get-tuple-element.56), channel_id=1, source_target_pairs={{1,2},{3,4},{5,6},{2,1},{4,3},{6,5},{9,10},{11,12},{13,14},{10,9},... | collective-permute-start | bytes 49160 | tf_op jit(solution)/shard_map/ppermute | solution.py:728
  47.2 7.6 %collective-permute-start.9 = (bf16[64,128]{1,0:T(8,128)(2,1)S(1)}, bf16[64,128]{1,0:T(8,128)(2,1)S(1)}, u32[]{:S(2)}, u32[]{:S(2)}) collective-permute-start(bf16[64,128]{1,0:T(8,128)(2,1)S(1)} %get-tuple-element.61.first_grad_ref), channel_id=1, source_target_pairs={{0,1},{2,3},{4,5},{6,7},{1,0},{3,2},{5,4},{7,6},{8,9},{10,11},{12,... | collective-permute-start | bytes 49160 | tf_op jit(solution)/shard_map/ppermute | solution.py:728
  52.2 2.6 %collective-permute-start.10 = (bf16[64,128]{1,0:T(8,128)(2,1)S(1)}, bf16[64,128]{1,0:T(8,128)(2,1)S(1)}, u32[]{:S(2)}, u32[]{:S(2)}) collective-permute-start(bf16[64,128]{1,0:T(8,128)(2,1)S(1)} %get-tuple-element.62.second_grad_ref), channel_id=1, source_target_pairs={{1,2},{3,4},{5,6},{2,1},{4,3},{6,5},{9,10},{11,12},{13,14},{10,9},... | collective-permute-start | bytes 49160 | tf_op jit(solution)/shard_map/ppermute | solution.py:728
  65.0 1.4 %collective-permute-start.13 = (f32[192,128]{1,0:T(8,128)S(1)}, f32[192,128]{1,0:T(8,128)S(1)}, u32[]{:S(2)}, u32[]{:S(2)}) collective-permute-start(f32[192,128]{1,0:T(8,128)S(1)} %get-tuple-element.78), channel_id=1, source_target_pairs={{0,8},{8,0},{16,24},{24,16},{1,9},{9,1},{17,25},{25,17},{2,10},{10... | collective-permute-start | bytes 294920 | tf_op jit(solution)/shard_map/ppermute | solution.py:732
  66.4 8.6 %collective-permute-start.14 = (bf16[320,128]{1,0:T(8,128)(2,1)S(1)}, bf16[320,128]{1,0:T(8,128)(2,1)S(1)}, u32[]{:S(2)}, u32[]{:S(2)}) collective-permute-start(bf16[320,128]{1,0:T(8,128)(2,1)S(1)} %shard_map.209.mine_ref), channel_id=1, source_target_pairs={{0,2},{1,3},{2,0},{3,1},{4,6},{5,7},{6,4},{7,5},{8,10},{9,11},{10,... | collective-permute-start | bytes 245768 | tf_op jit(solution)/shard_map/ppermute | solution.py:732
  72.3 5.6 %collective-permute-start.11 = (bf16[512,128]{1,0:T(8,128)(2,1)S(1)}, bf16[512,128]{1,0:T(8,128)(2,1)S(1)}, u32[]{:S(2)}, u32[]{:S(2)}) collective-permute-start(bf16[512,128]{1,0:T(8,128)(2,1)S(1)} %get-tuple-element.74), channel_id=1, source_target_pairs={{0,1},{2,3},{4,5},{6,7},{1,0},{3,2},{5,4},{7,6},{8,9},{10,11},{12,... | collective-permute-start | bytes 393224 | tf_op jit(solution)/shard_map/ppermute | solution.py:728
  73.8 4.1 %collective-permute-start.12 = (bf16[512,128]{1,0:T(8,128)(2,1)S(1)}, bf16[512,128]{1,0:T(8,128)(2,1)S(1)}, u32[]{:S(2)}, u32[]{:S(2)}) collective-permute-start(bf16[512,128]{1,0:T(8,128)(2,1)S(1)} %get-tuple-element.75), channel_id=1, source_target_pairs={{1,2},{3,4},{5,6},{2,1},{4,3},{6,5},{9,10},{11,12},{13,14},{10,9},... | collective-permute-start | bytes 393224 | tf_op jit(solution)/shard_map/ppermute | solution.py:728
  75.1 8.9 %collective-permute-start.15 = (bf16[320,128]{1,0:T(8,128)(2,1)S(1)}, bf16[320,128]{1,0:T(8,128)(2,1)S(1)}, u32[]{:S(2)}, u32[]{:S(2)}) collective-permute-start(bf16[320,128]{1,0:T(8,128)(2,1)S(1)} %shard_map.210.mine_ref), channel_id=1, source_target_pairs={{0,4},{1,5},{2,6},{3,7},{4,0},{5,1},{6,2},{7,3},{8,12},{9,13},{10,... | collective-permute-start | bytes 245768 | tf_op jit(solution)/shard_map/ppermute | solution.py:732
  83.9 8.8 %collective-permute-start.18 = (bf16[320,128]{1,0:T(8,128)(2,1)S(1)}, bf16[320,128]{1,0:T(8,128)(2,1)S(1)}, u32[]{:S(2)}, u32[]{:S(2)}) collective-permute-start(bf16[320,128]{1,0:T(8,128)(2,1)S(1)} %shard_map.211.mine_ref), channel_id=1, source_target_pairs={{0,17},{1,16},{2,19},{3,18},{4,21},{5,20},{6,23},{7,22},{8,25},{9,... | collective-permute-start | bytes 245768 | tf_op jit(solution)/shard_map/ppermute | solution.py:763
  88.1 4.6 %collective-permute-start.17 = (bf16[320,128]{1,0:T(8,128)(2,1)S(1)}, bf16[320,128]{1,0:T(8,128)(2,1)S(1)}, u32[]{:S(2)}, u32[]{:S(2)}) collective-permute-start(bf16[320,128]{1,0:T(8,128)(2,1)S(1)} %shard_map.211.mine_ref), channel_id=1, source_target_pairs={{0,16},{8,24},{16,0},{24,8},{1,17},{9,25},{17,1},{25,9},{2,18},{10... | collective-permute-start | bytes 245768 | tf_op jit(solution)/shard_map/ppermute | solution.py:732
  88.7 4.4 %collective-permute-start.16 = (bf16[320,128]{1,0:T(8,128)(2,1)S(1)}, bf16[320,128]{1,0:T(8,128)(2,1)S(1)}, u32[]{:S(2)}, u32[]{:S(2)}) collective-permute-start(bf16[320,128]{1,0:T(8,128)(2,1)S(1)} %shard_map.211.mine_ref), channel_id=1, source_target_pairs={{0,1},{1,0},{2,3},{3,2},{4,5},{5,4},{6,7},{7,6},{8,9},{9,8},{10,11... | collective-permute-start | bytes 245768 | tf_op jit(solution)/shard_map/ppermute | solution.py:732
  93.1 1.6 %collective-permute-start.19 = (f32[448,128]{1,0:T(8,128)S(1)}, f32[448,128]{1,0:T(8,128)S(1)}, u32[]{:S(2)}, u32[]{:S(2)}) collective-permute-start(f32[448,128]{1,0:T(8,128)S(1)} %shard_map.212.mine_ref), channel_id=1, source_target_pairs={{0,8},{8,0},{16,24},{24,16},{1,9},{9,1},{17,25},{25,17},{2,10},{10... | collective-permute-start | bytes 688136 | tf_op jit(solution)/shard_map/ppermute | solution.py:732

commit v12 on v11

--- a/solution.py
+++ b/solution.py
@@ -63,11 +63,27 @@
     return jax.ShapeDtypeStruct((rows, columns), dtype)
 
 
+def lanes(row, count):
+    return row[:, :count] if count < 128 else jnp.concatenate([row] * (count // 128), 1)
+
+
+def is_even(place_ref):
+    return place_ref[0:1, :]
+
+
+def group_of(place_ref):
+    return place_ref[8:9, :]
+
+
+def core_of(place_ref):
+    return lax.rem(place_ref[8:9, :], 2)
+
+
 def slot_columns(nbr, mask, halo_rows, even):
     rows = nbr.shape[1]
     block = lax.broadcasted_iota(jnp.int32, nbr.shape, 1) // BLOCK
     halo = lax.rem(block, halo_rows // BLOCK) * BLOCK
-    lower = jnp.where(even, 2 * BLOCK, BLOCK)
+    lower = BLOCK + BLOCK * lanes(even, rows)
     column = jnp.where(
         nbr < rows,
         nbr - block * BLOCK,
@@ -191,7 +207,20 @@
 
 
 def gather_kernel(
-    place_ref, lo_hbm, hi_hbm, x_hbm, first_ref, second_ref, x_ref, wide, up, down, lo, hi, sems
+    place_ref,
+    lo_hbm,
+    hi_hbm,
+    x_hbm,
+    first_ref,
+    second_ref,
+    x_ref,
+    vector_ref,
+    wide,
+    up,
+    down,
+    lo,
+    hi,
+    sems,
 ):
     fetch([(x_hbm, x_ref), (lo_hbm, lo), (hi_hbm, hi)], sems)
     wide[...] = x_ref[...].astype(f32)
@@ -203,6 +232,8 @@
 
     lax.fori_loop(0, up.shape[0], step, None, unroll=16)
     even = place_ref[0] > 0
+    vector_ref[:8, :] = jnp.full((8, 128), place_ref[0], jnp.int32)
+    vector_ref[8:, :] = jnp.full((8, 128), place_ref[1], jnp.int32)
     first_ref[...] = jnp.where(even, up[...], down[...]).astype(bf16)
     second_ref[...] = jnp.where(even, down[...], up[...]).astype(bf16)
 
@@ -213,7 +244,7 @@
     out = shape(count, features, bf16)
     return call(
         gather_kernel,
-        [out, out, shape(rows, features, bf16)],
+        [out, out, shape(rows, features, bf16), shape(16, 128, jnp.int32)],
         [place, send_lo, send_hi, x],
         [SMEM, HBM, HBM, HBM],
         [
@@ -295,13 +326,14 @@
         + [(w, weights_ref.at[pl.ds(128 * n, 128), :]) for n, w in enumerate(weight_hbms)],
         sems,
     )
-    even = place_ref[0] > 0
+    even = is_even(place_ref)
     for low, high, out in (
         (lo_ref, hi_ref, sends_ref),
         (coarse_lo_ref, coarse_hi_ref, coarse_sends_ref),
     ):
-        first = jnp.where(even, high[...], low[...])
-        second = jnp.where(even, low[...], high[...])
+        up = lanes(even, low.shape[1]) > 0
+        first = jnp.where(up, high[...], low[...])
+        second = jnp.where(up, low[...], high[...])
         out[...] = jnp.concatenate([first, second], 1)
     columns_ref[...] = slot_columns(nbr_ref[...], mask_ref[...], halo_rows, even)
     columns_t_ref[...] = columns_ref[...].T
@@ -346,7 +378,7 @@
 
 
 def keep_kernel(place_ref, owner_ref, new_ref, counts_ref, out_ref):
-    half_totals(owner_ref, new_ref, counts_ref, lax.rem(place_ref[1], 2), out_ref)
+    half_totals(owner_ref, new_ref, counts_ref, core_of(place_ref), out_ref)
 
 
 def fine_forward_kernel(
@@ -384,7 +416,7 @@
     new_ref[...] = (
         h_ref[...].astype(f32) + dot(summed_ref[...], matrix(weights_ref, 2))
     ).astype(bf16)
-    half_totals(owner_ref, new_ref, counts_ref, 1 - lax.rem(place_ref[1], 2), give_ref)
+    half_totals(owner_ref, new_ref, counts_ref, 1 - core_of(place_ref), give_ref)
     pltpu.make_async_copy(slope_ref, slope_hbm, sem).wait()
 
 
@@ -395,32 +427,38 @@
     tiles = counts_ref.shape[0]
     counts_ref[...] = DIGIT * digits[:tiles] + digits[tiles:]
     per_row = counts_ref[...].T
-    first = lax.rem(place_ref[1], 2) == 0
+    first = core_of(place_ref) == 0
     for tile in range(tiles // 2):
         here = slice(tile * 128, (tile + 1) * 128)
         later = tile + tiles // 2
-        count = jnp.where(first, per_row[:, tile : tile + 1], per_row[:, later : later + 1])
-        half_ref[here, :] = (totals[here] / count).astype(bf16)
+        low = jnp.broadcast_to(per_row[:, tile : tile + 1], (128, 128))
+        high = jnp.broadcast_to(per_row[:, later : later + 1], (128, 128))
+        half_ref[here, :] = (totals[here] / jnp.where(first, low, high)).astype(bf16)
 
 
 def coarse_input_kernel(
     place_ref,
     half_ref,
     their_half_ref,
+    sums_ref,
+    more_sums_ref,
     sends_ref,
     cin_ref,
     first_ref,
     second_ref,
+    chip_sums_ref,
 ):
-    mine, theirs = half_ref[...], their_half_ref[...]
-    first = lax.rem(place_ref[1], 2) == 0
+    mine, theirs = half_ref[...].astype(f32), their_half_ref[...].astype(f32)
+    first = core_of(place_ref) == 0
     cin = jnp.concatenate([jnp.where(first, mine, theirs), jnp.where(first, theirs, mine)], 0)
+    cin = cin.astype(bf16)
     cin_ref[...] = cin
     place = lax.broadcasted_iota(jnp.int32, (cin.shape[0], sends_ref.shape[1]), 0)
     sent = dot_tn(pick(sends_ref[...] == place), cin).astype(bf16)
     halo_rows = first_ref.shape[0]
     first_ref[...] = sent[:halo_rows]
     second_ref[...] = sent[halo_rows:]
+    chip_sums_ref[...] = (sums_ref[...].astype(f32) + more_sums_ref[...].astype(f32)).astype(bf16)
 
 
 def coarse_forward_kernel(
@@ -515,7 +553,7 @@
         dot_tn(summed_ref[...], ups_ref[...]),
         dot_tn(out, sums_ref[...]),
     ]
-    weights_ref[...] = choose(place_ref[1], grads).astype(bf16)
+    weights_ref[...] = choose(group_of(place_ref), grads).astype(bf16)
 
 
 def choose(place, values):
@@ -649,9 +687,10 @@
         + dot_tn(second_ref[...], second_grad)
     )
     weights[256:384, :] = dot_tn(summed_ref[...], ups_ref[...])
-    core = lax.rem(place_ref[1], 2)
-    give_ref[...] = weights[pl.ds(pl.multiple_of((1 - core) * 192, 64), 192), :]
-    keep_ref[:192, :] = weights[pl.ds(pl.multiple_of(core * 192, 64), 192), :]
+    first = core_of(place_ref) == 0
+    low, high = weights[:192, :], weights[192:, :]
+    give_ref[...] = jnp.where(first, high, low)
+    keep_ref[:192, :] = jnp.where(first, low, high)
     keep_ref[192:, :] = coarse_weights_ref[...].astype(f32)
 
 
@@ -707,15 +746,15 @@
 
 
 def weights_kernel(place_ref, mine_ref, theirs_ref, out_ref):
-    group = place_ref[1]
+    group = group_of(place_ref)
     low, high = lax.rem(group, 2), group // 2
     mine, theirs = mine_ref[:192, :], theirs_ref[:192, :]
     out_ref[:192, :] = jnp.where(low == 0, mine, theirs)
     out_ref[192:384, :] = jnp.where(low == 0, theirs, mine)
     for n in range(4):
-        row = jnp.where(high == n // 2, 192, 320)
-        here = pl.ds(pl.multiple_of(row, 64), 128)
-        value = jnp.where(low == n % 2, mine_ref[here, :], theirs_ref[here, :])
+        near = jnp.where(low == n % 2, mine_ref[192:320, :], theirs_ref[192:320, :])
+        far = jnp.where(low == n % 2, mine_ref[320:448, :], theirs_ref[320:448, :])
+        value = jnp.where(high == n // 2, near, far)
         out_ref[384 + 128 * n : 512 + 128 * n, :] = value
 
 
@@ -769,7 +808,7 @@
         weights_kernel,
         shape(896, 128, f32),
         [place, weights, swapped(weights, "grp", 1)],
-        [SMEM, VMEM, VMEM],
+        [VMEM] * 3,
     )
 
 
@@ -804,7 +843,7 @@
     def buffer(count, columns, dtype):
         return pltpu.VMEM((count, columns), dtype)
 
-    to_first, to_second, states = gather_rows(place, states, fine_send_lo, fine_send_hi)
+    to_first, to_second, states, place = gather_rows(place, states, fine_send_lo, fine_send_hi)
     first, second = exchange(to_first, to_second)
 
     (
@@ -830,7 +869,7 @@
             fine_self, fine_other, fine_node, coarse_self, coarse_other, coarse_node, prolong,
             to_first,
         ],
-        [SMEM] + [HBM] * 17 + [ANY],
+        [VMEM] + [HBM] * 17 + [ANY],
         [buffer(8, rows, jnp.int32)] * 2
         + [buffer(8, coarse_rows, jnp.int32)] * 2
         + [buffer(1, halo_rows, jnp.int32)] * 2
@@ -848,7 +887,7 @@
             shape(half_rows, features, bf16),
         ],
         [place, states, first, second, matrices, columns_t, owner, counts],
-        [SMEM] + [VMEM] * 7,
+        [VMEM] + [VMEM] * 7,
         [
             buffer(rows, features, f32),
             buffer(rows, features, bf16),
@@ -864,7 +903,7 @@
         keep_kernel,
         shape(half_rows, features, bf16),
         [place, owner, new, counts],
-        [SMEM] + [VMEM] * 3,
+        [VMEM] + [VMEM] * 3,
     )
     chip_totals = call(add_kernel, shape(half_rows, features, bf16), [keep, theirs])
     more_totals = swapped(chip_totals, "grp", 2)
@@ -881,19 +920,18 @@
         half_kernel,
         [shape(coarse_rows // 2, features, bf16), shape(count_rows, features, f32)],
         [place, chip_totals, more_totals, sums],
-        [SMEM, VMEM, VMEM, ANY],
+        [VMEM, VMEM, VMEM, ANY],
     )
     their_half = swapped(half, "grp", 1)
-    chip_sums = call(add_kernel, shape(coarse_rows, features, bf16), [sums, more_sums])
-    coarse_in, to_first, to_second = call(
+    coarse_in, to_first, to_second, chip_sums = call(
         coarse_input_kernel,
         [
             shape(coarse_rows, features, bf16),
             shape(coarse_halo, features, bf16),
             shape(coarse_halo, features, bf16),
-        ],
-        [place, half, their_half, coarse_sends],
-        [SMEM] + [VMEM] * 3,
+            shape(coarse_rows, features, bf16),
+        ],
+        [place, half, their_half, sums, more_sums, coarse_sends],
     )
     coarse_first, coarse_second = exchange(to_first, to_second)
     more_sums = swapped(chip_sums, "grp", 2)
@@ -933,7 +971,7 @@
             place, coarse_in, coarse_first, coarse_second, sums, matrices,
             first_grad, second_grad, coarse_sum, coarse_ups, coarse_downs,
         ],
-        [SMEM] + [VMEM] * 10,
+        [VMEM] + [VMEM] * 10,
     )
     result = call(
         result_kernel,
@@ -958,7 +996,7 @@
             coarse_part, counts, coarse_downs, first_back, second_back, coarse_sends,
             coarse_weights,
         ],
-        [SMEM] + [VMEM] * 5 + [HBM] + [VMEM] * 10,
+        [VMEM] + [VMEM] * 5 + [HBM] + [VMEM] * 10,
         [
             buffer(rows, features, bf16),
             buffer(2 * halo_rows, features, f32),

time: 97 us -> 91.2 us (0.940)
  Pallas kernels: 46.8 us -> 42.1 us
    pallas_call x21 -> x20, Pallas kernels: 46.8 us -> 42.1 us  [call(): pl.pallas_call(kernel, out_shape=out_shape, in_specs=in_specs, out_specs=...]
    ppermute x11, starting transfers between devices: 12.9 us -> 14.4 us  [swapped(): lax.ppermute(block, axis, [(i, i ^ distance) for i in range(lax.axis_size...]
    ppermute x11, waiting for transfers between devices: 10.3 us -> 9.08 us  [swapped(): lax.ppermute(block, axis, [(i, i ^ distance) for i in range(lax.axis_size...]
  transfers between devices with their start and end apart: 20 -> 20, of which waited for: 9 -> 11; matrix products, arithmetic and copies ran while one was open for 0% -> 0% of each run, Pallas kernels for 19% -> 20%
where the time goes in v12:
time: 91.2 us; the launch traced here: 90.4 us
  Pallas kernels  42.1 us (46%)
  starting transfers between devices  34.5 us (38%)
  waiting for transfers between devices  12.8 us (14%)
    pallas_call x20, Pallas kernels, call(): pl.pallas_call(kernel, out_shape=out_shape, in_specs=in_specs, out_specs=...  42.1 us
    ppermute x11, starting transfers between devices, swapped(): lax.ppermute(block, axis, [(i, i ^ distance) for i in range(lax.axis_size...  14.4 us
    ppermute x4, starting transfers between devices, exchange(): lax.ppermute(first, 'sub', routes[0])  14 us
    ppermute x11, waiting for transfers between devices, swapped(): lax.ppermute(block, axis, [(i, i ^ distance) for i in range(lax.axis_size...  9.08 us
    ppermute x4, waiting for transfers between devices, exchange(): lax.ppermute(first, 'sub', routes[0])  3.69 us
    ppermute x1, starting transfers between devices, total_weights(): lax.ppermute(weights, ('grp', 'sub'), corners)  3.34 us
    ppermute x4, starting transfers between devices, exchange(): lax.ppermute(second, 'sub', routes[1])  2.81 us
  transfers between devices with their start and end apart: 20, of which 11 were waited for; matrix products, arithmetic and copies ran while one was open for 0% of the time, Pallas kernels for 20%

profile of v12, /device:TPU:0, one launch (start us, length us, event | category | flops | bytes accessed | tf_op | source)
XLA Modules:
  0.0 90.4 jit_solution(235177591709069337)
XLA Ops:
  0.7 2.8 %shard_map.193 = (bf16[512,128]{1,0:T(8,128)(2,1)S(1)}, bf16[512,128]{1,0:T(8,128)(2,1)S(1)}, bf16[4096,128]{1,0:T(8,128)(2,1)S(1)}, s32[16,128]{1,0:T(8,128)S(1)}) custom-call(s32[2]{0:T(128)S(1)} %pad_add_fusion.place_ref, s32[512]{0:T(512)} %lo_hbm.1, s32[512]{0:T(512)} %hi_hbm.1, bf16[4096,128]{1,0:T(8,128)(2,1)} %x_hbm.1), custom_call_target="tpu_custom_call" | custom-call | tf_op jit(solution)/shard_map/pallas_call | solution.py:52
  4.2 5.8 %collective-permute-start = (bf16[512,128]{1,0:T(8,128)(2,1)S(1)}, bf16[512,128]{1,0:T(8,128)(2,1)S(1)}, u32[]{:S(2)}, u32[]{:S(2)}) collective-permute-start(bf16[512,128]{1,0:T(8,128)(2,1)S(1)} %get-tuple-element.45.rest_7_), channel_id=1, source_target_pairs={{0,1},{2,3},{4,5},{6,7},{1,0},{3,2},{5,4},{7,6},{8,9},{10,11},{12,... | collective-permute-start | bytes 393224 | tf_op jit(solution)/shard_map/ppermute | solution.py:767
  10.0 2.2 %shard_map.194 = (bf16[16,128]{1,0:T(8,128)(2,1)S(1)}, f32[8,4096]{1,0:T(8,128)S(1)}, f32[4096,8]{1,0:T(8,128)S(1)}, f32[8,1024]{1,0:T(8,128)S(1)}, f32[1024,8]{...) custom-call(s32[16,128]{1,0:T(8,128)S(1)} %get-tuple-element.44.plac, ...), custom_call_target="tpu_custom_call" | custom-call | tf_op jit(solution)/shard_map/pallas_call | solution.py:52
  12.2 2.6 %collective-permute-done.first_ref = bf16[512,128]{1,0:T(8,128)(2,1)S(1)} collective-permute-done((bf16[512,128]{1,0:T(8,128)(2,1)S(1)}, bf16[512,128]{1,0:T(8,128)(2,1)S(1)}, u32[]{:S(2)}, u32[]{:S(2)}) %collective-permute-start) | collective-permute-done | bytes 131104 | tf_op jit(solution)/shard_map/ppermute | solution.py:767
  14.9 9.2 %shard_map.195 = (bf16[4096,128]{1,0:T(8,128)(2,1)S(1)}, bf16[32768,128]{1,0:T(8,128)(2,1)}, bf16[4096,128]{1,0:T(8,128)(2,1)S(1)}, bf16[528,128]{1,0:T(8,128)(2,1)S(1)}) custom-call(s32[16,128]{1,0:T(8,128)S(1)} %get-tuple-element.44.place_ref, bf16[4096,128]{1,0:T(8,128)(2,1)S(1)} %get-tuple-element.43.h_ref, ...), custom_call_target="tpu_custom_call" | custom-call | tf_op jit(solution)/shard_map/pallas_call | solution.py:52
  25.5 1.6 %collective-permute-start.3 = (bf16[528,128]{1,0:T(8,128)(2,1)S(1)}, bf16[528,128]{1,0:T(8,128)(2,1)S(1)}, u32[]{:S(2)}, u32[]{:S(2)}) collective-permute-start(bf16[528,128]{1,0:T(8,128)(2,1)S(1)} %shard_map.197.after_ref.totals_ref), channel_id=1, source_target_pairs={{0,16},{8,24},{16,0},{24,8},{1,17},{9,25},{17,1},{25,9},{2,18},{10... | collective-permute-start | bytes 405512 | tf_op jit(solution)/shard_map/ppermute | solution.py:771
  27.0 2.8 %shard_map.198.after_ref.sums_ref = bf16[1024,128]{1,0:T(8,128)(2,1)S(1)} custom-call(s32[32,128]{1,0:T(8,128)S(1)} %get-tuple-element.49.owner_ref, bf16[4096,128]{1,0:T(8,128)(2,1)S(1)} %get-tuple-element.52.g_ref, bf16[528,128]{1,0:T(8,128)(2,1)S(1)} %shard_map.197.after_ref.totals_ref), custom_call_target="tpu_custom_call" | custom-call | tf_op jit(solution)/shard_map/pallas_call | solution.py:52
  30.1 1.4 %collective-permute-done.3.more_totals_ref = bf16[528,128]{1,0:T(8,128)(2,1)S(1)} collective-permute-done((bf16[528,128]{1,0:T(8,128)(2,1)S(1)}, bf16[528,128]{1,0:T(8,128)(2,1)S(1)}, u32[]{:S(2)}, u32[]{:S(2)}) %collective-permute-start.3) | collective-permute-done | bytes 135200 | tf_op jit(solution)/shard_map/ppermute | solution.py:771
  31.9 1.3 %collective-permute-done.4.their_half_ref = bf16[512,128]{1,0:T(8,128)(2,1)S(1)} collective-permute-done((bf16[512,128]{1,0:T(8,128)(2,1)S(1)}, bf16[512,128]{1,0:T(8,128)(2,1)S(1)}, u32[]{:S(2)}, u32[]{:S(2)}) %collective-permute-start.4) | collective-permute-done | bytes 131104 | tf_op jit(solution)/shard_map/ppermute | solution.py:771
  33.6 1.6 %collective-permute-start.8 = (bf16[1024,128]{1,0:T(8,128)(2,1)S(1)}, bf16[1024,128]{1,0:T(8,128)(2,1)S(1)}, u32[]{:S(2)}, u32[]{:S(2)}) collective-permute-start(bf16[1024,128]{1,0:T(8,128)(2,1)S(1)} %get-tuple-element.62.chip_sums_ref), channel_id=1, source_target_pairs={{0,16},{8,24},{16,0},{24,8},{1,17},{9,25},{17,1},{25,9},{2,18},{10... | collective-permute-start | bytes 786440 | tf_op jit(solution)/shard_map/ppermute | solution.py:771
  35.1 2.5 %collective-permute-start.6 = (bf16[64,128]{1,0:T(8,128)(2,1)S(1)}, bf16[64,128]{1,0:T(8,128)(2,1)S(1)}, u32[]{:S(2)}, u32[]{:S(2)}) collective-permute-start(bf16[64,128]{1,0:T(8,128)(2,1)S(1)} %get-tuple-element.58), channel_id=1, source_target_pairs={{0,1},{2,3},{4,5},{6,7},{1,0},{3,2},{5,4},{7,6},{8,9},{10,11},{12,... | collective-permute-start | bytes 49160 | tf_op jit(solution)/shard_map/ppermute | solution.py:767
  39.4 1.9 %shard_map.202 = (bf16[1024,128]{1,0:T(8,128)(2,1)S(1)}, bf16[8192,128]{1,0:T(8,128)(2,1)S(1)}) custom-call(bf16[1024,128]{1,0:T(8,128)(2,1)S(1)} %get-tuple-element.57.cin_ref, bf16[64,128]{1,0:T(8,128)(2,1)S(1)} %collective-permute-done.6.first_ref, bf16[64,128]{1,0:T(8,128)(2,1)S(1)} %collective-permute-done.7.second_ref, ...), custom_call_target="tpu_custom_call" | custom-call | tf_op jit(solution)/shard_map/pallas_call | solution.py:52
  42.0 1.6 %shard_map.203 = (f32[1024,128]{1,0:T(8,128)S(1)}, bf16[64,128]{1,0:T(8,128)(2,1)S(1)}, bf16[64,128]{1,0:T(8,128)(2,1)S(1)}, bf16[1024,128]{1,0:T(8,128)(2,1)S(1...) custom-call(bf16[8192,128]{1,0:T(8,128)(2,1)S(1)} %get-tuple-element.61.slope_ref, ...), custom_call_target="tpu_custom_call" | custom-call | tf_op jit(solution)/shard_map/pallas_call | solution.py:52
  43.6 4.2 %collective-permute-start.9 = (bf16[64,128]{1,0:T(8,128)(2,1)S(1)}, bf16[64,128]{1,0:T(8,128)(2,1)S(1)}, u32[]{:S(2)}, u32[]{:S(2)}) collective-permute-start(bf16[64,128]{1,0:T(8,128)(2,1)S(1)} %get-tuple-element.65.first_grad_ref), channel_id=1, source_target_pairs={{0,1},{2,3},{4,5},{6,7},{1,0},{3,2},{5,4},{7,6},{8,9},{10,11},{12,... | collective-permute-start | bytes 49160 | tf_op jit(solution)/shard_map/ppermute | solution.py:767
  49.9 9.3 %shard_map.206 = (bf16[4096,128]{1,0:T(8,128)(2,1)S(1)}, bf16[4096,256]{1,0:T(8,128)(2,1)S(1)}, bf16[512,128]{1,0:T(8,128)(2,1)S(1)}, bf16[512,128]{1,0:T(8,128)...) custom-call(s32[16,128]{1,0:T(8,128)S(1)} %get-tuple-element.44.place_ref, ...), custom_call_target="tpu_custom_call" | custom-call | tf_op jit(solution)/shard_map/pallas_call | solution.py:52
  60.6 6.4 %collective-permute-start.14 = (bf16[320,128]{1,0:T(8,128)(2,1)S(1)}, bf16[320,128]{1,0:T(8,128)(2,1)S(1)}, u32[]{:S(2)}, u32[]{:S(2)}) collective-permute-start(bf16[320,128]{1,0:T(8,128)(2,1)S(1)} %shard_map.208.mine_ref), channel_id=1, source_target_pairs={{0,2},{1,3},{2,0},{3,1},{4,6},{5,7},{6,4},{7,5},{8,10},{9,11},{10,... | collective-permute-start | bytes 245768 | tf_op jit(solution)/shard_map/ppermute | solution.py:771
  67.0 1.5 %collective-permute-start.11 = (bf16[512,128]{1,0:T(8,128)(2,1)S(1)}, bf16[512,128]{1,0:T(8,128)(2,1)S(1)}, u32[]{:S(2)}, u32[]{:S(2)}) collective-permute-start(bf16[512,128]{1,0:T(8,128)(2,1)S(1)} %get-tuple-element.78), channel_id=1, source_target_pairs={{0,1},{2,3},{4,5},{6,7},{1,0},{3,2},{5,4},{7,6},{8,9},{10,11},{12,... | collective-permute-start | bytes 393224 | tf_op jit(solution)/shard_map/ppermute | solution.py:767
  69.8 2.8 %collective-permute-start.15 = (bf16[320,128]{1,0:T(8,128)(2,1)S(1)}, bf16[320,128]{1,0:T(8,128)(2,1)S(1)}, u32[]{:S(2)}, u32[]{:S(2)}) collective-permute-start(bf16[320,128]{1,0:T(8,128)(2,1)S(1)} %shard_map.209.mine_ref), channel_id=1, source_target_pairs={{0,4},{1,5},{2,6},{3,7},{4,0},{5,1},{6,2},{7,3},{8,12},{9,13},{10,... | collective-permute-start | bytes 245768 | tf_op jit(solution)/shard_map/ppermute | solution.py:771
  72.6 4.4 %shard_map.207.rest_0_ = bf16[4096,128]{1,0:T(8,128)(2,1)} custom-call(bf16[4096,128]{1,0:T(8,128)(2,1)S(1)} %get-tuple-element.76.ups_ref, bf16[4096,256]{1,0:T(8,128)(2,1)S(1)} %get-tuple-element.77.downs_ref, bf16[512,128]{1,0:T(8,128)(2,1)S(1)} %collective-permute-done.11.first_back_ref, bf16[512,128]{1,0:T(8,128)(2,1)S(1)} %collective-permute-done.12.second_back_ref, ...), custom_call_target="tpu_custom_call" | custom-call | tf_op jit(solution)/shard_map/pallas_call | solution.py:52
  77.0 1.7 %collective-permute-done.15.theirs_ref = bf16[320,128]{1,0:T(8,128)(2,1)S(1)} collective-permute-done((bf16[320,128]{1,0:T(8,128)(2,1)S(1)}, bf16[320,128]{1,0:T(8,128)(2,1)S(1)}, u32[]{:S(2)}, u32[]{:S(2)}) %collective-permute-start.15) | collective-permute-done | bytes 81952 | tf_op jit(solution)/shard_map/ppermute | solution.py:771
  78.7 3.3 %collective-permute-start.18 = (bf16[320,128]{1,0:T(8,128)(2,1)S(1)}, bf16[320,128]{1,0:T(8,128)(2,1)S(1)}, u32[]{:S(2)}, u32[]{:S(2)}) collective-permute-start(bf16[320,128]{1,0:T(8,128)(2,1)S(1)} %shard_map.210.mine_ref), channel_id=1, source_target_pairs={{0,17},{1,16},{2,19},{3,18},{4,21},{5,20},{6,23},{7,22},{8,25},{9,... | collective-permute-start | bytes 245768 | tf_op jit(solution)/shard_map/ppermute | solution.py:802
  82.0 1.5 %collective-permute-start.17 = (bf16[320,128]{1,0:T(8,128)(2,1)S(1)}, bf16[320,128]{1,0:T(8,128)(2,1)S(1)}, u32[]{:S(2)}, u32[]{:S(2)}) collective-permute-start(bf16[320,128]{1,0:T(8,128)(2,1)S(1)} %shard_map.210.mine_ref), channel_id=1, source_target_pairs={{0,16},{8,24},{16,0},{24,8},{1,17},{9,25},{17,1},{25,9},{2,18},{10... | collective-permute-start | bytes 245768 | tf_op jit(solution)/shard_map/ppermute | solution.py:771
  83.5 3.9 %shard_map.205.after_ref = bf16[4096,128]{1,0:T(8,128)(2,1)} custom-call(bf16[4096,128]{1,0:T(8,128)(2,1)S(1)} %get-tuple-element.43.h_ref, bf16[4096,128]{1,0:T(8,128)(2,1)S(1)} %get-tuple-element.51.summed_ref, bf16[896,128]{1,0:T(8,128)(2,1)S(1)} %get-tuple-element.47.weights_ref.matrices_ref, f32[4096,8]{1,0:T(8,128)S(1)} %shard_map.199.owners_ref, ...), custom_call_target="tpu_custom_call" | custom-call | tf_op jit(solution)/shard_map/pallas_call | solution.py:52
  88.1 1.5 %collective-permute-done.19.theirs_ref = f32[448,128]{1,0:T(8,128)S(1)} collective-permute-done((f32[448,128]{1,0:T(8,128)S(1)}, f32[448,128]{1,0:T(8,128)S(1)}, u32[]{:S(2)}, u32[]{:S(2)}) %collective-permute-start.19) | collective-permute-done | bytes 229408 | tf_op jit(solution)/shard_map/ppermute | solution.py:771
  (37 shorter events, 11.8 us)
Async XLA Ops:
  3.5 8.7 %collective-permute-start.1 = (bf16[512,128]{1,0:T(8,128)(2,1)S(1)}, bf16[512,128]{1,0:T(8,128)(2,1)S(1)}, u32[]{:S(2)}, u32[]{:S(2)}) collective-permute-start(bf16[512,128]{1,0:T(8,128)(2,1)S(1)} %get-tuple-element.46), channel_id=1, source_target_pairs={{1,2},{3,4},{5,6},{2,1},{4,3},{6,5},{9,10},{11,12},{13,14},{10,9},... | collective-permute-start | bytes 393224 | tf_op jit(solution)/shard_map/ppermute | solution.py:767
  4.2 10.6 %collective-permute-start = (bf16[512,128]{1,0:T(8,128)(2,1)S(1)}, bf16[512,128]{1,0:T(8,128)(2,1)S(1)}, u32[]{:S(2)}, u32[]{:S(2)}) collective-permute-start(bf16[512,128]{1,0:T(8,128)(2,1)S(1)} %get-tuple-element.45.rest_7_), channel_id=1, source_target_pairs={{0,1},{2,3},{4,5},{6,7},{1,0},{3,2},{5,4},{7,6},{8,9},{10,11},{12,... | collective-permute-start | bytes 393224 | tf_op jit(solution)/shard_map/ppermute | solution.py:767
  24.0 1.4 %collective-permute-start.2 = (bf16[528,128]{1,0:T(8,128)(2,1)S(1)}, bf16[528,128]{1,0:T(8,128)(2,1)S(1)}, u32[]{:S(2)}, u32[]{:S(2)}) collective-permute-start(bf16[528,128]{1,0:T(8,128)(2,1)S(1)} %get-tuple-element.54), channel_id=1, source_target_pairs={{0,8},{8,0},{16,24},{24,16},{1,9},{9,1},{17,25},{25,17},{2,10},{10... | collective-permute-start | bytes 405512 | tf_op jit(solution)/shard_map/ppermute | solution.py:771
  25.5 6.0 %collective-permute-start.3 = (bf16[528,128]{1,0:T(8,128)(2,1)S(1)}, bf16[528,128]{1,0:T(8,128)(2,1)S(1)}, u32[]{:S(2)}, u32[]{:S(2)}) collective-permute-start(bf16[528,128]{1,0:T(8,128)(2,1)S(1)} %shard_map.197.after_ref.totals_ref), channel_id=1, source_target_pairs={{0,16},{8,24},{16,0},{24,8},{1,17},{9,25},{17,1},{25,9},{2,18},{10... | collective-permute-start | bytes 405512 | tf_op jit(solution)/shard_map/ppermute | solution.py:771
  29.9 2.0 %collective-permute-start.5 = (bf16[1024,128]{1,0:T(8,128)(2,1)S(1)}, bf16[1024,128]{1,0:T(8,128)(2,1)S(1)}, u32[]{:S(2)}, u32[]{:S(2)}) collective-permute-start(bf16[1024,128]{1,0:T(8,128)(2,1)S(1)} %shard_map.198.after_ref.sums_ref), channel_id=1, source_target_pairs={{0,8},{8,0},{16,24},{24,16},{1,9},{9,1},{17,25},{25,17},{2,10},{10... | collective-permute-start | bytes 786440 | tf_op jit(solution)/shard_map/ppermute | solution.py:771
  31.8 1.4 %collective-permute-start.4 = (bf16[512,128]{1,0:T(8,128)(2,1)S(1)}, bf16[512,128]{1,0:T(8,128)(2,1)S(1)}, u32[]{:S(2)}, u32[]{:S(2)}) collective-permute-start(bf16[512,128]{1,0:T(8,128)(2,1)S(1)} %get-tuple-element.55.half_ref), channel_id=1, source_target_pairs={{0,8},{8,0},{16,24},{24,16},{1,9},{9,1},{17,25},{25,17},{2,10},{10... | collective-permute-start | bytes 393224 | tf_op jit(solution)/shard_map/ppermute | solution.py:771
  33.6 8.4 %collective-permute-start.8 = (bf16[1024,128]{1,0:T(8,128)(2,1)S(1)}, bf16[1024,128]{1,0:T(8,128)(2,1)S(1)}, u32[]{:S(2)}, u32[]{:S(2)}) collective-permute-start(bf16[1024,128]{1,0:T(8,128)(2,1)S(1)} %get-tuple-element.62.chip_sums_ref), channel_id=1, source_target_pairs={{0,16},{8,24},{16,0},{24,8},{1,17},{9,25},{17,1},{25,9},{2,18},{10... | collective-permute-start | bytes 786440 | tf_op jit(solution)/shard_map/ppermute | solution.py:771
  35.1 4.2 %collective-permute-start.6 = (bf16[64,128]{1,0:T(8,128)(2,1)S(1)}, bf16[64,128]{1,0:T(8,128)(2,1)S(1)}, u32[]{:S(2)}, u32[]{:S(2)}) collective-permute-start(bf16[64,128]{1,0:T(8,128)(2,1)S(1)} %get-tuple-element.58), channel_id=1, source_target_pairs={{0,1},{2,3},{4,5},{6,7},{1,0},{3,2},{5,4},{7,6},{8,9},{10,11},{12,... | collective-permute-start | bytes 49160 | tf_op jit(solution)/shard_map/ppermute | solution.py:767
  37.6 1.7 %collective-permute-start.7 = (bf16[64,128]{1,0:T(8,128)(2,1)S(1)}, bf16[64,128]{1,0:T(8,128)(2,1)S(1)}, u32[]{:S(2)}, u32[]{:S(2)}) collective-permute-start(bf16[64,128]{1,0:T(8,128)(2,1)S(1)} %get-tuple-element.59), channel_id=1, source_target_pairs={{1,2},{3,4},{5,6},{2,1},{4,3},{6,5},{9,10},{11,12},{13,14},{10,9},... | collective-permute-start | bytes 49160 | tf_op jit(solution)/shard_map/ppermute | solution.py:767
  43.6 6.3 %collective-permute-start.9 = (bf16[64,128]{1,0:T(8,128)(2,1)S(1)}, bf16[64,128]{1,0:T(8,128)(2,1)S(1)}, u32[]{:S(2)}, u32[]{:S(2)}) collective-permute-start(bf16[64,128]{1,0:T(8,128)(2,1)S(1)} %get-tuple-element.65.first_grad_ref), channel_id=1, source_target_pairs={{0,1},{2,3},{4,5},{6,7},{1,0},{3,2},{5,4},{7,6},{8,9},{10,11},{12,... | collective-permute-start | bytes 49160 | tf_op jit(solution)/shard_map/ppermute | solution.py:767
  47.8 2.1 %collective-permute-start.10 = (bf16[64,128]{1,0:T(8,128)(2,1)S(1)}, bf16[64,128]{1,0:T(8,128)(2,1)S(1)}, u32[]{:S(2)}, u32[]{:S(2)}) collective-permute-start(bf16[64,128]{1,0:T(8,128)(2,1)S(1)} %get-tuple-element.66.second_grad_ref), channel_id=1, source_target_pairs={{1,2},{3,4},{5,6},{2,1},{4,3},{6,5},{9,10},{11,12},{13,14},{10,9},... | collective-permute-start | bytes 49160 | tf_op jit(solution)/shard_map/ppermute | solution.py:767
  59.2 1.4 %collective-permute-start.13 = (f32[192,128]{1,0:T(8,128)S(1)}, f32[192,128]{1,0:T(8,128)S(1)}, u32[]{:S(2)}, u32[]{:S(2)}) collective-permute-start(f32[192,128]{1,0:T(8,128)S(1)} %get-tuple-element.82), channel_id=1, source_target_pairs={{0,8},{8,0},{16,24},{24,16},{1,9},{9,1},{17,25},{25,17},{2,10},{10... | collective-permute-start | bytes 294920 | tf_op jit(solution)/shard_map/ppermute | solution.py:771
  60.6 9.2 %collective-permute-start.14 = (bf16[320,128]{1,0:T(8,128)(2,1)S(1)}, bf16[320,128]{1,0:T(8,128)(2,1)S(1)}, u32[]{:S(2)}, u32[]{:S(2)}) collective-permute-start(bf16[320,128]{1,0:T(8,128)(2,1)S(1)} %shard_map.208.mine_ref), channel_id=1, source_target_pairs={{0,2},{1,3},{2,0},{3,1},{4,6},{5,7},{6,4},{7,5},{8,10},{9,11},{10,... | collective-permute-start | bytes 245768 | tf_op jit(solution)/shard_map/ppermute | solution.py:771
  67.0 5.6 %collective-permute-start.11 = (bf16[512,128]{1,0:T(8,128)(2,1)S(1)}, bf16[512,128]{1,0:T(8,128)(2,1)S(1)}, u32[]{:S(2)}, u32[]{:S(2)}) collective-permute-start(bf16[512,128]{1,0:T(8,128)(2,1)S(1)} %get-tuple-element.78), channel_id=1, source_target_pairs={{0,1},{2,3},{4,5},{6,7},{1,0},{3,2},{5,4},{7,6},{8,9},{10,11},{12,... | collective-permute-start | bytes 393224 | tf_op jit(solution)/shard_map/ppermute | solution.py:767
  68.5 4.1 %collective-permute-start.12 = (bf16[512,128]{1,0:T(8,128)(2,1)S(1)}, bf16[512,128]{1,0:T(8,128)(2,1)S(1)}, u32[]{:S(2)}, u32[]{:S(2)}) collective-permute-start(bf16[512,128]{1,0:T(8,128)(2,1)S(1)} %get-tuple-element.79), channel_id=1, source_target_pairs={{1,2},{3,4},{5,6},{2,1},{4,3},{6,5},{9,10},{11,12},{13,14},{10,9},... | collective-permute-start | bytes 393224 | tf_op jit(solution)/shard_map/ppermute | solution.py:767
  69.8 8.9 %collective-permute-start.15 = (bf16[320,128]{1,0:T(8,128)(2,1)S(1)}, bf16[320,128]{1,0:T(8,128)(2,1)S(1)}, u32[]{:S(2)}, u32[]{:S(2)}) collective-permute-start(bf16[320,128]{1,0:T(8,128)(2,1)S(1)} %shard_map.209.mine_ref), channel_id=1, source_target_pairs={{0,4},{1,5},{2,6},{3,7},{4,0},{5,1},{6,2},{7,3},{8,12},{9,13},{10,... | collective-permute-start | bytes 245768 | tf_op jit(solution)/shard_map/ppermute | solution.py:771
  78.7 8.8 %collective-permute-start.18 = (bf16[320,128]{1,0:T(8,128)(2,1)S(1)}, bf16[320,128]{1,0:T(8,128)(2,1)S(1)}, u32[]{:S(2)}, u32[]{:S(2)}) collective-permute-start(bf16[320,128]{1,0:T(8,128)(2,1)S(1)} %shard_map.210.mine_ref), channel_id=1, source_target_pairs={{0,17},{1,16},{2,19},{3,18},{4,21},{5,20},{6,23},{7,22},{8,25},{9,... | collective-permute-start | bytes 245768 | tf_op jit(solution)/shard_map/ppermute | solution.py:802
  82.0 5.5 %collective-permute-start.17 = (bf16[320,128]{1,0:T(8,128)(2,1)S(1)}, bf16[320,128]{1,0:T(8,128)(2,1)S(1)}, u32[]{:S(2)}, u32[]{:S(2)}) collective-permute-start(bf16[320,128]{1,0:T(8,128)(2,1)S(1)} %shard_map.210.mine_ref), channel_id=1, source_target_pairs={{0,16},{8,24},{16,0},{24,8},{1,17},{9,25},{17,1},{25,9},{2,18},{10... | collective-permute-start | bytes 245768 | tf_op jit(solution)/shard_map/ppermute | solution.py:771
  83.5 4.4 %collective-permute-start.16 = (bf16[320,128]{1,0:T(8,128)(2,1)S(1)}, bf16[320,128]{1,0:T(8,128)(2,1)S(1)}, u32[]{:S(2)}, u32[]{:S(2)}) collective-permute-start(bf16[320,128]{1,0:T(8,128)(2,1)S(1)} %shard_map.210.mine_ref), channel_id=1, source_target_pairs={{0,1},{1,0},{2,3},{3,2},{4,5},{5,4},{6,7},{7,6},{8,9},{9,8},{10,11... | collective-permute-start | bytes 245768 | tf_op jit(solution)/shard_map/ppermute | solution.py:771
  88.0 1.6 %collective-permute-start.19 = (f32[448,128]{1,0:T(8,128)S(1)}, f32[448,128]{1,0:T(8,128)S(1)}, u32[]{:S(2)}, u32[]{:S(2)}) collective-permute-start(f32[448,128]{1,0:T(8,128)S(1)} %shard_map.211.mine_ref), channel_id=1, source_target_pairs={{0,8},{8,0},{16,24},{24,16},{1,9},{9,1},{17,25},{25,17},{2,10},{10... | collective-permute-start | bytes 688136 | tf_op jit(solution)/shard_map/ppermute | solution.py:771

commit v13 on v12

--- a/solution.py
+++ b/solution.py
@@ -207,7 +207,6 @@
 
 
 def gather_kernel(
-    place_ref,
     lo_hbm,
     hi_hbm,
     x_hbm,
@@ -231,22 +230,23 @@
         return carry
 
     lax.fori_loop(0, up.shape[0], step, None, unroll=16)
-    even = place_ref[0] > 0
-    vector_ref[:8, :] = jnp.full((8, 128), place_ref[0], jnp.int32)
-    vector_ref[8:, :] = jnp.full((8, 128), place_ref[1], jnp.int32)
+    parity = 1 - lax.rem(lax.axis_index("sub"), 2)
+    even = parity > 0
+    vector_ref[:8, :] = jnp.full((8, 128), parity, jnp.int32)
+    vector_ref[8:, :] = jnp.full((8, 128), lax.axis_index("grp"), jnp.int32)
     first_ref[...] = jnp.where(even, up[...], down[...]).astype(bf16)
     second_ref[...] = jnp.where(even, down[...], up[...]).astype(bf16)
 
 
-def gather_rows(place, x, send_lo, send_hi):
+def gather_rows(x, send_lo, send_hi):
     rows, features = x.shape
     count = send_lo.shape[0]
     out = shape(count, features, bf16)
     return call(
         gather_kernel,
         [out, out, shape(rows, features, bf16), shape(16, 128, jnp.int32)],
-        [place, send_lo, send_hi, x],
-        [SMEM, HBM, HBM, HBM],
+        [send_lo, send_hi, x],
+        [HBM, HBM, HBM],
         [
             pltpu.VMEM((rows, features), f32),
             pltpu.VMEM((count, features), f32),
@@ -365,6 +365,10 @@
     lax.fori_loop(0, sums_ref.shape[0] // 256, step, None)
 
 
+def relay_kernel(x_ref, after_ref, also_after_ref, out_ref):
+    out_ref[...] = x_ref[...]
+
+
 def owners_kernel(owner_ref, after_ref, owners_ref):
     owners_ref[...] = owner_columns(owner_ref)
 
@@ -390,6 +394,7 @@
     columns_t_ref,
     owner_ref,
     counts_ref,
+    after_ref,
     summed_ref,
     slope_hbm,
     new_ref,
@@ -440,13 +445,10 @@
     place_ref,
     half_ref,
     their_half_ref,
-    sums_ref,
-    more_sums_ref,
     sends_ref,
     cin_ref,
     first_ref,
     second_ref,
-    chip_sums_ref,
 ):
     mine, theirs = half_ref[...].astype(f32), their_half_ref[...].astype(f32)
     first = core_of(place_ref) == 0
@@ -458,7 +460,6 @@
     halo_rows = first_ref.shape[0]
     first_ref[...] = sent[:halo_rows]
     second_ref[...] = sent[halo_rows:]
-    chip_sums_ref[...] = (sums_ref[...].astype(f32) + more_sums_ref[...].astype(f32)).astype(bf16)
 
 
 def coarse_forward_kernel(
@@ -838,12 +839,11 @@
     coarse_halo = coarse_send_lo.shape[0]
     count_rows = coarse_rows // 128
     owner = coarse_owner.reshape(rows // 128, 128)
-    place = jnp.stack([1 - lax.rem(lax.axis_index("sub"), 2), lax.axis_index("grp")])
 
     def buffer(count, columns, dtype):
         return pltpu.VMEM((count, columns), dtype)
 
-    to_first, to_second, states, place = gather_rows(place, states, fine_send_lo, fine_send_hi)
+    to_first, to_second, states, place = gather_rows(states, fine_send_lo, fine_send_hi)
     first, second = exchange(to_first, to_second)
 
     (
@@ -877,6 +877,20 @@
         + [pltpu.SemaphoreType.DMA((17,))],
     )
 
+    sums = call(
+        sums_kernel,
+        shape(coarse_rows, features, bf16),
+        [owner, cotangent, sends],
+        [VMEM, VMEM, ANY],
+    )
+    sums = call(
+        relay_kernel,
+        shape(coarse_rows, features, bf16),
+        [sums, first, second],
+        [VMEM, ANY, ANY],
+    )
+    more_sums = swapped(sums, "grp", 1)
+
     half_rows = coarse_rows // 2 + 2 * count_rows
     summed, slope, new, give = call(
         fine_forward_kernel,
@@ -886,8 +900,8 @@
             shape(rows, features, bf16),
             shape(half_rows, features, bf16),
         ],
-        [place, states, first, second, matrices, columns_t, owner, counts],
-        [VMEM] + [VMEM] * 7,
+        [place, states, first, second, matrices, columns_t, owner, counts, sums],
+        [VMEM] * 8 + [ANY],
         [
             buffer(rows, features, f32),
             buffer(rows, features, bf16),
@@ -907,34 +921,32 @@
     )
     chip_totals = call(add_kernel, shape(half_rows, features, bf16), [keep, theirs])
     more_totals = swapped(chip_totals, "grp", 2)
-    sums = call(
-        sums_kernel,
+    chip_sums = call(
+        add_kernel,
         shape(coarse_rows, features, bf16),
-        [owner, cotangent, chip_totals],
+        [sums, more_sums, chip_totals],
         [VMEM, VMEM, ANY],
     )
-    more_sums = swapped(sums, "grp", 1)
-    owners_t = call(owners_kernel, shape(rows, 8, f32), [owner, sums], [VMEM, ANY])
+    more_sums = swapped(chip_sums, "grp", 2)
+    owners_t = call(owners_kernel, shape(rows, 8, f32), [owner, chip_totals], [VMEM, ANY])
 
     half, counts = call(
         half_kernel,
         [shape(coarse_rows // 2, features, bf16), shape(count_rows, features, f32)],
-        [place, chip_totals, more_totals, sums],
+        [place, chip_totals, more_totals, owners_t],
         [VMEM, VMEM, VMEM, ANY],
     )
     their_half = swapped(half, "grp", 1)
-    coarse_in, to_first, to_second, chip_sums = call(
+    coarse_in, to_first, to_second = call(
         coarse_input_kernel,
         [
             shape(coarse_rows, features, bf16),
             shape(coarse_halo, features, bf16),
             shape(coarse_halo, features, bf16),
-            shape(coarse_rows, features, bf16),
-        ],
-        [place, half, their_half, sums, more_sums, coarse_sends],
+        ],
+        [place, half, their_half, coarse_sends],
     )
     coarse_first, coarse_second = exchange(to_first, to_second)
-    more_sums = swapped(chip_sums, "grp", 2)
 
     coarse_sum, coarse_slope = call(
         coarse_forward_kernel,

time: 91.2 us -> 89.9 us (0.986)
  waiting for transfers between devices: 12.8 us -> 11.7 us
    ppermute x4, waiting for transfers between devices: 3.69 us -> 1.31 us  [exchange(): lax.ppermute(first, 'sub', routes[0])]
    ppermute x11, waiting for transfers between devices: 9.08 us -> 10.4 us  [swapped(): lax.ppermute(block, axis, [(i, i ^ distance) for i in range(lax.axis_size...]
    ppermute x11, starting transfers between devices: 14.4 us -> 13.3 us  [swapped(): lax.ppermute(block, axis, [(i, i ^ distance) for i in range(lax.axis_size...]
    ppermute x1, starting transfers between devices: 3.34 us -> 4.3 us  [total_weights(): lax.ppermute(weights, ('grp', 'sub'), corners)]
    pallas_call x20 -> x22, Pallas kernels: 42.1 us -> 41.5 us  [call(): pl.pallas_call(kernel, out_shape=out_shape, in_specs=in_specs, out_specs=...]
  transfers between devices with their start and end apart: 20 -> 20, of which waited for: 11 -> 9; matrix products, arithmetic and copies ran while one was open for 0% -> 0% of each run, Pallas kernels for 20% -> 31%
where the time goes in v13:
time: 89.9 us; the launch traced here: 89.1 us
  Pallas kernels  41.5 us (46%)
  starting transfers between devices  35 us (39%)
  waiting for transfers between devices  11.7 us (13%)
    pallas_call x22, Pallas kernels, call(): pl.pallas_call(kernel, out_shape=out_shape, in_specs=in_specs, out_specs=...  41.5 us
    ppermute x4, starting transfers between devices, exchange(): lax.ppermute(first, 'sub', routes[0])  14.6 us
    ppermute x11, starting transfers between devices, swapped(): lax.ppermute(block, axis, [(i, i ^ distance) for i in range(lax.axis_size...  13.3 us
    ppermute x11, waiting for transfers between devices, swapped(): lax.ppermute(block, axis, [(i, i ^ distance) for i in range(lax.axis_size...  10.4 us
    ppermute x1, starting transfers between devices, total_weights(): lax.ppermute(weights, ('grp', 'sub'), corners)  4.3 us
    ppermute x4, starting transfers between devices, exchange(): lax.ppermute(second, 'sub', routes[1])  2.81 us
  transfers between devices with their start and end apart: 20, of which 9 were waited for; matrix products, arithmetic and copies ran while one was open for 0% of the time, Pallas kernels for 31%

profile of v13, /device:TPU:0, one launch (start us, length us, event | category | flops | bytes accessed | tf_op | source)
XLA Modules:
  0.0 89.1 jit_solution(2716995435836605157)
XLA Ops:
  0.6 2.3 %shard_map.193 = (bf16[512,128]{1,0:T(8,128)(2,1)S(1)}, bf16[512,128]{1,0:T(8,128)(2,1)S(1)}, bf16[4096,128]{1,0:T(8,128)(2,1)S(1)}, s32[16,128]{1,0:T(8,128)S(1)}) custom-call(s32[512]{0:T(512)} %lo_hbm.1, s32[512]{0:T(512)} %hi_hbm.1, bf16[4096,128]{1,0:T(8,128)(2,1)} %x_hbm.1), custom_call_target="tpu_custom_call" | custom-call | tf_op jit(solution)/shard_map/pallas_call | solution.py:52
  3.6 5.8 %collective-permute-start = (bf16[512,128]{1,0:T(8,128)(2,1)S(1)}, bf16[512,128]{1,0:T(8,128)(2,1)S(1)}, u32[]{:S(2)}, u32[]{:S(2)}) collective-permute-start(bf16[512,128]{1,0:T(8,128)(2,1)S(1)} %get-tuple-element.44.rest_7_), channel_id=1, source_target_pairs={{0,1},{2,3},{4,5},{6,7},{1,0},{3,2},{5,4},{7,6},{8,9},{10,11},{12,... | collective-permute-start | bytes 393224 | tf_op jit(solution)/shard_map/ppermute | solution.py:768
  9.4 2.2 %shard_map.194 = (bf16[16,128]{1,0:T(8,128)(2,1)S(1)}, f32[8,4096]{1,0:T(8,128)S(1)}, f32[4096,8]{1,0:T(8,128)S(1)}, f32[8,1024]{1,0:T(8,128)S(1)}, f32[1024,8]{...) custom-call(s32[16,128]{1,0:T(8,128)S(1)} %get-tuple-element.43.plac, ...), custom_call_target="tpu_custom_call" | custom-call | tf_op jit(solution)/shard_map/pallas_call | solution.py:52
  11.6 2.8 %shard_map.195.x_ref = bf16[1024,128]{1,0:T(8,128)(2,1)S(1)} custom-call(s32[32,128]{1,0:T(8,128)S(1)} %get-tuple-element.48.owner_ref, bf16[4096,128]{1,0:T(8,128)(2,1)S(1)} %get-tuple-element.50.g_ref, s32[1,1024]{1,0:T(1,128)S(1)} %get-tuple-element.51.after_ref.sends_ref), custom_call_target="tpu_custom_call" | custom-call | tf_op jit(solution)/shard_map/pallas_call | solution.py:52
  14.5 9.2 %shard_map.197 = (bf16[4096,128]{1,0:T(8,128)(2,1)S(1)}, bf16[32768,128]{1,0:T(8,128)(2,1)}, bf16[4096,128]{1,0:T(8,128)(2,1)S(1)}, bf16[528,128]{1,0:T(8,128)(2,1)S(1)}) custom-call(s32[16,128]{1,0:T(8,128)S(1)} %get-tuple-element.43.place_ref, bf16[4096,128]{1,0:T(8,128)(2,1)S(1)} %get-tuple-element.42.h_ref, ...), custom_call_target="tpu_custom_call" | custom-call | tf_op jit(solution)/shard_map/pallas_call | solution.py:52
  24.3 1.2 %shard_map.198.mine_ref = bf16[528,128]{1,0:T(8,128)(2,1)S(1)} custom-call(s32[16,128]{1,0:T(8,128)S(1)} %get-tuple-element.43.place_ref, s32[32,128]{1,0:T(8,128)S(1)} %get-tuple-element.48.owner_ref, bf16[4096,128]{1,0:T(8,128)(2,1)S(1)} %get-tuple-element.53.new_ref, bf16[16,128]{1,0:T(8,128)(2,1)S(1)} %get-tuple-element.49.counts_ref), custom_call_target="tpu_custom_call" | custom-call | tf_op jit(solution)/shard_map/pallas_call | solution.py:52
  25.6 1.6 %collective-permute-start.3 = (bf16[528,128]{1,0:T(8,128)(2,1)S(1)}, bf16[528,128]{1,0:T(8,128)(2,1)S(1)}, u32[]{:S(2)}, u32[]{:S(2)}) collective-permute-start(bf16[528,128]{1,0:T(8,128)(2,1)S(1)} %shard_map.199.after_ref.totals_ref.rest_0_), channel_id=1, source_target_pairs={{0,16},{8,24},{16,0},{24,8},{1,17},{9,25},{17,1},{25,9},{2,18},{10... | collective-permute-start | bytes 405512 | tf_op jit(solution)/shard_map/ppermute | solution.py:772
  28.4 3.7 %collective-permute-done.3.more_totals_ref = bf16[528,128]{1,0:T(8,128)(2,1)S(1)} collective-permute-done((bf16[528,128]{1,0:T(8,128)(2,1)S(1)}, bf16[528,128]{1,0:T(8,128)(2,1)S(1)}, u32[]{:S(2)}, u32[]{:S(2)}) %collective-permute-start.3) | collective-permute-done | bytes 135200 | tf_op jit(solution)/shard_map/ppermute | solution.py:772
  32.5 1.3 %collective-permute-done.4.their_half_ref = bf16[512,128]{1,0:T(8,128)(2,1)S(1)} collective-permute-done((bf16[512,128]{1,0:T(8,128)(2,1)S(1)}, bf16[512,128]{1,0:T(8,128)(2,1)S(1)}, u32[]{:S(2)}, u32[]{:S(2)}) %collective-permute-start.4) | collective-permute-done | bytes 131104 | tf_op jit(solution)/shard_map/ppermute | solution.py:772
  34.2 2.4 %collective-permute-start.5 = (bf16[64,128]{1,0:T(8,128)(2,1)S(1)}, bf16[64,128]{1,0:T(8,128)(2,1)S(1)}, u32[]{:S(2)}, u32[]{:S(2)}) collective-permute-start(bf16[64,128]{1,0:T(8,128)(2,1)S(1)} %get-tuple-element.58), channel_id=1, source_target_pairs={{0,1},{2,3},{4,5},{6,7},{1,0},{3,2},{5,4},{7,6},{8,9},{10,11},{12,... | collective-permute-start | bytes 49160 | tf_op jit(solution)/shard_map/ppermute | solution.py:768
  37.3 0.9 collective-permute-done.5.first_ref
  38.2 1.8 %shard_map.203 = (bf16[1024,128]{1,0:T(8,128)(2,1)S(1)}, bf16[8192,128]{1,0:T(8,128)(2,1)S(1)}) custom-call(bf16[1024,128]{1,0:T(8,128)(2,1)S(1)} %get-tuple-element.57.cin_ref, bf16[64,128]{1,0:T(8,128)(2,1)S(1)} %collective-permute-done.5.first_ref, bf16[64,128]{1,0:T(8,128)(2,1)S(1)} %collective-permute-done.6.second_ref, ...), custom_call_target="tpu_custom_call" | custom-call | tf_op jit(solution)/shard_map/pallas_call | solution.py:52
  40.1 1.5 %shard_map.205 = (f32[1024,128]{1,0:T(8,128)S(1)}, bf16[64,128]{1,0:T(8,128)(2,1)S(1)}, bf16[64,128]{1,0:T(8,128)(2,1)S(1)}, bf16[1024,128]{1,0:T(8,128)(2,1)S(1...) custom-call(bf16[8192,128]{1,0:T(8,128)(2,1)S(1)} %get-tuple-element.61.slope_ref, ...), custom_call_target="tpu_custom_call" | custom-call | tf_op jit(solution)/shard_map/pallas_call | solution.py:52
  41.6 5.0 %collective-permute-start.9 = (bf16[64,128]{1,0:T(8,128)(2,1)S(1)}, bf16[64,128]{1,0:T(8,128)(2,1)S(1)}, u32[]{:S(2)}, u32[]{:S(2)}) collective-permute-start(bf16[64,128]{1,0:T(8,128)(2,1)S(1)} %get-tuple-element.64.first_grad_ref), channel_id=1, source_target_pairs={{0,1},{2,3},{4,5},{6,7},{1,0},{3,2},{5,4},{7,6},{8,9},{10,11},{12,... | collective-permute-start | bytes 49160 | tf_op jit(solution)/shard_map/ppermute | solution.py:768
  48.3 9.2 %shard_map.208 = (bf16[4096,128]{1,0:T(8,128)(2,1)S(1)}, bf16[4096,256]{1,0:T(8,128)(2,1)S(1)}, bf16[512,128]{1,0:T(8,128)(2,1)S(1)}, bf16[512,128]{1,0:T(8,128)...) custom-call(s32[16,128]{1,0:T(8,128)S(1)} %get-tuple-element.43.place_ref, ...), custom_call_target="tpu_custom_call" | custom-call | tf_op jit(solution)/shard_map/pallas_call | solution.py:52
  57.6 1.3 %collective-permute-done.13.theirs_ref = f32[192,128]{1,0:T(8,128)S(1)} collective-permute-done((f32[192,128]{1,0:T(8,128)S(1)}, f32[192,128]{1,0:T(8,128)S(1)}, u32[]{:S(2)}, u32[]{:S(2)}) %collective-permute-start.13) | collective-permute-done | bytes 98336 | tf_op jit(solution)/shard_map/ppermute | solution.py:772
  58.9 6.8 %collective-permute-start.14 = (bf16[320,128]{1,0:T(8,128)(2,1)S(1)}, bf16[320,128]{1,0:T(8,128)(2,1)S(1)}, u32[]{:S(2)}, u32[]{:S(2)}) collective-permute-start(bf16[320,128]{1,0:T(8,128)(2,1)S(1)} %shard_map.210.mine_ref), channel_id=1, source_target_pairs={{0,2},{1,3},{2,0},{3,1},{4,6},{5,7},{6,4},{7,5},{8,10},{9,11},{10,... | collective-permute-start | bytes 245768 | tf_op jit(solution)/shard_map/ppermute | solution.py:772
  65.7 1.5 %collective-permute-start.11 = (bf16[512,128]{1,0:T(8,128)(2,1)S(1)}, bf16[512,128]{1,0:T(8,128)(2,1)S(1)}, u32[]{:S(2)}, u32[]{:S(2)}) collective-permute-start(bf16[512,128]{1,0:T(8,128)(2,1)S(1)} %get-tuple-element.77), channel_id=1, source_target_pairs={{0,1},{2,3},{4,5},{6,7},{1,0},{3,2},{5,4},{7,6},{8,9},{10,11},{12,... | collective-permute-start | bytes 393224 | tf_op jit(solution)/shard_map/ppermute | solution.py:768
  68.5 2.8 %collective-permute-start.15 = (bf16[320,128]{1,0:T(8,128)(2,1)S(1)}, bf16[320,128]{1,0:T(8,128)(2,1)S(1)}, u32[]{:S(2)}, u32[]{:S(2)}) collective-permute-start(bf16[320,128]{1,0:T(8,128)(2,1)S(1)} %shard_map.211.mine_ref), channel_id=1, source_target_pairs={{0,4},{1,5},{2,6},{3,7},{4,0},{5,1},{6,2},{7,3},{8,12},{9,13},{10,... | collective-permute-start | bytes 245768 | tf_op jit(solution)/shard_map/ppermute | solution.py:772
  71.3 4.4 %shard_map.209.rest_0_ = bf16[4096,128]{1,0:T(8,128)(2,1)} custom-call(bf16[4096,128]{1,0:T(8,128)(2,1)S(1)} %get-tuple-element.75.ups_ref, bf16[4096,256]{1,0:T(8,128)(2,1)S(1)} %get-tuple-element.76.downs_ref, bf16[512,128]{1,0:T(8,128)(2,1)S(1)} %collective-permute-done.11.first_back_ref, bf16[512,128]{1,0:T(8,128)(2,1)S(1)} %collective-permute-done.12.second_back_ref, ...), custom_call_target="tpu_custom_call" | custom-call | tf_op jit(solution)/shard_map/pallas_call | solution.py:52
  75.7 1.7 %collective-permute-done.15.theirs_ref = bf16[320,128]{1,0:T(8,128)(2,1)S(1)} collective-permute-done((bf16[320,128]{1,0:T(8,128)(2,1)S(1)}, bf16[320,128]{1,0:T(8,128)(2,1)S(1)}, u32[]{:S(2)}, u32[]{:S(2)}) %collective-permute-start.15) | collective-permute-done | bytes 81952 | tf_op jit(solution)/shard_map/ppermute | solution.py:772
  77.4 4.3 %collective-permute-start.18 = (bf16[320,128]{1,0:T(8,128)(2,1)S(1)}, bf16[320,128]{1,0:T(8,128)(2,1)S(1)}, u32[]{:S(2)}, u32[]{:S(2)}) collective-permute-start(bf16[320,128]{1,0:T(8,128)(2,1)S(1)} %shard_map.212.mine_ref), channel_id=1, source_target_pairs={{0,17},{1,16},{2,19},{3,18},{4,21},{5,20},{6,23},{7,22},{8,25},{9,... | collective-permute-start | bytes 245768 | tf_op jit(solution)/shard_map/ppermute | solution.py:803
  82.4 3.9 %shard_map.207.after_ref = bf16[4096,128]{1,0:T(8,128)(2,1)} custom-call(bf16[4096,128]{1,0:T(8,128)(2,1)S(1)} %get-tuple-element.42.h_ref, bf16[4096,128]{1,0:T(8,128)(2,1)S(1)} %get-tuple-element.52.summed_ref, bf16[896,128]{1,0:T(8,128)(2,1)S(1)} %get-tuple-element.46.weights_ref.matrices_ref, f32[4096,8]{1,0:T(8,128)S(1)} %shard_map.200.after_ref.owners_ref, ...), custom_call_target="tpu_custom_call" | custom-call | tf_op jit(solution)/shard_map/pallas_call | solution.py:52
  86.8 1.5 %collective-permute-done.19.theirs_ref = f32[448,128]{1,0:T(8,128)S(1)} collective-permute-done((f32[448,128]{1,0:T(8,128)S(1)}, f32[448,128]{1,0:T(8,128)S(1)}, u32[]{:S(2)}, u32[]{:S(2)}) %collective-permute-start.19) | collective-permute-done | bytes 229408 | tf_op jit(solution)/shard_map/ppermute | solution.py:772
  (38 shorter events, 9.2 us)
Async XLA Ops:
  2.9 11.5 %collective-permute-start.1 = (bf16[512,128]{1,0:T(8,128)(2,1)S(1)}, bf16[512,128]{1,0:T(8,128)(2,1)S(1)}, u32[]{:S(2)}, u32[]{:S(2)}) collective-permute-start(bf16[512,128]{1,0:T(8,128)(2,1)S(1)} %get-tuple-element.45), channel_id=1, source_target_pairs={{1,2},{3,4},{5,6},{2,1},{4,3},{6,5},{9,10},{11,12},{13,14},{10,9},... | collective-permute-start | bytes 393224 | tf_op jit(solution)/shard_map/ppermute | solution.py:768
  3.6 10.8 %collective-permute-start = (bf16[512,128]{1,0:T(8,128)(2,1)S(1)}, bf16[512,128]{1,0:T(8,128)(2,1)S(1)}, u32[]{:S(2)}, u32[]{:S(2)}) collective-permute-start(bf16[512,128]{1,0:T(8,128)(2,1)S(1)} %get-tuple-element.44.rest_7_), channel_id=1, source_target_pairs={{0,1},{2,3},{4,5},{6,7},{1,0},{3,2},{5,4},{7,6},{8,9},{10,11},{12,... | collective-permute-start | bytes 393224 | tf_op jit(solution)/shard_map/ppermute | solution.py:768
  14.5 12.7 %collective-permute-start.7 = (bf16[1024,128]{1,0:T(8,128)(2,1)S(1)}, bf16[1024,128]{1,0:T(8,128)(2,1)S(1)}, u32[]{:S(2)}, u32[]{:S(2)}) collective-permute-start(bf16[1024,128]{1,0:T(8,128)(2,1)S(1)} %shard_map.196.after_ref.mine_ref), channel_id=1, source_target_pairs={{0,8},{8,0},{16,24},{24,16},{1,9},{9,1},{17,25},{25,17},{2,10},{10... | collective-permute-start | bytes 786440 | tf_op jit(solution)/shard_map/ppermute | solution.py:772
  23.7 1.8 %collective-permute-start.2 = (bf16[528,128]{1,0:T(8,128)(2,1)S(1)}, bf16[528,128]{1,0:T(8,128)(2,1)S(1)}, u32[]{:S(2)}, u32[]{:S(2)}) collective-permute-start(bf16[528,128]{1,0:T(8,128)(2,1)S(1)} %get-tuple-element.54), channel_id=1, source_target_pairs={{0,8},{8,0},{16,24},{24,16},{1,9},{9,1},{17,25},{25,17},{2,10},{10... | collective-permute-start | bytes 405512 | tf_op jit(solution)/shard_map/ppermute | solution.py:772
  25.6 6.5 %collective-permute-start.3 = (bf16[528,128]{1,0:T(8,128)(2,1)S(1)}, bf16[528,128]{1,0:T(8,128)(2,1)S(1)}, u32[]{:S(2)}, u32[]{:S(2)}) collective-permute-start(bf16[528,128]{1,0:T(8,128)(2,1)S(1)} %shard_map.199.after_ref.totals_ref.rest_0_), channel_id=1, source_target_pairs={{0,16},{8,24},{16,0},{24,8},{1,17},{9,25},{17,1},{25,9},{2,18},{10... | collective-permute-start | bytes 405512 | tf_op jit(solution)/shard_map/ppermute | solution.py:772
  27.2 12.9 %collective-permute-start.8 = (bf16[1024,128]{1,0:T(8,128)(2,1)S(1)}, bf16[1024,128]{1,0:T(8,128)(2,1)S(1)}, u32[]{:S(2)}, u32[]{:S(2)}) collective-permute-start(bf16[1024,128]{1,0:T(8,128)(2,1)S(1)} %shard_map.204.chip_sums_ref), channel_id=1, source_target_pairs={{0,16},{8,24},{16,0},{24,8},{1,17},{9,25},{17,1},{25,9},{2,18},{10... | collective-permute-start | bytes 786440 | tf_op jit(solution)/shard_map/ppermute | solution.py:772
  32.4 1.4 %collective-permute-start.4 = (bf16[512,128]{1,0:T(8,128)(2,1)S(1)}, bf16[512,128]{1,0:T(8,128)(2,1)S(1)}, u32[]{:S(2)}, u32[]{:S(2)}) collective-permute-start(bf16[512,128]{1,0:T(8,128)(2,1)S(1)} %get-tuple-element.55.half_ref), channel_id=1, source_target_pairs={{0,8},{8,0},{16,24},{24,16},{1,9},{9,1},{17,25},{25,17},{2,10},{10... | collective-permute-start | bytes 393224 | tf_op jit(solution)/shard_map/ppermute | solution.py:772
  34.2 4.1 %collective-permute-start.5 = (bf16[64,128]{1,0:T(8,128)(2,1)S(1)}, bf16[64,128]{1,0:T(8,128)(2,1)S(1)}, u32[]{:S(2)}, u32[]{:S(2)}) collective-permute-start(bf16[64,128]{1,0:T(8,128)(2,1)S(1)} %get-tuple-element.58), channel_id=1, source_target_pairs={{0,1},{2,3},{4,5},{6,7},{1,0},{3,2},{5,4},{7,6},{8,9},{10,11},{12,... | collective-permute-start | bytes 49160 | tf_op jit(solution)/shard_map/ppermute | solution.py:768
  36.5 1.7 %collective-permute-start.6 = (bf16[64,128]{1,0:T(8,128)(2,1)S(1)}, bf16[64,128]{1,0:T(8,128)(2,1)S(1)}, u32[]{:S(2)}, u32[]{:S(2)}) collective-permute-start(bf16[64,128]{1,0:T(8,128)(2,1)S(1)} %get-tuple-element.59), channel_id=1, source_target_pairs={{1,2},{3,4},{5,6},{2,1},{4,3},{6,5},{9,10},{11,12},{13,14},{10,9},... | collective-permute-start | bytes 49160 | tf_op jit(solution)/shard_map/ppermute | solution.py:768
  41.6 6.7 %collective-permute-start.9 = (bf16[64,128]{1,0:T(8,128)(2,1)S(1)}, bf16[64,128]{1,0:T(8,128)(2,1)S(1)}, u32[]{:S(2)}, u32[]{:S(2)}) collective-permute-start(bf16[64,128]{1,0:T(8,128)(2,1)S(1)} %get-tuple-element.64.first_grad_ref), channel_id=1, source_target_pairs={{0,1},{2,3},{4,5},{6,7},{1,0},{3,2},{5,4},{7,6},{8,9},{10,11},{12,... | collective-permute-start | bytes 49160 | tf_op jit(solution)/shard_map/ppermute | solution.py:768
  46.6 1.7 %collective-permute-start.10 = (bf16[64,128]{1,0:T(8,128)(2,1)S(1)}, bf16[64,128]{1,0:T(8,128)(2,1)S(1)}, u32[]{:S(2)}, u32[]{:S(2)}) collective-permute-start(bf16[64,128]{1,0:T(8,128)(2,1)S(1)} %get-tuple-element.65.second_grad_ref), channel_id=1, source_target_pairs={{1,2},{3,4},{5,6},{2,1},{4,3},{6,5},{9,10},{11,12},{13,14},{10,9},... | collective-permute-start | bytes 49160 | tf_op jit(solution)/shard_map/ppermute | solution.py:768
  57.5 1.4 %collective-permute-start.13 = (f32[192,128]{1,0:T(8,128)S(1)}, f32[192,128]{1,0:T(8,128)S(1)}, u32[]{:S(2)}, u32[]{:S(2)}) collective-permute-start(f32[192,128]{1,0:T(8,128)S(1)} %get-tuple-element.80), channel_id=1, source_target_pairs={{0,8},{8,0},{16,24},{24,16},{1,9},{9,1},{17,25},{25,17},{2,10},{10... | collective-permute-start | bytes 294920 | tf_op jit(solution)/shard_map/ppermute | solution.py:772
  58.9 9.6 %collective-permute-start.14 = (bf16[320,128]{1,0:T(8,128)(2,1)S(1)}, bf16[320,128]{1,0:T(8,128)(2,1)S(1)}, u32[]{:S(2)}, u32[]{:S(2)}) collective-permute-start(bf16[320,128]{1,0:T(8,128)(2,1)S(1)} %shard_map.210.mine_ref), channel_id=1, source_target_pairs={{0,2},{1,3},{2,0},{3,1},{4,6},{5,7},{6,4},{7,5},{8,10},{9,11},{10,... | collective-permute-start | bytes 245768 | tf_op jit(solution)/shard_map/ppermute | solution.py:772
  65.7 5.6 %collective-permute-start.11 = (bf16[512,128]{1,0:T(8,128)(2,1)S(1)}, bf16[512,128]{1,0:T(8,128)(2,1)S(1)}, u32[]{:S(2)}, u32[]{:S(2)}) collective-permute-start(bf16[512,128]{1,0:T(8,128)(2,1)S(1)} %get-tuple-element.77), channel_id=1, source_target_pairs={{0,1},{2,3},{4,5},{6,7},{1,0},{3,2},{5,4},{7,6},{8,9},{10,11},{12,... | collective-permute-start | bytes 393224 | tf_op jit(solution)/shard_map/ppermute | solution.py:768
  67.3 4.1 %collective-permute-start.12 = (bf16[512,128]{1,0:T(8,128)(2,1)S(1)}, bf16[512,128]{1,0:T(8,128)(2,1)S(1)}, u32[]{:S(2)}, u32[]{:S(2)}) collective-permute-start(bf16[512,128]{1,0:T(8,128)(2,1)S(1)} %get-tuple-element.78), channel_id=1, source_target_pairs={{1,2},{3,4},{5,6},{2,1},{4,3},{6,5},{9,10},{11,12},{13,14},{10,9},... | collective-permute-start | bytes 393224 | tf_op jit(solution)/shard_map/ppermute | solution.py:768
  68.5 8.9 %collective-permute-start.15 = (bf16[320,128]{1,0:T(8,128)(2,1)S(1)}, bf16[320,128]{1,0:T(8,128)(2,1)S(1)}, u32[]{:S(2)}, u32[]{:S(2)}) collective-permute-start(bf16[320,128]{1,0:T(8,128)(2,1)S(1)} %shard_map.211.mine_ref), channel_id=1, source_target_pairs={{0,4},{1,5},{2,6},{3,7},{4,0},{5,1},{6,2},{7,3},{8,12},{9,13},{10,... | collective-permute-start | bytes 245768 | tf_op jit(solution)/shard_map/ppermute | solution.py:772
  77.4 8.9 %collective-permute-start.18 = (bf16[320,128]{1,0:T(8,128)(2,1)S(1)}, bf16[320,128]{1,0:T(8,128)(2,1)S(1)}, u32[]{:S(2)}, u32[]{:S(2)}) collective-permute-start(bf16[320,128]{1,0:T(8,128)(2,1)S(1)} %shard_map.212.mine_ref), channel_id=1, source_target_pairs={{0,17},{1,16},{2,19},{3,18},{4,21},{5,20},{6,23},{7,22},{8,25},{9,... | collective-permute-start | bytes 245768 | tf_op jit(solution)/shard_map/ppermute | solution.py:803
  81.7 4.6 %collective-permute-start.17 = (bf16[320,128]{1,0:T(8,128)(2,1)S(1)}, bf16[320,128]{1,0:T(8,128)(2,1)S(1)}, u32[]{:S(2)}, u32[]{:S(2)}) collective-permute-start(bf16[320,128]{1,0:T(8,128)(2,1)S(1)} %shard_map.212.mine_ref), channel_id=1, source_target_pairs={{0,16},{8,24},{16,0},{24,8},{1,17},{9,25},{17,1},{25,9},{2,18},{10... | collective-permute-start | bytes 245768 | tf_op jit(solution)/shard_map/ppermute | solution.py:772
  82.3 4.4 %collective-permute-start.16 = (bf16[320,128]{1,0:T(8,128)(2,1)S(1)}, bf16[320,128]{1,0:T(8,128)(2,1)S(1)}, u32[]{:S(2)}, u32[]{:S(2)}) collective-permute-start(bf16[320,128]{1,0:T(8,128)(2,1)S(1)} %shard_map.212.mine_ref), channel_id=1, source_target_pairs={{0,1},{1,0},{2,3},{3,2},{4,5},{5,4},{6,7},{7,6},{8,9},{9,8},{10,11... | collective-permute-start | bytes 245768 | tf_op jit(solution)/shard_map/ppermute | solution.py:772
  86.7 1.6 %collective-permute-start.19 = (f32[448,128]{1,0:T(8,128)S(1)}, f32[448,128]{1,0:T(8,128)S(1)}, u32[]{:S(2)}, u32[]{:S(2)}) collective-permute-start(f32[448,128]{1,0:T(8,128)S(1)} %shard_map.213.mine_ref), channel_id=1, source_target_pairs={{0,8},{8,0},{16,24},{24,16},{1,9},{9,1},{17,25},{25,17},{2,10},{10... | collective-permute-start | bytes 688136 | tf_op jit(solution)/shard_map/ppermute | solution.py:772

commit v14 on v13

--- a/solution.py
+++ b/solution.py
@@ -784,7 +784,7 @@
             add_kernel,
             shape(320, 128, bf16),
             [weights, theirs, *waits],
-            [VMEM, VMEM] + [HBM] * len(waits),
+            [VMEM, VMEM] + [HBM, ANY, ANY][: len(waits)],
         )
         distance, number = 2 * distance, number + 1
     count = lax.axis_size("sub")
@@ -1028,7 +1028,9 @@
         scratch=[buffer(rows, features, bf16), pltpu.SemaphoreType.DMA],
         out_specs=HBM,
     )
-    grad_weights = total_weights(give, keep, place, ((), (grad_states,)), result)
+    grad_weights = total_weights(
+        give, keep, place, ((), (result, first_back, second_back)), grad_states
+    )
     return (result, grad_states, grad_weights.reshape(7, features, features))
 
 

time: 89.9 us -> 88 us (0.979)
  starting transfers between devices: 35 us -> 33.6 us
    ppermute x1, starting transfers between devices: 4.3 us -> 1.37 us  [total_weights(): lax.ppermute(weights, ('grp', 'sub'), corners)]
    ppermute x11, starting transfers between devices: 13.3 us -> 14.8 us  [swapped(): lax.ppermute(block, axis, [(i, i ^ distance) for i in range(lax.axis_size...]
  transfers between devices with their start and end apart: 20 -> 20, of which waited for: 9 -> 8; matrix products, arithmetic and copies ran while one was open for 0% -> 0% of each run, Pallas kernels for 31% -> 31%
where the time goes in v14:
time: 88 us; the launch traced here: 87.8 us
  Pallas kernels  41.5 us (47%)
  starting transfers between devices  33.6 us (38%)
  waiting for transfers between devices  11.8 us (13%)
  between operations  0.9 us (1%)
    pallas_call x22, Pallas kernels, call(): pl.pallas_call(kernel, out_shape=out_shape, in_specs=in_specs, out_specs=...  41.5 us
    ppermute x11, starting transfers between devices, swapped(): lax.ppermute(block, axis, [(i, i ^ distance) for i in range(lax.axis_size...  14.8 us
    ppermute x4, starting transfers between devices, exchange(): lax.ppermute(first, 'sub', routes[0])  14.6 us
    ppermute x11, waiting for transfers between devices, swapped(): lax.ppermute(block, axis, [(i, i ^ distance) for i in range(lax.axis_size...  10.4 us
    ppermute x4, starting transfers between devices, exchange(): lax.ppermute(second, 'sub', routes[1])  2.81 us
  transfers between devices with their start and end apart: 20, of which 8 were waited for; matrix products, arithmetic and copies ran while one was open for 0% of the time, Pallas kernels for 31%

profile of v14, /device:TPU:0, one launch (start us, length us, event | category | flops | bytes accessed | tf_op | source)
XLA Modules:
  0.0 87.8 jit_solution(10697396368810456252)
XLA Ops:
  0.6 2.3 %shard_map.193 = (bf16[512,128]{1,0:T(8,128)(2,1)S(1)}, bf16[512,128]{1,0:T(8,128)(2,1)S(1)}, bf16[4096,128]{1,0:T(8,128)(2,1)S(1)}, s32[16,128]{1,0:T(8,128)S(1)}) custom-call(s32[512]{0:T(512)} %lo_hbm.1, s32[512]{0:T(512)} %hi_hbm.1, bf16[4096,128]{1,0:T(8,128)(2,1)} %x_hbm.1), custom_call_target="tpu_custom_call" | custom-call | tf_op jit(solution)/shard_map/pallas_call | solution.py:52
  3.6 5.8 %collective-permute-start = (bf16[512,128]{1,0:T(8,128)(2,1)S(1)}, bf16[512,128]{1,0:T(8,128)(2,1)S(1)}, u32[]{:S(2)}, u32[]{:S(2)}) collective-permute-start(bf16[512,128]{1,0:T(8,128)(2,1)S(1)} %get-tuple-element.44.rest_7_), channel_id=1, source_target_pairs={{0,1},{2,3},{4,5},{6,7},{1,0},{3,2},{5,4},{7,6},{8,9},{10,11},{12,... | collective-permute-start | bytes 393224 | tf_op jit(solution)/shard_map/ppermute | solution.py:768
  9.4 2.2 %shard_map.194 = (bf16[16,128]{1,0:T(8,128)(2,1)S(1)}, f32[8,4096]{1,0:T(8,128)S(1)}, f32[4096,8]{1,0:T(8,128)S(1)}, f32[8,1024]{1,0:T(8,128)S(1)}, f32[1024,8]{...) custom-call(s32[16,128]{1,0:T(8,128)S(1)} %get-tuple-element.43.plac, ...), custom_call_target="tpu_custom_call" | custom-call | tf_op jit(solution)/shard_map/pallas_call | solution.py:52
  11.6 2.8 %shard_map.195.x_ref = bf16[1024,128]{1,0:T(8,128)(2,1)S(1)} custom-call(s32[32,128]{1,0:T(8,128)S(1)} %get-tuple-element.48.owner_ref, bf16[4096,128]{1,0:T(8,128)(2,1)S(1)} %get-tuple-element.50.g_ref, s32[1,1024]{1,0:T(1,128)S(1)} %get-tuple-element.51.after_ref.sends_ref), custom_call_target="tpu_custom_call" | custom-call | tf_op jit(solution)/shard_map/pallas_call | solution.py:52
  14.5 9.2 %shard_map.197 = (bf16[4096,128]{1,0:T(8,128)(2,1)S(1)}, bf16[32768,128]{1,0:T(8,128)(2,1)}, bf16[4096,128]{1,0:T(8,128)(2,1)S(1)}, bf16[528,128]{1,0:T(8,128)(2,1)S(1)}) custom-call(s32[16,128]{1,0:T(8,128)S(1)} %get-tuple-element.43.place_ref, bf16[4096,128]{1,0:T(8,128)(2,1)S(1)} %get-tuple-element.42.h_ref, ...), custom_call_target="tpu_custom_call" | custom-call | tf_op jit(solution)/shard_map/pallas_call | solution.py:52
  24.3 1.2 %shard_map.198.mine_ref = bf16[528,128]{1,0:T(8,128)(2,1)S(1)} custom-call(s32[16,128]{1,0:T(8,128)S(1)} %get-tuple-element.43.place_ref, s32[32,128]{1,0:T(8,128)S(1)} %get-tuple-element.48.owner_ref, bf16[4096,128]{1,0:T(8,128)(2,1)S(1)} %get-tuple-element.53.new_ref, bf16[16,128]{1,0:T(8,128)(2,1)S(1)} %get-tuple-element.49.counts_ref), custom_call_target="tpu_custom_call" | custom-call | tf_op jit(solution)/shard_map/pallas_call | solution.py:52
  25.6 1.6 %collective-permute-start.3 = (bf16[528,128]{1,0:T(8,128)(2,1)S(1)}, bf16[528,128]{1,0:T(8,128)(2,1)S(1)}, u32[]{:S(2)}, u32[]{:S(2)}) collective-permute-start(bf16[528,128]{1,0:T(8,128)(2,1)S(1)} %shard_map.199.after_ref.totals_ref.rest_0_), channel_id=1, source_target_pairs={{0,16},{8,24},{16,0},{24,8},{1,17},{9,25},{17,1},{25,9},{2,18},{10... | collective-permute-start | bytes 405512 | tf_op jit(solution)/shard_map/ppermute | solution.py:772
  28.4 3.7 %collective-permute-done.3.more_totals_ref = bf16[528,128]{1,0:T(8,128)(2,1)S(1)} collective-permute-done((bf16[528,128]{1,0:T(8,128)(2,1)S(1)}, bf16[528,128]{1,0:T(8,128)(2,1)S(1)}, u32[]{:S(2)}, u32[]{:S(2)}) %collective-permute-start.3) | collective-permute-done | bytes 135200 | tf_op jit(solution)/shard_map/ppermute | solution.py:772
  32.5 1.3 %collective-permute-done.4.their_half_ref = bf16[512,128]{1,0:T(8,128)(2,1)S(1)} collective-permute-done((bf16[512,128]{1,0:T(8,128)(2,1)S(1)}, bf16[512,128]{1,0:T(8,128)(2,1)S(1)}, u32[]{:S(2)}, u32[]{:S(2)}) %collective-permute-start.4) | collective-permute-done | bytes 131104 | tf_op jit(solution)/shard_map/ppermute | solution.py:772
  34.2 2.4 %collective-permute-start.5 = (bf16[64,128]{1,0:T(8,128)(2,1)S(1)}, bf16[64,128]{1,0:T(8,128)(2,1)S(1)}, u32[]{:S(2)}, u32[]{:S(2)}) collective-permute-start(bf16[64,128]{1,0:T(8,128)(2,1)S(1)} %get-tuple-element.58), channel_id=1, source_target_pairs={{0,1},{2,3},{4,5},{6,7},{1,0},{3,2},{5,4},{7,6},{8,9},{10,11},{12,... | collective-permute-start | bytes 49160 | tf_op jit(solution)/shard_map/ppermute | solution.py:768
  38.2 1.8 %shard_map.203 = (bf16[1024,128]{1,0:T(8,128)(2,1)S(1)}, bf16[8192,128]{1,0:T(8,128)(2,1)S(1)}) custom-call(bf16[1024,128]{1,0:T(8,128)(2,1)S(1)} %get-tuple-element.57.cin_ref, bf16[64,128]{1,0:T(8,128)(2,1)S(1)} %collective-permute-done.5.first_ref, bf16[64,128]{1,0:T(8,128)(2,1)S(1)} %collective-permute-done.6.second_ref, ...), custom_call_target="tpu_custom_call" | custom-call | tf_op jit(solution)/shard_map/pallas_call | solution.py:52
  40.1 1.5 %shard_map.205 = (f32[1024,128]{1,0:T(8,128)S(1)}, bf16[64,128]{1,0:T(8,128)(2,1)S(1)}, bf16[64,128]{1,0:T(8,128)(2,1)S(1)}, bf16[1024,128]{1,0:T(8,128)(2,1)S(1...) custom-call(bf16[8192,128]{1,0:T(8,128)(2,1)S(1)} %get-tuple-element.61.slope_ref, ...), custom_call_target="tpu_custom_call" | custom-call | tf_op jit(solution)/shard_map/pallas_call | solution.py:52
  41.6 5.0 %collective-permute-start.9 = (bf16[64,128]{1,0:T(8,128)(2,1)S(1)}, bf16[64,128]{1,0:T(8,128)(2,1)S(1)}, u32[]{:S(2)}, u32[]{:S(2)}) collective-permute-start(bf16[64,128]{1,0:T(8,128)(2,1)S(1)} %get-tuple-element.64.first_grad_ref), channel_id=1, source_target_pairs={{0,1},{2,3},{4,5},{6,7},{1,0},{3,2},{5,4},{7,6},{8,9},{10,11},{12,... | collective-permute-start | bytes 49160 | tf_op jit(solution)/shard_map/ppermute | solution.py:768
  48.3 9.2 %shard_map.208 = (bf16[4096,128]{1,0:T(8,128)(2,1)S(1)}, bf16[4096,256]{1,0:T(8,128)(2,1)S(1)}, bf16[512,128]{1,0:T(8,128)(2,1)S(1)}, bf16[512,128]{1,0:T(8,128)...) custom-call(s32[16,128]{1,0:T(8,128)S(1)} %get-tuple-element.43.place_ref, ...), custom_call_target="tpu_custom_call" | custom-call | tf_op jit(solution)/shard_map/pallas_call | solution.py:52
  57.6 1.3 %collective-permute-done.13.theirs_ref = f32[192,128]{1,0:T(8,128)S(1)} collective-permute-done((f32[192,128]{1,0:T(8,128)S(1)}, f32[192,128]{1,0:T(8,128)S(1)}, u32[]{:S(2)}, u32[]{:S(2)}) %collective-permute-start.13) | collective-permute-done | bytes 98336 | tf_op jit(solution)/shard_map/ppermute | solution.py:772
  58.9 6.8 %collective-permute-start.14 = (bf16[320,128]{1,0:T(8,128)(2,1)S(1)}, bf16[320,128]{1,0:T(8,128)(2,1)S(1)}, u32[]{:S(2)}, u32[]{:S(2)}) collective-permute-start(bf16[320,128]{1,0:T(8,128)(2,1)S(1)} %shard_map.210.mine_ref), channel_id=1, source_target_pairs={{0,2},{1,3},{2,0},{3,1},{4,6},{5,7},{6,4},{7,5},{8,10},{9,11},{10,... | collective-permute-start | bytes 245768 | tf_op jit(solution)/shard_map/ppermute | solution.py:772
  65.7 1.5 %collective-permute-start.11 = (bf16[512,128]{1,0:T(8,128)(2,1)S(1)}, bf16[512,128]{1,0:T(8,128)(2,1)S(1)}, u32[]{:S(2)}, u32[]{:S(2)}) collective-permute-start(bf16[512,128]{1,0:T(8,128)(2,1)S(1)} %get-tuple-element.77), channel_id=1, source_target_pairs={{0,1},{2,3},{4,5},{6,7},{1,0},{3,2},{5,4},{7,6},{8,9},{10,11},{12,... | collective-permute-start | bytes 393224 | tf_op jit(solution)/shard_map/ppermute | solution.py:768
  68.5 2.8 %collective-permute-start.15 = (bf16[320,128]{1,0:T(8,128)(2,1)S(1)}, bf16[320,128]{1,0:T(8,128)(2,1)S(1)}, u32[]{:S(2)}, u32[]{:S(2)}) collective-permute-start(bf16[320,128]{1,0:T(8,128)(2,1)S(1)} %shard_map.211.mine_ref), channel_id=1, source_target_pairs={{0,4},{1,5},{2,6},{3,7},{4,0},{5,1},{6,2},{7,3},{8,12},{9,13},{10,... | collective-permute-start | bytes 245768 | tf_op jit(solution)/shard_map/ppermute | solution.py:772
  71.3 3.9 %shard_map.207.rest_0_ = bf16[4096,128]{1,0:T(8,128)(2,1)} custom-call(bf16[4096,128]{1,0:T(8,128)(2,1)S(1)} %get-tuple-element.42.h_ref, bf16[4096,128]{1,0:T(8,128)(2,1)S(1)} %get-tuple-element.52.summed_ref, bf16[896,128]{1,0:T(8,128)(2,1)S(1)} %get-tuple-element.46.weights_ref.matrices_ref, f32[4096,8]{1,0:T(8,128)S(1)} %shard_map.200.after_ref.owners_ref, ...), custom_call_target="tpu_custom_call" | custom-call | tf_op jit(solution)/shard_map/pallas_call | solution.py:52
  75.3 2.1 %collective-permute-done.15.theirs_ref = bf16[320,128]{1,0:T(8,128)(2,1)S(1)} collective-permute-done((bf16[320,128]{1,0:T(8,128)(2,1)S(1)}, bf16[320,128]{1,0:T(8,128)(2,1)S(1)}, u32[]{:S(2)}, u32[]{:S(2)}) %collective-permute-start.15) | collective-permute-done | bytes 81952 | tf_op jit(solution)/shard_map/ppermute | solution.py:772
  77.4 1.4 %collective-permute-start.18 = (bf16[320,128]{1,0:T(8,128)(2,1)S(1)}, bf16[320,128]{1,0:T(8,128)(2,1)S(1)}, u32[]{:S(2)}, u32[]{:S(2)}) collective-permute-start(bf16[320,128]{1,0:T(8,128)(2,1)S(1)} %shard_map.212.mine_ref), channel_id=1, source_target_pairs={{0,17},{1,16},{2,19},{3,18},{4,21},{5,20},{6,23},{7,22},{8,25},{9,... | collective-permute-start | bytes 245768 | tf_op jit(solution)/shard_map/ppermute | solution.py:803
  79.3 1.7 %collective-permute-start.16 = (bf16[320,128]{1,0:T(8,128)(2,1)S(1)}, bf16[320,128]{1,0:T(8,128)(2,1)S(1)}, u32[]{:S(2)}, u32[]{:S(2)}) collective-permute-start(bf16[320,128]{1,0:T(8,128)(2,1)S(1)} %shard_map.212.mine_ref), channel_id=1, source_target_pairs={{0,1},{1,0},{2,3},{3,2},{4,5},{5,4},{6,7},{7,6},{8,9},{9,8},{10,11... | collective-permute-start | bytes 245768 | tf_op jit(solution)/shard_map/ppermute | solution.py:772
  81.0 4.3 %shard_map.209.after_ref = bf16[4096,128]{1,0:T(8,128)(2,1)} custom-call(bf16[4096,128]{1,0:T(8,128)(2,1)S(1)} %get-tuple-element.75.ups_ref, bf16[4096,256]{1,0:T(8,128)(2,1)S(1)} %get-tuple-element.76.downs_ref, bf16[512,128]{1,0:T(8,128)(2,1)S(1)} %collective-permute-done.11.first_back_ref.rest_1_, ...), custom_call_target="tpu_custom_call" | custom-call | tf_op jit(solution)/shard_map/pallas_call | solution.py:52
  85.5 1.5 %collective-permute-done.19.theirs_ref = f32[448,128]{1,0:T(8,128)S(1)} collective-permute-done((f32[448,128]{1,0:T(8,128)S(1)}, f32[448,128]{1,0:T(8,128)S(1)}, u32[]{:S(2)}, u32[]{:S(2)}) %collective-permute-start.19) | collective-permute-done | bytes 229408 | tf_op jit(solution)/shard_map/ppermute | solution.py:772
  (38 shorter events, 9.6 us)
Async XLA Ops:
  2.9 11.5 %collective-permute-start.1 = (bf16[512,128]{1,0:T(8,128)(2,1)S(1)}, bf16[512,128]{1,0:T(8,128)(2,1)S(1)}, u32[]{:S(2)}, u32[]{:S(2)}) collective-permute-start(bf16[512,128]{1,0:T(8,128)(2,1)S(1)} %get-tuple-element.45), channel_id=1, source_target_pairs={{1,2},{3,4},{5,6},{2,1},{4,3},{6,5},{9,10},{11,12},{13,14},{10,9},... | collective-permute-start | bytes 393224 | tf_op jit(solution)/shard_map/ppermute | solution.py:768
  3.6 10.8 %collective-permute-start = (bf16[512,128]{1,0:T(8,128)(2,1)S(1)}, bf16[512,128]{1,0:T(8,128)(2,1)S(1)}, u32[]{:S(2)}, u32[]{:S(2)}) collective-permute-start(bf16[512,128]{1,0:T(8,128)(2,1)S(1)} %get-tuple-element.44.rest_7_), channel_id=1, source_target_pairs={{0,1},{2,3},{4,5},{6,7},{1,0},{3,2},{5,4},{7,6},{8,9},{10,11},{12,... | collective-permute-start | bytes 393224 | tf_op jit(solution)/shard_map/ppermute | solution.py:768
  14.5 12.7 %collective-permute-start.7 = (bf16[1024,128]{1,0:T(8,128)(2,1)S(1)}, bf16[1024,128]{1,0:T(8,128)(2,1)S(1)}, u32[]{:S(2)}, u32[]{:S(2)}) collective-permute-start(bf16[1024,128]{1,0:T(8,128)(2,1)S(1)} %shard_map.196.after_ref.mine_ref), channel_id=1, source_target_pairs={{0,8},{8,0},{16,24},{24,16},{1,9},{9,1},{17,25},{25,17},{2,10},{10... | collective-permute-start | bytes 786440 | tf_op jit(solution)/shard_map/ppermute | solution.py:772
  23.7 1.8 %collective-permute-start.2 = (bf16[528,128]{1,0:T(8,128)(2,1)S(1)}, bf16[528,128]{1,0:T(8,128)(2,1)S(1)}, u32[]{:S(2)}, u32[]{:S(2)}) collective-permute-start(bf16[528,128]{1,0:T(8,128)(2,1)S(1)} %get-tuple-element.54), channel_id=1, source_target_pairs={{0,8},{8,0},{16,24},{24,16},{1,9},{9,1},{17,25},{25,17},{2,10},{10... | collective-permute-start | bytes 405512 | tf_op jit(solution)/shard_map/ppermute | solution.py:772
  25.6 6.5 %collective-permute-start.3 = (bf16[528,128]{1,0:T(8,128)(2,1)S(1)}, bf16[528,128]{1,0:T(8,128)(2,1)S(1)}, u32[]{:S(2)}, u32[]{:S(2)}) collective-permute-start(bf16[528,128]{1,0:T(8,128)(2,1)S(1)} %shard_map.199.after_ref.totals_ref.rest_0_), channel_id=1, source_target_pairs={{0,16},{8,24},{16,0},{24,8},{1,17},{9,25},{17,1},{25,9},{2,18},{10... | collective-permute-start | bytes 405512 | tf_op jit(solution)/shard_map/ppermute | solution.py:772
  27.2 12.9 %collective-permute-start.8 = (bf16[1024,128]{1,0:T(8,128)(2,1)S(1)}, bf16[1024,128]{1,0:T(8,128)(2,1)S(1)}, u32[]{:S(2)}, u32[]{:S(2)}) collective-permute-start(bf16[1024,128]{1,0:T(8,128)(2,1)S(1)} %shard_map.204.chip_sums_ref), channel_id=1, source_target_pairs={{0,16},{8,24},{16,0},{24,8},{1,17},{9,25},{17,1},{25,9},{2,18},{10... | collective-permute-start | bytes 786440 | tf_op jit(solution)/shard_map/ppermute | solution.py:772
  32.4 1.4 %collective-permute-start.4 = (bf16[512,128]{1,0:T(8,128)(2,1)S(1)}, bf16[512,128]{1,0:T(8,128)(2,1)S(1)}, u32[]{:S(2)}, u32[]{:S(2)}) collective-permute-start(bf16[512,128]{1,0:T(8,128)(2,1)S(1)} %get-tuple-element.55.half_ref), channel_id=1, source_target_pairs={{0,8},{8,0},{16,24},{24,16},{1,9},{9,1},{17,25},{25,17},{2,10},{10... | collective-permute-start | bytes 393224 | tf_op jit(solution)/shard_map/ppermute | solution.py:772
  34.2 4.1 %collective-permute-start.5 = (bf16[64,128]{1,0:T(8,128)(2,1)S(1)}, bf16[64,128]{1,0:T(8,128)(2,1)S(1)}, u32[]{:S(2)}, u32[]{:S(2)}) collective-permute-start(bf16[64,128]{1,0:T(8,128)(2,1)S(1)} %get-tuple-element.58), channel_id=1, source_target_pairs={{0,1},{2,3},{4,5},{6,7},{1,0},{3,2},{5,4},{7,6},{8,9},{10,11},{12,... | collective-permute-start | bytes 49160 | tf_op jit(solution)/shard_map/ppermute | solution.py:768
  36.5 1.7 %collective-permute-start.6 = (bf16[64,128]{1,0:T(8,128)(2,1)S(1)}, bf16[64,128]{1,0:T(8,128)(2,1)S(1)}, u32[]{:S(2)}, u32[]{:S(2)}) collective-permute-start(bf16[64,128]{1,0:T(8,128)(2,1)S(1)} %get-tuple-element.59), channel_id=1, source_target_pairs={{1,2},{3,4},{5,6},{2,1},{4,3},{6,5},{9,10},{11,12},{13,14},{10,9},... | collective-permute-start | bytes 49160 | tf_op jit(solution)/shard_map/ppermute | solution.py:768
  41.6 6.7 %collective-permute-start.9 = (bf16[64,128]{1,0:T(8,128)(2,1)S(1)}, bf16[64,128]{1,0:T(8,128)(2,1)S(1)}, u32[]{:S(2)}, u32[]{:S(2)}) collective-permute-start(bf16[64,128]{1,0:T(8,128)(2,1)S(1)} %get-tuple-element.64.first_grad_ref), channel_id=1, source_target_pairs={{0,1},{2,3},{4,5},{6,7},{1,0},{3,2},{5,4},{7,6},{8,9},{10,11},{12,... | collective-permute-start | bytes 49160 | tf_op jit(solution)/shard_map/ppermute | solution.py:768
  46.6 1.7 %collective-permute-start.10 = (bf16[64,128]{1,0:T(8,128)(2,1)S(1)}, bf16[64,128]{1,0:T(8,128)(2,1)S(1)}, u32[]{:S(2)}, u32[]{:S(2)}) collective-permute-start(bf16[64,128]{1,0:T(8,128)(2,1)S(1)} %get-tuple-element.65.second_grad_ref), channel_id=1, source_target_pairs={{1,2},{3,4},{5,6},{2,1},{4,3},{6,5},{9,10},{11,12},{13,14},{10,9},... | collective-permute-start | bytes 49160 | tf_op jit(solution)/shard_map/ppermute | solution.py:768
  57.5 1.4 %collective-permute-start.13 = (f32[192,128]{1,0:T(8,128)S(1)}, f32[192,128]{1,0:T(8,128)S(1)}, u32[]{:S(2)}, u32[]{:S(2)}) collective-permute-start(f32[192,128]{1,0:T(8,128)S(1)} %get-tuple-element.80), channel_id=1, source_target_pairs={{0,8},{8,0},{16,24},{24,16},{1,9},{9,1},{17,25},{25,17},{2,10},{10... | collective-permute-start | bytes 294920 | tf_op jit(solution)/shard_map/ppermute | solution.py:772
  58.9 9.6 %collective-permute-start.14 = (bf16[320,128]{1,0:T(8,128)(2,1)S(1)}, bf16[320,128]{1,0:T(8,128)(2,1)S(1)}, u32[]{:S(2)}, u32[]{:S(2)}) collective-permute-start(bf16[320,128]{1,0:T(8,128)(2,1)S(1)} %shard_map.210.mine_ref), channel_id=1, source_target_pairs={{0,2},{1,3},{2,0},{3,1},{4,6},{5,7},{6,4},{7,5},{8,10},{9,11},{10,... | collective-permute-start | bytes 245768 | tf_op jit(solution)/shard_map/ppermute | solution.py:772
  65.7 9.6 %collective-permute-start.11 = (bf16[512,128]{1,0:T(8,128)(2,1)S(1)}, bf16[512,128]{1,0:T(8,128)(2,1)S(1)}, u32[]{:S(2)}, u32[]{:S(2)}) collective-permute-start(bf16[512,128]{1,0:T(8,128)(2,1)S(1)} %get-tuple-element.77), channel_id=1, source_target_pairs={{0,1},{2,3},{4,5},{6,7},{1,0},{3,2},{5,4},{7,6},{8,9},{10,11},{12,... | collective-permute-start | bytes 393224 | tf_op jit(solution)/shard_map/ppermute | solution.py:768
  67.3 8.0 %collective-permute-start.12 = (bf16[512,128]{1,0:T(8,128)(2,1)S(1)}, bf16[512,128]{1,0:T(8,128)(2,1)S(1)}, u32[]{:S(2)}, u32[]{:S(2)}) collective-permute-start(bf16[512,128]{1,0:T(8,128)(2,1)S(1)} %get-tuple-element.78), channel_id=1, source_target_pairs={{1,2},{3,4},{5,6},{2,1},{4,3},{6,5},{9,10},{11,12},{13,14},{10,9},... | collective-permute-start | bytes 393224 | tf_op jit(solution)/shard_map/ppermute | solution.py:768
  68.5 8.9 %collective-permute-start.15 = (bf16[320,128]{1,0:T(8,128)(2,1)S(1)}, bf16[320,128]{1,0:T(8,128)(2,1)S(1)}, u32[]{:S(2)}, u32[]{:S(2)}) collective-permute-start(bf16[320,128]{1,0:T(8,128)(2,1)S(1)} %shard_map.211.mine_ref), channel_id=1, source_target_pairs={{0,4},{1,5},{2,6},{3,7},{4,0},{5,1},{6,2},{7,3},{8,12},{9,13},{10,... | collective-permute-start | bytes 245768 | tf_op jit(solution)/shard_map/ppermute | solution.py:772
  77.4 7.9 %collective-permute-start.18 = (bf16[320,128]{1,0:T(8,128)(2,1)S(1)}, bf16[320,128]{1,0:T(8,128)(2,1)S(1)}, u32[]{:S(2)}, u32[]{:S(2)}) collective-permute-start(bf16[320,128]{1,0:T(8,128)(2,1)S(1)} %shard_map.212.mine_ref), channel_id=1, source_target_pairs={{0,17},{1,16},{2,19},{3,18},{4,21},{5,20},{6,23},{7,22},{8,25},{9,... | collective-permute-start | bytes 245768 | tf_op jit(solution)/shard_map/ppermute | solution.py:803
  78.8 6.6 %collective-permute-start.17 = (bf16[320,128]{1,0:T(8,128)(2,1)S(1)}, bf16[320,128]{1,0:T(8,128)(2,1)S(1)}, u32[]{:S(2)}, u32[]{:S(2)}) collective-permute-start(bf16[320,128]{1,0:T(8,128)(2,1)S(1)} %shard_map.212.mine_ref), channel_id=1, source_target_pairs={{0,16},{8,24},{16,0},{24,8},{1,17},{9,25},{17,1},{25,9},{2,18},{10... | collective-permute-start | bytes 245768 | tf_op jit(solution)/shard_map/ppermute | solution.py:772
  79.3 6.0 %collective-permute-start.16 = (bf16[320,128]{1,0:T(8,128)(2,1)S(1)}, bf16[320,128]{1,0:T(8,128)(2,1)S(1)}, u32[]{:S(2)}, u32[]{:S(2)}) collective-permute-start(bf16[320,128]{1,0:T(8,128)(2,1)S(1)} %shard_map.212.mine_ref), channel_id=1, source_target_pairs={{0,1},{1,0},{2,3},{3,2},{4,5},{5,4},{6,7},{7,6},{8,9},{9,8},{10,11... | collective-permute-start | bytes 245768 | tf_op jit(solution)/shard_map/ppermute | solution.py:772
  85.4 1.6 %collective-permute-start.19 = (f32[448,128]{1,0:T(8,128)S(1)}, f32[448,128]{1,0:T(8,128)S(1)}, u32[]{:S(2)}, u32[]{:S(2)}) collective-permute-start(f32[448,128]{1,0:T(8,128)S(1)} %shard_map.213.mine_ref), channel_id=1, source_target_pairs={{0,8},{8,0},{16,24},{24,16},{1,9},{9,1},{17,25},{25,17},{2,10},{10... | collective-permute-start | bytes 688136 | tf_op jit(solution)/shard_map/ppermute | solution.py:772

commit v15 on v14

--- a/solution.py
+++ b/solution.py
@@ -623,6 +623,7 @@
     mean,
     slope_ref,
     weights,
+    pair,
     slope_sems,
 ):
     count = STEP * BLOCK
@@ -656,6 +657,7 @@
         grad_up = g_ref[here, :].astype(f32) + owner_rows(owners_ref[here, :], mean[...])
         ups = grad_up.astype(bf16)
         ups_ref[here, :] = ups
+        weights[256:384, :] += dot_tn(summed_ref[here, :], ups)
         grad_sum[here, :] = (dot_nt(ups, matrix(matrices_ref, 2)) * 0.5).astype(bf16)
 
     def edge_step(index):
@@ -663,10 +665,12 @@
         slope_copy(index).wait()
         slope = slope_ref[chunk_of(index, 8 * count), :]
         slopes = [slope[n * 8 * BLOCK : (n + 1) * 8 * BLOCK] for n in range(STEP)]
-        downs_ref[here, :] = edges_back(
-            slopes, grad_sum[here, :], columns_ref[:, here], halo_grad
-        )
-
+        both = edges_back(slopes, grad_sum[here, :], columns_ref[:, here], halo_grad)
+        downs_ref[here, :] = both
+        pair[...] += dot_tn(h_ref[here, :], both)
+
+    pair[...] = jnp.zeros_like(pair)
+    weights[256:384, :] = jnp.zeros((128, 128), f32)
     owner_step(0)
 
     def step(index, carry):
@@ -680,14 +684,12 @@
     second_grad = halo_grad[halo_rows:, :].astype(bf16)
     first_grad_ref[...] = first_grad
     second_grad_ref[...] = second_grad
-    pair_grad = dot_tn(h_ref[...], downs_ref[...])
-    weights[0:128, :] = pair_grad[:, :128]
+    weights[0:128, :] = pair[:, :128]
     weights[128:256, :] = (
-        pair_grad[:, 128:]
+        pair[:, 128:]
         + dot_tn(first_ref[...], first_grad)
         + dot_tn(second_ref[...], second_grad)
     )
-    weights[256:384, :] = dot_tn(summed_ref[...], ups_ref[...])
     first = core_of(place_ref) == 0
     low, high = weights[:192, :], weights[192:, :]
     give_ref[...] = jnp.where(first, high, low)
@@ -1015,6 +1017,7 @@
             buffer(coarse_rows, features, bf16),
             buffer(8 * rows, features, bf16),
             buffer(384, features, f32),
+            buffer(features, 2 * features, f32),
             pltpu.SemaphoreType.DMA((rows // (STEP * BLOCK),)),
         ],
         mib=32,

time: 88 us -> 87.7 us (level)
  transfers between devices with their start and end apart: 20 -> 20, of which waited for: 8 -> 8; matrix products, arithmetic and copies ran while one was open for 0% -> 0% of each run, Pallas kernels for 31% -> 32%
where the time goes in v15:
time: 87.7 us; the launch traced here: 87.4 us
  Pallas kernels  41.1 us (47%)
  starting transfers between devices  33.6 us (38%)
  waiting for transfers between devices  11.8 us (13%)
  between operations  0.9 us (1%)
    pallas_call x22, Pallas kernels, call(): pl.pallas_call(kernel, out_shape=out_shape, in_specs=in_specs, out_specs=...  41.1 us
    ppermute x11, starting transfers between devices, swapped(): lax.ppermute(block, axis, [(i, i ^ distance) for i in range(lax.axis_size...  14.8 us
    ppermute x4, starting transfers between devices, exchange(): lax.ppermute(first, 'sub', routes[0])  14.6 us
    ppermute x11, waiting for transfers between devices, swapped(): lax.ppermute(block, axis, [(i, i ^ distance) for i in range(lax.axis_size...  10.4 us
    ppermute x4, starting transfers between devices, exchange(): lax.ppermute(second, 'sub', routes[1])  2.81 us
  transfers between devices with their start and end apart: 20, of which 8 were waited for; matrix products, arithmetic and copies ran while one was open for 0% of the time, Pallas kernels for 32%

profile of v15, /device:TPU:0, one launch (start us, length us, event | category | flops | bytes accessed | tf_op | source)
XLA Modules:
  0.0 87.4 jit_solution(3925224161858996997)
XLA Ops:
  0.6 2.3 %shard_map.193 = (bf16[512,128]{1,0:T(8,128)(2,1)S(1)}, bf16[512,128]{1,0:T(8,128)(2,1)S(1)}, bf16[4096,128]{1,0:T(8,128)(2,1)S(1)}, s32[16,128]{1,0:T(8,128)S(1)}) custom-call(s32[512]{0:T(512)} %lo_hbm.1, s32[512]{0:T(512)} %hi_hbm.1, bf16[4096,128]{1,0:T(8,128)(2,1)} %x_hbm.1), custom_call_target="tpu_custom_call" | custom-call | tf_op jit(solution)/shard_map/pallas_call | solution.py:52
  3.6 5.8 %collective-permute-start = (bf16[512,128]{1,0:T(8,128)(2,1)S(1)}, bf16[512,128]{1,0:T(8,128)(2,1)S(1)}, u32[]{:S(2)}, u32[]{:S(2)}) collective-permute-start(bf16[512,128]{1,0:T(8,128)(2,1)S(1)} %get-tuple-element.44.rest_7_), channel_id=1, source_target_pairs={{0,1},{2,3},{4,5},{6,7},{1,0},{3,2},{5,4},{7,6},{8,9},{10,11},{12,... | collective-permute-start | bytes 393224 | tf_op jit(solution)/shard_map/ppermute | solution.py:770
  9.4 2.2 %shard_map.194 = (bf16[16,128]{1,0:T(8,128)(2,1)S(1)}, f32[8,4096]{1,0:T(8,128)S(1)}, f32[4096,8]{1,0:T(8,128)S(1)}, f32[8,1024]{1,0:T(8,128)S(1)}, f32[1024,8]{...) custom-call(s32[16,128]{1,0:T(8,128)S(1)} %get-tuple-element.43.plac, ...), custom_call_target="tpu_custom_call" | custom-call | tf_op jit(solution)/shard_map/pallas_call | solution.py:52
  11.6 2.8 %shard_map.195.x_ref = bf16[1024,128]{1,0:T(8,128)(2,1)S(1)} custom-call(s32[32,128]{1,0:T(8,128)S(1)} %get-tuple-element.48.owner_ref, bf16[4096,128]{1,0:T(8,128)(2,1)S(1)} %get-tuple-element.50.g_ref, s32[1,1024]{1,0:T(1,128)S(1)} %get-tuple-element.51.after_ref.sends_ref), custom_call_target="tpu_custom_call" | custom-call | tf_op jit(solution)/shard_map/pallas_call | solution.py:52
  14.5 9.2 %shard_map.197 = (bf16[4096,128]{1,0:T(8,128)(2,1)S(1)}, bf16[32768,128]{1,0:T(8,128)(2,1)}, bf16[4096,128]{1,0:T(8,128)(2,1)S(1)}, bf16[528,128]{1,0:T(8,128)(2,1)S(1)}) custom-call(s32[16,128]{1,0:T(8,128)S(1)} %get-tuple-element.43.place_ref, bf16[4096,128]{1,0:T(8,128)(2,1)S(1)} %get-tuple-element.42.h_ref, ...), custom_call_target="tpu_custom_call" | custom-call | tf_op jit(solution)/shard_map/pallas_call | solution.py:52
  24.3 1.2 %shard_map.198.mine_ref = bf16[528,128]{1,0:T(8,128)(2,1)S(1)} custom-call(s32[16,128]{1,0:T(8,128)S(1)} %get-tuple-element.43.place_ref, s32[32,128]{1,0:T(8,128)S(1)} %get-tuple-element.48.owner_ref, bf16[4096,128]{1,0:T(8,128)(2,1)S(1)} %get-tuple-element.53.new_ref, bf16[16,128]{1,0:T(8,128)(2,1)S(1)} %get-tuple-element.49.counts_ref), custom_call_target="tpu_custom_call" | custom-call | tf_op jit(solution)/shard_map/pallas_call | solution.py:52
  25.6 1.6 %collective-permute-start.3 = (bf16[528,128]{1,0:T(8,128)(2,1)S(1)}, bf16[528,128]{1,0:T(8,128)(2,1)S(1)}, u32[]{:S(2)}, u32[]{:S(2)}) collective-permute-start(bf16[528,128]{1,0:T(8,128)(2,1)S(1)} %shard_map.199.after_ref.totals_ref.rest_0_), channel_id=1, source_target_pairs={{0,16},{8,24},{16,0},{24,8},{1,17},{9,25},{17,1},{25,9},{2,18},{10... | collective-permute-start | bytes 405512 | tf_op jit(solution)/shard_map/ppermute | solution.py:774
  28.4 3.7 %collective-permute-done.3.more_totals_ref = bf16[528,128]{1,0:T(8,128)(2,1)S(1)} collective-permute-done((bf16[528,128]{1,0:T(8,128)(2,1)S(1)}, bf16[528,128]{1,0:T(8,128)(2,1)S(1)}, u32[]{:S(2)}, u32[]{:S(2)}) %collective-permute-start.3) | collective-permute-done | bytes 135200 | tf_op jit(solution)/shard_map/ppermute | solution.py:774
  32.5 1.3 %collective-permute-done.4.their_half_ref = bf16[512,128]{1,0:T(8,128)(2,1)S(1)} collective-permute-done((bf16[512,128]{1,0:T(8,128)(2,1)S(1)}, bf16[512,128]{1,0:T(8,128)(2,1)S(1)}, u32[]{:S(2)}, u32[]{:S(2)}) %collective-permute-start.4) | collective-permute-done | bytes 131104 | tf_op jit(solution)/shard_map/ppermute | solution.py:774
  34.2 2.4 %collective-permute-start.5 = (bf16[64,128]{1,0:T(8,128)(2,1)S(1)}, bf16[64,128]{1,0:T(8,128)(2,1)S(1)}, u32[]{:S(2)}, u32[]{:S(2)}) collective-permute-start(bf16[64,128]{1,0:T(8,128)(2,1)S(1)} %get-tuple-element.58), channel_id=1, source_target_pairs={{0,1},{2,3},{4,5},{6,7},{1,0},{3,2},{5,4},{7,6},{8,9},{10,11},{12,... | collective-permute-start | bytes 49160 | tf_op jit(solution)/shard_map/ppermute | solution.py:770
  38.2 1.8 %shard_map.203 = (bf16[1024,128]{1,0:T(8,128)(2,1)S(1)}, bf16[8192,128]{1,0:T(8,128)(2,1)S(1)}) custom-call(bf16[1024,128]{1,0:T(8,128)(2,1)S(1)} %get-tuple-element.57.cin_ref, bf16[64,128]{1,0:T(8,128)(2,1)S(1)} %collective-permute-done.5.first_ref, bf16[64,128]{1,0:T(8,128)(2,1)S(1)} %collective-permute-done.6.second_ref, ...), custom_call_target="tpu_custom_call" | custom-call | tf_op jit(solution)/shard_map/pallas_call | solution.py:52
  40.1 1.5 %shard_map.205 = (f32[1024,128]{1,0:T(8,128)S(1)}, bf16[64,128]{1,0:T(8,128)(2,1)S(1)}, bf16[64,128]{1,0:T(8,128)(2,1)S(1)}, bf16[1024,128]{1,0:T(8,128)(2,1)S(1...) custom-call(bf16[8192,128]{1,0:T(8,128)(2,1)S(1)} %get-tuple-element.61.slope_ref, ...), custom_call_target="tpu_custom_call" | custom-call | tf_op jit(solution)/shard_map/pallas_call | solution.py:52
  41.6 5.0 %collective-permute-start.9 = (bf16[64,128]{1,0:T(8,128)(2,1)S(1)}, bf16[64,128]{1,0:T(8,128)(2,1)S(1)}, u32[]{:S(2)}, u32[]{:S(2)}) collective-permute-start(bf16[64,128]{1,0:T(8,128)(2,1)S(1)} %get-tuple-element.64.first_grad_ref), channel_id=1, source_target_pairs={{0,1},{2,3},{4,5},{6,7},{1,0},{3,2},{5,4},{7,6},{8,9},{10,11},{12,... | collective-permute-start | bytes 49160 | tf_op jit(solution)/shard_map/ppermute | solution.py:770
  48.3 8.8 %shard_map.208 = (bf16[4096,128]{1,0:T(8,128)(2,1)S(1)}, bf16[4096,256]{1,0:T(8,128)(2,1)S(1)}, bf16[512,128]{1,0:T(8,128)(2,1)S(1)}, bf16[512,128]{1,0:T(8,128)...) custom-call(s32[16,128]{1,0:T(8,128)S(1)} %get-tuple-element.43.place_ref, ...), custom_call_target="tpu_custom_call" | custom-call | tf_op jit(solution)/shard_map/pallas_call | solution.py:52
  57.2 1.3 %collective-permute-done.13.theirs_ref = f32[192,128]{1,0:T(8,128)S(1)} collective-permute-done((f32[192,128]{1,0:T(8,128)S(1)}, f32[192,128]{1,0:T(8,128)S(1)}, u32[]{:S(2)}, u32[]{:S(2)}) %collective-permute-start.13) | collective-permute-done | bytes 98336 | tf_op jit(solution)/shard_map/ppermute | solution.py:774
  58.6 6.8 %collective-permute-start.14 = (bf16[320,128]{1,0:T(8,128)(2,1)S(1)}, bf16[320,128]{1,0:T(8,128)(2,1)S(1)}, u32[]{:S(2)}, u32[]{:S(2)}) collective-permute-start(bf16[320,128]{1,0:T(8,128)(2,1)S(1)} %shard_map.210.mine_ref), channel_id=1, source_target_pairs={{0,2},{1,3},{2,0},{3,1},{4,6},{5,7},{6,4},{7,5},{8,10},{9,11},{10,... | collective-permute-start | bytes 245768 | tf_op jit(solution)/shard_map/ppermute | solution.py:774
  65.4 1.5 %collective-permute-start.11 = (bf16[512,128]{1,0:T(8,128)(2,1)S(1)}, bf16[512,128]{1,0:T(8,128)(2,1)S(1)}, u32[]{:S(2)}, u32[]{:S(2)}) collective-permute-start(bf16[512,128]{1,0:T(8,128)(2,1)S(1)} %get-tuple-element.77), channel_id=1, source_target_pairs={{0,1},{2,3},{4,5},{6,7},{1,0},{3,2},{5,4},{7,6},{8,9},{10,11},{12,... | collective-permute-start | bytes 393224 | tf_op jit(solution)/shard_map/ppermute | solution.py:770
  68.2 2.8 %collective-permute-start.15 = (bf16[320,128]{1,0:T(8,128)(2,1)S(1)}, bf16[320,128]{1,0:T(8,128)(2,1)S(1)}, u32[]{:S(2)}, u32[]{:S(2)}) collective-permute-start(bf16[320,128]{1,0:T(8,128)(2,1)S(1)} %shard_map.211.mine_ref), channel_id=1, source_target_pairs={{0,4},{1,5},{2,6},{3,7},{4,0},{5,1},{6,2},{7,3},{8,12},{9,13},{10,... | collective-permute-start | bytes 245768 | tf_op jit(solution)/shard_map/ppermute | solution.py:774
  71.0 3.9 %shard_map.207.rest_0_ = bf16[4096,128]{1,0:T(8,128)(2,1)} custom-call(bf16[4096,128]{1,0:T(8,128)(2,1)S(1)} %get-tuple-element.42.h_ref, bf16[4096,128]{1,0:T(8,128)(2,1)S(1)} %get-tuple-element.52.summed_ref, bf16[896,128]{1,0:T(8,128)(2,1)S(1)} %get-tuple-element.46.weights_ref.matrices_ref, f32[4096,8]{1,0:T(8,128)S(1)} %shard_map.200.after_ref.owners_ref, ...), custom_call_target="tpu_custom_call" | custom-call | tf_op jit(solution)/shard_map/pallas_call | solution.py:52
  74.9 2.1 %collective-permute-done.15.theirs_ref = bf16[320,128]{1,0:T(8,128)(2,1)S(1)} collective-permute-done((bf16[320,128]{1,0:T(8,128)(2,1)S(1)}, bf16[320,128]{1,0:T(8,128)(2,1)S(1)}, u32[]{:S(2)}, u32[]{:S(2)}) %collective-permute-start.15) | collective-permute-done | bytes 81952 | tf_op jit(solution)/shard_map/ppermute | solution.py:774
  77.0 1.4 %collective-permute-start.18 = (bf16[320,128]{1,0:T(8,128)(2,1)S(1)}, bf16[320,128]{1,0:T(8,128)(2,1)S(1)}, u32[]{:S(2)}, u32[]{:S(2)}) collective-permute-start(bf16[320,128]{1,0:T(8,128)(2,1)S(1)} %shard_map.212.mine_ref), channel_id=1, source_target_pairs={{0,17},{1,16},{2,19},{3,18},{4,21},{5,20},{6,23},{7,22},{8,25},{9,... | collective-permute-start | bytes 245768 | tf_op jit(solution)/shard_map/ppermute | solution.py:805
  78.9 1.7 %collective-permute-start.16 = (bf16[320,128]{1,0:T(8,128)(2,1)S(1)}, bf16[320,128]{1,0:T(8,128)(2,1)S(1)}, u32[]{:S(2)}, u32[]{:S(2)}) collective-permute-start(bf16[320,128]{1,0:T(8,128)(2,1)S(1)} %shard_map.212.mine_ref), channel_id=1, source_target_pairs={{0,1},{1,0},{2,3},{3,2},{4,5},{5,4},{6,7},{7,6},{8,9},{9,8},{10,11... | collective-permute-start | bytes 245768 | tf_op jit(solution)/shard_map/ppermute | solution.py:774
  80.6 4.3 %shard_map.209.after_ref = bf16[4096,128]{1,0:T(8,128)(2,1)} custom-call(bf16[4096,128]{1,0:T(8,128)(2,1)S(1)} %get-tuple-element.75.ups_ref, bf16[4096,256]{1,0:T(8,128)(2,1)S(1)} %get-tuple-element.76.downs_ref, bf16[512,128]{1,0:T(8,128)(2,1)S(1)} %collective-permute-done.11.first_back_ref.rest_1_, ...), custom_call_target="tpu_custom_call" | custom-call | tf_op jit(solution)/shard_map/pallas_call | solution.py:52
  85.1 1.5 %collective-permute-done.19.theirs_ref = f32[448,128]{1,0:T(8,128)S(1)} collective-permute-done((f32[448,128]{1,0:T(8,128)S(1)}, f32[448,128]{1,0:T(8,128)S(1)}, u32[]{:S(2)}, u32[]{:S(2)}) %collective-permute-start.19) | collective-permute-done | bytes 229408 | tf_op jit(solution)/shard_map/ppermute | solution.py:774
  (38 shorter events, 9.6 us)
Async XLA Ops:
  2.9 11.5 %collective-permute-start.1 = (bf16[512,128]{1,0:T(8,128)(2,1)S(1)}, bf16[512,128]{1,0:T(8,128)(2,1)S(1)}, u32[]{:S(2)}, u32[]{:S(2)}) collective-permute-start(bf16[512,128]{1,0:T(8,128)(2,1)S(1)} %get-tuple-element.45), channel_id=1, source_target_pairs={{1,2},{3,4},{5,6},{2,1},{4,3},{6,5},{9,10},{11,12},{13,14},{10,9},... | collective-permute-start | bytes 393224 | tf_op jit(solution)/shard_map/ppermute | solution.py:770
  3.6 10.8 %collective-permute-start = (bf16[512,128]{1,0:T(8,128)(2,1)S(1)}, bf16[512,128]{1,0:T(8,128)(2,1)S(1)}, u32[]{:S(2)}, u32[]{:S(2)}) collective-permute-start(bf16[512,128]{1,0:T(8,128)(2,1)S(1)} %get-tuple-element.44.rest_7_), channel_id=1, source_target_pairs={{0,1},{2,3},{4,5},{6,7},{1,0},{3,2},{5,4},{7,6},{8,9},{10,11},{12,... | collective-permute-start | bytes 393224 | tf_op jit(solution)/shard_map/ppermute | solution.py:770
  14.5 12.7 %collective-permute-start.7 = (bf16[1024,128]{1,0:T(8,128)(2,1)S(1)}, bf16[1024,128]{1,0:T(8,128)(2,1)S(1)}, u32[]{:S(2)}, u32[]{:S(2)}) collective-permute-start(bf16[1024,128]{1,0:T(8,128)(2,1)S(1)} %shard_map.196.after_ref.mine_ref), channel_id=1, source_target_pairs={{0,8},{8,0},{16,24},{24,16},{1,9},{9,1},{17,25},{25,17},{2,10},{10... | collective-permute-start | bytes 786440 | tf_op jit(solution)/shard_map/ppermute | solution.py:774
  23.7 1.8 %collective-permute-start.2 = (bf16[528,128]{1,0:T(8,128)(2,1)S(1)}, bf16[528,128]{1,0:T(8,128)(2,1)S(1)}, u32[]{:S(2)}, u32[]{:S(2)}) collective-permute-start(bf16[528,128]{1,0:T(8,128)(2,1)S(1)} %get-tuple-element.54), channel_id=1, source_target_pairs={{0,8},{8,0},{16,24},{24,16},{1,9},{9,1},{17,25},{25,17},{2,10},{10... | collective-permute-start | bytes 405512 | tf_op jit(solution)/shard_map/ppermute | solution.py:774
  25.6 6.5 %collective-permute-start.3 = (bf16[528,128]{1,0:T(8,128)(2,1)S(1)}, bf16[528,128]{1,0:T(8,128)(2,1)S(1)}, u32[]{:S(2)}, u32[]{:S(2)}) collective-permute-start(bf16[528,128]{1,0:T(8,128)(2,1)S(1)} %shard_map.199.after_ref.totals_ref.rest_0_), channel_id=1, source_target_pairs={{0,16},{8,24},{16,0},{24,8},{1,17},{9,25},{17,1},{25,9},{2,18},{10... | collective-permute-start | bytes 405512 | tf_op jit(solution)/shard_map/ppermute | solution.py:774
  27.2 12.9 %collective-permute-start.8 = (bf16[1024,128]{1,0:T(8,128)(2,1)S(1)}, bf16[1024,128]{1,0:T(8,128)(2,1)S(1)}, u32[]{:S(2)}, u32[]{:S(2)}) collective-permute-start(bf16[1024,128]{1,0:T(8,128)(2,1)S(1)} %shard_map.204.chip_sums_ref), channel_id=1, source_target_pairs={{0,16},{8,24},{16,0},{24,8},{1,17},{9,25},{17,1},{25,9},{2,18},{10... | collective-permute-start | bytes 786440 | tf_op jit(solution)/shard_map/ppermute | solution.py:774
  32.4 1.4 %collective-permute-start.4 = (bf16[512,128]{1,0:T(8,128)(2,1)S(1)}, bf16[512,128]{1,0:T(8,128)(2,1)S(1)}, u32[]{:S(2)}, u32[]{:S(2)}) collective-permute-start(bf16[512,128]{1,0:T(8,128)(2,1)S(1)} %get-tuple-element.55.half_ref), channel_id=1, source_target_pairs={{0,8},{8,0},{16,24},{24,16},{1,9},{9,1},{17,25},{25,17},{2,10},{10... | collective-permute-start | bytes 393224 | tf_op jit(solution)/shard_map/ppermute | solution.py:774
  34.2 4.1 %collective-permute-start.5 = (bf16[64,128]{1,0:T(8,128)(2,1)S(1)}, bf16[64,128]{1,0:T(8,128)(2,1)S(1)}, u32[]{:S(2)}, u32[]{:S(2)}) collective-permute-start(bf16[64,128]{1,0:T(8,128)(2,1)S(1)} %get-tuple-element.58), channel_id=1, source_target_pairs={{0,1},{2,3},{4,5},{6,7},{1,0},{3,2},{5,4},{7,6},{8,9},{10,11},{12,... | collective-permute-start | bytes 49160 | tf_op jit(solution)/shard_map/ppermute | solution.py:770
  36.5 1.7 %collective-permute-start.6 = (bf16[64,128]{1,0:T(8,128)(2,1)S(1)}, bf16[64,128]{1,0:T(8,128)(2,1)S(1)}, u32[]{:S(2)}, u32[]{:S(2)}) collective-permute-start(bf16[64,128]{1,0:T(8,128)(2,1)S(1)} %get-tuple-element.59), channel_id=1, source_target_pairs={{1,2},{3,4},{5,6},{2,1},{4,3},{6,5},{9,10},{11,12},{13,14},{10,9},... | collective-permute-start | bytes 49160 | tf_op jit(solution)/shard_map/ppermute | solution.py:770
  41.6 6.7 %collective-permute-start.9 = (bf16[64,128]{1,0:T(8,128)(2,1)S(1)}, bf16[64,128]{1,0:T(8,128)(2,1)S(1)}, u32[]{:S(2)}, u32[]{:S(2)}) collective-permute-start(bf16[64,128]{1,0:T(8,128)(2,1)S(1)} %get-tuple-element.64.first_grad_ref), channel_id=1, source_target_pairs={{0,1},{2,3},{4,5},{6,7},{1,0},{3,2},{5,4},{7,6},{8,9},{10,11},{12,... | collective-permute-start | bytes 49160 | tf_op jit(solution)/shard_map/ppermute | solution.py:770
  46.6 1.7 %collective-permute-start.10 = (bf16[64,128]{1,0:T(8,128)(2,1)S(1)}, bf16[64,128]{1,0:T(8,128)(2,1)S(1)}, u32[]{:S(2)}, u32[]{:S(2)}) collective-permute-start(bf16[64,128]{1,0:T(8,128)(2,1)S(1)} %get-tuple-element.65.second_grad_ref), channel_id=1, source_target_pairs={{1,2},{3,4},{5,6},{2,1},{4,3},{6,5},{9,10},{11,12},{13,14},{10,9},... | collective-permute-start | bytes 49160 | tf_op jit(solution)/shard_map/ppermute | solution.py:770
  57.2 1.4 %collective-permute-start.13 = (f32[192,128]{1,0:T(8,128)S(1)}, f32[192,128]{1,0:T(8,128)S(1)}, u32[]{:S(2)}, u32[]{:S(2)}) collective-permute-start(f32[192,128]{1,0:T(8,128)S(1)} %get-tuple-element.80), channel_id=1, source_target_pairs={{0,8},{8,0},{16,24},{24,16},{1,9},{9,1},{17,25},{25,17},{2,10},{10... | collective-permute-start | bytes 294920 | tf_op jit(solution)/shard_map/ppermute | solution.py:774
  58.6 9.6 %collective-permute-start.14 = (bf16[320,128]{1,0:T(8,128)(2,1)S(1)}, bf16[320,128]{1,0:T(8,128)(2,1)S(1)}, u32[]{:S(2)}, u32[]{:S(2)}) collective-permute-start(bf16[320,128]{1,0:T(8,128)(2,1)S(1)} %shard_map.210.mine_ref), channel_id=1, source_target_pairs={{0,2},{1,3},{2,0},{3,1},{4,6},{5,7},{6,4},{7,5},{8,10},{9,11},{10,... | collective-permute-start | bytes 245768 | tf_op jit(solution)/shard_map/ppermute | solution.py:774
  65.4 9.6 %collective-permute-start.11 = (bf16[512,128]{1,0:T(8,128)(2,1)S(1)}, bf16[512,128]{1,0:T(8,128)(2,1)S(1)}, u32[]{:S(2)}, u32[]{:S(2)}) collective-permute-start(bf16[512,128]{1,0:T(8,128)(2,1)S(1)} %get-tuple-element.77), channel_id=1, source_target_pairs={{0,1},{2,3},{4,5},{6,7},{1,0},{3,2},{5,4},{7,6},{8,9},{10,11},{12,... | collective-permute-start | bytes 393224 | tf_op jit(solution)/shard_map/ppermute | solution.py:770
  66.9 8.1 %collective-permute-start.12 = (bf16[512,128]{1,0:T(8,128)(2,1)S(1)}, bf16[512,128]{1,0:T(8,128)(2,1)S(1)}, u32[]{:S(2)}, u32[]{:S(2)}) collective-permute-start(bf16[512,128]{1,0:T(8,128)(2,1)S(1)} %get-tuple-element.78), channel_id=1, source_target_pairs={{1,2},{3,4},{5,6},{2,1},{4,3},{6,5},{9,10},{11,12},{13,14},{10,9},... | collective-permute-start | bytes 393224 | tf_op jit(solution)/shard_map/ppermute | solution.py:770
  68.2 8.9 %collective-permute-start.15 = (bf16[320,128]{1,0:T(8,128)(2,1)S(1)}, bf16[320,128]{1,0:T(8,128)(2,1)S(1)}, u32[]{:S(2)}, u32[]{:S(2)}) collective-permute-start(bf16[320,128]{1,0:T(8,128)(2,1)S(1)} %shard_map.211.mine_ref), channel_id=1, source_target_pairs={{0,4},{1,5},{2,6},{3,7},{4,0},{5,1},{6,2},{7,3},{8,12},{9,13},{10,... | collective-permute-start | bytes 245768 | tf_op jit(solution)/shard_map/ppermute | solution.py:774
  77.0 7.9 %collective-permute-start.18 = (bf16[320,128]{1,0:T(8,128)(2,1)S(1)}, bf16[320,128]{1,0:T(8,128)(2,1)S(1)}, u32[]{:S(2)}, u32[]{:S(2)}) collective-permute-start(bf16[320,128]{1,0:T(8,128)(2,1)S(1)} %shard_map.212.mine_ref), channel_id=1, source_target_pairs={{0,17},{1,16},{2,19},{3,18},{4,21},{5,20},{6,23},{7,22},{8,25},{9,... | collective-permute-start | bytes 245768 | tf_op jit(solution)/shard_map/ppermute | solution.py:805
  78.4 6.6 %collective-permute-start.17 = (bf16[320,128]{1,0:T(8,128)(2,1)S(1)}, bf16[320,128]{1,0:T(8,128)(2,1)S(1)}, u32[]{:S(2)}, u32[]{:S(2)}) collective-permute-start(bf16[320,128]{1,0:T(8,128)(2,1)S(1)} %shard_map.212.mine_ref), channel_id=1, source_target_pairs={{0,16},{8,24},{16,0},{24,8},{1,17},{9,25},{17,1},{25,9},{2,18},{10... | collective-permute-start | bytes 245768 | tf_op jit(solution)/shard_map/ppermute | solution.py:774
  78.9 6.0 %collective-permute-start.16 = (bf16[320,128]{1,0:T(8,128)(2,1)S(1)}, bf16[320,128]{1,0:T(8,128)(2,1)S(1)}, u32[]{:S(2)}, u32[]{:S(2)}) collective-permute-start(bf16[320,128]{1,0:T(8,128)(2,1)S(1)} %shard_map.212.mine_ref), channel_id=1, source_target_pairs={{0,1},{1,0},{2,3},{3,2},{4,5},{5,4},{6,7},{7,6},{8,9},{9,8},{10,11... | collective-permute-start | bytes 245768 | tf_op jit(solution)/shard_map/ppermute | solution.py:774
  85.0 1.6 %collective-permute-start.19 = (f32[448,128]{1,0:T(8,128)S(1)}, f32[448,128]{1,0:T(8,128)S(1)}, u32[]{:S(2)}, u32[]{:S(2)}) collective-permute-start(f32[448,128]{1,0:T(8,128)S(1)} %shard_map.213.mine_ref), channel_id=1, source_target_pairs={{0,8},{8,0},{16,24},{24,16},{1,9},{9,1},{17,25},{25,17},{2,10},{10... | collective-permute-start | bytes 688136 | tf_op jit(solution)/shard_map/ppermute | solution.py:774
